TPU v7x, 512 devices: a whole 4x8x8 slice. The times are simulated.
512 devices in a mesh: tower: 4 (over y_lo), dp: 128 (over y_hi, z, x, core).
Axes of the slice: x: 4, y: 8 (y_hi: 2, y_lo: 4; y = y_hi * 4 + y_lo), z: 8, core: 2. Of those that a mesh axis runs over, the one named last changes fastest.
Arguments:
- image_in: bfloat16 [1536, 48, 1664], P('dp')
- text_in: bfloat16 [1536, 64, 1280], P('dp')
- proj_img: bfloat16 [1664, 1280], P('dp')
- proj_txt: bfloat16 [1280, 1280], P('dp')
- img_gain: float32 [1664], replicated, may hold values from 0.5 to 1.5
- txt_gain: float32 [1280], replicated, may hold values from 0.5 to 1.5
- logit_scale: float32 [1], replicated, may hold values from 60 to 100
- positive: int32 [1536], P('dp'), may hold values from 0 to 1535, each once
Outputs:
- mean_loss: float32 [1], replicated
- grad_image: bfloat16 [4, 384, 48, 1664], P('tower', 'dp')
- grad_text: bfloat16 [4, 384, 64, 1280], P('tower', 'dp')
Inputs may be any that keep to these rules, and one draw needn't show every extreme that they name: positive is a permutation: every text index appears once.
All inputs are finite; a program needn't handle non-finite values.
Results may differ from a plain program's by a relative error of at most 0.0095.
Values may be sent and summed in bfloat16 or wider, within the bound.
No kernel may reach another device: no remote copies, remote signals or barrier semaphores. Data moves between devices by JAX's collectives and lax.ppermute only.
A program may use at most 128 MiB of HBM per device.

v0:
```python
import jax
import jax.numpy as jnp
from jax import lax
from jax.sharding import PartitionSpec as P


def norm_tokens(token_block, gain_vector):
    values = token_block.astype(jnp.float32)
    center = values - jnp.mean(values, axis=-1, keepdims=True)
    spread = jnp.mean(center * center, axis=-1, keepdims=True)
    return center * lax.rsqrt(spread + 1e-05) * gain_vector


def project_rows(token_block, gain_vector, weight):
    pooled = jnp.mean(norm_tokens(token_block, gain_vector), axis=1).astype(jnp.bfloat16)
    return jnp.dot(pooled, weight, preferred_element_type=jnp.float32)


def unit_rows(projected):
    return projected * lax.rsqrt(jnp.sum(projected * projected, axis=-1, keepdims=True) + 1e-06)


def pooled_back(projected, weight, cotangent):
    _, pull_back = jax.vjp(unit_rows, projected)
    proj_cot = pull_back(cotangent)[0].astype(jnp.bfloat16)
    return lax.dot_general(
        proj_cot, weight, (((1,), (1,)), ((), ())), preferred_element_type=jnp.float32
    )


def token_back(token_block, gain_vector, pool_cot):
    spread_cot = jnp.broadcast_to(pool_cot[:, None, :], token_block.shape)
    _, pull_back = jax.vjp(lambda token_piece: norm_tokens(token_piece, gain_vector), token_block)
    return pull_back(spread_cot)[0]


def log_total(scores, along):
    largest = jnp.max(scores, axis=along, keepdims=True)
    summed = jnp.sum(jnp.exp(scores - largest), axis=along, keepdims=True)
    return jnp.squeeze(largest + jnp.log(summed), axis=along)


def all_weights(proj_img, proj_txt):
    return (
        lax.all_gather(proj_img, "dp", axis=0, tiled=True),
        lax.all_gather(proj_txt, "dp", axis=0, tiled=True),
    )


def per_device(image_in, text_in, proj_img, proj_txt, img_gain, txt_gain, logit_scale, positive):
    tower_index = lax.axis_index("tower")
    group_size = image_in.shape[0]
    quarter = group_size // 4
    image_rows = group_size // 3
    emb_width = proj_img.shape[1]
    image_width = image_in.shape[2]
    text_width = text_in.shape[2]
    logit = logit_scale[0]
    row_start = tower_index * quarter
    img_start = jnp.minimum(tower_index, 2) * image_rows
    img_quarter = lax.dynamic_slice_in_dim(image_in, row_start, quarter, 0)
    txt_quarter = lax.dynamic_slice_in_dim(text_in, row_start, quarter, 0)
    w_img, w_txt = all_weights(proj_img, proj_txt)
    img_block = lax.dynamic_slice_in_dim(image_in, img_start, image_rows, 0)

    def image_side(unused):
        made = project_rows(img_block, img_gain, w_img)
        return (made, jnp.zeros((group_size, emb_width), jnp.float32))

    def text_side(unused):
        made = project_rows(text_in, txt_gain, w_txt)
        return (jnp.zeros((image_rows, emb_width), jnp.float32), made)

    img_projected, txt_projected = lax.cond(tower_index == 3, text_side, image_side, 0)
    img_part = unit_rows(img_projected).astype(jnp.bfloat16)
    txt_part = unit_rows(txt_projected).astype(jnp.bfloat16)
    img_four, txt_four = (
        lax.all_gather(img_part, "tower", axis=0, tiled=True),
        lax.all_gather(txt_part, "tower", axis=0, tiled=True),
    )
    group_img = img_four[:group_size]
    group_txt = txt_four[3 * group_size :]
    all_img, all_txt, all_pos = (
        lax.all_gather(group_img, "dp", axis=0, tiled=True),
        lax.all_gather(group_txt, "dp", axis=0, tiled=True),
        lax.all_gather(positive, "dp", axis=0, tiled=True),
    )
    pairs = all_img.shape[0]
    group_start = lax.axis_index("dp") * group_size
    row_scores = logit * lax.dot_general(
        group_img, all_txt, (((1,), (1,)), ((), ())), preferred_element_type=jnp.float32
    )
    col_scores = logit * lax.dot_general(
        all_img, group_txt, (((1,), (1,)), ((), ())), preferred_element_type=jnp.float32
    )
    row_lse = log_total(row_scores, 1)
    col_lse = log_total(col_scores, 0)
    row_match = (positive[:, None] == lax.iota(jnp.int32, pairs)[None, :]).astype(jnp.float32)
    col_match = (
        all_pos[:, None] == (group_start + lax.iota(jnp.int32, group_size))[None, :]
    ).astype(jnp.float32)
    partial_value = jnp.sum(row_lse) + jnp.sum(col_lse) - 2.0 * jnp.sum(row_match * row_scores)
    every_row, every_col, partials = (
        lax.all_gather(row_lse, "dp", axis=0, tiled=True),
        lax.all_gather(col_lse, "dp", axis=0, tiled=True),
        lax.all_gather(partial_value.reshape(1), "dp", axis=0, tiled=True),
    )
    mean_loss = (jnp.sum(partials) / (2.0 * pairs)).reshape(1)
    row_coef = (
        0.5
        * logit
        * (
            jnp.exp(row_scores - row_lse[:, None])
            + jnp.exp(row_scores - every_col[None, :])
            - 2.0 * row_match
        )
    ).astype(jnp.bfloat16)
    col_coef = (
        0.5
        * logit
        * (
            jnp.exp(col_scores - every_row[:, None])
            + jnp.exp(col_scores - col_lse[None, :])
            - 2.0 * col_match
        )
    ).astype(jnp.bfloat16)
    img_cot = jnp.dot(row_coef, all_txt, preferred_element_type=jnp.float32)
    txt_cot = lax.dot_general(
        col_coef, all_img, (((0,), (0,)), ((), ())), preferred_element_type=jnp.float32
    )

    def image_back(unused):
        cotangent = lax.dynamic_slice_in_dim(img_cot, img_start, image_rows, 0)
        made = pooled_back(img_projected, w_img, cotangent)
        return (made, jnp.zeros((group_size, text_width), jnp.float32))

    def text_back(unused):
        made = pooled_back(txt_projected, w_txt, txt_cot)
        return (jnp.zeros((image_rows, image_width), jnp.float32), made)

    img_back, txt_back = lax.cond(tower_index == 3, text_back, image_back, 0)
    img_four_back, txt_four_back = (
        lax.all_gather(img_back, "tower", axis=0, tiled=True),
        lax.all_gather(txt_back, "tower", axis=0, tiled=True),
    )
    img_pool_cot = lax.dynamic_slice_in_dim(img_four_back[:group_size], row_start, quarter, 0)
    txt_pool_cot = lax.dynamic_slice_in_dim(txt_four_back[3 * group_size :], row_start, quarter, 0)
    img_grads = token_back(img_quarter, img_gain, img_pool_cot)
    txt_grads = token_back(txt_quarter, txt_gain, txt_pool_cot)
    return (mean_loss, img_grads[None], txt_grads[None])


def solution(mesh):
    in_specs = (
        P("dp", None, None),
        P("dp", None, None),
        P("dp", None),
        P("dp", None),
        P(),
        P(),
        P(),
        P("dp"),
    )
    out_specs = (P(), P("tower", "dp", None, None), P("tower", "dp", None, None))
    return jax.shard_map(
        per_device, mesh=mesh, in_specs=in_specs, out_specs=out_specs, check_vma=False
    )
```

profile of v0, /device:TPU:1, one launch (start us, length us, event | category | flops | bytes accessed | tf_op | source)
XLA Modules:
  0.0 1458.3 jit_solution(197053829267960303)
XLA Ops:
  8.7 152.5 %all-gather.15.cloned.1.call-done = bf16[128,10,1280]{2,1,0:T(8,128)(2,1)} async-done(((bf16[1,10,1280]{2,1,0:T(8,128)(2,1)}), bf16[128,10,1280]{2,1,0:T(8,128)(2,1)}) %all-gather.15.cloned.1.call-update) | async-done | bytes 3276816 | tf_op jit(solution)/shard_map/all_gather | solution.py:46
  161.2 7.0 reshape.173
  168.3 133.3 %all-gather.13.cloned.1.call-done = bf16[128,13,1280]{2,1,0:T(8,128)(2,1)} async-done(((bf16[1,13,1280]{2,1,0:T(8,128)(2,1)}), bf16[128,13,1280]{2,1,0:T(8,128)(2,1)}) %all-gather.13.cloned.1.call-update) | async-done | bytes 4259856 | tf_op jit(solution)/shard_map/all_gather | solution.py:45
  301.5 7.4 reshape.171
  309.0 7.2 conditional.2
  311.6 1.5 fusion.4
  313.1 3.0 multiply_reduce_fusion
  316.2 10.2 all-gather.2
  327.4 11.1 all-gather.3
  342.0 22.2 %all-reduce.3 = s32[1536]{0:T(1024)S(1)} all-reduce(s32[1536]{0:T(1024)S(1)} %dynamic-update-slice.3), channel_id=1, replica_groups=mesh['tower'=4,'dp'=128] {'dp'}, use_global_device_ids=true, to_apply=%add.3 | all-reduce | flops 1536 | bytes 12288
  365.6 100.5 %all-gather.19.cloned.1.call-done = bf16[128,12,1280]{2,1,0:T(8,128)(2,1)} async-done(((bf16[1,12,1280]{2,1,0:T(8,128)(2,1)}), bf16[128,12,1280]{2,1,0:T(8,128)(2,1)}) %all-gather.19.cloned.1.call-update) | async-done | bytes 3932176 | tf_op jit(solution)/shard_map/all_gather | solution.py:84
  466.1 7.0 reshape.181
  473.1 3.3 fusion.67
  477.4 129.4 %all-gather.17.cloned.1.call-done = bf16[128,12,1280]{2,1,0:T(8,128)(2,1)} async-done(((bf16[1,12,1280]{2,1,0:T(8,128)(2,1)}), bf16[128,12,1280]{2,1,0:T(8,128)(2,1)}) %all-gather.17.cloned.1.call-update) | async-done | bytes 3932176 | tf_op jit(solution)/shard_map/all_gather | solution.py:85
  606.8 7.1 reshape.179
  613.9 3.3 fusion.66
  621.3 788.5 %all-reduce.4 = (f32[128]{0:T(128)S(1)}, f32[1536]{0:T(1024)S(1)}, f32[1536]{0:T(1024)S(1)}) all-reduce(f32[128]{0:T(128)S(1)} %dynamic-update-slice, f32[1536]{0:T(1024)S(1)} %get-tuple-element.116, f32[1536]{0:T(1024)S(1)} %get-tuple-element.114), channel_id=1, replica_groups=mesh['tower'=4,'dp'=128] {'dp'}, use_global_device_ids=true, to_apply=%add | all-reduce | flops 3200 | bytes 25600
  1409.8 2.9 fusion.40
  1413.8 3.6 conditional.3
  1414.0 3.4 fusion.17
  1417.4 14.2 all-gather.7
  1433.5 10.8 all-gather.6
  1445.8 1.4 fusion.36
  1447.2 2.1 fusion.38
  (68 shorter events, 17.0 us)
Async XLA Ops:
  7.2 154.0 %all-gather.15.cloned.1.call-start = ((), (), s32[]{:S(2)}) async-start(), calls=%async_computation.1 | async-start | bytes 5283840 | tf_op jit(solution)/shard_map/all_gather | solution.py:46
  7.9 293.6 %all-gather.13.cloned.1.call-start = ((), (), s32[]{:S(2)}) async-start(), calls=%async_computation | async-start | bytes 5283840 | tf_op jit(solution)/shard_map/all_gather | solution.py:45
  8.6 457.4 %all-gather.19.cloned.1.call-start = ((), (), s32[]{:S(2)}) async-start(), calls=%async_computation.3 | async-start | bytes 5283840 | tf_op jit(solution)/shard_map/all_gather | solution.py:84
  168.2 140.7 %copy-start.1 = (bf16[12,64,1280]{2,1,0:T(8,128)(2,1)S(1)}, bf16[12,64,1280]{2,1,0:T(8,128)(2,1)}, u32[]{:S(2)}) copy-start(bf16[12,64,1280]{2,1,0:T(8,128)(2,1)} %param.13) | copy-start | bytes 5898244
  168.2 140.7 %copy-start.3 = (f32[1280]{0:T(1024)S(1)}, f32[1280]{0:T(1024)}, u32[]{:S(2)}) copy-start(f32[1280]{0:T(1024)} %param.17) | copy-start | bytes 15364
  168.2 140.7 %copy-start.4 = (f32[1664]{0:T(1024)S(1)}, f32[1664]{0:T(1024)}, u32[]{:S(2)}) copy-start(f32[1664]{0:T(1024)} %param.16) | copy-start | bytes 19972
  308.9 32.8 %copy-start.5 = (s32[12]{0:T(128)S(1)}, s32[12]{0:T(128)}, u32[]{:S(2)}) copy-start(s32[12]{0:T(128)} %param.19) | copy-start | bytes 148
  327.2 279.7 %all-gather.17.cloned.1.call-start = ((), (), s32[]{:S(2)}) async-start(), calls=%async_computation.2 | async-start | bytes 5283840 | tf_op jit(solution)/shard_map/all_gather | solution.py:85
  1409.8 3.3 copy-start
Sparse Core Ops, SparseCore 0:
  12.5 148.6 all-gather.14
  165.7 135.8 all-gather.12
  327.3 138.7 all-gather.18
  471.0 135.8 all-gather.16
where the time goes:
time: 1470 us; the launch traced here: 1460 us
  blocking collectives  857 us (58%)
  waiting for transfers between devices  517 us (35%)
  local copies, waits for them, and re-layouts  32.6 us (2%)
  between operations  18.9 us (1%)
  matrix products  16.7 us (1%)
  other arithmetic  15.7 us (1%)
    unnamed x2, blocking collectives  811 us
    all_gather x1, waiting for transfers between devices, all_weights(): lax.all_gather(proj_txt, 'dp', axis=0, tiled=True)  153 us
    all_gather x1, waiting for transfers between devices, all_weights(): lax.all_gather(proj_img, 'dp', axis=0, tiled=True)  133 us
    all_gather x1, waiting for transfers between devices, per_device(): lax.all_gather(group_txt, 'dp', axis=0, tiled=True)  129 us
    all_gather x1, waiting for transfers between devices, per_device(): lax.all_gather(group_img, 'dp', axis=0, tiled=True)  100 us
    unnamed x22, local copies, waits for them, and re-layouts  31.8 us
  transfers between devices with their start and end apart: 4, of which 4 were waited for; matrix products, arithmetic and copies ran while one was open for 2% of the time, Pallas kernels for 0%

commit v1 on v0

v1 whole, which is shorter than its diff:
```python
import jax
import jax.numpy as jnp
from jax import lax
from jax.sharding import Mesh, PartitionSpec as P

BF = jnp.bfloat16
F32 = jnp.float32
Y = ("h", "t")
ZX = ("z", "x")
ZXC = ("z", "x", "c")
DP = ("h", "z", "x", "c")


def norm_tokens(token_block, gain_vector):
    values = token_block.astype(F32)
    center = values - jnp.mean(values, axis=-1, keepdims=True)
    spread = jnp.mean(center * center, axis=-1, keepdims=True)
    return center * lax.rsqrt(spread + 1e-05) * gain_vector


def token_back(token_block, gain_vector, pool_cot):
    spread_cot = jnp.broadcast_to(pool_cot[:, None, :], token_block.shape)
    _, pull_back = jax.vjp(lambda token_piece: norm_tokens(token_piece, gain_vector), token_block)
    return pull_back(spread_cot)[0]


def exchange(blocks, axes):
    return lax.all_to_all(blocks, axes, 0, 0, tiled=True)


def spread_to(block, axes, count):
    return exchange(jnp.broadcast_to(block[None], (count,) + block.shape), axes)


def both_cores(blocks):
    half = blocks.shape[0] // 2
    parts = [lax.all_gather(part, "c", axis=0) for part in (blocks[:half], blocks[half:])]
    return jnp.concatenate(parts, axis=1)


def per_device(image_in, text_in, proj_img, proj_txt, img_gain, txt_gain, logit_scale, positive):
    t_index = lax.axis_index("t")
    h_index = lax.axis_index("h")
    g_index = (lax.axis_index("z") * 4 + lax.axis_index("x")) * 2 + lax.axis_index("c")
    logit = logit_scale[0]
    emb = proj_img.shape[1]
    slab_i, slab_t = proj_img.shape[0], proj_txt.shape[0]
    half_i, half_t = slab_i * 64, slab_t * 64
    own = h_index * 12 + t_index * 3

    w = jnp.pad(jnp.concatenate([proj_img, proj_txt], 0), ((0, 1), (0, 256)))
    w = lax.dynamic_slice(w, (0, 384 * t_index), (24, 384))
    w = both_cores(spread_to(w, ZX, 32)).transpose(1, 0, 2, 3)
    w_img = w[:, :, :slab_i].reshape(half_i, 384)
    w_txt = w[:, :, slab_i : slab_i + slab_t].reshape(half_t, 384)

    pooled_i = jnp.mean(norm_tokens(image_in, img_gain), axis=1).astype(BF)
    pooled_t = jnp.mean(norm_tokens(text_in, txt_gain), axis=1).astype(BF)

    def feature_half(which):
        return jnp.concatenate(
            [
                lax.dynamic_slice(pooled_i, (0, half_i * which), (12, half_i)),
                lax.dynamic_slice(pooled_t, (0, half_t * which), (12, half_t)),
            ],
            1,
        )

    mine = feature_half(h_index)
    theirs = lax.ppermute(feature_half(1 - h_index), "h", [(0, 1), (1, 0)])
    first = h_index == 0
    pooled = jnp.concatenate([jnp.where(first, mine, theirs), jnp.where(first, theirs, mine)], 0)

    part = jnp.concatenate(
        [
            jnp.dot(pooled[:, :half_i], w_img, preferred_element_type=F32),
            jnp.dot(pooled[:, half_i:], w_txt, preferred_element_type=F32),
        ],
        0,
    ).astype(BF)
    parts = spread_to(part, Y, 8).astype(F32)
    parts = parts[:4] + parts[4:]
    projected = jnp.concatenate([parts[k] for k in range(4)], 1)
    inv = lax.rsqrt(jnp.sum(projected * projected, axis=-1, keepdims=True) + 1e-06)
    unit = projected * inv
    rows = unit[:, :emb].astype(BF)

    blank = jnp.zeros((1, emb), BF)
    block = jnp.concatenate(
        [
            lax.dynamic_slice(rows, (own, 0), (3, emb)),
            blank,
            lax.dynamic_slice(rows, (24 + own, 0), (3, emb)),
            blank,
        ],
        0,
    )
    items = both_cores(spread_to(block, ZX, 32)).reshape(512, emb)
    scores = logit * lax.dot_general(
        rows, items, (((1,), (1,)), ((), ())), preferred_element_type=F32
    )

    place = lax.iota(jnp.int32, 512)
    item_g = ((place // 8) % 32) * 2 + place // 256
    item_pair = (h_index * 64 + item_g) * 12 + 3 * t_index + place % 4
    item_txt = (place % 8) // 4 == 1
    item_real = place % 4 < 3
    row = lax.iota(jnp.int32, 48)
    row_txt = row >= 24
    row_pair = (((row // 12) % 2) * 64 + g_index) * 12 + row % 12
    valid = (row_txt[:, None] != item_txt[None, :]) & item_real[None, :]
    valid_scores = jnp.where(valid, scores, -1e30)
    top = jnp.max(valid_scores, axis=1)
    total = jnp.sum(jnp.exp(valid_scores - top[:, None]), axis=1)

    seen = spread_to(
        jnp.stack([top, total, jnp.pad(positive.astype(F32), (0, 36))]), Y, 8
    )
    every_top = jnp.max(seen[:, 0], axis=0)
    row_lse = every_top + jnp.log(
        jnp.sum(seen[:, 1] * jnp.exp(seen[:, 0] - every_top[None]), axis=0)
    )
    row_pos = jnp.concatenate([seen[0, 2, :12], seen[4, 2, :12], jnp.full((24,), -1.0)])
    img_match = valid & (row_pos[:, None] == item_pair[None, :].astype(F32))
    img_lse = lax.dynamic_slice(row_lse, (own,), (3,))
    txt_lse = lax.dynamic_slice(row_lse, (24 + own,), (3,))
    part_value = (
        jnp.sum(img_lse) + jnp.sum(txt_lse) - 2.0 * jnp.sum(jnp.where(img_match, scores, 0.0))
    )
    zero = jnp.zeros((1,), F32)
    own_pos = lax.dynamic_slice(positive, (3 * t_index,), (3,)).astype(F32)
    told = spread_to(
        jnp.concatenate(
            [img_lse, zero, txt_lse, zero, own_pos, zero, part_value[None], jnp.zeros((115,), F32)]
        )[None],
        ZXC,
        64,
    )[:, 0]
    item_lse = told[:, :8].reshape(32, 2, 8).transpose(1, 0, 2).reshape(512)
    item_pos = jnp.pad(told[:, 8:12], ((0, 0), (0, 4)), constant_values=-1.0)
    item_pos = item_pos.reshape(32, 2, 8).transpose(1, 0, 2).reshape(512)
    y_value = jnp.sum(told[:, 12])

    match = img_match | (
        valid
        & row_txt[:, None]
        & (item_pos[None, :] == row_pair[:, None].astype(F32))
    )
    coef = (
        0.5
        * logit
        * (
            jnp.exp(valid_scores - row_lse[:, None])
            + jnp.exp(jnp.where(valid, scores - item_lse[None, :], -1e30))
            - 2.0 * match.astype(F32)
        )
    ).astype(BF)
    along = jnp.sum(coef.astype(F32) * scores, axis=1) / logit
    cot = jnp.dot(coef, items, preferred_element_type=F32).astype(BF)
    cot = jnp.pad(cot, ((0, 0), (0, 256)))

    def two_parts(values):
        high = values.astype(BF)
        return high, (values - high.astype(F32)).astype(BF)

    along_high, along_low = two_parts(along)
    value_high, value_low = two_parts(jnp.broadcast_to(y_value[None], (48,)))
    extra = jnp.pad(
        jnp.stack([along_high, along_low, value_high, value_low]), ((0, 4), (0, 336))
    )
    sent = jnp.stack(
        [jnp.concatenate([cot[:, 384 * k : 384 * k + 384], extra], 0) for k in (0, 1, 2, 3)] * 2
    )
    summed = jnp.sum(exchange(sent, Y).astype(F32), axis=0)
    along = summed[48, :48] + summed[49, :48]
    mean_loss = ((summed[50, :1] + summed[51, :1]) / (2.0 * 1536)).reshape(1)

    unit_part = lax.dynamic_slice(unit, (0, 384 * t_index), (48, 384))
    proj_cot = (inv * (summed[:48] - unit_part * along[:, None])).astype(BF)
    back = (((1,), (1,)), ((), ()))
    pool = jnp.concatenate(
        [
            lax.dot_general(proj_cot[:24], w_img, back, preferred_element_type=F32),
            lax.dot_general(proj_cot[24:], w_txt, back, preferred_element_type=F32),
        ],
        1,
    ).astype(BF)
    pool = exchange(pool.reshape(8, 3, half_i + half_t), Y).astype(F32)
    pool = jnp.sum(pool.reshape(2, 4, 3, half_i + half_t), axis=1)
    img_pool_cot = jnp.concatenate([pool[0, :, :half_i], pool[1, :, :half_i]], 1)
    txt_pool_cot = jnp.concatenate([pool[0, :, half_i:], pool[1, :, half_i:]], 1)
    img_own = lax.dynamic_slice_in_dim(image_in, 3 * t_index, 3, 0)
    txt_own = lax.dynamic_slice_in_dim(text_in, 3 * t_index, 3, 0)
    img_grads = token_back(img_own, img_gain, img_pool_cot)
    txt_grads = token_back(txt_own, txt_gain, txt_pool_cot)
    return (mean_loss, img_grads[None], txt_grads[None])


def solution(mesh):
    fine = Mesh(mesh.devices.reshape(4, 2, 8, 4, 2), ("t", "h", "z", "x", "c"))
    in_specs = (
        P(DP, None, None),
        P(DP, None, None),
        P(DP, None),
        P(DP, None),
        P(),
        P(),
        P(),
        P(DP),
    )
    out_specs = (P(), P("t", DP, None, None), P("t", DP, None, None))
    return jax.shard_map(
        per_device, mesh=fine, in_specs=in_specs, out_specs=out_specs, check_vma=False
    )
```

time: 1470 us -> 187 us (0.13)
  blocking collectives: 857 us -> 13.4 us
  waiting for transfers between devices: 517 us -> 62.7 us
  starting transfers between devices: 0.16 us -> 55.4 us
  local copies, waits for them, and re-layouts: 32.6 us -> 12.2 us
    unnamed x2 -> x0, blocking collectives: 811 us -> none
    all_gather x4 -> x0, waiting for transfers between devices: 516 us -> none  [the longest x1 153 us: all_weights(): lax.all_gather(proj_txt, 'dp', axis=0, tiled=True)]
    all_to_all x0 -> x7, waiting for transfers between devices: none -> 61.2 us  [exchange(): return lax.all_to_all(blocks, axes, 0, 0, tiled=True)]
    all_to_all x0 -> x7, starting transfers between devices: none -> 48 us  [exchange(): return lax.all_to_all(blocks, axes, 0, 0, tiled=True)]
    all_gather x4, blocking collectives: 46.4 us -> 13.4 us  [both_cores(): lax.all_gather(part, 'c', axis=0)]
    unnamed x22 -> x30, local copies, waits for them, and re-layouts: 31.8 us -> 1.53 us
  transfers between devices with their start and end apart: 4 -> 8, of which waited for: 4 -> 7; matrix products, arithmetic and copies ran while one was open for 2% -> 7% of each run, Pallas kernels for 0% -> 0%
where the time goes in v1:
time: 187 us; the launch traced here: 186 us
  waiting for transfers between devices  62.7 us (34%)
  starting transfers between devices  55.4 us (30%)
  other arithmetic  28.9 us (15%)
  blocking collectives  13.4 us (7%)
  local copies, waits for them, and re-layouts  12.2 us (7%)
  between operations  7.54 us (4%)
  matrix products  5.87 us (3%)
    all_to_all x7, waiting for transfers between devices, exchange(): return lax.all_to_all(blocks, axes, 0, 0, tiled=True)  61.2 us
    all_to_all x7, starting transfers between devices, exchange(): return lax.all_to_all(blocks, axes, 0, 0, tiled=True)  48 us
    all_gather x4, blocking collectives, both_cores(): lax.all_gather(part, 'c', axis=0)  13.4 us
    ppermute x1, starting transfers between devices, per_device(): theirs = lax.ppermute(feature_half(1 - h_index), 'h', [(0, 1), (1, 0)])  7.44 us
    reduce_sum x6, other arithmetic, norm_tokens(): center = values - jnp.mean(values, axis=-1, keepdims=True)  5.02 us
    reduce_sum x4, other arithmetic, norm_tokens(): spread = jnp.mean(center * center, axis=-1, keepdims=True)  4.52 us
    unnamed x7, other arithmetic  4.37 us
  transfers between devices with their start and end apart: 8, of which 7 were waited for; matrix products, arithmetic and copies ran while one was open for 7% of the time, Pallas kernels for 0%

profile of v1, /device:TPU:1, one launch (start us, length us, event | category | flops | bytes accessed | tf_op | source)
XLA Modules:
  0.0 186.0 jit_solution(3000064283237915213)
XLA Ops:
  2.3 13.7 %all-to-all-start = ((bf16[32,24,384]{2,1,0:T(8,128)(2,1)}), bf16[32,24,384]{2,1,0:T(8,128)(2,1)S(1)}, u32[]{:S(2)}, u32[]{:S(2)}) async-start(bf16[32,24,384]{2,1,0:T(8,128)(2,1)} %broadcast_in_dim.42), calls=%async_computation | async-start | bytes 1179648 | tf_op jit(solution)/shard_map/all_to_all | solution.py:28
  16.1 2.0 %convert_reduce_fusion.1 = f32[12,48]{1,0:T(8,128)S(1)} fusion(bf16[12,48,1664]{2,1,0:T(8,128)(2,1)} %param.8), kind=kLoop, calls=%fused_computation.3 | loop fusion | flops 1916352 | bytes 1919232 | tf_op jit(solution)/shard_map/reduce_sum | solution.py:16
  18.1 2.2 %fusion.7 = f32[12,48]{1,0:T(8,128)S(1)} fusion(bf16[12,48,1664]{2,1,0:T(8,128)(2,1)} %param.8, f32[12,48]{1,0:T(8,128)S(1)} %broadcast_multiply_fusion.1), kind=kLoop, calls=%fused_computation.11 | loop fusion | flops 3833280 | bytes 1921536 | tf_op jit(solution)/shard_map/reduce_sum | solution.py:17
  22.3 2.4 %fusion.9 = f32[12,1664]{1,0:T(8,128)S(1)} fusion(bf16[12,48,1664]{2,1,0:T(8,128)(2,1)} %param.8, f32[1664]{0:T(1024)S(1)} %copy-done.8, f32[12,48]{1,0:T(8,128)S(1)} %add_rsqrt_fusion.1, f32[12,48]{1,0:T(8,128)S(1)} %broadcast_multiply_fusion.1), kind=kLoop, calls=%fused_computation.13 | loop fusion | flops 4772352 | bytes 2008064 | tf_op jit(solution)/shard_map/reduce_sum | solution.py:57
  25.0 7.4 %collective-permute-start = (bf16[12,1472]{1,0:T(8,128)(2,1)S(1)}, bf16[12,1472]{1,0:T(8,128)(2,1)S(1)}, u32[]{:S(2)}, u32[]{:S(2)}) collective-permute-start(bf16[12,1472]{1,0:T(8,128)(2,1)S(1)} %pad_maximum_fusion.4), channel_id=1, source_target_pairs={{0,64},{64,0},{1,65},{65,1},{2,66},{66,2},{3,67},{67,3},{4,68},{68... | collective-permute-start | bytes 105992 | tf_op jit(solution)/shard_map/ppermute | solution.py:70
  32.4 1.5 collective-permute-done
  34.7 3.8 %all-gather = bf16[32,24,384]{2,1,0:T(8,128)(2,1)S(1)} all-gather(bf16[16,24,384]{2,1,0:T(8,128)(2,1)S(1)} %get-tuple-element.15), channel_id=2, replica_groups=mesh['t'=4,'h'=2,'z'=8,'x'=4,'c'=2] {'c'}, dimensions={0}, use_global_device_ids=true | all-gather | bytes 884736 | tf_op jit(solution)/shard_map/all_gather | solution.py:37
  38.5 2.2 %all-gather.1 = bf16[32,24,384]{2,1,0:T(8,128)(2,1)S(1)} all-gather(bf16[16,24,384]{2,1,0:T(8,128)(2,1)S(1)} %get-tuple-element.16), channel_id=3, replica_groups=mesh['t'=4,'h'=2,'z'=8,'x'=4,'c'=2] {'c'}, dimensions={0}, use_global_device_ids=true | all-gather | bytes 884736 | tf_op jit(solution)/shard_map/all_gather | solution.py:37
  44.9 1.3 convolution_convert_fusion.3
  47.0 7.3 %all-to-all-start.1 = ((bf16[8,48,384]{2,1,0:T(8,128)(2,1)}), bf16[8,48,384]{2,1,0:T(8,128)(2,1)S(1)}, u32[]{:S(2)}, u32[]{:S(2)}) async-start(bf16[8,48,384]{2,1,0:T(8,128)(2,1)} %broadcast_in_dim.43), calls=%async_computation.1 | async-start | bytes 589824 | tf_op jit(solution)/shard_map/all_to_all | solution.py:28
  54.3 12.4 %all-to-all-done.1 = bf16[8,48,384]{2,1,0:T(8,128)(2,1)S(1)} async-done(((bf16[8,48,384]{2,1,0:T(8,128)(2,1)}), bf16[8,48,384]{2,1,0:T(8,128)(2,1)S(1)}, u32[]{:S(2)}, u32[]{:S(2)}) %all-to-all-start.1) | async-done | bytes 294944 | tf_op jit(solution)/shard_map/all_to_all | solution.py:28
  68.8 9.5 %all-to-all-start.2 = ((bf16[32,8,1280]{2,1,0:T(8,128)(2,1)}), bf16[32,8,1280]{2,1,0:T(8,128)(2,1)S(1)}, u32[]{:S(2)}, u32[]{:S(2)}) async-start(bf16[32,8,1280]{2,1,0:T(8,128)(2,1)} %broadcast_in_dim.45), calls=%async_computation.2 | async-start | bytes 1310720 | tf_op jit(solution)/shard_map/all_to_all | solution.py:28
  79.1 17.3 %all-to-all-done.2 = bf16[32,8,1280]{2,1,0:T(8,128)(2,1)S(1)} async-done(((bf16[32,8,1280]{2,1,0:T(8,128)(2,1)}), bf16[32,8,1280]{2,1,0:T(8,128)(2,1)S(1)}, u32[]{:S(2)}, u32[]{:S(2)}) %all-to-all-start.2) | async-done | bytes 655392 | tf_op jit(solution)/shard_map/all_to_all | solution.py:28
  96.4 5.0 %all-gather.2 = bf16[32,8,1280]{2,1,0:T(8,128)(2,1)S(1)} all-gather(bf16[16,8,1280]{2,1,0:T(8,128)(2,1)S(1)} %get-tuple-element.13), channel_id=4, replica_groups=mesh['t'=4,'h'=2,'z'=8,'x'=4,'c'=2] {'c'}, dimensions={0}, use_global_device_ids=true | all-gather | bytes 983040 | tf_op jit(solution)/shard_map/all_gather | solution.py:37
  101.5 2.4 %all-gather.3 = bf16[32,8,1280]{2,1,0:T(8,128)(2,1)S(1)} all-gather(bf16[16,8,1280]{2,1,0:T(8,128)(2,1)S(1)} %get-tuple-element.14), channel_id=5, replica_groups=mesh['t'=4,'h'=2,'z'=8,'x'=4,'c'=2] {'c'}, dimensions={0}, use_global_device_ids=true | all-gather | bytes 983040 | tf_op jit(solution)/shard_map/all_gather | solution.py:37
  105.5 3.3 %all-to-all-start.3 = ((f32[8,1,144]{2,1,0:T(1,128)}), f32[8,1,144]{2,1,0:T(1,128)S(1)}, u32[]{:S(2)}, u32[]{:S(2)}) async-start(f32[8,1,144]{2,1,0:T(1,128)} %reshape.318), calls=%async_computation.3 | async-start | bytes 16384 | tf_op jit(solution)/shard_map/all_to_all | solution.py:28
  108.9 6.4 %all-to-all-done.3 = f32[8,1,144]{2,1,0:T(1,128)S(1)} async-done(((f32[8,1,144]{2,1,0:T(1,128)}), f32[8,1,144]{2,1,0:T(1,128)S(1)}, u32[]{:S(2)}, u32[]{:S(2)}) %all-to-all-start.3) | async-done | bytes 4640 | tf_op jit(solution)/shard_map/all_to_all | solution.py:28
  120.9 6.7 %all-to-all-start.4 = ((f32[64,1,128]{2,1,0:T(1,128)}), f32[64,1,128]{2,1,0:T(1,128)S(1)}, u32[]{:S(2)}, u32[]{:S(2)}) async-start(f32[64,1,128]{2,1,0:T(1,128)} %broadcast_in_dim.51), calls=%async_computation.4 | async-start | bytes 65536 | tf_op jit(solution)/shard_map/all_to_all | solution.py:28
  127.6 9.3 %all-to-all-done.4 = f32[64,1,128]{2,1,0:T(1,128)S(1)} async-done(((f32[64,1,128]{2,1,0:T(1,128)}), f32[64,1,128]{2,1,0:T(1,128)S(1)}, u32[]{:S(2)}, u32[]{:S(2)}) %all-to-all-start.4) | async-done | bytes 32800 | tf_op jit(solution)/shard_map/all_to_all | solution.py:28
  146.7 4.1 %all-to-all-start.5 = ((bf16[8,56,384]{2,1,0:T(8,128)(2,1)}), bf16[8,56,384]{2,1,0:T(8,128)(2,1)}, u32[]{:S(2)}, u32[]{:S(2)}) async-start(bf16[8,56,384]{2,1,0:T(8,128)(2,1)} %fusion.49), calls=%async_computation.5 | async-start | bytes 688128 | tf_op jit(solution)/shard_map/all_to_all | solution.py:28
  154.4 10.2 %all-to-all-done.5 = bf16[8,56,384]{2,1,0:T(8,128)(2,1)} async-done(((bf16[8,56,384]{2,1,0:T(8,128)(2,1)}), bf16[8,56,384]{2,1,0:T(8,128)(2,1)}, u32[]{:S(2)}, u32[]{:S(2)}) %all-to-all-start.5) | async-done | bytes 344096 | tf_op jit(solution)/shard_map/all_to_all | solution.py:28
  169.1 3.4 %all-to-all-start.6 = ((bf16[8,3,1472]{2,1,0:T(4,128)(2,1)}), bf16[8,3,1472]{2,1,0:T(4,128)(2,1)S(1)}, u32[]{:S(2)}, u32[]{:S(2)}) async-start(bf16[8,3,1472]{2,1,0:T(4,128)(2,1)} %copy.31), calls=%async_computation.6 | async-start | bytes 196608 | tf_op jit(solution)/shard_map/all_to_all | solution.py:28
  174.3 5.5 %all-to-all-done.6 = bf16[8,3,1472]{2,1,0:T(4,128)(2,1)S(1)} async-done(((bf16[8,3,1472]{2,1,0:T(4,128)(2,1)}), bf16[8,3,1472]{2,1,0:T(4,128)(2,1)S(1)}, u32[]{:S(2)}, u32[]{:S(2)}) %all-to-all-start.6) | async-done | bytes 70688 | tf_op jit(solution)/shard_map/all_to_all | solution.py:28
  180.9 1.4 fusion.16
  (149 shorter events, 37.6 us)
Async XLA Ops:
  2.3 32.3 %all-to-all-start = ((bf16[32,24,384]{2,1,0:T(8,128)(2,1)}), bf16[32,24,384]{2,1,0:T(8,128)(2,1)S(1)}, u32[]{:S(2)}, u32[]{:S(2)}) async-start(bf16[32,24,384]{2,1,0:T(8,128)(2,1)} %broadcast_in_dim.42), calls=%async_computation | async-start | bytes 1179648 | tf_op jit(solution)/shard_map/all_to_all | solution.py:28
  16.0 4.2 %copy-start = (bf16[12,64,1280]{2,1,0:T(8,128)(2,1)S(1)}, bf16[12,64,1280]{2,1,0:T(8,128)(2,1)}, u32[]{:S(2)}) copy-start(bf16[12,64,1280]{2,1,0:T(8,128)(2,1)} %param.9) | copy-start | bytes 5898244
  20.2 1.0 copy-start.9
  20.6 1.7 copy-start.8
  25.0 9.0 %collective-permute-start = (bf16[12,1472]{1,0:T(8,128)(2,1)S(1)}, bf16[12,1472]{1,0:T(8,128)(2,1)S(1)}, u32[]{:S(2)}, u32[]{:S(2)}) collective-permute-start(bf16[12,1472]{1,0:T(8,128)(2,1)S(1)} %pad_maximum_fusion.4), channel_id=1, source_target_pairs={{0,64},{64,0},{1,65},{65,1},{2,66},{66,2},{3,67},{67,3},{4,68},{68... | collective-permute-start | bytes 105992 | tf_op jit(solution)/shard_map/ppermute | solution.py:70
  41.3 2.3 %copy-start.4 = (bf16[32,2,13,384]{3,2,1,0:T(8,128)(2,1)}, bf16[32,2,13,384]{3,2,1,0:T(8,128)(2,1)S(1)}, u32[]{:S(2)}) copy-start(bf16[32,2,13,384]{3,2,1,0:T(8,128)(2,1)S(1)} %copy.24) | copy-start | bytes 1916932
  41.4 4.9 %copy-start.2 = (bf16[32,2,10,384]{3,2,1,0:T(8,128)(2,1)}, bf16[32,2,10,384]{3,2,1,0:T(8,128)(2,1)S(1)}, u32[]{:S(2)}) copy-start(bf16[32,2,10,384]{3,2,1,0:T(8,128)(2,1)S(1)} %copy.25) | copy-start | bytes 1474564
  47.0 19.7 %all-to-all-start.1 = ((bf16[8,48,384]{2,1,0:T(8,128)(2,1)}), bf16[8,48,384]{2,1,0:T(8,128)(2,1)S(1)}, u32[]{:S(2)}, u32[]{:S(2)}) async-start(bf16[8,48,384]{2,1,0:T(8,128)(2,1)} %broadcast_in_dim.43), calls=%async_computation.1 | async-start | bytes 589824 | tf_op jit(solution)/shard_map/all_to_all | solution.py:28
  66.8 12.2 %copy-start.13 = (s32[12]{0:T(128)S(1)}, s32[12]{0:T(128)}, u32[]{:S(2)}) copy-start(s32[12]{0:T(128)} %param.15) | copy-start | bytes 148
  67.0 0.9 copy-start.12
  67.1 0.7 copy-start.6
  68.8 27.5 %all-to-all-start.2 = ((bf16[32,8,1280]{2,1,0:T(8,128)(2,1)}), bf16[32,8,1280]{2,1,0:T(8,128)(2,1)S(1)}, u32[]{:S(2)}, u32[]{:S(2)}) async-start(bf16[32,8,1280]{2,1,0:T(8,128)(2,1)} %broadcast_in_dim.45), calls=%async_computation.2 | async-start | bytes 1310720 | tf_op jit(solution)/shard_map/all_to_all | solution.py:28
  101.5 2.5 %copy-start.7 = (f32[48,1536]{1,0:T(8,128)S(1)}, f32[48,1536]{1,0:T(8,128)}, u32[]{:S(2)}) copy-start(f32[48,1536]{1,0:T(8,128)} %copy-done.6) | copy-start | bytes 884740
  105.5 9.9 %all-to-all-start.3 = ((f32[8,1,144]{2,1,0:T(1,128)}), f32[8,1,144]{2,1,0:T(1,128)S(1)}, u32[]{:S(2)}, u32[]{:S(2)}) async-start(f32[8,1,144]{2,1,0:T(1,128)} %reshape.318), calls=%async_computation.3 | async-start | bytes 16384 | tf_op jit(solution)/shard_map/all_to_all | solution.py:28
  120.9 16.0 %all-to-all-start.4 = ((f32[64,1,128]{2,1,0:T(1,128)}), f32[64,1,128]{2,1,0:T(1,128)S(1)}, u32[]{:S(2)}, u32[]{:S(2)}) async-start(f32[64,1,128]{2,1,0:T(1,128)} %broadcast_in_dim.51), calls=%async_computation.4 | async-start | bytes 65536 | tf_op jit(solution)/shard_map/all_to_all | solution.py:28
  138.9 14.3 %copy-start.3 = (bf16[32,2,10,384]{3,2,1,0:T(8,128)(2,1)S(1)}, bf16[32,2,10,384]{3,2,1,0:T(8,128)(2,1)}, u32[]{:S(2)}) copy-start(bf16[32,2,10,384]{3,2,1,0:T(8,128)(2,1)} %copy-done.2) | copy-start | bytes 1474564
  140.7 13.5 %copy-start.5 = (bf16[32,2,13,384]{3,2,1,0:T(8,128)(2,1)S(1)}, bf16[32,2,13,384]{3,2,1,0:T(8,128)(2,1)}, u32[]{:S(2)}) copy-start(bf16[32,2,13,384]{3,2,1,0:T(8,128)(2,1)} %copy-done.4) | copy-start | bytes 1916932
  146.7 18.0 %all-to-all-start.5 = ((bf16[8,56,384]{2,1,0:T(8,128)(2,1)}), bf16[8,56,384]{2,1,0:T(8,128)(2,1)}, u32[]{:S(2)}, u32[]{:S(2)}) async-start(bf16[8,56,384]{2,1,0:T(8,128)(2,1)} %fusion.49), calls=%async_computation.5 | async-start | bytes 688128 | tf_op jit(solution)/shard_map/all_to_all | solution.py:28
  154.4 18.1 %copy-start.11 = (f32[3,64]{1,0:T(4,128)S(1)}, f32[3,64]{1,0:T(4,128)}, u32[]{:S(2)}) copy-start(f32[3,64]{1,0:T(4,128)} %convert_reduce_fusion.2) | copy-start | bytes 2308
  154.4 26.4 %copy-start.10 = (f32[3,48]{1,0:T(4,128)S(1)}, f32[3,48]{1,0:T(4,128)}, u32[]{:S(2)}) copy-start(f32[3,48]{1,0:T(4,128)} %broadcast_multiply_fusion.3) | copy-start | bytes 1732
  169.1 10.7 %all-to-all-start.6 = ((bf16[8,3,1472]{2,1,0:T(4,128)(2,1)}), bf16[8,3,1472]{2,1,0:T(4,128)(2,1)S(1)}, u32[]{:S(2)}, u32[]{:S(2)}) async-start(bf16[8,3,1472]{2,1,0:T(4,128)(2,1)} %copy.31), calls=%async_computation.6 | async-start | bytes 196608 | tf_op jit(solution)/shard_map/all_to_all | solution.py:28
  179.9 2.4 %copy-start.1 = (bf16[12,48,1664]{2,1,0:T(8,128)(2,1)S(1)}, bf16[12,48,1664]{2,1,0:T(8,128)(2,1)}, u32[]{:S(2)}) copy-start(bf16[12,48,1664]{2,1,0:T(8,128)(2,1)} %param.8) | copy-start | bytes 5750788

commit v2 on v1

v2 whole, which is shorter than its diff:
```python
import jax
import jax.numpy as jnp
from jax import lax
from jax.sharding import Mesh, PartitionSpec as P

BF = jnp.bfloat16
F32 = jnp.float32
Y = ("h", "t")
ZX = ("z", "x")
ZXC = ("z", "x", "c")
DP = ("h", "z", "x", "c")


def norm_tokens(token_block, gain_vector):
    values = token_block.astype(F32)
    center = values - jnp.mean(values, axis=-1, keepdims=True)
    spread = jnp.mean(center * center, axis=-1, keepdims=True)
    return center * lax.rsqrt(spread + 1e-05) * gain_vector


def token_back(token_block, gain_vector, pool_cot):
    spread_cot = jnp.broadcast_to(pool_cot[:, None, :], token_block.shape)
    _, pull_back = jax.vjp(lambda token_piece: norm_tokens(token_piece, gain_vector), token_block)
    return pull_back(spread_cot)[0]


def exchange(blocks, axes):
    return lax.all_to_all(blocks, axes, 0, 0, tiled=True)


def spread_to(block, axes, count):
    return exchange(jnp.broadcast_to(block[None], (count,) + block.shape), axes)


def both_cores(blocks):
    half = blocks.shape[0] // 2
    parts = [lax.all_gather(part, "c", axis=0) for part in (blocks[:half], blocks[half:])]
    return jnp.concatenate(parts, axis=1)


def per_device(image_in, text_in, proj_img, proj_txt, img_gain, txt_gain, logit_scale, positive):
    t_index = lax.axis_index("t")
    h_index = lax.axis_index("h")
    g_index = (lax.axis_index("z") * 4 + lax.axis_index("x")) * 2 + lax.axis_index("c")
    logit = logit_scale[0]
    emb = proj_img.shape[1]
    slab_i, slab_t = proj_img.shape[0], proj_txt.shape[0]
    half_i, half_t = slab_i * 64, slab_t * 64

    w = jnp.pad(jnp.concatenate([proj_img, proj_txt], 0), ((0, 1), (0, 256)))
    w = lax.dynamic_slice(w, (0, 384 * t_index), (24, 384))
    w = both_cores(spread_to(w, ZX, 32)).transpose(1, 0, 2, 3)
    w_img = w[:, :, :slab_i].reshape(half_i, 384)
    w_txt = w[:, :, slab_i : slab_i + slab_t].reshape(half_t, 384)

    pooled_i = jnp.mean(norm_tokens(image_in, img_gain), axis=1).astype(BF)
    pooled_t = jnp.mean(norm_tokens(text_in, txt_gain), axis=1).astype(BF)

    def feature_half(which):
        return jnp.concatenate(
            [
                lax.dynamic_slice(pooled_i, (0, half_i * which), (12, half_i)),
                lax.dynamic_slice(pooled_t, (0, half_t * which), (12, half_t)),
            ],
            1,
        )

    mine = feature_half(h_index)
    theirs = lax.ppermute(feature_half(1 - h_index), "h", [(0, 1), (1, 0)])
    first = h_index == 0
    pooled = jnp.concatenate([jnp.where(first, mine, theirs), jnp.where(first, theirs, mine)], 0)

    def in_blocks(img_rows, txt_rows):
        quad = lambda x: jnp.pad(x.reshape(8, 3, x.shape[1]), ((0, 0), (0, 1), (0, 0)))
        return jnp.concatenate([quad(img_rows), quad(txt_rows)], 1)

    part = in_blocks(
        jnp.dot(pooled[:, :half_i], w_img, preferred_element_type=F32).astype(BF),
        jnp.dot(pooled[:, half_i:], w_txt, preferred_element_type=F32).astype(BF),
    )
    parts = exchange(part, Y).astype(F32)
    parts = parts[:4] + parts[4:]
    projected = jnp.concatenate([parts[k] for k in range(4)], 1)[:, :emb]
    inv = lax.rsqrt(jnp.sum(projected * projected, axis=-1, keepdims=True) + 1e-06)
    unit = (projected * inv).astype(BF)

    own_pos = lax.dynamic_slice(positive, (3 * t_index,), (3,))
    digits = jnp.pad(jnp.concatenate([own_pos // 32, own_pos % 32]).astype(BF), (0, emb - 6))
    in_block = lax.iota(jnp.int32, 8)[:, None]
    block = jnp.where(in_block == 3, digits[None], unit)
    near = spread_to(block, Y, 8)
    far = both_cores(spread_to(block, ZX, 32))
    rows = near.reshape(64, emb)
    items = far.reshape(512, emb)

    def positions(blocks):
        count = blocks.shape[0]
        found = blocks[:, 3, :6].astype(F32)
        found = found[:, :3] * 32.0 + found[:, 3:]
        return jnp.pad(found, ((0, 0), (0, 5)), constant_values=-1.0).reshape(count * 8)

    row_pos = positions(near)
    item_pos = positions(far.reshape(64, 8, emb))
    scores = logit * lax.dot_general(
        rows, items, (((1,), (1,)), ((), ())), preferred_element_type=F32
    )

    place = lax.iota(jnp.int32, 512)
    item_g = ((place // 8) % 32) * 2 + place // 256
    item_pair = ((h_index * 64 + item_g) * 12 + 3 * t_index + place % 4).astype(F32)
    item_txt = (place % 8) // 4 == 1
    item_real = place % 4 < 3
    row = lax.iota(jnp.int32, 64)
    row_txt = (row % 8) // 4 == 1
    row_real = row % 4 < 3
    row_pair = ((row // 32) * 64 + g_index) * 12 + ((row // 8) % 4) * 3 + row % 4
    row_pair = row_pair.astype(F32)
    real = row_real[:, None] & item_real[None, :]
    valid = (row_txt[:, None] != item_txt[None, :]) & real
    img_match = valid & (row_pos[:, None] == item_pair[None, :])
    match = img_match | (valid & (item_pos[None, :] == row_pair[:, None]))
    valid_scores = jnp.where(valid, scores, -1e30)

    def log_total(values, axis):
        largest = jnp.max(values, axis=axis, keepdims=True)
        summed = jnp.sum(jnp.exp(values - largest), axis=axis, keepdims=True)
        return jnp.squeeze(largest + jnp.log(summed), axis)

    row_part = jnp.where(row_real, log_total(valid_scores, 1), 0.0)
    item_part = jnp.where(item_real, log_total(valid_scores, 0), 0.0)
    matched_part = jnp.sum(jnp.where(img_match, scores, 0.0))
    item_part = jnp.where(place == 3, matched_part, item_part)
    row_seen = spread_to(row_part[None], Y, 8)[:, 0]
    item_seen = spread_to(item_part[None], ZXC, 64)[:, 0]
    row_lse = log_total(row_seen, 0)
    item_lse = log_total(item_seen, 0)
    y_value = jnp.sum(jnp.where(item_real, item_lse, 0.0)) - 2.0 * jnp.sum(item_seen[:, 3])

    coef = jnp.where(
        valid,
        0.5
        * logit
        * (
            jnp.exp(valid_scores - row_lse[:, None])
            + jnp.exp(valid_scores - item_lse[None, :])
            - 2.0 * match.astype(F32)
        ),
        0.0,
    ).astype(BF)
    along = jnp.sum(coef.astype(F32) * scores, axis=1) / logit
    cot = jnp.dot(coef, items, preferred_element_type=F32).astype(BF)
    cot = jnp.pad(cot, ((0, 0), (0, 256)))

    def two_parts(values):
        high = values.astype(BF)
        return high, (values - high.astype(F32)).astype(BF)

    along_high, along_low = two_parts(along)
    value_high, value_low = two_parts(jnp.broadcast_to(y_value[None], (64,)))
    riders = jnp.pad(
        jnp.stack([along_high, along_low, value_high, value_low]), ((0, 0), (0, 320))
    )
    at = lax.iota(jnp.int32, 64)[:, None]
    extra = jnp.zeros((64, 384), BF)
    for k in range(4):
        extra = jnp.where(at == 4 * k + 3, riders[k][None], extra)
    ways = jnp.stack([cot[:, 384 * k : 384 * k + 384] + extra for k in range(4)])
    summed = jnp.sum(exchange(jnp.concatenate([ways, ways], 0), Y).astype(F32), axis=0)
    along = summed[3, :64] + summed[7, :64]
    mean_loss = ((summed[11, :1] + summed[15, :1]) / (2.0 * 1536)).reshape(1)

    rows_part = lax.dynamic_slice(
        jnp.pad(rows, ((0, 0), (0, 256))), (0, 384 * t_index), (64, 384)
    ).astype(F32)
    proj_cot = (summed - rows_part * along[:, None]).astype(BF)
    back = (((1,), (1,)), ((), ()))
    pool_i = lax.dot_general(proj_cot, w_img, back, preferred_element_type=F32).astype(BF)
    pool_t = lax.dot_general(proj_cot, w_txt, back, preferred_element_type=F32).astype(BF)
    pool = jnp.concatenate(
        [pool_i.reshape(8, 8, half_i)[:, :4], pool_t.reshape(8, 8, half_t)[:, 4:]], 2
    )
    pool = exchange(pool, Y).astype(F32)
    pool = jnp.sum(pool.reshape(2, 4, 4, half_i + half_t), axis=1)
    img_pool_cot = jnp.concatenate([pool[0, :3, :half_i], pool[1, :3, :half_i]], 1) * inv[:3]
    txt_pool_cot = jnp.concatenate([pool[0, :3, half_i:], pool[1, :3, half_i:]], 1) * inv[4:7]
    img_own = lax.dynamic_slice_in_dim(image_in, 3 * t_index, 3, 0)
    txt_own = lax.dynamic_slice_in_dim(text_in, 3 * t_index, 3, 0)
    img_grads = token_back(img_own, img_gain, img_pool_cot)
    txt_grads = token_back(txt_own, txt_gain, txt_pool_cot)
    return (mean_loss, img_grads[None], txt_grads[None])


def solution(mesh):
    fine = Mesh(mesh.devices.reshape(4, 2, 8, 4, 2), ("t", "h", "z", "x", "c"))
    in_specs = (
        P(DP, None, None),
        P(DP, None, None),
        P(DP, None),
        P(DP, None),
        P(),
        P(),
        P(),
        P(DP),
    )
    out_specs = (P(), P("t", DP, None, None), P("t", DP, None, None))
    return jax.shard_map(
        per_device, mesh=fine, in_specs=in_specs, out_specs=out_specs, check_vma=False
    )
```

time: 187 us -> 194 us (1.037)
  blocking collectives: 13.4 us -> 26.9 us
  waiting for transfers between devices: 62.7 us -> 55.8 us
  other arithmetic: 28.9 us -> 34.1 us
  starting transfers between devices: 55.4 us -> 51.8 us
  local copies, waits for them, and re-layouts: 12.2 us -> 14.8 us
  matrix products: 5.87 us -> 3.59 us
    all_to_all x0 -> x1, blocking collectives: none -> 10.7 us  [exchange(): return lax.all_to_all(blocks, axes, 0, 0, tiled=True)]
    all_to_all x7, waiting for transfers between devices: 61.2 us -> 54.5 us  [exchange(): return lax.all_to_all(blocks, axes, 0, 0, tiled=True)]
    unnamed x7, other arithmetic: 4.37 us -> 9.81 us
    all_to_all x7, starting transfers between devices: 48 us -> 44.4 us  [exchange(): return lax.all_to_all(blocks, axes, 0, 0, tiled=True)]
    dot_general x4, matrix products: 4.19 us -> 1.1 us  [the longest x1 0.36 us: per_device(): lax.dot_general(proj_cot, w_img, back, preferred_element_type=F32)]
    all_gather x4, blocking collectives: 13.4 us -> 16.2 us  [both_cores(): lax.all_gather(part, 'c', axis=0)]
    concatenate x6 -> x4, other arithmetic: 0.3 us -> 2.88 us  [the longest x1 1.4 us: per_device(): jnp.concatenate([ways, ways], 0)]
    reduce_sum x4, other arithmetic: 4.52 us -> 1.97 us  [norm_tokens(): spread = jnp.mean(center * center, axis=-1, keepdims=True)]
  transfers between devices with their start and end apart: 8 -> 8, of which waited for: 7 -> 8; matrix products, arithmetic and copies ran while one was open for 7% -> 7% of each run, Pallas kernels for 0% -> 0%
where the time goes in v2:
time: 194 us; the launch traced here: 193 us
  waiting for transfers between devices  55.8 us (29%)
  starting transfers between devices  51.8 us (27%)
  other arithmetic  34.1 us (18%)
  blocking collectives  26.9 us (14%)
  local copies, waits for them, and re-layouts  14.8 us (8%)
  between operations  5.64 us (3%)
  matrix products  3.59 us (2%)
    all_to_all x7, waiting for transfers between devices, exchange(): return lax.all_to_all(blocks, axes, 0, 0, tiled=True)  54.5 us
    all_to_all x7, starting transfers between devices, exchange(): return lax.all_to_all(blocks, axes, 0, 0, tiled=True)  44.4 us
    all_gather x4, blocking collectives, both_cores(): lax.all_gather(part, 'c', axis=0)  16.2 us
    all_to_all x1, blocking collectives, exchange(): return lax.all_to_all(blocks, axes, 0, 0, tiled=True)  10.7 us
    unnamed x7, other arithmetic  9.81 us
    ppermute x1, starting transfers between devices, per_device(): theirs = lax.ppermute(feature_half(1 - h_index), 'h', [(0, 1), (1, 0)])  7.44 us
  transfers between devices with their start and end apart: 8, of which 8 were waited for; matrix products, arithmetic and copies ran while one was open for 7% of the time, Pallas kernels for 0%

profile of v2, /device:TPU:1, one launch (start us, length us, event | category | flops | bytes accessed | tf_op | source)
XLA Modules:
  0.0 192.6 jit_solution(3581360872378084796)
XLA Ops:
  2.5 13.7 %all-to-all-start = ((bf16[32,24,384]{2,1,0:T(8,128)(2,1)}), bf16[32,24,384]{2,1,0:T(8,128)(2,1)S(1)}, u32[]{:S(2)}, u32[]{:S(2)}) async-start(bf16[32,24,384]{2,1,0:T(8,128)(2,1)} %broadcast_in_dim.191), calls=%async_computation | async-start | bytes 1179648 | tf_op jit(solution)/shard_map/all_to_all | solution.py:28
  21.6 7.4 %collective-permute-start = (bf16[12,1472]{1,0:T(8,128)(2,1)S(1)}, bf16[12,1472]{1,0:T(8,128)(2,1)S(1)}, u32[]{:S(2)}, u32[]{:S(2)}) collective-permute-start(bf16[12,1472]{1,0:T(8,128)(2,1)S(1)} %pad_maximum_fusion.3), channel_id=1, source_target_pairs={{0,64},{64,0},{1,65},{65,1},{2,66},{66,2},{3,67},{67,3},{4,68},{68... | collective-permute-start | bytes 105992 | tf_op jit(solution)/shard_map/ppermute | solution.py:69
  30.7 3.0 %all-to-all-done = bf16[32,24,384]{2,1,0:T(8,128)(2,1)S(1)} async-done(((bf16[32,24,384]{2,1,0:T(8,128)(2,1)}), bf16[32,24,384]{2,1,0:T(8,128)(2,1)S(1)}, u32[]{:S(2)}, u32[]{:S(2)}) %all-to-all-start) | async-done | bytes 589856 | tf_op jit(solution)/shard_map/all_to_all | solution.py:28
  33.7 4.3 %all-gather = bf16[32,24,384]{2,1,0:T(8,128)(2,1)S(1)} all-gather(bf16[16,24,384]{2,1,0:T(8,128)(2,1)S(1)} %get-tuple-element.22), channel_id=2, replica_groups=mesh['t'=4,'h'=2,'z'=8,'x'=4,'c'=2] {'c'}, dimensions={0}, use_global_device_ids=true | all-gather | bytes 884736 | tf_op jit(solution)/shard_map/all_gather | solution.py:37
  38.1 2.2 %all-gather.1 = bf16[32,24,384]{2,1,0:T(8,128)(2,1)S(1)} all-gather(bf16[16,24,384]{2,1,0:T(8,128)(2,1)S(1)} %get-tuple-element.23), channel_id=3, replica_groups=mesh['t'=4,'h'=2,'z'=8,'x'=4,'c'=2] {'c'}, dimensions={0}, use_global_device_ids=true | all-gather | bytes 884736 | tf_op jit(solution)/shard_map/all_gather | solution.py:37
  46.6 6.8 %all-to-all-start.1 = ((bf16[8,8,384]{2,1,0:T(8,128)(2,1)}), bf16[8,8,384]{2,1,0:T(8,128)(2,1)S(1)}, u32[]{:S(2)}, u32[]{:S(2)}) async-start(bf16[8,8,384]{2,1,0:T(8,128)(2,1)} %fusion.27), calls=%async_computation.1 | async-start | bytes 98304 | tf_op jit(solution)/shard_map/all_to_all | solution.py:28
  53.4 7.1 %all-to-all-done.1 = bf16[8,8,384]{2,1,0:T(8,128)(2,1)S(1)} async-done(((bf16[8,8,384]{2,1,0:T(8,128)(2,1)}), bf16[8,8,384]{2,1,0:T(8,128)(2,1)S(1)}, u32[]{:S(2)}, u32[]{:S(2)}) %all-to-all-start.1) | async-done | bytes 49184 | tf_op jit(solution)/shard_map/all_to_all | solution.py:28
  61.2 10.7 %all_to_all.40 = bf16[8,8,1280]{2,1,0:T(8,128)(2,1)S(1)} all-to-all(bf16[8,8,1280]{2,1,0:T(8,128)(2,1)S(1)} %broadcast_in_dim.192), channel_id=1, replica_groups=mesh['t'=4,'h'=2,'z'=8,'x'=4,'c'=2] {'h','t'}, dimensions={0} | all-to-all | bytes 327680 | tf_op jit(solution)/shard_map/all_to_all | solution.py:28
  72.8 6.5 %all-to-all-start.3 = ((bf16[32,8,1280]{2,1,0:T(8,128)(2,1)}), bf16[32,8,1280]{2,1,0:T(8,128)(2,1)}, u32[]{:S(2)}, u32[]{:S(2)}) async-start(bf16[32,8,1280]{2,1,0:T(8,128)(2,1)} %broadcast_in_dim.193), calls=%async_computation.3 | async-start | bytes 1310720 | tf_op jit(solution)/shard_map/all_to_all | solution.py:28
  81.9 13.4 %all-to-all-done.3 = bf16[32,8,1280]{2,1,0:T(8,128)(2,1)} async-done(((bf16[32,8,1280]{2,1,0:T(8,128)(2,1)}), bf16[32,8,1280]{2,1,0:T(8,128)(2,1)}, u32[]{:S(2)}, u32[]{:S(2)}) %all-to-all-start.3) | async-done | bytes 655392 | tf_op jit(solution)/shard_map/all_to_all | solution.py:28
  96.4 7.4 %all-gather.3 = bf16[32,8,1280]{2,1,0:T(8,128)(2,1)S(1)} all-gather(bf16[16,8,1280]{2,1,0:T(8,128)(2,1)S(1)} %get-tuple-element.21), channel_id=5, replica_groups=mesh['t'=4,'h'=2,'z'=8,'x'=4,'c'=2] {'c'}, dimensions={0}, use_global_device_ids=true | all-gather | bytes 983040 | tf_op jit(solution)/shard_map/all_gather | solution.py:37
  103.8 2.3 %all-gather.2 = bf16[32,8,1280]{2,1,0:T(8,128)(2,1)S(1)} all-gather(bf16[16,8,1280]{2,1,0:T(8,128)(2,1)S(1)} %get-tuple-element.20), channel_id=4, replica_groups=mesh['t'=4,'h'=2,'z'=8,'x'=4,'c'=2] {'c'}, dimensions={0}, use_global_device_ids=true | all-gather | bytes 983040 | tf_op jit(solution)/shard_map/all_gather | solution.py:37
  109.3 3.3 %all-to-all-start.4 = ((f32[8,1,64]{2,1,0:T(1,128)}), f32[8,1,64]{2,1,0:T(1,128)S(1)}, u32[]{:S(2)}, u32[]{:S(2)}) async-start(f32[8,1,64]{2,1,0:T(1,128)} %broadcast_in_dim.196), calls=%async_computation.4 | async-start | bytes 8192 | tf_op jit(solution)/shard_map/all_to_all | solution.py:28
  115.1 3.8 %all-to-all-done.4 = f32[8,1,64]{2,1,0:T(1,128)S(1)} async-done(((f32[8,1,64]{2,1,0:T(1,128)}), f32[8,1,64]{2,1,0:T(1,128)S(1)}, u32[]{:S(2)}, u32[]{:S(2)}) %all-to-all-start.4) | async-done | bytes 2080 | tf_op jit(solution)/shard_map/all_to_all | solution.py:28
  119.7 6.4 %all-to-all-start.5 = ((f32[64,1,512]{2,1,0:T(1,128)}), f32[64,1,512]{2,1,0:T(1,128)S(1)}, u32[]{:S(2)}, u32[]{:S(2)}) async-start(f32[64,1,512]{2,1,0:T(1,128)} %broadcast_in_dim.200), calls=%async_computation.5 | async-start | bytes 262144 | tf_op jit(solution)/shard_map/all_to_all | solution.py:28
  128.0 9.2 %all-to-all-done.5 = f32[64,1,512]{2,1,0:T(1,128)S(1)} async-done(((f32[64,1,512]{2,1,0:T(1,128)}), f32[64,1,512]{2,1,0:T(1,128)S(1)}, u32[]{:S(2)}, u32[]{:S(2)}) %all-to-all-start.5) | async-done | bytes 131104 | tf_op jit(solution)/shard_map/all_to_all | solution.py:28
  138.0 1.9 convolution_convert_fusion
  139.8 1.8 multiply_reduce_fusion
  144.6 1.4 constant_dynamic-update-slice_fusion.7
  147.4 1.4 constant_dynamic-update-slice_fusion.5
  155.8 4.3 %all-to-all-start.6 = ((bf16[8,64,384]{2,1,0:T(8,128)(2,1)}), bf16[8,64,384]{2,1,0:T(8,128)(2,1)}, u32[]{:S(2)}, u32[]{:S(2)}) async-start(bf16[8,64,384]{2,1,0:T(8,128)(2,1)} %constant_dynamic-update-slice_fusion), calls=%async_computation.6 | async-start | bytes 786432 | tf_op jit(solution)/shard_map/all_to_all | solution.py:28
  161.5 12.6 %all-to-all-done.6 = bf16[8,64,384]{2,1,0:T(8,128)(2,1)} async-done(((bf16[8,64,384]{2,1,0:T(8,128)(2,1)}), bf16[8,64,384]{2,1,0:T(8,128)(2,1)}, u32[]{:S(2)}, u32[]{:S(2)}) %all-to-all-start.6) | async-done | bytes 393248 | tf_op jit(solution)/shard_map/all_to_all | solution.py:28
  176.7 3.4 %all-to-all-start.7 = ((bf16[8,4,1472]{2,1,0:T(4,128)(2,1)}), bf16[8,4,1472]{2,1,0:T(4,128)(2,1)S(1)}, u32[]{:S(2)}, u32[]{:S(2)}) async-start(bf16[8,4,1472]{2,1,0:T(4,128)(2,1)} %pad_maximum_fusion.1), calls=%async_computation.7 | async-start | bytes 196608 | tf_op jit(solution)/shard_map/all_to_all | solution.py:28
  182.0 5.5 %all-to-all-done.7 = bf16[8,4,1472]{2,1,0:T(4,128)(2,1)S(1)} async-done(((bf16[8,4,1472]{2,1,0:T(4,128)(2,1)}), bf16[8,4,1472]{2,1,0:T(4,128)(2,1)S(1)}, u32[]{:S(2)}, u32[]{:S(2)}) %all-to-all-start.7) | async-done | bytes 94240 | tf_op jit(solution)/shard_map/all_to_all | solution.py:28
  (156 shorter events, 47.2 us)
Async XLA Ops:
  0.6 15.6 %copy-start.1 = (bf16[12,48,1664]{2,1,0:T(8,128)(2,1)S(1)}, bf16[12,48,1664]{2,1,0:T(8,128)(2,1)}, u32[]{:S(2)}) copy-start(bf16[12,48,1664]{2,1,0:T(8,128)(2,1)} %param.8) | copy-start | bytes 5750788
  2.5 31.2 %all-to-all-start = ((bf16[32,24,384]{2,1,0:T(8,128)(2,1)}), bf16[32,24,384]{2,1,0:T(8,128)(2,1)S(1)}, u32[]{:S(2)}, u32[]{:S(2)}) async-start(bf16[32,24,384]{2,1,0:T(8,128)(2,1)} %broadcast_in_dim.191), calls=%async_computation | async-start | bytes 1179648 | tf_op jit(solution)/shard_map/all_to_all | solution.py:28
  16.2 2.2 %copy-start.8 = (f32[1664]{0:T(1024)S(1)}, f32[1664]{0:T(1024)}, u32[]{:S(2)}) copy-start(f32[1664]{0:T(1024)} %param.12) | copy-start | bytes 19972
  16.2 1.5 copy-start.2
  17.7 1.6 copy-start
  19.7 9.3 %copy-start.19 = (s32[12]{0:T(128)S(1)}, s32[12]{0:T(128)}, u32[]{:S(2)}) copy-start(s32[12]{0:T(128)} %param.15) | copy-start | bytes 148
  21.6 9.0 %collective-permute-start = (bf16[12,1472]{1,0:T(8,128)(2,1)S(1)}, bf16[12,1472]{1,0:T(8,128)(2,1)S(1)}, u32[]{:S(2)}, u32[]{:S(2)}) collective-permute-start(bf16[12,1472]{1,0:T(8,128)(2,1)S(1)} %pad_maximum_fusion.3), channel_id=1, source_target_pairs={{0,64},{64,0},{1,65},{65,1},{2,66},{66,2},{3,67},{67,3},{4,68},{68... | collective-permute-start | bytes 105992 | tf_op jit(solution)/shard_map/ppermute | solution.py:69
  46.6 13.9 %all-to-all-start.1 = ((bf16[8,8,384]{2,1,0:T(8,128)(2,1)}), bf16[8,8,384]{2,1,0:T(8,128)(2,1)S(1)}, u32[]{:S(2)}, u32[]{:S(2)}) async-start(bf16[8,8,384]{2,1,0:T(8,128)(2,1)} %fusion.27), calls=%async_computation.1 | async-start | bytes 98304 | tf_op jit(solution)/shard_map/all_to_all | solution.py:28
  72.8 22.5 %all-to-all-start.3 = ((bf16[32,8,1280]{2,1,0:T(8,128)(2,1)}), bf16[32,8,1280]{2,1,0:T(8,128)(2,1)}, u32[]{:S(2)}, u32[]{:S(2)}) async-start(bf16[32,8,1280]{2,1,0:T(8,128)(2,1)} %broadcast_in_dim.193), calls=%async_computation.3 | async-start | bytes 1310720 | tf_op jit(solution)/shard_map/all_to_all | solution.py:28
  80.5 32.1 %copy-start.12 = (pred[512]{0:T(512)(128)(4,1)}, pred[512]{0:T(512)(128)(4,1)S(1)}, u32[]{:S(2)}) copy-start(pred[512]{0:T(512)(128)(4,1)S(1)} %get-tuple-element.48) | copy-start | bytes 1540
  80.5 32.1 %copy-start.13 = (pred[512]{0:T(512)(128)(4,1)}, pred[512]{0:T(512)(128)(4,1)S(1)}, u32[]{:S(2)}) copy-start(pred[512]{0:T(512)(128)(4,1)S(1)} %get-tuple-element.49) | copy-start | bytes 1540
  80.5 32.1 %copy-start.14 = (pred[64]{0:T(512)(128)(4,1)}, pred[64]{0:T(512)(128)(4,1)S(1)}, u32[]{:S(2)}) copy-start(pred[64]{0:T(512)(128)(4,1)S(1)} %get-tuple-element.50) | copy-start | bytes 196
  80.6 32.1 %copy-start.15 = (pred[64]{0:T(512)(128)(4,1)}, pred[64]{0:T(512)(128)(4,1)S(1)}, u32[]{:S(2)}) copy-start(pred[64]{0:T(512)(128)(4,1)S(1)} %get-tuple-element.51) | copy-start | bytes 196
  81.7 26.1 %copy-start.11 = (f32[512]{0:T(512)}, f32[512]{0:T(512)S(1)}, u32[]{:S(2)}) copy-start(f32[512]{0:T(512)S(1)} %fusion.56) | copy-start | bytes 6148
  81.9 26.0 %copy-start.16 = (f32[64]{0:T(128)}, f32[64]{0:T(128)S(1)}, u32[]{:S(2)}) copy-start(f32[64]{0:T(128)S(1)} %eq.133) | copy-start | bytes 772
  107.9 30.1 %copy-start.5 = (f32[64,512]{1,0:T(8,128)}, f32[64,512]{1,0:T(8,128)S(1)}, u32[]{:S(2)}) copy-start(f32[64,512]{1,0:T(8,128)S(1)} %get-tuple-element.47) | copy-start | bytes 393220
  109.3 9.7 %all-to-all-start.4 = ((f32[8,1,64]{2,1,0:T(1,128)}), f32[8,1,64]{2,1,0:T(1,128)S(1)}, u32[]{:S(2)}, u32[]{:S(2)}) async-start(f32[8,1,64]{2,1,0:T(1,128)} %broadcast_in_dim.196), calls=%async_computation.4 | async-start | bytes 8192 | tf_op jit(solution)/shard_map/all_to_all | solution.py:28
  119.7 17.5 %all-to-all-start.5 = ((f32[64,1,512]{2,1,0:T(1,128)}), f32[64,1,512]{2,1,0:T(1,128)S(1)}, u32[]{:S(2)}, u32[]{:S(2)}) async-start(f32[64,1,512]{2,1,0:T(1,128)} %broadcast_in_dim.200), calls=%async_computation.5 | async-start | bytes 262144 | tf_op jit(solution)/shard_map/all_to_all | solution.py:28
  155.8 18.3 %all-to-all-start.6 = ((bf16[8,64,384]{2,1,0:T(8,128)(2,1)}), bf16[8,64,384]{2,1,0:T(8,128)(2,1)}, u32[]{:S(2)}, u32[]{:S(2)}) async-start(bf16[8,64,384]{2,1,0:T(8,128)(2,1)} %constant_dynamic-update-slice_fusion), calls=%async_computation.6 | async-start | bytes 786432 | tf_op jit(solution)/shard_map/all_to_all | solution.py:28
  160.1 19.9 %copy-start.18 = (f32[8]{0:T(128)S(1)}, f32[8]{0:T(128)}, u32[]{:S(2)}) copy-start(f32[8]{0:T(128)} %copy-done.17) | copy-start | bytes 100
  161.3 26.3 %copy-start.7 = (f32[1280]{0:T(1024)S(1)}, f32[1280]{0:T(1024)}, u32[]{:S(2)}) copy-start(f32[1280]{0:T(1024)} %param.13) | copy-start | bytes 15364
  175.6 14.0 %copy-start.9 = (f32[1664]{0:T(1024)S(1)}, f32[1664]{0:T(1024)}, u32[]{:S(2)}) copy-start(f32[1664]{0:T(1024)} %param.12) | copy-start | bytes 19972
  176.7 10.7 %all-to-all-start.7 = ((bf16[8,4,1472]{2,1,0:T(4,128)(2,1)}), bf16[8,4,1472]{2,1,0:T(4,128)(2,1)S(1)}, u32[]{:S(2)}, u32[]{:S(2)}) async-start(bf16[8,4,1472]{2,1,0:T(4,128)(2,1)} %pad_maximum_fusion.1), calls=%async_computation.7 | async-start | bytes 196608 | tf_op jit(solution)/shard_map/all_to_all | solution.py:28
  187.4 2.2 %copy-start.3 = (bf16[12,48,1664]{2,1,0:T(8,128)(2,1)S(1)}, bf16[12,48,1664]{2,1,0:T(8,128)(2,1)}, u32[]{:S(2)}) copy-start(bf16[12,48,1664]{2,1,0:T(8,128)(2,1)} %param.8) | copy-start | bytes 5750788
  (4 other events, 3.3 us)

commit v3 on v2

v3 whole, which is shorter than its diff:
```python
import jax
import jax.numpy as jnp
from jax import lax
from jax.experimental import pallas as pl
from jax.experimental.pallas import tpu as pltpu
from jax.sharding import Mesh, PartitionSpec as P

BF = jnp.bfloat16
F32 = jnp.float32
Y = ("h", "t")
ZX = ("z", "x")
ZXC = ("z", "x", "c")
DP = ("h", "z", "x", "c")
LOW = -1e30
ROWS_DOT = (((1,), (1,)), ((), ()))


def norm_tokens(token_block, gain_vector):
    values = token_block.astype(F32)
    center = values - jnp.mean(values, axis=-1, keepdims=True)
    spread = jnp.mean(center * center, axis=-1, keepdims=True)
    return center * lax.rsqrt(spread + 1e-05) * gain_vector


def token_back(token_block, gain_vector, pool_cot):
    spread_cot = jnp.broadcast_to(pool_cot[:, None, :], token_block.shape)
    _, pull_back = jax.vjp(lambda token_piece: norm_tokens(token_piece, gain_vector), token_block)
    return pull_back(spread_cot)[0]


def exchange(blocks, axes):
    return lax.all_to_all(blocks, axes, 0, 0, tiled=True)


def both_cores(blocks):
    half = blocks.shape[0] // 2
    parts = [lax.all_gather(part, "c", axis=0) for part in (blocks[:half], blocks[half:])]
    return [part.reshape(-1, blocks.shape[2]) for part in parts]


def kernel_call(body, outs, args, scratch=(), smem=()):
    vmem = pl.BlockSpec(memory_space=pltpu.VMEM)
    return pl.pallas_call(
        body,
        out_shape=[jax.ShapeDtypeStruct(shape, kind) for shape, kind in outs],
        in_specs=[
            pl.BlockSpec(memory_space=pltpu.SMEM) if k in smem else vmem for k in range(len(args))
        ],
        out_specs=[vmem] * len(outs),
        scratch_shapes=list(scratch),
        compiler_params=pltpu.CompilerParams(vmem_limit_bytes=40 * 1024 * 1024),
    )(*args)


def project_kernel(left_ref, wa_ref, wb_ref, out_ref):
    half = wa_ref.shape[0]
    part = jnp.dot(left_ref[:, :half], wa_ref[...], preferred_element_type=F32)
    part += jnp.dot(left_ref[:, half:], wb_ref[...], preferred_element_type=F32)
    part = part.astype(BF)
    for k in range(8):
        out_ref[48 * k : 48 * k + 48, :] = part


def unit_kernel(place_ref, parts_ref, digits_ref, rows_ref, far_ref, inv_ref, held, held_inv):
    spread = parts_ref[...].astype(F32)
    emb = rows_ref.shape[1]
    blocks = [spread[48 * k : 48 * k + 48] + spread[192 + 48 * k : 240 + 48 * k] for k in range(4)]
    projected = jnp.concatenate(blocks, 1)[:, :emb]
    inv = lax.rsqrt(jnp.sum(projected * projected, axis=1, keepdims=True) + 1e-06)

    def in_blocks(values):
        blank = jnp.zeros((1, values.shape[1]), F32)
        pieces = []
        for k in range(8):
            pieces += [values[6 * k : 6 * k + 3], blank, values[6 * k + 3 : 6 * k + 6], blank]
        return jnp.concatenate(pieces, 0)

    unit = in_blocks(projected * inv)
    rows_ref[...] = unit.astype(BF)
    held[...] = unit
    held_inv[...] = in_blocks(jnp.broadcast_to(inv, (48, 128)))
    own = pl.ds(pl.multiple_of(8 * place_ref[0], 8), 8)
    inv_ref[...] = held_inv[own, :]
    block = held[own, :]
    at = lax.broadcasted_iota(jnp.int32, (8, 128), 0)
    start = jnp.where(at == 3, digits_ref[...], block[:, :128])
    block = jnp.concatenate([start, block[:, 128:]], 1)
    block = jnp.concatenate([block, block], 0).astype(BF)
    for k in range(16):
        far_ref[16 * k : 16 * k + 16, :] = block


def tile_masks(place_ref):
    h, t, g = place_ref[1], place_ref[2], place_ref[3]
    row = lax.broadcasted_iota(jnp.int32, (64, 512), 0)
    item = lax.broadcasted_iota(jnp.int32, (64, 512), 1)
    item_g = ((item // 256) * 16 + (item % 128) // 8) * 2 + (item // 128) % 2
    item_pair = (h * 64 + item_g) * 12 + 3 * t + item % 4
    row_pair = ((row // 32) * 64 + g) * 12 + ((row // 8) % 4) * 3 + row % 4
    row_txt, item_txt = (row % 8) // 4, (item % 8) // 4
    valid = (row_txt != item_txt) & (row % 4 < 3) & (item % 4 < 3)
    return valid, row_pair, item_pair, row_txt, item


def square_mask():
    down = lax.broadcasted_iota(jnp.int32, (64, 128), 0)
    along = lax.broadcasted_iota(jnp.int32, (64, 128), 1)
    return down == along


def as_lanes(column):
    return jnp.sum(jnp.where(square_mask(), column, 0.0), axis=0, keepdims=True)


def as_column(lanes):
    return jnp.sum(jnp.where(square_mask(), lanes, 0.0), axis=1, keepdims=True)


def log_total(values, axis):
    largest = jnp.max(values, axis=axis, keepdims=True)
    return largest + jnp.log(jnp.sum(jnp.exp(values - largest), axis=axis, keepdims=True))


def score_kernel(
    place_ref, logit_ref, rows_ref, fa_ref, fb_ref, row_pos_ref, scores_ref, near_ref, far_ref
):
    rows = rows_ref[...]
    scores = jnp.concatenate(
        [
            lax.dot_general(rows, ref[...], ROWS_DOT, preferred_element_type=F32)
            for ref in (fa_ref, fb_ref)
        ],
        1,
    )
    scores = logit_ref[0] * scores
    scores_ref[...] = scores
    valid, _, item_pair, row_txt, _ = tile_masks(place_ref)
    masked = jnp.where(valid, scores, LOW)
    row_part = as_lanes(log_total(masked, 1))
    near_ref[...] = jnp.broadcast_to(row_part, (8, 128))
    item_part = log_total(masked, 0)
    hit = valid & (row_txt == 0) & (row_pos_ref[...] == item_pair)
    matched = jnp.sum(
        jnp.sum(jnp.where(hit, scores, 0.0), axis=1, keepdims=True), axis=0, keepdims=True
    )
    lane = lax.broadcasted_iota(jnp.int32, (1, 512), 1)
    item_part = jnp.where(lane == 3, matched, item_part)
    lines = jnp.concatenate([item_part[:, 128 * k : 128 * k + 128] for k in range(4)] * 2, 0)
    for k in range(32):
        far_ref[8 * k : 8 * k + 8, :] = lines


def coef_kernel(
    place_ref,
    logit_ref,
    scores_ref,
    near_ref,
    far_ref,
    row_pos_ref,
    item_pos_ref,
    fa_ref,
    fb_ref,
    out_ref,
):
    logit = logit_ref[0]
    scores = scores_ref[...]
    row_lse = as_column(log_total(near_ref[...], 0))
    seen = far_ref[...].reshape(32, 8, 128)
    largest = jnp.max(seen, axis=0)
    largest = jnp.maximum(largest[:4], largest[4:])
    both = jnp.concatenate([largest, largest], 0)
    total = jnp.sum(jnp.exp(seen - both[None]), axis=0)
    lines = largest + jnp.log(total[:4] + total[4:])
    item_lse = jnp.concatenate([lines[k : k + 1] for k in range(4)], 1)
    summed = jnp.sum(seen, axis=0)
    summed = summed[:1] + summed[4:5]
    valid, row_pair, item_pair, row_txt, item = tile_masks(place_ref)
    from_img = row_txt == 0
    hit = valid & (
        jnp.where(from_img, row_pos_ref[...], row_pair)
        == jnp.where(from_img, item_pair, item_pos_ref[...])
    )
    real = item[:1] % 4 < 3
    lse_total = jnp.sum(jnp.where(real, item_lse, 0.0), axis=1, keepdims=True)
    lane = lax.broadcasted_iota(jnp.int32, (1, 128), 1)
    matched = jnp.sum(jnp.where(lane == 3, summed, 0.0), axis=1, keepdims=True)
    value = lse_total - 2.0 * matched
    masked = jnp.where(valid, scores, LOW)
    coef = (0.5 * logit) * (
        jnp.exp(masked - row_lse) + jnp.exp(masked - item_lse) - jnp.where(hit, 2.0, 0.0)
    )
    coef = jnp.where(valid, coef, 0.0).astype(BF)
    along = jnp.sum(coef.astype(F32) * scores, axis=1, keepdims=True) / logit
    cot = jnp.dot(coef[:, :256], fa_ref[...], preferred_element_type=F32)
    cot += jnp.dot(coef[:, 256:], fb_ref[...], preferred_element_type=F32)

    riders = []
    for lanes in (as_lanes(along), jnp.broadcast_to(value, (1, 128))):
        high = lanes.astype(BF).astype(F32)
        riders += [high, lanes - high]
    at = lax.broadcasted_iota(jnp.int32, (64, 128), 0)
    extra = jnp.zeros((64, 128), F32)
    for k in range(4):
        extra = jnp.where(at == 4 * k + 3, riders[k], extra)
    blank = jnp.zeros((64, 256), F32)
    extra = jnp.concatenate([extra, blank], 1)
    cot = jnp.concatenate([cot, blank], 1)
    for k in range(4):
        way = (cot[:, 384 * k : 384 * k + 384] + extra).astype(BF)
        out_ref[64 * k : 64 * k + 64, :] = way
        out_ref[256 + 64 * k : 320 + 64 * k, :] = way


def back_kernel(got_ref, unit_ref, wa_ref, wb_ref, out_ref, loss_ref):
    summed = got_ref[:64, :].astype(F32)
    for k in range(1, 8):
        summed += got_ref[64 * k : 64 * k + 64, :].astype(F32)
    along = as_column(summed[3:4, :128] + summed[7:8, :128])
    loss_ref[...] = jnp.broadcast_to(
        (summed[11:12, :128] + summed[15:16, :128]) / (2.0 * 1536), (8, 128)
    )
    proj_cot = (summed - unit_ref[...].astype(F32) * along).astype(BF)
    a, b = [
        lax.dot_general(proj_cot, ref[...], ROWS_DOT, preferred_element_type=F32)
        for ref in (wa_ref, wb_ref)
    ]
    is_img = lax.broadcasted_iota(jnp.int32, a.shape, 1) % 24 < 13
    first = lax.broadcasted_iota(jnp.int32, a.shape, 0) % 8 < 4
    a = jnp.where(is_img, a, pltpu.roll(a, 60, 0))
    b = jnp.where(is_img, pltpu.roll(b, 4, 0), b)
    out_ref[...] = jnp.where(first, a, b).astype(BF)


def per_device(image_in, text_in, proj_img, proj_txt, img_gain, txt_gain, logit_scale, positive):
    t_index = lax.axis_index("t")
    h_index = lax.axis_index("h")
    g_index = (lax.axis_index("z") * 4 + lax.axis_index("x")) * 2 + lax.axis_index("c")
    y_index = h_index * 4 + t_index
    place = jnp.stack([y_index, h_index, t_index, g_index]).astype(jnp.int32)
    emb = proj_img.shape[1]

    w = jnp.pad(jnp.concatenate([proj_img, proj_txt], 0), ((0, 1), (0, 256)))
    w = lax.dynamic_slice(w, (0, 384 * t_index), (24, 384))
    wa, wb = both_cores(exchange(jnp.broadcast_to(w[None], (32, 24, 384)), ZX))

    pooled_i = jnp.mean(norm_tokens(image_in, img_gain), axis=1).astype(BF)
    pooled_t = jnp.mean(norm_tokens(text_in, txt_gain), axis=1).astype(BF)
    slabs = jnp.concatenate(
        [
            pooled_i.reshape(12, 128, 13),
            pooled_t.reshape(12, 128, 10),
            jnp.zeros((12, 128, 1), BF),
        ],
        2,
    )
    slabs = slabs.reshape(12, 2, 2, 16, 2, 24).transpose(0, 1, 2, 4, 3, 5).reshape(12, 2, 1536)
    first = h_index == 0
    mine = jnp.where(first, slabs[:, 0], slabs[:, 1])
    theirs = jnp.where(first, slabs[:, 1], slabs[:, 0])
    digits = jnp.stack([positive // 32, positive % 32], 1).astype(BF)
    spot = lax.iota(jnp.int32, 1536)[None, :]
    theirs = jnp.where(spot == 23, digits[:, :1], jnp.where(spot == 47, digits[:, 1:], theirs))
    theirs = lax.ppermute(theirs, "h", [(0, 1), (1, 0)])
    pooled = jnp.concatenate([jnp.where(first, mine, theirs), jnp.where(first, theirs, mine)], 0)
    own_pos = positive.astype(F32)
    their_pos = theirs[:, 23].astype(F32) * 32.0 + theirs[:, 47].astype(F32)
    row_pos = jnp.concatenate(
        [jnp.where(first, own_pos, their_pos), jnp.where(first, their_pos, own_pos)]
    )
    row_pos = jnp.pad(row_pos.reshape(8, 3), ((0, 0), (0, 5)), constant_values=-1.0)
    row_pos = row_pos.reshape(64, 1).astype(jnp.int32)
    is_img = spot % 24 < 13
    is_txt = (spot % 24 >= 13) & (spot % 24 < 23)
    left = jnp.stack(
        [
            jnp.where(is_img, pooled, 0).reshape(8, 3, 1536),
            jnp.where(is_txt, pooled, 0).reshape(8, 3, 1536),
        ],
        1,
    ).reshape(48, 1536)

    (part,) = kernel_call(project_kernel, [((384, 384), BF)], [left, wa, wb])
    parts = exchange(part.reshape(8, 48, 384), Y).reshape(384, 384)

    own_digits = lax.dynamic_slice(positive, (3 * t_index,), (3,))
    own_digits = jnp.concatenate([own_digits // 32, own_digits % 32]).astype(F32)
    own_digits = jnp.pad(own_digits, (0, 122))[None]
    rows, far, inv = kernel_call(
        unit_kernel,
        [((64, emb), BF), ((256, emb), BF), ((8, 128), F32)],
        [place, parts, own_digits],
        scratch=[pltpu.VMEM((64, emb), F32), pltpu.VMEM((64, 128), F32)],
        smem=(0,),
    )
    fa, fb = both_cores(exchange(far.reshape(32, 8, emb), ZX))

    scores, near, far = kernel_call(
        score_kernel,
        [((64, 512), F32), ((8, 128), F32), ((256, 128), F32)],
        [place, logit_scale, rows, fa, fb, row_pos],
        smem=(0, 1),
    )
    near = exchange(near.reshape(8, 1, 128), Y).reshape(8, 128)
    far = exchange(far.reshape(64, 4, 128), ZXC).reshape(256, 128)

    item_pos = jnp.concatenate([fa.reshape(32, 8, emb)[:, 3, :6], fb.reshape(32, 8, emb)[:, 3, :6]])
    item_pos = item_pos.astype(F32)
    item_pos = item_pos[:, :3] * 32.0 + item_pos[:, 3:]
    item_pos = jnp.pad(item_pos, ((0, 0), (0, 5)), constant_values=-1.0).reshape(1, 512)
    item_pos = item_pos.astype(jnp.int32)
    (ways,) = kernel_call(
        coef_kernel,
        [((512, 384), BF)],
        [place, logit_scale, scores, near, far, row_pos, item_pos, fa, fb],
        smem=(0, 1),
    )
    got = exchange(ways.reshape(8, 64, 384), Y).reshape(512, 384)
    unit_part = lax.dynamic_slice(
        jnp.pad(rows, ((0, 0), (0, 256))), (0, 384 * t_index), (64, 384)
    )
    pool, loss = kernel_call(
        back_kernel, [((64, 768), BF), ((8, 128), F32)], [got, unit_part, wa, wb]
    )
    mean_loss = loss[0, :1]
    pool = exchange(pool.reshape(8, 8, 768), Y).astype(F32)
    pool = jnp.sum(pool.reshape(2, 4, 2, 4, 2, 16, 24), axis=1)
    pool = pool.transpose(2, 0, 1, 4, 3, 5)[:3].reshape(3, 128, 24)
    img_pool_cot = pool[:, :, :13].reshape(3, -1) * inv[:3, :1]
    txt_pool_cot = pool[:, :, 13:23].reshape(3, -1) * inv[4:7, :1]
    img_own = lax.dynamic_slice_in_dim(image_in, 3 * t_index, 3, 0)
    txt_own = lax.dynamic_slice_in_dim(text_in, 3 * t_index, 3, 0)
    img_grads = token_back(img_own, img_gain, img_pool_cot)
    txt_grads = token_back(txt_own, txt_gain, txt_pool_cot)
    return (mean_loss, img_grads[None], txt_grads[None])


def solution(mesh):
    fine = Mesh(mesh.devices.reshape(4, 2, 8, 4, 2), ("t", "h", "z", "x", "c"))
    in_specs = (
        P(DP, None, None),
        P(DP, None, None),
        P(DP, None),
        P(DP, None),
        P(),
        P(),
        P(),
        P(DP),
    )
    out_specs = (P(), P("t", DP, None, None), P("t", DP, None, None))
    return jax.shard_map(
        per_device, mesh=fine, in_specs=in_specs, out_specs=out_specs, check_vma=False
    )
```

time: 194 us -> 179 us (0.923)
  waiting for transfers between devices: 55.8 us -> 83 us
  other arithmetic: 34.1 us -> 19.5 us
  blocking collectives: 26.9 us -> 14 us
  local copies, waits for them, and re-layouts: 14.8 us -> 6.16 us
  Pallas kernels: 0 us -> 7.55 us
  starting transfers between devices: 51.8 us -> 45.9 us
  between operations: 5.64 us -> 1.77 us
  matrix products: 3.59 us -> 0 us
    all_to_all x7, waiting for transfers between devices: 54.5 us -> 83 us  [exchange(): return lax.all_to_all(blocks, axes, 0, 0, tiled=True)]
    all_to_all x1 -> x0, blocking collectives: 10.7 us -> none  [exchange(): return lax.all_to_all(blocks, axes, 0, 0, tiled=True)]
    unnamed x7 -> x0, other arithmetic: 9.81 us -> none
    pallas_call x0 -> x5, Pallas kernels: none -> 7.55 us  [kernel_call(): pl.pallas_call(body, out_shape=[jax.ShapeDtypeStruct(shape, kind) for sha...]
    all_to_all x7, starting transfers between devices: 44.4 us -> 37.6 us  [exchange(): return lax.all_to_all(blocks, axes, 0, 0, tiled=True)]
    reduce_sum x10 -> x1, other arithmetic: 6.01 us -> 0.12 us  [per_device(): pool = jnp.sum(pool.reshape(2, 4, 2, 4, 2, 16, 24), axis=1)]
    slice x12 -> x9, local copies, waits for them, and re-layouts: 5.06 us -> 1.03 us  [the longest x1 0.52 us: per_device(): mean_loss = loss[0, :1]]
    dot_general x6 -> x0, matrix products: 3.59 us -> none  [the longest x1 1.88 us: per_device(): cot = jnp.dot(coef, items, preferred_element_type=F32).astype(BF)]
  transfers between devices with their start and end apart: 8 -> 8, of which waited for: 8 -> 7; matrix products, arithmetic and copies ran while one was open for 7% -> 3% of each run, Pallas kernels for 0% -> 0%
where the time goes in v3:
time: 179 us; the launch traced here: 178 us
  waiting for transfers between devices  83 us (46%)
  starting transfers between devices  45.9 us (26%)
  other arithmetic  19.5 us (11%)
  blocking collectives  14 us (8%)
  Pallas kernels  7.55 us (4%)
  local copies, waits for them, and re-layouts  6.16 us (3%)
    all_to_all x7, waiting for transfers between devices, exchange(): return lax.all_to_all(blocks, axes, 0, 0, tiled=True)  83 us
    all_to_all x7, starting transfers between devices, exchange(): return lax.all_to_all(blocks, axes, 0, 0, tiled=True)  37.6 us
    all_gather x4, blocking collectives, both_cores(): lax.all_gather(part, 'c', axis=0)  14 us
    ppermute x1, starting transfers between devices, per_device(): theirs = lax.ppermute(theirs, 'h', [(0, 1), (1, 0)])  8.27 us
    pallas_call x5, Pallas kernels, kernel_call(): pl.pallas_call(body, out_shape=[jax.ShapeDtypeStruct(shape, kind) for sha...  7.55 us
    reduce_sum x6, other arithmetic, norm_tokens(): center = values - jnp.mean(values, axis=-1, keepdims=True)  6.36 us
    reduce_sum x4, other arithmetic, norm_tokens(): spread = jnp.mean(center * center, axis=-1, keepdims=True)  4.51 us
  transfers between devices with their start and end apart: 8, of which 7 were waited for; matrix products, arithmetic and copies ran while one was open for 3% of the time, Pallas kernels for 0%

profile of v3, /device:TPU:1, one launch (start us, length us, event | category | flops | bytes accessed | tf_op | source)
XLA Modules:
  0.0 177.9 jit_solution(4037707798483858287)
XLA Ops:
  1.5 1.9 %convert_reduce_fusion.1 = f32[12,48]{1,0:T(8,128)S(1)} fusion(bf16[12,48,1664]{2,1,0:T(8,128)(2,1)} %param.8), kind=kLoop, calls=%fused_computation.3 | loop fusion | flops 1916352 | bytes 1919232 | tf_op jit(solution)/shard_map/reduce_sum | solution.py:20
  3.3 2.2 %fusion.7 = f32[12,48]{1,0:T(8,128)S(1)} fusion(bf16[12,48,1664]{2,1,0:T(8,128)(2,1)} %param.8, f32[12,48]{1,0:T(8,128)S(1)} %broadcast_multiply_fusion.3), kind=kLoop, calls=%fused_computation.11 | loop fusion | flops 3833280 | bytes 1921536 | tf_op jit(solution)/shard_map/reduce_sum | solution.py:21
  12.3 8.3 %collective-permute-start = (bf16[12,1536]{1,0:T(8,128)(2,1)S(1)}, bf16[12,1536]{1,0:T(8,128)(2,1)S(1)}, u32[]{:S(2)}, u32[]{:S(2)}) collective-permute-start(bf16[12,1536]{1,0:T(8,128)(2,1)S(1)} %fusion.22), channel_id=1, source_target_pairs={{0,64},{64,0},{1,65},{65,1},{2,66},{66,2},{3,67},{67,3},{4,68},{68... | collective-permute-start | bytes 110600 | tf_op jit(solution)/shard_map/ppermute | solution.py:263
  21.6 12.9 %all-to-all-start = ((bf16[32,24,384]{2,1,0:T(8,128)(2,1)}), bf16[32,24,384]{2,1,0:T(8,128)(2,1)S(1)}, u32[]{:S(2)}, u32[]{:S(2)}) async-start(bf16[32,24,384]{2,1,0:T(8,128)(2,1)} %broadcast_in_dim.107), calls=%async_computation | async-start | bytes 1179648 | tf_op jit(solution)/shard_map/all_to_all | solution.py:32
  35.1 16.1 %all-to-all-done = bf16[32,24,384]{2,1,0:T(8,128)(2,1)S(1)} async-done(((bf16[32,24,384]{2,1,0:T(8,128)(2,1)}), bf16[32,24,384]{2,1,0:T(8,128)(2,1)S(1)}, u32[]{:S(2)}, u32[]{:S(2)}) %all-to-all-start) | async-done | bytes 589856 | tf_op jit(solution)/shard_map/all_to_all | solution.py:32
  51.3 5.0 %all-gather.1 = bf16[32,24,384]{2,1,0:T(8,128)(2,1)S(1)} all-gather(bf16[16,24,384]{2,1,0:T(8,128)(2,1)S(1)} %get-tuple-element.29), channel_id=3, replica_groups=mesh['t'=4,'h'=2,'z'=8,'x'=4,'c'=2] {'c'}, dimensions={0}, use_global_device_ids=true | all-gather | bytes 884736 | tf_op jit(solution)/shard_map/all_gather | solution.py:37
  56.3 2.2 %all-gather = bf16[32,24,384]{2,1,0:T(8,128)(2,1)S(1)} all-gather(bf16[16,24,384]{2,1,0:T(8,128)(2,1)S(1)} %get-tuple-element.30), channel_id=2, replica_groups=mesh['t'=4,'h'=2,'z'=8,'x'=4,'c'=2] {'c'}, dimensions={0}, use_global_device_ids=true | all-gather | bytes 884736 | tf_op jit(solution)/shard_map/all_gather | solution.py:37
  59.5 3.4 %all-to-all-start.1 = ((bf16[8,48,384]{2,1,0:T(8,128)(2,1)}), bf16[8,48,384]{2,1,0:T(8,128)(2,1)S(1)}, u32[]{:S(2)}, u32[]{:S(2)}) async-start(bf16[8,48,384]{2,1,0:T(8,128)(2,1)} %bitcast.7), calls=%async_computation.1 | async-start | bytes 589824 | tf_op jit(solution)/shard_map/all_to_all | solution.py:32
  63.1 12.8 %all-to-all-done.1 = bf16[8,48,384]{2,1,0:T(8,128)(2,1)S(1)} async-done(((bf16[8,48,384]{2,1,0:T(8,128)(2,1)}), bf16[8,48,384]{2,1,0:T(8,128)(2,1)S(1)}, u32[]{:S(2)}, u32[]{:S(2)}) %all-to-all-start.1) | async-done | bytes 294944 | tf_op jit(solution)/shard_map/all_to_all | solution.py:32
  77.5 4.5 %all-to-all-start.2 = ((bf16[32,8,1280]{2,1,0:T(8,128)(2,1)}), bf16[32,8,1280]{2,1,0:T(8,128)(2,1)S(1)}, u32[]{:S(2)}, u32[]{:S(2)}) async-start(bf16[32,8,1280]{2,1,0:T(8,128)(2,1)} %bitcast.10), calls=%async_computation.2 | async-start | bytes 1310720 | tf_op jit(solution)/shard_map/all_to_all | solution.py:32
  83.2 17.5 %all-to-all-done.2 = bf16[32,8,1280]{2,1,0:T(8,128)(2,1)S(1)} async-done(((bf16[32,8,1280]{2,1,0:T(8,128)(2,1)}), bf16[32,8,1280]{2,1,0:T(8,128)(2,1)S(1)}, u32[]{:S(2)}, u32[]{:S(2)}) %all-to-all-start.2) | async-done | bytes 655392 | tf_op jit(solution)/shard_map/all_to_all | solution.py:32
  100.8 4.5 %all-gather.3 = bf16[32,8,1280]{2,1,0:T(8,128)(2,1)S(1)} all-gather(bf16[16,8,1280]{2,1,0:T(8,128)(2,1)S(1)} %get-tuple-element.27), channel_id=5, replica_groups=mesh['t'=4,'h'=2,'z'=8,'x'=4,'c'=2] {'c'}, dimensions={0}, use_global_device_ids=true | all-gather | bytes 983040 | tf_op jit(solution)/shard_map/all_gather | solution.py:37
  105.4 2.3 %all-gather.2 = bf16[32,8,1280]{2,1,0:T(8,128)(2,1)S(1)} all-gather(bf16[16,8,1280]{2,1,0:T(8,128)(2,1)S(1)} %get-tuple-element.28), channel_id=4, replica_groups=mesh['t'=4,'h'=2,'z'=8,'x'=4,'c'=2] {'c'}, dimensions={0}, use_global_device_ids=true | all-gather | bytes 983040 | tf_op jit(solution)/shard_map/all_gather | solution.py:37
  107.8 2.0 %shard_map.105 = (f32[64,512]{1,0:T(8,128)S(1)}, f32[8,128]{1,0:T(8,128)}, f32[256,128]{1,0:T(8,128)}) custom-call(s32[4]{0:T(128)S(1)} %pad_add_fusion.place_ref, f32[1]{0:T(128)S(6)} %copy.78.logit_ref, bf16[64,1280]{1,0:T(8,128)(2,1)S(1)} %get-tuple-element.11.rows_ref, bf16[256,1280]{1,0:T(8,128)(2,1)S(1)} %bitcast.46, bf16[256,1280]{1,0:T(8,128)(2,1)S(1)} %bitcast.44, ...), custom_call_target="tpu_custom_call" | custom-call | tf_op jit(solution)/shard_map/pallas_call | solution.py:43
  109.8 3.3 %all-to-all-start.3 = ((f32[8,1,128]{2,1,0:T(1,128)}), f32[8,1,128]{2,1,0:T(1,128)S(1)}, u32[]{:S(2)}, u32[]{:S(2)}) async-start(f32[8,1,128]{2,1,0:T(1,128)} %bitcast.14), calls=%async_computation.3 | async-start | bytes 8192 | tf_op jit(solution)/shard_map/all_to_all | solution.py:32
  113.1 6.3 %all-to-all-done.3 = f32[8,1,128]{2,1,0:T(1,128)S(1)} async-done(((f32[8,1,128]{2,1,0:T(1,128)}), f32[8,1,128]{2,1,0:T(1,128)S(1)}, u32[]{:S(2)}, u32[]{:S(2)}) %all-to-all-start.3) | async-done | bytes 4128 | tf_op jit(solution)/shard_map/all_to_all | solution.py:32
  119.4 6.6 %all-to-all-start.4 = ((f32[64,4,128]{2,1,0:T(4,128)}), f32[64,4,128]{2,1,0:T(4,128)S(1)}, u32[]{:S(2)}, u32[]{:S(2)}) async-start(f32[64,4,128]{2,1,0:T(4,128)} %bitcast.16), calls=%async_computation.4 | async-start | bytes 262144 | tf_op jit(solution)/shard_map/all_to_all | solution.py:32
  126.3 10.9 %all-to-all-done.4 = f32[64,4,128]{2,1,0:T(4,128)S(1)} async-done(((f32[64,4,128]{2,1,0:T(4,128)}), f32[64,4,128]{2,1,0:T(4,128)S(1)}, u32[]{:S(2)}, u32[]{:S(2)}) %all-to-all-start.4) | async-done | bytes 131104 | tf_op jit(solution)/shard_map/all_to_all | solution.py:32
  137.2 1.8 %shard_map.106 = bf16[512,384]{1,0:T(8,128)(2,1)} custom-call(s32[4]{0:T(128)S(1)} %pad_add_fusion.place_ref, f32[1]{0:T(128)S(6)} %copy.78.logit_ref, f32[64,512]{1,0:T(8,128)S(1)} %get-tuple-element.13.scores_ref, f32[8,128]{1,0:T(8,128)S(1)} %bitcast.55, f32[256,128]{1,0:T(8,128)S(1)} %bitcast.54, s32[64,1]{1,0:T(8,128)S(1)} %convert_element_type.91.row_pos_ref, ...), custom_call_target="tpu_custom_call" | custom-call | tf_op jit(solution)/shard_map/pallas_call | solution.py:43
  139.0 3.5 %all-to-all-start.5 = ((bf16[8,64,384]{2,1,0:T(8,128)(2,1)}), bf16[8,64,384]{2,1,0:T(8,128)(2,1)S(1)}, u32[]{:S(2)}, u32[]{:S(2)}) async-start(bf16[8,64,384]{2,1,0:T(8,128)(2,1)} %bitcast.20), calls=%async_computation.5 | async-start | bytes 786432 | tf_op jit(solution)/shard_map/all_to_all | solution.py:32
  144.8 12.7 %all-to-all-done.5 = bf16[8,64,384]{2,1,0:T(8,128)(2,1)S(1)} async-done(((bf16[8,64,384]{2,1,0:T(8,128)(2,1)}), bf16[8,64,384]{2,1,0:T(8,128)(2,1)S(1)}, u32[]{:S(2)}, u32[]{:S(2)}) %all-to-all-start.5) | async-done | bytes 393248 | tf_op jit(solution)/shard_map/all_to_all | solution.py:32
  158.7 3.4 %all-to-all-start.6 = ((bf16[8,8,768]{2,1,0:T(8,128)(2,1)}), bf16[8,8,768]{2,1,0:T(8,128)(2,1)S(1)}, u32[]{:S(2)}, u32[]{:S(2)}) async-start(bf16[8,8,768]{2,1,0:T(8,128)(2,1)} %bitcast.23), calls=%async_computation.6 | async-start | bytes 196608 | tf_op jit(solution)/shard_map/all_to_all | solution.py:32
  162.7 6.7 %all-to-all-done.6 = bf16[8,8,768]{2,1,0:T(8,128)(2,1)S(1)} async-done(((bf16[8,8,768]{2,1,0:T(8,128)(2,1)}), bf16[8,8,768]{2,1,0:T(8,128)(2,1)S(1)}, u32[]{:S(2)}, u32[]{:S(2)}) %all-to-all-start.6) | async-done | bytes 98336 | tf_op jit(solution)/shard_map/all_to_all | solution.py:32
  174.7 2.1 %fusion.21 = bf16[1,3,48,1664]{3,2,1,0:T(8,128)(2,1)} fusion(f32[3,48]{1,0:T(4,128)S(1)} %negate_multiply_fusion.1, f32[3,48]{1,0:T(4,128)S(1)} %get-tuple-element.40, f32[3,48]{1,0:T(4,128)S(1)} %get-tuple-element.39, f32[3,48]{1,0:T(4,128)S(1)} %broadcast_multiply_fusion.5, f32[1664]{0:T(1024)S(1)} %copy-done.3, f32[3,1664]{1,0:T(4,128)S(1)} %broadcast_multiply_fusion, ...), kind=kLoop, calls=%fused_computation.37 | loop fusion | flops 2156544 | bytes 987396 | tf_op jit(solution)/shard_map/broadcast_in_dim | solution.py:334
  (97 shorter events, 23.4 us)
Async XLA Ops:
  0.6 4.9 %copy-start = (bf16[12,64,1280]{2,1,0:T(8,128)(2,1)S(1)}, bf16[12,64,1280]{2,1,0:T(8,128)(2,1)}, u32[]{:S(2)}) copy-start(bf16[12,64,1280]{2,1,0:T(8,128)(2,1)} %param.9) | copy-start | bytes 5898244
  5.5 1.0 copy-start.4
  5.9 1.7 copy-start.2
  5.9 1.7 copy-start.3
  8.5 12.0 %copy-start.5 = (bf16[13,1280]{1,0:T(8,128)(2,1)S(1)}, bf16[13,1280]{1,0:T(8,128)(2,1)}, u32[]{:S(2)}) copy-start(bf16[13,1280]{1,0:T(8,128)(2,1)} %param.10) | copy-start | bytes 99844
  8.6 12.0 %copy-start.6 = (bf16[10,1280]{1,0:T(8,128)(2,1)S(1)}, bf16[10,1280]{1,0:T(8,128)(2,1)}, u32[]{:S(2)}) copy-start(bf16[10,1280]{1,0:T(8,128)(2,1)} %param.11) | copy-start | bytes 76804
  11.4 23.1 %copy-start.7 = (s32[12]{0:T(128)S(1)}, s32[12]{0:T(128)}, u32[]{:S(2)}) copy-start(s32[12]{0:T(128)} %param.15) | copy-start | bytes 148
  12.3 22.3 %collective-permute-start = (bf16[12,1536]{1,0:T(8,128)(2,1)S(1)}, bf16[12,1536]{1,0:T(8,128)(2,1)S(1)}, u32[]{:S(2)}, u32[]{:S(2)}) collective-permute-start(bf16[12,1536]{1,0:T(8,128)(2,1)S(1)} %fusion.22), channel_id=1, source_target_pairs={{0,64},{64,0},{1,65},{65,1},{2,66},{66,2},{3,67},{67,3},{4,68},{68... | collective-permute-start | bytes 110600 | tf_op jit(solution)/shard_map/ppermute | solution.py:263
  21.6 29.7 %all-to-all-start = ((bf16[32,24,384]{2,1,0:T(8,128)(2,1)}), bf16[32,24,384]{2,1,0:T(8,128)(2,1)S(1)}, u32[]{:S(2)}, u32[]{:S(2)}) async-start(bf16[32,24,384]{2,1,0:T(8,128)(2,1)} %broadcast_in_dim.107), calls=%async_computation | async-start | bytes 1179648 | tf_op jit(solution)/shard_map/all_to_all | solution.py:32
  59.5 16.4 %all-to-all-start.1 = ((bf16[8,48,384]{2,1,0:T(8,128)(2,1)}), bf16[8,48,384]{2,1,0:T(8,128)(2,1)S(1)}, u32[]{:S(2)}, u32[]{:S(2)}) async-start(bf16[8,48,384]{2,1,0:T(8,128)(2,1)} %bitcast.7), calls=%async_computation.1 | async-start | bytes 589824 | tf_op jit(solution)/shard_map/all_to_all | solution.py:32
  77.5 23.2 %all-to-all-start.2 = ((bf16[32,8,1280]{2,1,0:T(8,128)(2,1)}), bf16[32,8,1280]{2,1,0:T(8,128)(2,1)S(1)}, u32[]{:S(2)}, u32[]{:S(2)}) async-start(bf16[32,8,1280]{2,1,0:T(8,128)(2,1)} %bitcast.10), calls=%async_computation.2 | async-start | bytes 1310720 | tf_op jit(solution)/shard_map/all_to_all | solution.py:32
  109.8 9.7 %all-to-all-start.3 = ((f32[8,1,128]{2,1,0:T(1,128)}), f32[8,1,128]{2,1,0:T(1,128)S(1)}, u32[]{:S(2)}, u32[]{:S(2)}) async-start(f32[8,1,128]{2,1,0:T(1,128)} %bitcast.14), calls=%async_computation.3 | async-start | bytes 8192 | tf_op jit(solution)/shard_map/all_to_all | solution.py:32
  119.4 17.7 %all-to-all-start.4 = ((f32[64,4,128]{2,1,0:T(4,128)}), f32[64,4,128]{2,1,0:T(4,128)S(1)}, u32[]{:S(2)}, u32[]{:S(2)}) async-start(f32[64,4,128]{2,1,0:T(4,128)} %bitcast.16), calls=%async_computation.4 | async-start | bytes 262144 | tf_op jit(solution)/shard_map/all_to_all | solution.py:32
  139.0 18.5 %all-to-all-start.5 = ((bf16[8,64,384]{2,1,0:T(8,128)(2,1)}), bf16[8,64,384]{2,1,0:T(8,128)(2,1)S(1)}, u32[]{:S(2)}, u32[]{:S(2)}) async-start(bf16[8,64,384]{2,1,0:T(8,128)(2,1)} %bitcast.20), calls=%async_computation.5 | async-start | bytes 786432 | tf_op jit(solution)/shard_map/all_to_all | solution.py:32
  158.7 10.7 %all-to-all-start.6 = ((bf16[8,8,768]{2,1,0:T(8,128)(2,1)}), bf16[8,8,768]{2,1,0:T(8,128)(2,1)S(1)}, u32[]{:S(2)}, u32[]{:S(2)}) async-start(bf16[8,8,768]{2,1,0:T(8,128)(2,1)} %bitcast.23), calls=%async_computation.6 | async-start | bytes 196608 | tf_op jit(solution)/shard_map/all_to_all | solution.py:32
  170.2 3.7 %copy-start.1 = (bf16[12,64,1280]{2,1,0:T(8,128)(2,1)S(1)}, bf16[12,64,1280]{2,1,0:T(8,128)(2,1)}, u32[]{:S(2)}) copy-start(bf16[12,64,1280]{2,1,0:T(8,128)(2,1)} %param.9) | copy-start | bytes 5898244

commit v4 on v3

--- a/solution.py
+++ b/solution.py
@@ -20,12 +20,6 @@
     center = values - jnp.mean(values, axis=-1, keepdims=True)
     spread = jnp.mean(center * center, axis=-1, keepdims=True)
     return center * lax.rsqrt(spread + 1e-05) * gain_vector
-
-
-def token_back(token_block, gain_vector, pool_cot):
-    spread_cot = jnp.broadcast_to(pool_cot[:, None, :], token_block.shape)
-    _, pull_back = jax.vjp(lambda token_piece: norm_tokens(token_piece, gain_vector), token_block)
-    return pull_back(spread_cot)[0]
 
 
 def exchange(blocks, axes):
@@ -231,6 +225,40 @@
     out_ref[...] = jnp.where(first, a, b).astype(BF)
 
 
+def token_kernel(pool_ref, inv_ref, img_ref, txt_ref, ig_ref, tg_ref, img_out, txt_out):
+    pool = pool_ref[...]
+    inv = inv_ref[...][:, :1]
+    for x_ref, gain_ref, out_ref, wide, skip, at in (
+        (img_ref, ig_ref, img_out, 13, 0, 0),
+        (txt_ref, tg_ref, txt_out, 10, 13, 4),
+    ):
+        dense = lax.broadcasted_iota(jnp.int32, (1, 32 * wide), 1)
+        place = ((dense // wide) % 2) * 384 + (dense // (2 * wide)) * 24 + skip + dense % wide
+        lane = lax.broadcasted_iota(jnp.int32, (768, 32 * wide), 0)
+        pick = jnp.where(lane == place, 1.0, 0.0).astype(BF)
+        found = jnp.dot(pool, pick, preferred_element_type=F32)
+        halves = [
+            found[32 * k : 32 * k + 8]
+            + found[32 * k + 8 : 32 * k + 16]
+            + found[32 * k + 16 : 32 * k + 24]
+            + found[32 * k + 24 : 32 * k + 32]
+            for k in range(2)
+        ]
+        cot = jnp.concatenate([halves[0][:4], halves[0][4:], halves[1][:4], halves[1][4:]], 1)
+        cot = cot * inv[at : at + 4] * gain_ref[...]
+        mean_cot = jnp.mean(cot, axis=1, keepdims=True)
+        count = x_ref.shape[0] // 3
+        for q in range(3):
+            span = slice(count * q, count * q + count)
+            values = x_ref[span, :].astype(F32)
+            center = values - jnp.mean(values, axis=1, keepdims=True)
+            inner = lax.rsqrt(jnp.mean(center * center, axis=1, keepdims=True) + 1e-05)
+            mine = cot[q : q + 1]
+            along = jnp.mean(center * mine, axis=1, keepdims=True)
+            out = inner * (mine - mean_cot[q : q + 1]) - center * (inner * inner * inner * along)
+            out_ref[span, :] = out.astype(BF)
+
+
 def per_device(image_in, text_in, proj_img, proj_txt, img_gain, txt_gain, logit_scale, positive):
     t_index = lax.axis_index("t")
     h_index = lax.axis_index("h")
@@ -254,19 +282,12 @@
         2,
     )
     slabs = slabs.reshape(12, 2, 2, 16, 2, 24).transpose(0, 1, 2, 4, 3, 5).reshape(12, 2, 1536)
-    first = h_index == 0
-    mine = jnp.where(first, slabs[:, 0], slabs[:, 1])
-    theirs = jnp.where(first, slabs[:, 1], slabs[:, 0])
-    digits = jnp.stack([positive // 32, positive % 32], 1).astype(BF)
+    digits = jnp.stack([positive // 32, positive % 32], 1).astype(BF)[:, :, None]
     spot = lax.iota(jnp.int32, 1536)[None, :]
-    theirs = jnp.where(spot == 23, digits[:, :1], jnp.where(spot == 47, digits[:, 1:], theirs))
-    theirs = lax.ppermute(theirs, "h", [(0, 1), (1, 0)])
-    pooled = jnp.concatenate([jnp.where(first, mine, theirs), jnp.where(first, theirs, mine)], 0)
-    own_pos = positive.astype(F32)
-    their_pos = theirs[:, 23].astype(F32) * 32.0 + theirs[:, 47].astype(F32)
-    row_pos = jnp.concatenate(
-        [jnp.where(first, own_pos, their_pos), jnp.where(first, their_pos, own_pos)]
-    )
+    slabs = jnp.where(spot == 23, digits[:, :1], jnp.where(spot == 47, digits[:, 1:], slabs))
+    both = lax.all_gather(slabs.transpose(1, 0, 2), "h", axis=0)
+    pooled = lax.dynamic_index_in_dim(both, h_index, 1, keepdims=False).reshape(24, 1536)
+    row_pos = pooled[:, 23].astype(F32) * 32.0 + pooled[:, 47].astype(F32)
     row_pos = jnp.pad(row_pos.reshape(8, 3), ((0, 0), (0, 5)), constant_values=-1.0)
     row_pos = row_pos.reshape(64, 1).astype(jnp.int32)
     is_img = spot % 24 < 13
@@ -322,15 +343,18 @@
         back_kernel, [((64, 768), BF), ((8, 128), F32)], [got, unit_part, wa, wb]
     )
     mean_loss = loss[0, :1]
-    pool = exchange(pool.reshape(8, 8, 768), Y).astype(F32)
-    pool = jnp.sum(pool.reshape(2, 4, 2, 4, 2, 16, 24), axis=1)
-    pool = pool.transpose(2, 0, 1, 4, 3, 5)[:3].reshape(3, 128, 24)
-    img_pool_cot = pool[:, :, :13].reshape(3, -1) * inv[:3, :1]
-    txt_pool_cot = pool[:, :, 13:23].reshape(3, -1) * inv[4:7, :1]
-    img_own = lax.dynamic_slice_in_dim(image_in, 3 * t_index, 3, 0)
-    txt_own = lax.dynamic_slice_in_dim(text_in, 3 * t_index, 3, 0)
-    img_grads = token_back(img_own, img_gain, img_pool_cot)
-    txt_grads = token_back(txt_own, txt_gain, txt_pool_cot)
+    pool = exchange(pool.reshape(8, 8, 768), Y).reshape(64, 768)
+    count_i, width_i = image_in.shape[1:]
+    count_t, width_t = text_in.shape[1:]
+    img_own = lax.dynamic_slice_in_dim(image_in, 3 * t_index, 3, 0).reshape(-1, width_i)
+    txt_own = lax.dynamic_slice_in_dim(text_in, 3 * t_index, 3, 0).reshape(-1, width_t)
+    img_grads, txt_grads = kernel_call(
+        token_kernel,
+        [(img_own.shape, BF), (txt_own.shape, BF)],
+        [pool, inv, img_own, txt_own, img_gain[None], txt_gain[None]],
+    )
+    img_grads = img_grads.reshape(3, count_i, width_i)
+    txt_grads = txt_grads.reshape(3, count_t, width_t)
     return (mean_loss, img_grads[None], txt_grads[None])
 
 

time: 179 us -> 164 us (0.916)
  waiting for transfers between devices: 83 us -> 66.1 us
  other arithmetic: 19.5 us -> 8.53 us
  blocking collectives: 14 us -> 22.9 us
  Pallas kernels: 7.55 us -> 9.58 us
    all_to_all x7, waiting for transfers between devices: 83 us -> 66.1 us  [exchange(): return lax.all_to_all(blocks, axes, 0, 0, tiled=True)]
    all_to_all x7, starting transfers between devices: 37.6 us -> 47.1 us  [exchange(): return lax.all_to_all(blocks, axes, 0, 0, tiled=True)]
    all_gather x0 -> x1, blocking collectives: none -> 8.38 us  [per_device(): both = lax.all_gather(slabs.transpose(1, 0, 2), 'h', axis=0)]
    ppermute x1 -> x0, starting transfers between devices: 8.27 us -> none  [per_device(): theirs = lax.ppermute(theirs, 'h', [(0, 1), (1, 0)])]
    reduce_sum x6 -> x2, other arithmetic: 6.36 us -> 2.32 us  [norm_tokens(): center = values - jnp.mean(values, axis=-1, keepdims=True)]
    reduce_sum x4 -> x2, other arithmetic: 4.51 us -> 1.28 us  [norm_tokens(): spread = jnp.mean(center * center, axis=-1, keepdims=True)]
    broadcast_in_dim x2 -> x0, other arithmetic: 3.24 us -> none  [per_device(): return (mean_loss, img_grads[None], txt_grads[None])]
    dynamic_slice x0 -> x3, local copies, waits for them, and re-layouts: none -> 2.14 us  [the longest x1 1.07 us: per_device(): lax.dynamic_slice_in_dim(text_in, 3 * t_index, 3, 0).reshape(-1, width_t)]
  transfers between devices with their start and end apart: 8 -> 7, of which waited for: 7 -> 6; matrix products, arithmetic and copies ran while one was open for 3% -> 8% of each run, Pallas kernels for 0% -> 0%
where the time goes in v4:
time: 164 us; the launch traced here: 163 us
  waiting for transfers between devices  66.1 us (40%)
  starting transfers between devices  47.1 us (29%)
  blocking collectives  22.9 us (14%)
  Pallas kernels  9.58 us (6%)
  other arithmetic  8.53 us (5%)
  local copies, waits for them, and re-layouts  6.84 us (4%)
  between operations  1.67 us (1%)
    all_to_all x7, waiting for transfers between devices, exchange(): return lax.all_to_all(blocks, axes, 0, 0, tiled=True)  66.1 us
    all_to_all x7, starting transfers between devices, exchange(): return lax.all_to_all(blocks, axes, 0, 0, tiled=True)  47.1 us
    all_gather x4, blocking collectives, both_cores(): lax.all_gather(part, 'c', axis=0)  14.5 us
    pallas_call x6, Pallas kernels, kernel_call(): pl.pallas_call(body, out_shape=[jax.ShapeDtypeStruct(shape, kind) for sha...  9.58 us
    all_gather x1, blocking collectives, per_device(): both = lax.all_gather(slabs.transpose(1, 0, 2), 'h', axis=0)  8.38 us
  transfers between devices with their start and end apart: 7, of which 6 were waited for; matrix products, arithmetic and copies ran while one was open for 8% of the time, Pallas kernels for 0%

profile of v4, /device:TPU:1, one launch (start us, length us, event | category | flops | bytes accessed | tf_op | source)
XLA Modules:
  0.0 162.8 jit_solution(5504987621319465725)
XLA Ops:
  2.3 13.7 %all-to-all-start = ((bf16[32,24,384]{2,1,0:T(8,128)(2,1)}), bf16[32,24,384]{2,1,0:T(8,128)(2,1)S(1)}, u32[]{:S(2)}, u32[]{:S(2)}) async-start(bf16[32,24,384]{2,1,0:T(8,128)(2,1)} %broadcast_in_dim.78), calls=%async_computation | async-start | bytes 1179648 | tf_op jit(solution)/shard_map/all_to_all | solution.py:26
  16.1 2.0 %convert_reduce_fusion.1 = f32[12,48]{1,0:T(8,128)S(1)} fusion(bf16[12,48,1664]{2,1,0:T(8,128)(2,1)} %param.8), kind=kLoop, calls=%fused_computation.3 | loop fusion | flops 1916352 | bytes 1919232 | tf_op jit(solution)/shard_map/reduce_sum | solution.py:20
  25.5 8.4 %all-gather = bf16[4,12,1536]{2,1,0:T(8,128)(2,1)S(1)} all-gather(bf16[2,12,1536]{2,1,0:T(8,128)(2,1)S(1)} %copy.37), channel_id=2, replica_groups=mesh['t'=4,'h'=2,'z'=8,'x'=4,'c'=2] {'h'}, dimensions={0}, use_global_device_ids=true | all-gather | bytes 221184 | tf_op jit(solution)/shard_map/all_gather | solution.py:288
  34.6 5.0 %all-gather.1 = bf16[32,24,384]{2,1,0:T(8,128)(2,1)S(1)} all-gather(bf16[16,24,384]{2,1,0:T(8,128)(2,1)S(1)} %get-tuple-element.28), channel_id=3, replica_groups=mesh['t'=4,'h'=2,'z'=8,'x'=4,'c'=2] {'c'}, dimensions={0}, use_global_device_ids=true | all-gather | bytes 884736 | tf_op jit(solution)/shard_map/all_gather | solution.py:31
  39.6 2.2 %all-gather.2 = bf16[32,24,384]{2,1,0:T(8,128)(2,1)S(1)} all-gather(bf16[16,24,384]{2,1,0:T(8,128)(2,1)S(1)} %get-tuple-element.27), channel_id=4, replica_groups=mesh['t'=4,'h'=2,'z'=8,'x'=4,'c'=2] {'c'}, dimensions={0}, use_global_device_ids=true | all-gather | bytes 884736 | tf_op jit(solution)/shard_map/all_gather | solution.py:31
  42.8 7.4 %all-to-all-start.1 = ((bf16[8,48,384]{2,1,0:T(8,128)(2,1)}), bf16[8,48,384]{2,1,0:T(8,128)(2,1)S(1)}, u32[]{:S(2)}, u32[]{:S(2)}) async-start(bf16[8,48,384]{2,1,0:T(8,128)(2,1)} %bitcast.9), calls=%async_computation.1 | async-start | bytes 589824 | tf_op jit(solution)/shard_map/all_to_all | solution.py:26
  50.4 12.2 %all-to-all-done.1 = bf16[8,48,384]{2,1,0:T(8,128)(2,1)S(1)} async-done(((bf16[8,48,384]{2,1,0:T(8,128)(2,1)}), bf16[8,48,384]{2,1,0:T(8,128)(2,1)S(1)}, u32[]{:S(2)}, u32[]{:S(2)}) %all-to-all-start.1) | async-done | bytes 294944 | tf_op jit(solution)/shard_map/all_to_all | solution.py:26
  62.6 1.6 shard_map.104
  64.2 9.2 %all-to-all-start.2 = ((bf16[32,8,1280]{2,1,0:T(8,128)(2,1)}), bf16[32,8,1280]{2,1,0:T(8,128)(2,1)S(1)}, u32[]{:S(2)}, u32[]{:S(2)}) async-start(bf16[32,8,1280]{2,1,0:T(8,128)(2,1)} %bitcast.12), calls=%async_computation.2 | async-start | bytes 1310720 | tf_op jit(solution)/shard_map/all_to_all | solution.py:26
  74.5 17.0 %all-to-all-done.2 = bf16[32,8,1280]{2,1,0:T(8,128)(2,1)S(1)} async-done(((bf16[32,8,1280]{2,1,0:T(8,128)(2,1)}), bf16[32,8,1280]{2,1,0:T(8,128)(2,1)S(1)}, u32[]{:S(2)}, u32[]{:S(2)}) %all-to-all-start.2) | async-done | bytes 655392 | tf_op jit(solution)/shard_map/all_to_all | solution.py:26
  91.5 5.0 %all-gather.3 = bf16[32,8,1280]{2,1,0:T(8,128)(2,1)S(1)} all-gather(bf16[16,8,1280]{2,1,0:T(8,128)(2,1)S(1)} %get-tuple-element.26), channel_id=5, replica_groups=mesh['t'=4,'h'=2,'z'=8,'x'=4,'c'=2] {'c'}, dimensions={0}, use_global_device_ids=true | all-gather | bytes 983040 | tf_op jit(solution)/shard_map/all_gather | solution.py:31
  96.7 2.3 %all-gather.4 = bf16[32,8,1280]{2,1,0:T(8,128)(2,1)S(1)} all-gather(bf16[16,8,1280]{2,1,0:T(8,128)(2,1)S(1)} %get-tuple-element.25), channel_id=6, replica_groups=mesh['t'=4,'h'=2,'z'=8,'x'=4,'c'=2] {'c'}, dimensions={0}, use_global_device_ids=true | all-gather | bytes 983040 | tf_op jit(solution)/shard_map/all_gather | solution.py:31
  99.0 2.0 %shard_map.105 = (f32[64,512]{1,0:T(8,128)S(1)}, f32[8,128]{1,0:T(8,128)}, f32[256,128]{1,0:T(8,128)}) custom-call(s32[4]{0:T(128)S(1)} %pad_add_fusion.place_ref, f32[1]{0:T(128)S(6)} %copy.53.logit_ref, bf16[64,1280]{1,0:T(8,128)(2,1)S(1)} %get-tuple-element.13.rows_ref, bf16[256,1280]{1,0:T(8,128)(2,1)S(1)} %bitcast.44, bf16[256,1280]{1,0:T(8,128)(2,1)S(1)} %bitcast.46, ...), custom_call_target="tpu_custom_call" | custom-call | tf_op jit(solution)/shard_map/pallas_call | solution.py:37
  101.0 3.3 %all-to-all-start.3 = ((f32[8,1,128]{2,1,0:T(1,128)}), f32[8,1,128]{2,1,0:T(1,128)S(1)}, u32[]{:S(2)}, u32[]{:S(2)}) async-start(f32[8,1,128]{2,1,0:T(1,128)} %bitcast.16), calls=%async_computation.3 | async-start | bytes 8192 | tf_op jit(solution)/shard_map/all_to_all | solution.py:26
  104.4 6.3 %all-to-all-done.3 = f32[8,1,128]{2,1,0:T(1,128)S(1)} async-done(((f32[8,1,128]{2,1,0:T(1,128)}), f32[8,1,128]{2,1,0:T(1,128)S(1)}, u32[]{:S(2)}, u32[]{:S(2)}) %all-to-all-start.3) | async-done | bytes 4128 | tf_op jit(solution)/shard_map/all_to_all | solution.py:26
  110.7 6.7 %all-to-all-start.4 = ((f32[64,4,128]{2,1,0:T(4,128)}), f32[64,4,128]{2,1,0:T(4,128)S(1)}, u32[]{:S(2)}, u32[]{:S(2)}) async-start(f32[64,4,128]{2,1,0:T(4,128)} %bitcast.18), calls=%async_computation.4 | async-start | bytes 262144 | tf_op jit(solution)/shard_map/all_to_all | solution.py:26
  117.6 10.9 %all-to-all-done.4 = f32[64,4,128]{2,1,0:T(4,128)S(1)} async-done(((f32[64,4,128]{2,1,0:T(4,128)}), f32[64,4,128]{2,1,0:T(4,128)S(1)}, u32[]{:S(2)}, u32[]{:S(2)}) %all-to-all-start.4) | async-done | bytes 131104 | tf_op jit(solution)/shard_map/all_to_all | solution.py:26
  128.5 1.8 %shard_map.106 = bf16[512,384]{1,0:T(8,128)(2,1)} custom-call(s32[4]{0:T(128)S(1)} %pad_add_fusion.place_ref, f32[1]{0:T(128)S(6)} %copy.53.logit_ref, f32[64,512]{1,0:T(8,128)S(1)} %get-tuple-element.15.scores_ref, f32[8,128]{1,0:T(8,128)S(1)} %bitcast.58, f32[256,128]{1,0:T(8,128)S(1)} %bitcast.56, s32[64,1]{1,0:T(8,128)S(1)} %convert_element_type.79.row_pos_ref, ...), custom_call_target="tpu_custom_call" | custom-call | tf_op jit(solution)/shard_map/pallas_call | solution.py:37
  130.3 3.5 %all-to-all-start.5 = ((bf16[8,64,384]{2,1,0:T(8,128)(2,1)}), bf16[8,64,384]{2,1,0:T(8,128)(2,1)S(1)}, u32[]{:S(2)}, u32[]{:S(2)}) async-start(bf16[8,64,384]{2,1,0:T(8,128)(2,1)} %bitcast.22), calls=%async_computation.5 | async-start | bytes 786432 | tf_op jit(solution)/shard_map/all_to_all | solution.py:26
  134.9 13.9 %all-to-all-done.5 = bf16[8,64,384]{2,1,0:T(8,128)(2,1)S(1)} async-done(((bf16[8,64,384]{2,1,0:T(8,128)(2,1)}), bf16[8,64,384]{2,1,0:T(8,128)(2,1)S(1)}, u32[]{:S(2)}, u32[]{:S(2)}) %all-to-all-start.5) | async-done | bytes 393248 | tf_op jit(solution)/shard_map/all_to_all | solution.py:26
  148.8 1.2 shard_map.107
  150.0 3.4 %all-to-all-start.6 = ((bf16[8,8,768]{2,1,0:T(8,128)(2,1)}), bf16[8,8,768]{2,1,0:T(8,128)(2,1)S(1)}, u32[]{:S(2)}, u32[]{:S(2)}) async-start(bf16[8,8,768]{2,1,0:T(8,128)(2,1)} %bitcast.25), calls=%async_computation.6 | async-start | bytes 196608 | tf_op jit(solution)/shard_map/all_to_all | solution.py:26
  155.0 5.8 %all-to-all-done.6 = bf16[8,8,768]{2,1,0:T(8,128)(2,1)S(1)} async-done(((bf16[8,8,768]{2,1,0:T(8,128)(2,1)}), bf16[8,8,768]{2,1,0:T(8,128)(2,1)S(1)}, u32[]{:S(2)}, u32[]{:S(2)}) %all-to-all-start.6) | async-done | bytes 98336 | tf_op jit(solution)/shard_map/all_to_all | solution.py:26
  160.7 2.0 %shard_map.108 = (bf16[144,1664]{1,0:T(8,128)(2,1)}, bf16[192,1280]{1,0:T(8,128)(2,1)}) custom-call(bf16[64,768]{1,0:T(8,128)(2,1)S(1)} %bitcast.57, f32[8,128]{1,0:T(8,128)S(1)} %get-tuple-element.20.inv_ref, bf16[144,1664]{1,0:T(8,128)(2,1)S(1)} %bitcast.53, bf16[192,1280]{1,0:T(8,128)(2,1)S(1)} %bitcast.52, f32[1,1664]{1,0:T(1,128)S(1)} %broadcast_in_dim.80.ig_ref, ...), custom_call_target="tpu_custom_call" | custom-call | tf_op jit(solution)/shard_map/pallas_call | solution.py:37
  (69 shorter events, 14.4 us)
Async XLA Ops:
  2.3 32.2 %all-to-all-start = ((bf16[32,24,384]{2,1,0:T(8,128)(2,1)}), bf16[32,24,384]{2,1,0:T(8,128)(2,1)S(1)}, u32[]{:S(2)}, u32[]{:S(2)}) async-start(bf16[32,24,384]{2,1,0:T(8,128)(2,1)} %broadcast_in_dim.78), calls=%async_computation | async-start | bytes 1179648 | tf_op jit(solution)/shard_map/all_to_all | solution.py:26
  16.0 2.1 %copy-start.1 = (bf16[12,48,1664]{2,1,0:T(8,128)(2,1)S(1)}, bf16[12,48,1664]{2,1,0:T(8,128)(2,1)}, u32[]{:S(2)}) copy-start(bf16[12,48,1664]{2,1,0:T(8,128)(2,1)} %param.8) | copy-start | bytes 5750788
  16.1 2.7 %copy-start.2 = (f32[1664]{0:T(1024)S(1)}, f32[1664]{0:T(1024)}, u32[]{:S(2)}) copy-start(f32[1664]{0:T(1024)} %param.12) | copy-start | bytes 19972
  18.2 2.4 %copy-start = (bf16[12,64,1280]{2,1,0:T(8,128)(2,1)S(1)}, bf16[12,64,1280]{2,1,0:T(8,128)(2,1)}, u32[]{:S(2)}) copy-start(bf16[12,64,1280]{2,1,0:T(8,128)(2,1)} %param.9) | copy-start | bytes 5898244
  20.6 1.0 copy-start.3
  22.6 2.7 %copy-start.4 = (s32[12]{0:T(128)S(1)}, s32[12]{0:T(128)}, u32[]{:S(2)}) copy-start(s32[12]{0:T(128)} %param.15) | copy-start | bytes 148
  42.8 19.8 %all-to-all-start.1 = ((bf16[8,48,384]{2,1,0:T(8,128)(2,1)}), bf16[8,48,384]{2,1,0:T(8,128)(2,1)S(1)}, u32[]{:S(2)}, u32[]{:S(2)}) async-start(bf16[8,48,384]{2,1,0:T(8,128)(2,1)} %bitcast.9), calls=%async_computation.1 | async-start | bytes 589824 | tf_op jit(solution)/shard_map/all_to_all | solution.py:26
  64.2 27.2 %all-to-all-start.2 = ((bf16[32,8,1280]{2,1,0:T(8,128)(2,1)}), bf16[32,8,1280]{2,1,0:T(8,128)(2,1)S(1)}, u32[]{:S(2)}, u32[]{:S(2)}) async-start(bf16[32,8,1280]{2,1,0:T(8,128)(2,1)} %bitcast.12), calls=%async_computation.2 | async-start | bytes 1310720 | tf_op jit(solution)/shard_map/all_to_all | solution.py:26
  101.0 9.7 %all-to-all-start.3 = ((f32[8,1,128]{2,1,0:T(1,128)}), f32[8,1,128]{2,1,0:T(1,128)S(1)}, u32[]{:S(2)}, u32[]{:S(2)}) async-start(f32[8,1,128]{2,1,0:T(1,128)} %bitcast.16), calls=%async_computation.3 | async-start | bytes 8192 | tf_op jit(solution)/shard_map/all_to_all | solution.py:26
  110.7 17.8 %all-to-all-start.4 = ((f32[64,4,128]{2,1,0:T(4,128)}), f32[64,4,128]{2,1,0:T(4,128)S(1)}, u32[]{:S(2)}, u32[]{:S(2)}) async-start(f32[64,4,128]{2,1,0:T(4,128)} %bitcast.18), calls=%async_computation.4 | async-start | bytes 262144 | tf_op jit(solution)/shard_map/all_to_all | solution.py:26
  130.3 18.5 %all-to-all-start.5 = ((bf16[8,64,384]{2,1,0:T(8,128)(2,1)}), bf16[8,64,384]{2,1,0:T(8,128)(2,1)S(1)}, u32[]{:S(2)}, u32[]{:S(2)}) async-start(bf16[8,64,384]{2,1,0:T(8,128)(2,1)} %bitcast.22), calls=%async_computation.5 | async-start | bytes 786432 | tf_op jit(solution)/shard_map/all_to_all | solution.py:26
  150.0 10.7 %all-to-all-start.6 = ((bf16[8,8,768]{2,1,0:T(8,128)(2,1)}), bf16[8,8,768]{2,1,0:T(8,128)(2,1)S(1)}, u32[]{:S(2)}, u32[]{:S(2)}) async-start(bf16[8,8,768]{2,1,0:T(8,128)(2,1)} %bitcast.25), calls=%async_computation.6 | async-start | bytes 196608 | tf_op jit(solution)/shard_map/all_to_all | solution.py:26

commit v5 on v4

--- a/solution.py
+++ b/solution.py
@@ -55,23 +55,23 @@
         out_ref[48 * k : 48 * k + 48, :] = part
 
 
+def in_blocks(values):
+    blank = jnp.zeros((1, values.shape[1]), F32)
+    pieces = []
+    for k in range(8):
+        pieces += [values[6 * k : 6 * k + 3], blank, values[6 * k + 3 : 6 * k + 6], blank]
+    return jnp.concatenate(pieces, 0)
+
+
 def unit_kernel(place_ref, parts_ref, digits_ref, rows_ref, far_ref, inv_ref, held, held_inv):
     spread = parts_ref[...].astype(F32)
     emb = rows_ref.shape[1]
     blocks = [spread[48 * k : 48 * k + 48] + spread[192 + 48 * k : 240 + 48 * k] for k in range(4)]
     projected = jnp.concatenate(blocks, 1)[:, :emb]
     inv = lax.rsqrt(jnp.sum(projected * projected, axis=1, keepdims=True) + 1e-06)
-
-    def in_blocks(values):
-        blank = jnp.zeros((1, values.shape[1]), F32)
-        pieces = []
-        for k in range(8):
-            pieces += [values[6 * k : 6 * k + 3], blank, values[6 * k + 3 : 6 * k + 6], blank]
-        return jnp.concatenate(pieces, 0)
-
-    unit = in_blocks(projected * inv)
+    unit = projected * inv
     rows_ref[...] = unit.astype(BF)
-    held[...] = unit
+    held[...] = in_blocks(unit)
     held_inv[...] = in_blocks(jnp.broadcast_to(inv, (48, 128)))
     own = pl.ds(pl.multiple_of(8 * place_ref[0], 8), 8)
     inv_ref[...] = held_inv[own, :]
@@ -86,19 +86,19 @@
 
 def tile_masks(place_ref):
     h, t, g = place_ref[1], place_ref[2], place_ref[3]
-    row = lax.broadcasted_iota(jnp.int32, (64, 512), 0)
-    item = lax.broadcasted_iota(jnp.int32, (64, 512), 1)
+    row = lax.broadcasted_iota(jnp.int32, (48, 512), 0)
+    item = lax.broadcasted_iota(jnp.int32, (48, 512), 1)
     item_g = ((item // 256) * 16 + (item % 128) // 8) * 2 + (item // 128) % 2
     item_pair = (h * 64 + item_g) * 12 + 3 * t + item % 4
-    row_pair = ((row // 32) * 64 + g) * 12 + ((row // 8) % 4) * 3 + row % 4
-    row_txt, item_txt = (row % 8) // 4, (item % 8) // 4
-    valid = (row_txt != item_txt) & (row % 4 < 3) & (item % 4 < 3)
+    row_pair = ((row // 24) * 64 + g) * 12 + ((row // 6) % 4) * 3 + row % 3
+    row_txt, item_txt = (row % 6) // 3, (item % 8) // 4
+    valid = (row_txt != item_txt) & (item % 4 < 3)
     return valid, row_pair, item_pair, row_txt, item
 
 
 def square_mask():
-    down = lax.broadcasted_iota(jnp.int32, (64, 128), 0)
-    along = lax.broadcasted_iota(jnp.int32, (64, 128), 1)
+    down = lax.broadcasted_iota(jnp.int32, (48, 128), 0)
+    along = lax.broadcasted_iota(jnp.int32, (48, 128), 1)
     return down == along
 
 
@@ -115,9 +115,7 @@
     return largest + jnp.log(jnp.sum(jnp.exp(values - largest), axis=axis, keepdims=True))
 
 
-def score_kernel(
-    place_ref, logit_ref, rows_ref, fa_ref, fb_ref, row_pos_ref, scores_ref, near_ref, far_ref
-):
+def score_kernel(place_ref, logit_ref, rows_ref, fa_ref, fb_ref, row_pos_ref, scores_ref, far_ref):
     rows = rows_ref[...]
     scores = jnp.concatenate(
         [
@@ -130,8 +128,6 @@
     scores_ref[...] = scores
     valid, _, item_pair, row_txt, _ = tile_masks(place_ref)
     masked = jnp.where(valid, scores, LOW)
-    row_part = as_lanes(log_total(masked, 1))
-    near_ref[...] = jnp.broadcast_to(row_part, (8, 128))
     item_part = log_total(masked, 0)
     hit = valid & (row_txt == 0) & (row_pos_ref[...] == item_pair)
     matched = jnp.sum(
@@ -144,21 +140,20 @@
         far_ref[8 * k : 8 * k + 8, :] = lines
 
 
+def in_parts(values, count):
+    parts = []
+    for _ in range(count):
+        part = values.astype(BF).astype(F32)
+        parts.append(part)
+        values = values - part
+    return parts
+
+
 def coef_kernel(
-    place_ref,
-    logit_ref,
-    scores_ref,
-    near_ref,
-    far_ref,
-    row_pos_ref,
-    item_pos_ref,
-    fa_ref,
-    fb_ref,
-    out_ref,
+    place_ref, logit_ref, scores_ref, far_ref, row_pos_ref, item_pos_ref, fa_ref, fb_ref, out_ref
 ):
     logit = logit_ref[0]
     scores = scores_ref[...]
-    row_lse = as_column(log_total(near_ref[...], 0))
     seen = far_ref[...].reshape(32, 8, 128)
     largest = jnp.max(seen, axis=0)
     largest = jnp.maximum(largest[:4], largest[4:])
@@ -180,49 +175,59 @@
     matched = jnp.sum(jnp.where(lane == 3, summed, 0.0), axis=1, keepdims=True)
     value = lse_total - 2.0 * matched
     masked = jnp.where(valid, scores, LOW)
-    coef = (0.5 * logit) * (
-        jnp.exp(masked - row_lse) + jnp.exp(masked - item_lse) - jnp.where(hit, 2.0, 0.0)
-    )
-    coef = jnp.where(valid, coef, 0.0).astype(BF)
-    along = jnp.sum(coef.astype(F32) * scores, axis=1, keepdims=True) / logit
+    row_part = log_total(masked, 1)
+    by_row = (0.5 * logit) * jnp.exp(masked - row_part)
+    by_item = (0.5 * logit) * (jnp.exp(masked - item_lse) - jnp.where(hit, 2.0, 0.0))
+    coefs = [jnp.where(valid, part, 0.0).astype(BF) for part in (by_row, by_item)]
+    along = [
+        as_lanes(jnp.sum(part.astype(F32) * scores, axis=1, keepdims=True) / logit)
+        for part in coefs
+    ]
+    coef = jnp.concatenate(coefs, 0)
     cot = jnp.dot(coef[:, :256], fa_ref[...], preferred_element_type=F32)
     cot += jnp.dot(coef[:, 256:], fb_ref[...], preferred_element_type=F32)
 
-    riders = []
-    for lanes in (as_lanes(along), jnp.broadcast_to(value, (1, 128))):
-        high = lanes.astype(BF).astype(F32)
-        riders += [high, lanes - high]
-    at = lax.broadcasted_iota(jnp.int32, (64, 128), 0)
-    extra = jnp.zeros((64, 128), F32)
-    for k in range(4):
-        extra = jnp.where(at == 4 * k + 3, riders[k], extra)
-    blank = jnp.zeros((64, 256), F32)
-    extra = jnp.concatenate([extra, blank], 1)
-    cot = jnp.concatenate([cot, blank], 1)
-    for k in range(4):
-        way = (cot[:, 384 * k : 384 * k + 384] + extra).astype(BF)
-        out_ref[64 * k : 64 * k + 64, :] = way
-        out_ref[256 + 64 * k : 320 + 64 * k, :] = way
+    riders = (
+        in_parts(as_lanes(row_part), 3)
+        + in_parts(along[0], 2)
+        + in_parts(along[1], 2)
+        + in_parts(jnp.broadcast_to(value, (1, 128)), 2)
+        + [jnp.zeros((7, 128), F32)]
+    )
+    riders = jnp.concatenate([jnp.concatenate(riders, 0), jnp.zeros((16, 256), F32)], 1).astype(BF)
+    cot = jnp.concatenate([cot, jnp.zeros((96, 256), F32)], 1).astype(BF)
+    for k in range(8):
+        way = k % 4
+        out_ref[112 * k : 112 * k + 96, :] = cot[:, 384 * way : 384 * way + 384]
+        out_ref[112 * k + 96 : 112 * k + 112, :] = riders
 
 
 def back_kernel(got_ref, unit_ref, wa_ref, wb_ref, out_ref, loss_ref):
-    summed = got_ref[:64, :].astype(F32)
-    for k in range(1, 8):
-        summed += got_ref[64 * k : 64 * k + 64, :].astype(F32)
-    along = as_column(summed[3:4, :128] + summed[7:8, :128])
-    loss_ref[...] = jnp.broadcast_to(
-        (summed[11:12, :128] + summed[15:16, :128]) / (2.0 * 1536), (8, 128)
-    )
-    proj_cot = (summed - unit_ref[...].astype(F32) * along).astype(BF)
-    a, b = [
-        lax.dot_general(proj_cot, ref[...], ROWS_DOT, preferred_element_type=F32)
-        for ref in (wa_ref, wb_ref)
-    ]
-    is_img = lax.broadcasted_iota(jnp.int32, a.shape, 1) % 24 < 13
-    first = lax.broadcasted_iota(jnp.int32, a.shape, 0) % 8 < 4
-    a = jnp.where(is_img, a, pltpu.roll(a, 60, 0))
-    b = jnp.where(is_img, pltpu.roll(b, 4, 0), b)
-    out_ref[...] = jnp.where(first, a, b).astype(BF)
+    riders = [got_ref[112 * k + 96 : 112 * k + 112, :128].astype(F32) for k in range(8)]
+    parts = jnp.concatenate([r[0:1] + r[1:2] + r[2:3] for r in riders], 0)
+    weights = jnp.exp(parts - log_total(parts, 0))
+    along = jnp.zeros((1, 128), F32)
+    value = jnp.zeros((1, 128), F32)
+    summed = jnp.zeros((48, 384), F32)
+    for k, r in enumerate(riders):
+        weight = weights[k : k + 1]
+        along += weight * (r[3:4] + r[4:5]) + (r[5:6] + r[6:7])
+        value += r[7:8] + r[8:9]
+        summed += as_column(weight) * got_ref[112 * k : 112 * k + 48, :].astype(F32)
+        summed += got_ref[112 * k + 48 : 112 * k + 96, :].astype(F32)
+    loss_ref[...] = jnp.broadcast_to(value / (2.0 * 1536), (8, 128))
+    proj_cot = (summed - unit_ref[...].astype(F32) * as_column(along)).astype(BF)
+    mixed = []
+    for ref in (wa_ref, wb_ref):
+        pool = lax.dot_general(proj_cot, ref[...], ROWS_DOT, preferred_element_type=F32)
+        is_img = lax.broadcasted_iota(jnp.int32, pool.shape, 1) % 24 < 13
+        mixed.append(jnp.where(is_img, pool, pltpu.roll(pool, 45, 0)))
+    blank = jnp.zeros((1, pool.shape[1]), F32)
+    pieces = []
+    for k in range(8):
+        for pool in mixed:
+            pieces += [pool[6 * k : 6 * k + 3], blank]
+    out_ref[...] = jnp.concatenate(pieces, 0).astype(BF)
 
 
 def token_kernel(pool_ref, inv_ref, img_ref, txt_ref, ig_ref, tg_ref, img_out, txt_out):
@@ -288,8 +293,8 @@
     both = lax.all_gather(slabs.transpose(1, 0, 2), "h", axis=0)
     pooled = lax.dynamic_index_in_dim(both, h_index, 1, keepdims=False).reshape(24, 1536)
     row_pos = pooled[:, 23].astype(F32) * 32.0 + pooled[:, 47].astype(F32)
-    row_pos = jnp.pad(row_pos.reshape(8, 3), ((0, 0), (0, 5)), constant_values=-1.0)
-    row_pos = row_pos.reshape(64, 1).astype(jnp.int32)
+    row_pos = jnp.pad(row_pos.reshape(8, 3), ((0, 0), (0, 3)), constant_values=-1.0)
+    row_pos = row_pos.reshape(48, 1).astype(jnp.int32)
     is_img = spot % 24 < 13
     is_txt = (spot % 24 >= 13) & (spot % 24 < 23)
     left = jnp.stack(
@@ -308,20 +313,19 @@
     own_digits = jnp.pad(own_digits, (0, 122))[None]
     rows, far, inv = kernel_call(
         unit_kernel,
-        [((64, emb), BF), ((256, emb), BF), ((8, 128), F32)],
+        [((48, emb), BF), ((256, emb), BF), ((8, 128), F32)],
         [place, parts, own_digits],
         scratch=[pltpu.VMEM((64, emb), F32), pltpu.VMEM((64, 128), F32)],
         smem=(0,),
     )
     fa, fb = both_cores(exchange(far.reshape(32, 8, emb), ZX))
 
-    scores, near, far = kernel_call(
+    scores, far = kernel_call(
         score_kernel,
-        [((64, 512), F32), ((8, 128), F32), ((256, 128), F32)],
+        [((48, 512), F32), ((256, 128), F32)],
         [place, logit_scale, rows, fa, fb, row_pos],
         smem=(0, 1),
     )
-    near = exchange(near.reshape(8, 1, 128), Y).reshape(8, 128)
     far = exchange(far.reshape(64, 4, 128), ZXC).reshape(256, 128)
 
     item_pos = jnp.concatenate([fa.reshape(32, 8, emb)[:, 3, :6], fb.reshape(32, 8, emb)[:, 3, :6]])
@@ -331,13 +335,13 @@
     item_pos = item_pos.astype(jnp.int32)
     (ways,) = kernel_call(
         coef_kernel,
-        [((512, 384), BF)],
-        [place, logit_scale, scores, near, far, row_pos, item_pos, fa, fb],
+        [((896, 384), BF)],
+        [place, logit_scale, scores, far, row_pos, item_pos, fa, fb],
         smem=(0, 1),
     )
-    got = exchange(ways.reshape(8, 64, 384), Y).reshape(512, 384)
+    got = exchange(ways.reshape(8, 112, 384), Y).reshape(896, 384)
     unit_part = lax.dynamic_slice(
-        jnp.pad(rows, ((0, 0), (0, 256))), (0, 384 * t_index), (64, 384)
+        jnp.pad(rows, ((0, 0), (0, 256))), (0, 384 * t_index), (48, 384)
     )
     pool, loss = kernel_call(
         back_kernel, [((64, 768), BF), ((8, 128), F32)], [got, unit_part, wa, wb]

time: 164 us -> 159 us (0.970)
  starting transfers between devices: 47.1 us -> 42.7 us
    all_to_all x7 -> x6, starting transfers between devices: 47.1 us -> 42.7 us  [exchange(): return lax.all_to_all(blocks, axes, 0, 0, tiled=True)]
    all_to_all x7 -> x6, waiting for transfers between devices: 66.1 us -> 66.1 us  [exchange(): return lax.all_to_all(blocks, axes, 0, 0, tiled=True)]
  transfers between devices with their start and end apart: 7 -> 6, of which waited for: 6 -> 5; matrix products, arithmetic and copies ran while one was open for 8% -> 8% of each run, Pallas kernels for 0% -> 0%
where the time goes in v5:
time: 159 us; the launch traced here: 158 us
  waiting for transfers between devices  66.1 us (42%)
  starting transfers between devices  42.7 us (27%)
  blocking collectives  22.9 us (14%)
  Pallas kernels  9.74 us (6%)
  other arithmetic  8.53 us (5%)
  local copies, waits for them, and re-layouts  6.84 us (4%)
  between operations  1.65 us (1%)
    all_to_all x6, waiting for transfers between devices, exchange(): return lax.all_to_all(blocks, axes, 0, 0, tiled=True)  66.1 us
    all_to_all x6, starting transfers between devices, exchange(): return lax.all_to_all(blocks, axes, 0, 0, tiled=True)  42.7 us
    all_gather x4, blocking collectives, both_cores(): lax.all_gather(part, 'c', axis=0)  14.5 us
    pallas_call x6, Pallas kernels, kernel_call(): pl.pallas_call(body, out_shape=[jax.ShapeDtypeStruct(shape, kind) for sha...  9.74 us
    all_gather x1, blocking collectives, per_device(): both = lax.all_gather(slabs.transpose(1, 0, 2), 'h', axis=0)  8.38 us
  transfers between devices with their start and end apart: 6, of which 5 were waited for; matrix products, arithmetic and copies ran while one was open for 8% of the time, Pallas kernels for 0%

profile of v5, /device:TPU:1, one launch (start us, length us, event | category | flops | bytes accessed | tf_op | source)
XLA Modules:
  0.0 158.5 jit_solution(971538280681077346)
XLA Ops:
  2.3 13.7 %all-to-all-start = ((bf16[32,24,384]{2,1,0:T(8,128)(2,1)}), bf16[32,24,384]{2,1,0:T(8,128)(2,1)S(1)}, u32[]{:S(2)}, u32[]{:S(2)}) async-start(bf16[32,24,384]{2,1,0:T(8,128)(2,1)} %broadcast_in_dim.78), calls=%async_computation | async-start | bytes 1179648 | tf_op jit(solution)/shard_map/all_to_all | solution.py:26
  16.1 2.0 %convert_reduce_fusion.1 = f32[12,48]{1,0:T(8,128)S(1)} fusion(bf16[12,48,1664]{2,1,0:T(8,128)(2,1)} %param.8), kind=kLoop, calls=%fused_computation.3 | loop fusion | flops 1916352 | bytes 1919232 | tf_op jit(solution)/shard_map/reduce_sum | solution.py:20
  23.5 1.2 maximum_bitcast_fusion
  25.5 8.4 %all-gather = bf16[4,12,1536]{2,1,0:T(8,128)(2,1)S(1)} all-gather(bf16[2,12,1536]{2,1,0:T(8,128)(2,1)S(1)} %copy.37), channel_id=2, replica_groups=mesh['t'=4,'h'=2,'z'=8,'x'=4,'c'=2] {'h'}, dimensions={0}, use_global_device_ids=true | all-gather | bytes 221184 | tf_op jit(solution)/shard_map/all_gather | solution.py:293
  34.6 5.0 %all-gather.1 = bf16[32,24,384]{2,1,0:T(8,128)(2,1)S(1)} all-gather(bf16[16,24,384]{2,1,0:T(8,128)(2,1)S(1)} %get-tuple-element.26), channel_id=3, replica_groups=mesh['t'=4,'h'=2,'z'=8,'x'=4,'c'=2] {'c'}, dimensions={0}, use_global_device_ids=true | all-gather | bytes 884736 | tf_op jit(solution)/shard_map/all_gather | solution.py:31
  39.6 2.2 %all-gather.2 = bf16[32,24,384]{2,1,0:T(8,128)(2,1)S(1)} all-gather(bf16[16,24,384]{2,1,0:T(8,128)(2,1)S(1)} %get-tuple-element.25), channel_id=4, replica_groups=mesh['t'=4,'h'=2,'z'=8,'x'=4,'c'=2] {'c'}, dimensions={0}, use_global_device_ids=true | all-gather | bytes 884736 | tf_op jit(solution)/shard_map/all_gather | solution.py:31
  42.8 7.4 %all-to-all-start.1 = ((bf16[8,48,384]{2,1,0:T(8,128)(2,1)}), bf16[8,48,384]{2,1,0:T(8,128)(2,1)S(1)}, u32[]{:S(2)}, u32[]{:S(2)}) async-start(bf16[8,48,384]{2,1,0:T(8,128)(2,1)} %bitcast.9), calls=%async_computation.1 | async-start | bytes 589824 | tf_op jit(solution)/shard_map/all_to_all | solution.py:26
  50.4 12.2 %all-to-all-done.1 = bf16[8,48,384]{2,1,0:T(8,128)(2,1)S(1)} async-done(((bf16[8,48,384]{2,1,0:T(8,128)(2,1)}), bf16[8,48,384]{2,1,0:T(8,128)(2,1)S(1)}, u32[]{:S(2)}, u32[]{:S(2)}) %all-to-all-start.1) | async-done | bytes 294944 | tf_op jit(solution)/shard_map/all_to_all | solution.py:26
  62.6 1.6 %shard_map.104 = (bf16[48,1280]{1,0:T(8,128)(2,1)S(1)}, bf16[256,1280]{1,0:T(8,128)(2,1)}, f32[8,128]{1,0:T(8,128)S(1)}) custom-call(s32[4]{0:T(128)S(1)} %pad_add_fusion.place_ref, bf16[384,384]{1,0:T(8,128)(2,1)S(1)} %bitcast.51, f32[1,128]{1,0:T(1,128)S(1)} %pad_bitcast_fusion.digits_ref), custom_call_target="tpu_custom_call" | custom-call | tf_op jit(solution)/shard_map/pallas_call | solution.py:37
  64.2 9.2 %all-to-all-start.2 = ((bf16[32,8,1280]{2,1,0:T(8,128)(2,1)}), bf16[32,8,1280]{2,1,0:T(8,128)(2,1)S(1)}, u32[]{:S(2)}, u32[]{:S(2)}) async-start(bf16[32,8,1280]{2,1,0:T(8,128)(2,1)} %bitcast.12), calls=%async_computation.2 | async-start | bytes 1310720 | tf_op jit(solution)/shard_map/all_to_all | solution.py:26
  74.5 17.0 %all-to-all-done.2 = bf16[32,8,1280]{2,1,0:T(8,128)(2,1)S(1)} async-done(((bf16[32,8,1280]{2,1,0:T(8,128)(2,1)}), bf16[32,8,1280]{2,1,0:T(8,128)(2,1)S(1)}, u32[]{:S(2)}, u32[]{:S(2)}) %all-to-all-start.2) | async-done | bytes 655392 | tf_op jit(solution)/shard_map/all_to_all | solution.py:26
  91.5 5.1 %all-gather.3 = bf16[32,8,1280]{2,1,0:T(8,128)(2,1)S(1)} all-gather(bf16[16,8,1280]{2,1,0:T(8,128)(2,1)S(1)} %get-tuple-element.24), channel_id=5, replica_groups=mesh['t'=4,'h'=2,'z'=8,'x'=4,'c'=2] {'c'}, dimensions={0}, use_global_device_ids=true | all-gather | bytes 983040 | tf_op jit(solution)/shard_map/all_gather | solution.py:31
  96.6 2.3 %all-gather.4 = bf16[32,8,1280]{2,1,0:T(8,128)(2,1)S(1)} all-gather(bf16[16,8,1280]{2,1,0:T(8,128)(2,1)S(1)} %get-tuple-element.23), channel_id=6, replica_groups=mesh['t'=4,'h'=2,'z'=8,'x'=4,'c'=2] {'c'}, dimensions={0}, use_global_device_ids=true | all-gather | bytes 983040 | tf_op jit(solution)/shard_map/all_gather | solution.py:31
  99.0 1.8 %shard_map.105 = (f32[48,512]{1,0:T(8,128)S(1)}, f32[256,128]{1,0:T(8,128)}) custom-call(s32[4]{0:T(128)S(1)} %pad_add_fusion.place_ref, f32[1]{0:T(128)S(6)} %copy.52.logit_ref, bf16[48,1280]{1,0:T(8,128)(2,1)S(1)} %get-tuple-element.12.rows_ref, bf16[256,1280]{1,0:T(8,128)(2,1)S(1)} %bitcast.40, bf16[256,1280]{1,0:T(8,128)(2,1)S(1)} %bitcast.42, ...), custom_call_target="tpu_custom_call" | custom-call | tf_op jit(solution)/shard_map/pallas_call | solution.py:37
  100.8 5.5 %all-to-all-start.3 = ((f32[64,4,128]{2,1,0:T(4,128)}), f32[64,4,128]{2,1,0:T(4,128)S(1)}, u32[]{:S(2)}, u32[]{:S(2)}) async-start(f32[64,4,128]{2,1,0:T(4,128)} %bitcast.15), calls=%async_computation.3 | async-start | bytes 262144 | tf_op jit(solution)/shard_map/all_to_all | solution.py:26
  106.7 10.8 %all-to-all-done.3 = f32[64,4,128]{2,1,0:T(4,128)S(1)} async-done(((f32[64,4,128]{2,1,0:T(4,128)}), f32[64,4,128]{2,1,0:T(4,128)S(1)}, u32[]{:S(2)}, u32[]{:S(2)}) %all-to-all-start.3) | async-done | bytes 131104 | tf_op jit(solution)/shard_map/all_to_all | solution.py:26
  117.5 2.0 %shard_map.106 = bf16[896,384]{1,0:T(8,128)(2,1)} custom-call(s32[4]{0:T(128)S(1)} %pad_add_fusion.place_ref, f32[1]{0:T(128)S(6)} %copy.52.logit_ref, f32[48,512]{1,0:T(8,128)S(1)} %get-tuple-element.14.scores_ref, f32[256,128]{1,0:T(8,128)S(1)} %bitcast.52, s32[48,1]{1,0:T(8,128)S(1)} %convert_element_type.79.row_pos_ref, ...), custom_call_target="tpu_custom_call" | custom-call | tf_op jit(solution)/shard_map/pallas_call | solution.py:37
  119.5 3.5 %all-to-all-start.4 = ((bf16[8,112,384]{2,1,0:T(8,128)(2,1)}), bf16[8,112,384]{2,1,0:T(8,128)(2,1)S(1)}, u32[]{:S(2)}, u32[]{:S(2)}) async-start(bf16[8,112,384]{2,1,0:T(8,128)(2,1)} %bitcast.19), calls=%async_computation.4 | async-start | bytes 1376256 | tf_op jit(solution)/shard_map/all_to_all | solution.py:26
  123.1 1.1 constant_dynamic-slice_fusion
  124.2 20.3 %all-to-all-done.4 = bf16[8,112,384]{2,1,0:T(8,128)(2,1)S(1)} async-done(((bf16[8,112,384]{2,1,0:T(8,128)(2,1)}), bf16[8,112,384]{2,1,0:T(8,128)(2,1)S(1)}, u32[]{:S(2)}, u32[]{:S(2)}) %all-to-all-start.4) | async-done | bytes 688160 | tf_op jit(solution)/shard_map/all_to_all | solution.py:26
  144.5 1.3 shard_map.107
  145.7 3.4 %all-to-all-start.5 = ((bf16[8,8,768]{2,1,0:T(8,128)(2,1)}), bf16[8,8,768]{2,1,0:T(8,128)(2,1)S(1)}, u32[]{:S(2)}, u32[]{:S(2)}) async-start(bf16[8,8,768]{2,1,0:T(8,128)(2,1)} %bitcast.22), calls=%async_computation.5 | async-start | bytes 196608 | tf_op jit(solution)/shard_map/all_to_all | solution.py:26
  150.7 5.8 %all-to-all-done.5 = bf16[8,8,768]{2,1,0:T(8,128)(2,1)S(1)} async-done(((bf16[8,8,768]{2,1,0:T(8,128)(2,1)}), bf16[8,8,768]{2,1,0:T(8,128)(2,1)S(1)}, u32[]{:S(2)}, u32[]{:S(2)}) %all-to-all-start.5) | async-done | bytes 98336 | tf_op jit(solution)/shard_map/all_to_all | solution.py:26
  156.4 2.0 %shard_map.108 = (bf16[144,1664]{1,0:T(8,128)(2,1)}, bf16[192,1280]{1,0:T(8,128)(2,1)}) custom-call(bf16[64,768]{1,0:T(8,128)(2,1)S(1)} %bitcast.53, f32[8,128]{1,0:T(8,128)S(1)} %get-tuple-element.18.inv_ref, bf16[144,1664]{1,0:T(8,128)(2,1)S(1)} %bitcast.50, bf16[192,1280]{1,0:T(8,128)(2,1)S(1)} %bitcast.49, f32[1,1664]{1,0:T(1,128)S(1)} %broadcast_in_dim.80.ig_ref, ...), custom_call_target="tpu_custom_call" | custom-call | tf_op jit(solution)/shard_map/pallas_call | solution.py:37
  (67 shorter events, 12.2 us)
Async XLA Ops:
  2.3 32.2 %all-to-all-start = ((bf16[32,24,384]{2,1,0:T(8,128)(2,1)}), bf16[32,24,384]{2,1,0:T(8,128)(2,1)S(1)}, u32[]{:S(2)}, u32[]{:S(2)}) async-start(bf16[32,24,384]{2,1,0:T(8,128)(2,1)} %broadcast_in_dim.78), calls=%async_computation | async-start | bytes 1179648 | tf_op jit(solution)/shard_map/all_to_all | solution.py:26
  16.0 2.1 %copy-start.1 = (bf16[12,48,1664]{2,1,0:T(8,128)(2,1)S(1)}, bf16[12,48,1664]{2,1,0:T(8,128)(2,1)}, u32[]{:S(2)}) copy-start(bf16[12,48,1664]{2,1,0:T(8,128)(2,1)} %param.8) | copy-start | bytes 5750788
  16.0 2.7 %copy-start.2 = (f32[1664]{0:T(1024)S(1)}, f32[1664]{0:T(1024)}, u32[]{:S(2)}) copy-start(f32[1664]{0:T(1024)} %param.12) | copy-start | bytes 19972
  18.1 2.4 %copy-start = (bf16[12,64,1280]{2,1,0:T(8,128)(2,1)S(1)}, bf16[12,64,1280]{2,1,0:T(8,128)(2,1)}, u32[]{:S(2)}) copy-start(bf16[12,64,1280]{2,1,0:T(8,128)(2,1)} %param.9) | copy-start | bytes 5898244
  20.5 1.0 copy-start.3
  22.5 2.7 %copy-start.4 = (s32[12]{0:T(128)S(1)}, s32[12]{0:T(128)}, u32[]{:S(2)}) copy-start(s32[12]{0:T(128)} %param.15) | copy-start | bytes 148
  42.8 19.8 %all-to-all-start.1 = ((bf16[8,48,384]{2,1,0:T(8,128)(2,1)}), bf16[8,48,384]{2,1,0:T(8,128)(2,1)S(1)}, u32[]{:S(2)}, u32[]{:S(2)}) async-start(bf16[8,48,384]{2,1,0:T(8,128)(2,1)} %bitcast.9), calls=%async_computation.1 | async-start | bytes 589824 | tf_op jit(solution)/shard_map/all_to_all | solution.py:26
  64.2 27.2 %all-to-all-start.2 = ((bf16[32,8,1280]{2,1,0:T(8,128)(2,1)}), bf16[32,8,1280]{2,1,0:T(8,128)(2,1)S(1)}, u32[]{:S(2)}, u32[]{:S(2)}) async-start(bf16[32,8,1280]{2,1,0:T(8,128)(2,1)} %bitcast.12), calls=%async_computation.2 | async-start | bytes 1310720 | tf_op jit(solution)/shard_map/all_to_all | solution.py:26
  100.8 16.7 %all-to-all-start.3 = ((f32[64,4,128]{2,1,0:T(4,128)}), f32[64,4,128]{2,1,0:T(4,128)S(1)}, u32[]{:S(2)}, u32[]{:S(2)}) async-start(f32[64,4,128]{2,1,0:T(4,128)} %bitcast.15), calls=%async_computation.3 | async-start | bytes 262144 | tf_op jit(solution)/shard_map/all_to_all | solution.py:26
  119.5 24.9 %all-to-all-start.4 = ((bf16[8,112,384]{2,1,0:T(8,128)(2,1)}), bf16[8,112,384]{2,1,0:T(8,128)(2,1)S(1)}, u32[]{:S(2)}, u32[]{:S(2)}) async-start(bf16[8,112,384]{2,1,0:T(8,128)(2,1)} %bitcast.19), calls=%async_computation.4 | async-start | bytes 1376256 | tf_op jit(solution)/shard_map/all_to_all | solution.py:26
  145.7 10.7 %all-to-all-start.5 = ((bf16[8,8,768]{2,1,0:T(8,128)(2,1)}), bf16[8,8,768]{2,1,0:T(8,128)(2,1)S(1)}, u32[]{:S(2)}, u32[]{:S(2)}) async-start(bf16[8,8,768]{2,1,0:T(8,128)(2,1)} %bitcast.22), calls=%async_computation.5 | async-start | bytes 196608 | tf_op jit(solution)/shard_map/all_to_all | solution.py:26

commit v6 on v5

--- a/solution.py
+++ b/solution.py
@@ -13,13 +13,6 @@
 DP = ("h", "z", "x", "c")
 LOW = -1e30
 ROWS_DOT = (((1,), (1,)), ((), ()))
-
-
-def norm_tokens(token_block, gain_vector):
-    values = token_block.astype(F32)
-    center = values - jnp.mean(values, axis=-1, keepdims=True)
-    spread = jnp.mean(center * center, axis=-1, keepdims=True)
-    return center * lax.rsqrt(spread + 1e-05) * gain_vector
 
 
 def exchange(blocks, axes):
@@ -46,10 +39,84 @@
     )(*args)
 
 
-def project_kernel(left_ref, wa_ref, wb_ref, out_ref):
-    half = wa_ref.shape[0]
-    part = jnp.dot(left_ref[:, :half], wa_ref[...], preferred_element_type=F32)
-    part += jnp.dot(left_ref[:, half:], wb_ref[...], preferred_element_type=F32)
+def slab_place(dense, wide, skip):
+    return ((dense // wide) % 2) * 384 + (dense // (2 * wide)) * 24 + skip + dense % wide
+
+
+def pool_kernel(img_ref, txt_ref, ig_ref, tg_ref, digits_ref, out_ref, img_rows, txt_rows):
+    step = pl.program_id(0)
+
+    @pl.when(step == 0)
+    def _():
+        img_rows[...] = jnp.zeros_like(img_rows)
+        txt_rows[...] = jnp.zeros_like(txt_rows)
+
+    for x_ref, gain_ref, rows in ((img_ref, ig_ref, img_rows), (txt_ref, tg_ref, txt_rows)):
+        values = x_ref[0].astype(F32)
+        center = values - jnp.mean(values, axis=1, keepdims=True)
+        spread = jnp.mean(center * center, axis=1, keepdims=True)
+        mean = jnp.mean(center * lax.rsqrt(spread + 1e-05), axis=0, keepdims=True)
+        rows[pl.ds(step, 1), :] = mean * gain_ref[...]
+
+    @pl.when(step == 11)
+    def _():
+        found = jnp.zeros((64, 768), F32)
+        for rows, wide, skip in ((img_rows, 13, 0), (txt_rows, 10, 13)):
+            width = 32 * wide
+            dense = lax.broadcasted_iota(jnp.int32, (width, 768), 0)
+            lane = lax.broadcasted_iota(jnp.int32, (width, 768), 1)
+            pick = jnp.where(lane == slab_place(dense, wide, skip), 1.0, 0.0).astype(BF)
+            held = rows[...]
+            quarters = [held[:, width * k : width * k + width] for k in range(4)]
+            quarters = jnp.concatenate(quarters, 0).astype(BF)
+            found += jnp.dot(quarters, pick, preferred_element_type=F32)
+        digits = digits_ref[...]
+        blank = jnp.zeros_like(digits)
+        digits = jnp.concatenate([digits, blank, digits, blank], 0)
+        found = jnp.concatenate([found[:, :128] + digits, found[:, 128:]], 1)
+        out_ref[...] = found.astype(BF)
+
+
+def pool_call(image_in, text_in, img_gain, txt_gain, digits):
+    pairs, count_i, width_i = image_in.shape
+    _, count_t, width_t = text_in.shape
+    whole = lambda shape: pl.BlockSpec(shape, lambda k: (0, 0))
+    return pl.pallas_call(
+        pool_kernel,
+        grid=(pairs,),
+        out_shape=jax.ShapeDtypeStruct((64, 768), BF),
+        in_specs=[
+            pl.BlockSpec((1, count_i, width_i), lambda k: (k, 0, 0)),
+            pl.BlockSpec((1, count_t, width_t), lambda k: (k, 0, 0)),
+            whole((1, width_i)),
+            whole((1, width_t)),
+            whole((16, 128)),
+        ],
+        out_specs=whole((64, 768)),
+        scratch_shapes=[pltpu.VMEM((16, width_i), F32), pltpu.VMEM((16, width_t), F32)],
+        cost_estimate=pl.CostEstimate(
+            flops=10 * (image_in.size + text_in.size),
+            bytes_accessed=2 * (image_in.size + text_in.size),
+            transcendentals=0,
+        ),
+        compiler_params=pltpu.CompilerParams(vmem_limit_bytes=40 * 1024 * 1024),
+    )(image_in, text_in, img_gain[None], txt_gain[None], digits)
+
+
+def project_kernel(place_ref, pooled_ref, wa_ref, wb_ref, out_ref):
+    part = jnp.zeros((48, wa_ref.shape[1]), F32)
+    inside = lax.broadcasted_iota(jnp.int32, (12, 768), 1) % 24
+    for a, w_ref in enumerate((wa_ref, wb_ref)):
+        pieces = []
+        for h in range(2):
+            start = pl.multiple_of(64 * h + 32 * place_ref[1] + 16 * a, 16)
+            rows = pooled_ref[pl.ds(start, 16), :].astype(F32)[:12]
+            img_rows = jnp.where(inside < 13, rows, 0.0)
+            txt_rows = jnp.where((inside >= 13) & (inside < 23), rows, 0.0)
+            for t in range(4):
+                pieces += [img_rows[3 * t : 3 * t + 3], txt_rows[3 * t : 3 * t + 3]]
+        left = jnp.concatenate(pieces, 0).astype(BF)
+        part += jnp.dot(left, w_ref[...], preferred_element_type=F32)
     part = part.astype(BF)
     for k in range(8):
         out_ref[48 * k : 48 * k + 48, :] = part
@@ -238,9 +305,8 @@
         (txt_ref, tg_ref, txt_out, 10, 13, 4),
     ):
         dense = lax.broadcasted_iota(jnp.int32, (1, 32 * wide), 1)
-        place = ((dense // wide) % 2) * 384 + (dense // (2 * wide)) * 24 + skip + dense % wide
         lane = lax.broadcasted_iota(jnp.int32, (768, 32 * wide), 0)
-        pick = jnp.where(lane == place, 1.0, 0.0).astype(BF)
+        pick = jnp.where(lane == slab_place(dense, wide, skip), 1.0, 0.0).astype(BF)
         found = jnp.dot(pool, pick, preferred_element_type=F32)
         halves = [
             found[32 * k : 32 * k + 8]
@@ -276,36 +342,22 @@
     w = lax.dynamic_slice(w, (0, 384 * t_index), (24, 384))
     wa, wb = both_cores(exchange(jnp.broadcast_to(w[None], (32, 24, 384)), ZX))
 
-    pooled_i = jnp.mean(norm_tokens(image_in, img_gain), axis=1).astype(BF)
-    pooled_t = jnp.mean(norm_tokens(text_in, txt_gain), axis=1).astype(BF)
-    slabs = jnp.concatenate(
-        [
-            pooled_i.reshape(12, 128, 13),
-            pooled_t.reshape(12, 128, 10),
-            jnp.zeros((12, 128, 1), BF),
-        ],
-        2,
-    )
-    slabs = slabs.reshape(12, 2, 2, 16, 2, 24).transpose(0, 1, 2, 4, 3, 5).reshape(12, 2, 1536)
-    digits = jnp.stack([positive // 32, positive % 32], 1).astype(BF)[:, :, None]
-    spot = lax.iota(jnp.int32, 1536)[None, :]
-    slabs = jnp.where(spot == 23, digits[:, :1], jnp.where(spot == 47, digits[:, 1:], slabs))
-    both = lax.all_gather(slabs.transpose(1, 0, 2), "h", axis=0)
-    pooled = lax.dynamic_index_in_dim(both, h_index, 1, keepdims=False).reshape(24, 1536)
-    row_pos = pooled[:, 23].astype(F32) * 32.0 + pooled[:, 47].astype(F32)
+    spot = lax.iota(jnp.int32, 128)[None, :]
+    digits = jnp.where(spot == 23, positive[:, None] // 32, 0)
+    digits = jnp.where(spot == 47, positive[:, None] % 32, digits).astype(F32)
+    digits = jnp.pad(digits, ((0, 4), (0, 0)))
+    pooled = pool_call(image_in, text_in, img_gain, txt_gain, digits)
+    pooled = lax.all_gather(pooled, "h", axis=0)
+    row_pos = pooled[:, :12, 23].astype(F32) * 32.0 + pooled[:, :12, 47].astype(F32)
     row_pos = jnp.pad(row_pos.reshape(8, 3), ((0, 0), (0, 3)), constant_values=-1.0)
     row_pos = row_pos.reshape(48, 1).astype(jnp.int32)
-    is_img = spot % 24 < 13
-    is_txt = (spot % 24 >= 13) & (spot % 24 < 23)
-    left = jnp.stack(
-        [
-            jnp.where(is_img, pooled, 0).reshape(8, 3, 1536),
-            jnp.where(is_txt, pooled, 0).reshape(8, 3, 1536),
-        ],
-        1,
-    ).reshape(48, 1536)
-
-    (part,) = kernel_call(project_kernel, [((384, 384), BF)], [left, wa, wb])
+
+    (part,) = kernel_call(
+        project_kernel,
+        [((384, 384), BF)],
+        [place, pooled.reshape(128, 768), wa, wb],
+        smem=(0,),
+    )
     parts = exchange(part.reshape(8, 48, 384), Y).reshape(384, 384)
 
     own_digits = lax.dynamic_slice(positive, (3 * t_index,), (3,))

time: 159 us -> 158 us (level)
  other arithmetic: 8.53 us -> 1.4 us
  Pallas kernels: 9.74 us -> 14.8 us
    reduce_sum x6 -> x0, other arithmetic: 5.52 us -> none  [the longest x2 2.32 us: norm_tokens(): center = values - jnp.mean(values, axis=-1, keepdims=True)]
    pallas_call x0 -> x1, Pallas kernels: none -> 4.5 us  [pool_call(): pl.pallas_call(pool_kernel, grid=(pairs,), out_shape=jax.ShapeDtypeStruct...]
    unnamed x12 -> x10, local copies, waits for them, and re-layouts: 0.29 us -> 1.94 us
  transfers between devices with their start and end apart: 6 -> 6, of which waited for: 5 -> 6; matrix products, arithmetic and copies ran while one was open for 8% -> 3% of each run, Pallas kernels for 0% -> 3%
where the time goes in v6:
time: 158 us; the launch traced here: 157 us
  waiting for transfers between devices  67.6 us (43%)
  starting transfers between devices  42 us (27%)
  blocking collectives  22.1 us (14%)
  Pallas kernels  14.8 us (9%)
  local copies, waits for them, and re-layouts  7.46 us (5%)
    all_to_all x6, waiting for transfers between devices, exchange(): return lax.all_to_all(blocks, axes, 0, 0, tiled=True)  67.6 us
    all_to_all x6, starting transfers between devices, exchange(): return lax.all_to_all(blocks, axes, 0, 0, tiled=True)  42 us
    all_gather x4, blocking collectives, both_cores(): lax.all_gather(part, 'c', axis=0)  13.8 us
    pallas_call x6, Pallas kernels, kernel_call(): pl.pallas_call(body, out_shape=[jax.ShapeDtypeStruct(shape, kind) for sha...  10.3 us
    all_gather x1, blocking collectives, per_device(): pooled = lax.all_gather(pooled, 'h', axis=0)  8.3 us
    pallas_call x1, Pallas kernels, pool_call(): pl.pallas_call(pool_kernel, grid=(pairs,), out_shape=jax.ShapeDtypeStruct...  4.5 us
  transfers between devices with their start and end apart: 6, of which 6 were waited for; matrix products, arithmetic and copies ran while one was open for 3% of the time, Pallas kernels for 3%

profile of v6, /device:TPU:1, one launch (start us, length us, event | category | flops | bytes accessed | tf_op | source)
XLA Modules:
  0.0 156.8 jit_solution(10239166859279160969)
XLA Ops:
  2.5 13.7 %all-to-all-start = ((bf16[32,24,384]{2,1,0:T(8,128)(2,1)}), bf16[32,24,384]{2,1,0:T(8,128)(2,1)S(1)}, u32[]{:S(2)}, u32[]{:S(2)}) async-start(bf16[32,24,384]{2,1,0:T(8,128)(2,1)} %broadcast_in_dim.63), calls=%async_computation | async-start | bytes 1179648 | tf_op jit(solution)/shard_map/all_to_all | solution.py:19
  17.8 1.5 copy-done.1
  19.3 4.5 %shard_map.103 = bf16[64,768]{1,0:T(8,128)(2,1)S(1)} custom-call(bf16[12,48,1664]{2,1,0:T(8,128)(2,1)S(1)} %copy-done.1, bf16[12,64,1280]{2,1,0:T(8,128)(2,1)S(1)} %copy-done, f32[1,1664]{1,0:T(1,128)S(1)} %broadcast_in_dim.56.ig_ref, f32[1,1280]{1,0:T(1,128)S(1)} %broadcast_in_dim.57.tg_ref, f32[16,128]{1,0:T(8,128)S(1)} %pad.24.digits_ref), custom_call_target="tpu_custom_call" | custom-call | flops 19415040 | bytes 3883008 | tf_op jit(solution)/shard_map/pallas_call | solution.py:84
  23.8 8.3 %all-gather.pooled_ref = bf16[128,768]{1,0:T(8,128)(2,1)S(1)} all-gather(bf16[64,768]{1,0:T(8,128)(2,1)S(1)} %shard_map.103), channel_id=2, replica_groups=mesh['t'=4,'h'=2,'z'=8,'x'=4,'c'=2] {'h'}, dimensions={0}, use_global_device_ids=true | all-gather | bytes 294912 | tf_op jit(solution)/shard_map/all_gather | solution.py:350
  32.2 1.5 all-to-all-done
  33.8 4.3 %all-gather.1 = bf16[32,24,384]{2,1,0:T(8,128)(2,1)S(1)} all-gather(bf16[16,24,384]{2,1,0:T(8,128)(2,1)S(1)} %get-tuple-element.26), channel_id=3, replica_groups=mesh['t'=4,'h'=2,'z'=8,'x'=4,'c'=2] {'c'}, dimensions={0}, use_global_device_ids=true | all-gather | bytes 884736 | tf_op jit(solution)/shard_map/all_gather | solution.py:24
  38.1 2.2 %all-gather.2 = bf16[32,24,384]{2,1,0:T(8,128)(2,1)S(1)} all-gather(bf16[16,24,384]{2,1,0:T(8,128)(2,1)S(1)} %get-tuple-element.25), channel_id=4, replica_groups=mesh['t'=4,'h'=2,'z'=8,'x'=4,'c'=2] {'c'}, dimensions={0}, use_global_device_ids=true | all-gather | bytes 884736 | tf_op jit(solution)/shard_map/all_gather | solution.py:24
  40.3 1.6 shard_map.104
  41.9 6.8 %all-to-all-start.1 = ((bf16[8,48,384]{2,1,0:T(8,128)(2,1)}), bf16[8,48,384]{2,1,0:T(8,128)(2,1)S(1)}, u32[]{:S(2)}, u32[]{:S(2)}) async-start(bf16[8,48,384]{2,1,0:T(8,128)(2,1)} %bitcast.6), calls=%async_computation.1 | async-start | bytes 589824 | tf_op jit(solution)/shard_map/all_to_all | solution.py:19
  48.9 12.2 %all-to-all-done.1 = bf16[8,48,384]{2,1,0:T(8,128)(2,1)S(1)} async-done(((bf16[8,48,384]{2,1,0:T(8,128)(2,1)}), bf16[8,48,384]{2,1,0:T(8,128)(2,1)S(1)}, u32[]{:S(2)}, u32[]{:S(2)}) %all-to-all-start.1) | async-done | bytes 294944 | tf_op jit(solution)/shard_map/all_to_all | solution.py:19
  61.1 1.6 %shard_map.105 = (bf16[48,1280]{1,0:T(8,128)(2,1)S(1)}, bf16[256,1280]{1,0:T(8,128)(2,1)}, f32[8,128]{1,0:T(8,128)S(1)}) custom-call(s32[4]{0:T(128)S(1)} %pad_add_fusion.place_ref, bf16[384,384]{1,0:T(8,128)(2,1)S(1)} %bitcast.40, f32[1,128]{1,0:T(1,128)S(1)} %pad_bitcast_fusion.digits_ref), custom_call_target="tpu_custom_call" | custom-call | tf_op jit(solution)/shard_map/pallas_call | solution.py:30
  62.7 9.0 %all-to-all-start.2 = ((bf16[32,8,1280]{2,1,0:T(8,128)(2,1)}), bf16[32,8,1280]{2,1,0:T(8,128)(2,1)S(1)}, u32[]{:S(2)}, u32[]{:S(2)}) async-start(bf16[32,8,1280]{2,1,0:T(8,128)(2,1)} %bitcast.9), calls=%async_computation.2 | async-start | bytes 1310720 | tf_op jit(solution)/shard_map/all_to_all | solution.py:19
  72.8 16.9 %all-to-all-done.2 = bf16[32,8,1280]{2,1,0:T(8,128)(2,1)S(1)} async-done(((bf16[32,8,1280]{2,1,0:T(8,128)(2,1)}), bf16[32,8,1280]{2,1,0:T(8,128)(2,1)S(1)}, u32[]{:S(2)}, u32[]{:S(2)}) %all-to-all-start.2) | async-done | bytes 655392 | tf_op jit(solution)/shard_map/all_to_all | solution.py:19
  89.8 5.0 %all-gather.3 = bf16[32,8,1280]{2,1,0:T(8,128)(2,1)S(1)} all-gather(bf16[16,8,1280]{2,1,0:T(8,128)(2,1)S(1)} %get-tuple-element.24), channel_id=5, replica_groups=mesh['t'=4,'h'=2,'z'=8,'x'=4,'c'=2] {'c'}, dimensions={0}, use_global_device_ids=true | all-gather | bytes 983040 | tf_op jit(solution)/shard_map/all_gather | solution.py:24
  94.9 2.3 %all-gather.4 = bf16[32,8,1280]{2,1,0:T(8,128)(2,1)S(1)} all-gather(bf16[16,8,1280]{2,1,0:T(8,128)(2,1)S(1)} %get-tuple-element.23), channel_id=6, replica_groups=mesh['t'=4,'h'=2,'z'=8,'x'=4,'c'=2] {'c'}, dimensions={0}, use_global_device_ids=true | all-gather | bytes 983040 | tf_op jit(solution)/shard_map/all_gather | solution.py:24
  97.3 1.8 %shard_map.106 = (f32[48,512]{1,0:T(8,128)S(1)}, f32[256,128]{1,0:T(8,128)}) custom-call(s32[4]{0:T(128)S(1)} %pad_add_fusion.place_ref, f32[1]{0:T(128)S(6)} %copy.37.logit_ref, bf16[48,1280]{1,0:T(8,128)(2,1)S(1)} %get-tuple-element.12.rows_ref, bf16[256,1280]{1,0:T(8,128)(2,1)S(1)} %bitcast.29, bf16[256,1280]{1,0:T(8,128)(2,1)S(1)} %bitcast.31, ...), custom_call_target="tpu_custom_call" | custom-call | tf_op jit(solution)/shard_map/pallas_call | solution.py:30
  99.1 5.6 %all-to-all-start.3 = ((f32[64,4,128]{2,1,0:T(4,128)}), f32[64,4,128]{2,1,0:T(4,128)S(1)}, u32[]{:S(2)}, u32[]{:S(2)}) async-start(f32[64,4,128]{2,1,0:T(4,128)} %bitcast.13), calls=%async_computation.3 | async-start | bytes 262144 | tf_op jit(solution)/shard_map/all_to_all | solution.py:19
  105.0 10.8 %all-to-all-done.3 = f32[64,4,128]{2,1,0:T(4,128)S(1)} async-done(((f32[64,4,128]{2,1,0:T(4,128)}), f32[64,4,128]{2,1,0:T(4,128)S(1)}, u32[]{:S(2)}, u32[]{:S(2)}) %all-to-all-start.3) | async-done | bytes 131104 | tf_op jit(solution)/shard_map/all_to_all | solution.py:19
  115.8 2.0 %shard_map.107 = bf16[896,384]{1,0:T(8,128)(2,1)} custom-call(s32[4]{0:T(128)S(1)} %pad_add_fusion.place_ref, f32[1]{0:T(128)S(6)} %copy.37.logit_ref, f32[48,512]{1,0:T(8,128)S(1)} %get-tuple-element.14.scores_ref, f32[256,128]{1,0:T(8,128)S(1)} %bitcast.42, s32[48,1]{1,0:T(8,128)S(1)} %convert_element_type.46.row_pos_ref, ...), custom_call_target="tpu_custom_call" | custom-call | tf_op jit(solution)/shard_map/pallas_call | solution.py:30
  117.8 3.5 %all-to-all-start.4 = ((bf16[8,112,384]{2,1,0:T(8,128)(2,1)}), bf16[8,112,384]{2,1,0:T(8,128)(2,1)S(1)}, u32[]{:S(2)}, u32[]{:S(2)}) async-start(bf16[8,112,384]{2,1,0:T(8,128)(2,1)} %bitcast.17), calls=%async_computation.4 | async-start | bytes 1376256 | tf_op jit(solution)/shard_map/all_to_all | solution.py:19
  122.5 20.3 %all-to-all-done.4 = bf16[8,112,384]{2,1,0:T(8,128)(2,1)S(1)} async-done(((bf16[8,112,384]{2,1,0:T(8,128)(2,1)}), bf16[8,112,384]{2,1,0:T(8,128)(2,1)S(1)}, u32[]{:S(2)}, u32[]{:S(2)}) %all-to-all-start.4) | async-done | bytes 688160 | tf_op jit(solution)/shard_map/all_to_all | solution.py:19
  144.0 3.4 %all-to-all-start.5 = ((bf16[8,8,768]{2,1,0:T(8,128)(2,1)}), bf16[8,8,768]{2,1,0:T(8,128)(2,1)S(1)}, u32[]{:S(2)}, u32[]{:S(2)}) async-start(bf16[8,8,768]{2,1,0:T(8,128)(2,1)} %bitcast.20), calls=%async_computation.5 | async-start | bytes 196608 | tf_op jit(solution)/shard_map/all_to_all | solution.py:19
  149.0 5.8 %all-to-all-done.5 = bf16[8,8,768]{2,1,0:T(8,128)(2,1)S(1)} async-done(((bf16[8,8,768]{2,1,0:T(8,128)(2,1)}), bf16[8,8,768]{2,1,0:T(8,128)(2,1)S(1)}, u32[]{:S(2)}, u32[]{:S(2)}) %all-to-all-start.5) | async-done | bytes 98336 | tf_op jit(solution)/shard_map/all_to_all | solution.py:19
  154.7 2.0 %shard_map.109 = (bf16[144,1664]{1,0:T(8,128)(2,1)}, bf16[192,1280]{1,0:T(8,128)(2,1)}) custom-call(bf16[64,768]{1,0:T(8,128)(2,1)S(1)} %bitcast.43, f32[8,128]{1,0:T(8,128)S(1)} %get-tuple-element.18.inv_ref, bf16[144,1664]{1,0:T(8,128)(2,1)S(1)} %bitcast.39, bf16[192,1280]{1,0:T(8,128)(2,1)S(1)} %bitcast.38, f32[1,1664]{1,0:T(1,128)S(1)} %broadcast_in_dim.56.ig_ref, ...), custom_call_target="tpu_custom_call" | custom-call | tf_op jit(solution)/shard_map/pallas_call | solution.py:30
  (41 shorter events, 8.6 us)
Async XLA Ops:
  0.6 17.0 %copy-start.2 = (s32[12]{0:T(128)S(1)}, s32[12]{0:T(128)}, u32[]{:S(2)}) copy-start(s32[12]{0:T(128)} %param.15) | copy-start | bytes 148
  0.6 17.1 %copy-start = (bf16[12,64,1280]{2,1,0:T(8,128)(2,1)S(1)}, bf16[12,64,1280]{2,1,0:T(8,128)(2,1)}, u32[]{:S(2)}) copy-start(bf16[12,64,1280]{2,1,0:T(8,128)(2,1)} %txt_ref.1) | copy-start | bytes 5898244
  2.5 31.2 %all-to-all-start = ((bf16[32,24,384]{2,1,0:T(8,128)(2,1)}), bf16[32,24,384]{2,1,0:T(8,128)(2,1)S(1)}, u32[]{:S(2)}, u32[]{:S(2)}) async-start(bf16[32,24,384]{2,1,0:T(8,128)(2,1)} %broadcast_in_dim.63), calls=%async_computation | async-start | bytes 1179648 | tf_op jit(solution)/shard_map/all_to_all | solution.py:19
  17.7 1.5 copy-start.1
  41.9 19.2 %all-to-all-start.1 = ((bf16[8,48,384]{2,1,0:T(8,128)(2,1)}), bf16[8,48,384]{2,1,0:T(8,128)(2,1)S(1)}, u32[]{:S(2)}, u32[]{:S(2)}) async-start(bf16[8,48,384]{2,1,0:T(8,128)(2,1)} %bitcast.6), calls=%async_computation.1 | async-start | bytes 589824 | tf_op jit(solution)/shard_map/all_to_all | solution.py:19
  62.7 27.0 %all-to-all-start.2 = ((bf16[32,8,1280]{2,1,0:T(8,128)(2,1)}), bf16[32,8,1280]{2,1,0:T(8,128)(2,1)S(1)}, u32[]{:S(2)}, u32[]{:S(2)}) async-start(bf16[32,8,1280]{2,1,0:T(8,128)(2,1)} %bitcast.9), calls=%async_computation.2 | async-start | bytes 1310720 | tf_op jit(solution)/shard_map/all_to_all | solution.py:19
  99.1 16.7 %all-to-all-start.3 = ((f32[64,4,128]{2,1,0:T(4,128)}), f32[64,4,128]{2,1,0:T(4,128)S(1)}, u32[]{:S(2)}, u32[]{:S(2)}) async-start(f32[64,4,128]{2,1,0:T(4,128)} %bitcast.13), calls=%async_computation.3 | async-start | bytes 262144 | tf_op jit(solution)/shard_map/all_to_all | solution.py:19
  117.8 24.9 %all-to-all-start.4 = ((bf16[8,112,384]{2,1,0:T(8,128)(2,1)}), bf16[8,112,384]{2,1,0:T(8,128)(2,1)S(1)}, u32[]{:S(2)}, u32[]{:S(2)}) async-start(bf16[8,112,384]{2,1,0:T(8,128)(2,1)} %bitcast.17), calls=%async_computation.4 | async-start | bytes 1376256 | tf_op jit(solution)/shard_map/all_to_all | solution.py:19
  144.0 10.7 %all-to-all-start.5 = ((bf16[8,8,768]{2,1,0:T(8,128)(2,1)}), bf16[8,8,768]{2,1,0:T(8,128)(2,1)S(1)}, u32[]{:S(2)}, u32[]{:S(2)}) async-start(bf16[8,8,768]{2,1,0:T(8,128)(2,1)} %bitcast.20), calls=%async_computation.5 | async-start | bytes 196608 | tf_op jit(solution)/shard_map/all_to_all | solution.py:19

commit v7 on v6

--- a/solution.py
+++ b/solution.py
@@ -1,3 +1,5 @@
+import functools
+
 import jax
 import jax.numpy as jnp
 from jax import lax
@@ -56,7 +58,7 @@
         center = values - jnp.mean(values, axis=1, keepdims=True)
         spread = jnp.mean(center * center, axis=1, keepdims=True)
         mean = jnp.mean(center * lax.rsqrt(spread + 1e-05), axis=0, keepdims=True)
-        rows[pl.ds(step, 1), :] = mean * gain_ref[...]
+        rows[pl.ds(step, 1), :] = mean * gain_ref[...][None]
 
     @pl.when(step == 11)
     def _():
@@ -80,7 +82,7 @@
 def pool_call(image_in, text_in, img_gain, txt_gain, digits):
     pairs, count_i, width_i = image_in.shape
     _, count_t, width_t = text_in.shape
-    whole = lambda shape: pl.BlockSpec(shape, lambda k: (0, 0))
+    whole = lambda shape: pl.BlockSpec(shape, lambda k: (0,) * len(shape))
     return pl.pallas_call(
         pool_kernel,
         grid=(pairs,),
@@ -88,8 +90,8 @@
         in_specs=[
             pl.BlockSpec((1, count_i, width_i), lambda k: (k, 0, 0)),
             pl.BlockSpec((1, count_t, width_t), lambda k: (k, 0, 0)),
-            whole((1, width_i)),
-            whole((1, width_t)),
+            whole((width_i,)),
+            whole((width_t,)),
             whole((16, 128)),
         ],
         out_specs=whole((64, 768)),
@@ -99,8 +101,26 @@
             bytes_accessed=2 * (image_in.size + text_in.size),
             transcendentals=0,
         ),
-        compiler_params=pltpu.CompilerParams(vmem_limit_bytes=40 * 1024 * 1024),
-    )(image_in, text_in, img_gain[None], txt_gain[None], digits)
+        compiler_params=pltpu.CompilerParams(vmem_limit_bytes=60 * 1024 * 1024),
+    )(image_in, text_in, img_gain, txt_gain, digits)
+
+
+def weight_kernel(place_ref, img_ref, txt_ref, out_ref):
+    width = out_ref.shape[1]
+    rows = jnp.concatenate(
+        [
+            img_ref[...].astype(F32),
+            txt_ref[...].astype(F32),
+            jnp.zeros((1, img_ref.shape[1]), F32),
+        ],
+        0,
+    )
+    mine = rows[:, :width]
+    for k in range(1, 4):
+        mine = jnp.where(place_ref[2] == k, rows[:, width * k : width * k + width], mine)
+    mine = jnp.concatenate([mine, mine], 0).astype(BF)
+    for k in range(16):
+        out_ref[48 * k : 48 * k + 48, :] = mine
 
 
 def project_kernel(place_ref, pooled_ref, wa_ref, wb_ref, out_ref):
@@ -117,9 +137,8 @@
                 pieces += [img_rows[3 * t : 3 * t + 3], txt_rows[3 * t : 3 * t + 3]]
         left = jnp.concatenate(pieces, 0).astype(BF)
         part += jnp.dot(left, w_ref[...], preferred_element_type=F32)
-    part = part.astype(BF)
-    for k in range(8):
-        out_ref[48 * k : 48 * k + 48, :] = part
+    packed = jnp.concatenate([part[:24], part[24:]], 1)
+    out_ref[...] = jnp.concatenate([packed] * 8, 0).astype(BF)
 
 
 def in_blocks(values):
@@ -132,9 +151,10 @@
 
 def unit_kernel(place_ref, parts_ref, digits_ref, rows_ref, far_ref, inv_ref, held, held_inv):
     spread = parts_ref[...].astype(F32)
-    emb = rows_ref.shape[1]
-    blocks = [spread[48 * k : 48 * k + 48] + spread[192 + 48 * k : 240 + 48 * k] for k in range(4)]
-    projected = jnp.concatenate(blocks, 1)[:, :emb]
+    width = spread.shape[1] // 2
+    blocks = [spread[24 * k : 24 * k + 24] + spread[96 + 24 * k : 120 + 24 * k] for k in range(4)]
+    blocks = [jnp.concatenate([part[:, :width], part[:, width:]], 0) for part in blocks]
+    projected = jnp.concatenate(blocks, 1)
     inv = lax.rsqrt(jnp.sum(projected * projected, axis=1, keepdims=True) + 1e-06)
     unit = projected * inv
     rows_ref[...] = unit.astype(BF)
@@ -143,9 +163,12 @@
     own = pl.ds(pl.multiple_of(8 * place_ref[0], 8), 8)
     inv_ref[...] = held_inv[own, :]
     block = held[own, :]
-    at = lax.broadcasted_iota(jnp.int32, (8, 128), 0)
-    start = jnp.where(at == 3, digits_ref[...], block[:, :128])
-    block = jnp.concatenate([start, block[:, 128:]], 1)
+    free = jnp.concatenate([digits_ref[...], jnp.zeros((1, 128), F32)], 1)
+    pieces = []
+    for k in (0, 4):
+        ends = [block[k + q : k + q + 1, 1024:] for q in range(3)]
+        pieces += [block[k : k + 3, :1024], jnp.concatenate(ends + [free], 1)]
+    block = jnp.concatenate(pieces, 0)
     block = jnp.concatenate([block, block], 0).astype(BF)
     for k in range(16):
         far_ref[16 * k : 16 * k + 16, :] = block
@@ -163,20 +186,6 @@
     return valid, row_pair, item_pair, row_txt, item
 
 
-def square_mask():
-    down = lax.broadcasted_iota(jnp.int32, (48, 128), 0)
-    along = lax.broadcasted_iota(jnp.int32, (48, 128), 1)
-    return down == along
-
-
-def as_lanes(column):
-    return jnp.sum(jnp.where(square_mask(), column, 0.0), axis=0, keepdims=True)
-
-
-def as_column(lanes):
-    return jnp.sum(jnp.where(square_mask(), lanes, 0.0), axis=1, keepdims=True)
-
-
 def log_total(values, axis):
     largest = jnp.max(values, axis=axis, keepdims=True)
     return largest + jnp.log(jnp.sum(jnp.exp(values - largest), axis=axis, keepdims=True))
@@ -184,13 +193,26 @@
 
 def score_kernel(place_ref, logit_ref, rows_ref, fa_ref, fb_ref, row_pos_ref, scores_ref, far_ref):
     rows = rows_ref[...]
-    scores = jnp.concatenate(
-        [
-            lax.dot_general(rows, ref[...], ROWS_DOT, preferred_element_type=F32)
-            for ref in (fa_ref, fb_ref)
-        ],
-        1,
-    )
+    ends = rows[:, 1024:]
+    blank = jnp.zeros_like(ends)
+    ends = [[ends if k == q else blank for k in range(3)] for q in range(3)]
+    ends = jnp.concatenate([jnp.concatenate(line, 1) for line in ends], 0)
+
+    def dots(left, width):
+        return jnp.concatenate(
+            [
+                lax.dot_general(left, ref[:, :width], ROWS_DOT, preferred_element_type=F32)
+                for ref in (fa_ref, fb_ref)
+            ],
+            1,
+        )
+
+    scores = dots(rows[:, :1024], 1024)
+    ends = dots(ends, 768)
+    lane = lax.broadcasted_iota(jnp.int32, (48, 512), 1) % 4
+    for q in range(3):
+        moved = pltpu.roll(ends[48 * q : 48 * q + 48], 512 - (3 - q), 1)
+        scores += jnp.where(lane == q, moved, 0.0)
     scores = logit_ref[0] * scores
     scores_ref[...] = scores
     valid, _, item_pair, row_txt, _ = tile_masks(place_ref)
@@ -247,43 +269,61 @@
     by_item = (0.5 * logit) * (jnp.exp(masked - item_lse) - jnp.where(hit, 2.0, 0.0))
     coefs = [jnp.where(valid, part, 0.0).astype(BF) for part in (by_row, by_item)]
     along = [
-        as_lanes(jnp.sum(part.astype(F32) * scores, axis=1, keepdims=True) / logit)
-        for part in coefs
+        jnp.sum(part.astype(F32) * scores, axis=1, keepdims=True) / logit for part in coefs
     ]
     coef = jnp.concatenate(coefs, 0)
-    cot = jnp.dot(coef[:, :256], fa_ref[...], preferred_element_type=F32)
-    cot += jnp.dot(coef[:, 256:], fb_ref[...], preferred_element_type=F32)
+
+    def times_items(left, columns):
+        return jnp.dot(left[:, :256], fa_ref[:, columns], preferred_element_type=F32) + jnp.dot(
+            left[:, 256:], fb_ref[:, columns], preferred_element_type=F32
+        )
+
+    cot = times_items(coef, slice(0, 1024))
+    last = lax.broadcasted_iota(jnp.int32, (96, 512), 1) % 4 == 3
+    wide = coef.astype(F32)
+    ends = jnp.zeros((96, 256), F32)
+    for q in range(3):
+        moved = jnp.where(last, pltpu.roll(wide, 3 - q, 1), 0.0).astype(BF)
+        ends += times_items(moved, slice(256 * q, 256 * q + 256))
+    cot = jnp.concatenate([cot, ends], 1)
 
     riders = (
-        in_parts(as_lanes(row_part), 3)
+        in_parts(row_part, 3)
         + in_parts(along[0], 2)
         + in_parts(along[1], 2)
-        + in_parts(jnp.broadcast_to(value, (1, 128)), 2)
-        + [jnp.zeros((7, 128), F32)]
-    )
-    riders = jnp.concatenate([jnp.concatenate(riders, 0), jnp.zeros((16, 256), F32)], 1).astype(BF)
-    cot = jnp.concatenate([cot, jnp.zeros((96, 256), F32)], 1).astype(BF)
-    for k in range(8):
-        way = k % 4
-        out_ref[112 * k : 112 * k + 96, :] = cot[:, 384 * way : 384 * way + 384]
-        out_ref[112 * k + 96 : 112 * k + 112, :] = riders
+        + in_parts(jnp.broadcast_to(value, (48, 1)), 2)
+    )
+    column = lax.broadcasted_iota(jnp.int32, (48, 64), 1)
+    extra = jnp.zeros((48, 64), F32)
+    for k, rider in enumerate(riders):
+        extra = jnp.where(column == k, rider, extra)
+    blank = jnp.zeros((48, 64), F32)
+    width = cot.shape[1] // 4
+    for k in range(4):
+        part = cot[:, width * k : width * k + width]
+        way = jnp.concatenate([part[:48], extra, part[48:], blank], 1).astype(BF)
+        out_ref[48 * k : 48 * k + 48, :] = way
+        out_ref[192 + 48 * k : 240 + 48 * k, :] = way
 
 
 def back_kernel(got_ref, unit_ref, wa_ref, wb_ref, out_ref, loss_ref):
-    riders = [got_ref[112 * k + 96 : 112 * k + 112, :128].astype(F32) for k in range(8)]
-    parts = jnp.concatenate([r[0:1] + r[1:2] + r[2:3] for r in riders], 0)
-    weights = jnp.exp(parts - log_total(parts, 0))
-    along = jnp.zeros((1, 128), F32)
-    value = jnp.zeros((1, 128), F32)
-    summed = jnp.zeros((48, 384), F32)
-    for k, r in enumerate(riders):
-        weight = weights[k : k + 1]
-        along += weight * (r[3:4] + r[4:5]) + (r[5:6] + r[6:7])
-        value += r[7:8] + r[8:9]
-        summed += as_column(weight) * got_ref[112 * k : 112 * k + 48, :].astype(F32)
-        summed += got_ref[112 * k + 48 : 112 * k + 96, :].astype(F32)
-    loss_ref[...] = jnp.broadcast_to(value / (2.0 * 1536), (8, 128))
-    proj_cot = (summed - unit_ref[...].astype(F32) * as_column(along)).astype(BF)
+    width = unit_ref.shape[1]
+    got = [got_ref[48 * k : 48 * k + 48, :].astype(F32) for k in range(8)]
+    riders = [[part[:, width + k : width + k + 1] for k in range(9)] for part in got]
+    parts = [r[0] + r[1] + r[2] for r in riders]
+    largest = functools.reduce(jnp.maximum, parts)
+    total = sum(jnp.exp(part - largest) for part in parts)
+    lse = largest + jnp.log(total)
+    along = jnp.zeros((48, 1), F32)
+    value = jnp.zeros((48, 1), F32)
+    summed = jnp.zeros((48, width), F32)
+    for part, r, own in zip(got, riders, parts):
+        weight = jnp.exp(own - lse)
+        along += weight * (r[3] + r[4]) + (r[5] + r[6])
+        value += r[7] + r[8]
+        summed += weight * part[:, :width] + part[:, width + 64 : 2 * width + 64]
+    loss_ref[...] = jnp.broadcast_to(value[:8] / (2.0 * 1536), (8, 128))
+    proj_cot = (summed - unit_ref[...].astype(F32) * along).astype(BF)
     mixed = []
     for ref in (wa_ref, wb_ref):
         pool = lax.dot_general(proj_cot, ref[...], ROWS_DOT, preferred_element_type=F32)
@@ -316,7 +356,7 @@
             for k in range(2)
         ]
         cot = jnp.concatenate([halves[0][:4], halves[0][4:], halves[1][:4], halves[1][4:]], 1)
-        cot = cot * inv[at : at + 4] * gain_ref[...]
+        cot = cot * inv[at : at + 4] * gain_ref[...][None]
         mean_cot = jnp.mean(cot, axis=1, keepdims=True)
         count = x_ref.shape[0] // 3
         for q in range(3):
@@ -338,9 +378,9 @@
     place = jnp.stack([y_index, h_index, t_index, g_index]).astype(jnp.int32)
     emb = proj_img.shape[1]
 
-    w = jnp.pad(jnp.concatenate([proj_img, proj_txt], 0), ((0, 1), (0, 256)))
-    w = lax.dynamic_slice(w, (0, 384 * t_index), (24, 384))
-    wa, wb = both_cores(exchange(jnp.broadcast_to(w[None], (32, 24, 384)), ZX))
+    width = emb // 4
+    (w,) = kernel_call(weight_kernel, [((768, width), BF)], [place, proj_img, proj_txt], smem=(0,))
+    wa, wb = both_cores(exchange(w.reshape(32, 24, width), ZX))
 
     spot = lax.iota(jnp.int32, 128)[None, :]
     digits = jnp.where(spot == 23, positive[:, None] // 32, 0)
@@ -354,23 +394,23 @@
 
     (part,) = kernel_call(
         project_kernel,
-        [((384, 384), BF)],
+        [((192, 2 * width), BF)],
         [place, pooled.reshape(128, 768), wa, wb],
         smem=(0,),
     )
-    parts = exchange(part.reshape(8, 48, 384), Y).reshape(384, 384)
+    parts = exchange(part.reshape(8, 24, 2 * width), Y).reshape(192, 2 * width)
 
     own_digits = lax.dynamic_slice(positive, (3 * t_index,), (3,))
     own_digits = jnp.concatenate([own_digits // 32, own_digits % 32]).astype(F32)
     own_digits = jnp.pad(own_digits, (0, 122))[None]
     rows, far, inv = kernel_call(
         unit_kernel,
-        [((48, emb), BF), ((256, emb), BF), ((8, 128), F32)],
+        [((48, emb), BF), ((256, 1024), BF), ((8, 128), F32)],
         [place, parts, own_digits],
         scratch=[pltpu.VMEM((64, emb), F32), pltpu.VMEM((64, 128), F32)],
         smem=(0,),
     )
-    fa, fb = both_cores(exchange(far.reshape(32, 8, emb), ZX))
+    fa, fb = both_cores(exchange(far.reshape(32, 8, 1024), ZX))
 
     scores, far = kernel_call(
         score_kernel,
@@ -380,21 +420,19 @@
     )
     far = exchange(far.reshape(64, 4, 128), ZXC).reshape(256, 128)
 
-    item_pos = jnp.concatenate([fa.reshape(32, 8, emb)[:, 3, :6], fb.reshape(32, 8, emb)[:, 3, :6]])
+    item_pos = jnp.concatenate([fa.reshape(32, 8, 1024)[:, 3, 768:774], fb.reshape(32, 8, 1024)[:, 3, 768:774]])
     item_pos = item_pos.astype(F32)
     item_pos = item_pos[:, :3] * 32.0 + item_pos[:, 3:]
     item_pos = jnp.pad(item_pos, ((0, 0), (0, 5)), constant_values=-1.0).reshape(1, 512)
     item_pos = item_pos.astype(jnp.int32)
     (ways,) = kernel_call(
         coef_kernel,
-        [((896, 384), BF)],
+        [((384, 768), BF)],
         [place, logit_scale, scores, far, row_pos, item_pos, fa, fb],
         smem=(0, 1),
     )
-    got = exchange(ways.reshape(8, 112, 384), Y).reshape(896, 384)
-    unit_part = lax.dynamic_slice(
-        jnp.pad(rows, ((0, 0), (0, 256))), (0, 384 * t_index), (48, 384)
-    )
+    got = exchange(ways.reshape(8, 48, 768), Y).reshape(384, 768)
+    unit_part = lax.dynamic_slice(rows, (0, width * t_index), (48, width))
     pool, loss = kernel_call(
         back_kernel, [((64, 768), BF), ((8, 128), F32)], [got, unit_part, wa, wb]
     )
@@ -407,7 +445,7 @@
     img_grads, txt_grads = kernel_call(
         token_kernel,
         [(img_own.shape, BF), (txt_own.shape, BF)],
-        [pool, inv, img_own, txt_own, img_gain[None], txt_gain[None]],
+        [pool, inv, img_own, txt_own, img_gain, txt_gain],
     )
     img_grads = img_grads.reshape(3, count_i, width_i)
     txt_grads = txt_grads.reshape(3, count_t, width_t)

time: 158 us -> 157 us (level)
  waiting for transfers between devices: 67.6 us -> 58.7 us
  Pallas kernels: 14.8 us -> 22.5 us
  blocking collectives: 22.1 us -> 24.1 us
  local copies, waits for them, and re-layouts: 7.46 us -> 5.88 us
    all_to_all x6, waiting for transfers between devices: 67.6 us -> 58.7 us  [exchange(): return lax.all_to_all(blocks, axes, 0, 0, tiled=True)]
    pallas_call x1, Pallas kernels: 4.5 us -> 9.76 us  [pool_call(): pl.pallas_call(pool_kernel, grid=(pairs,), out_shape=jax.ShapeDtypeStruct...]
    pallas_call x6 -> x7, Pallas kernels: 10.3 us -> 12.7 us  [kernel_call(): pl.pallas_call(body, out_shape=[jax.ShapeDtypeStruct(shape, kind) for sha...]
    broadcast_in_dim x3 -> x0, local copies, waits for them, and re-layouts: 2.28 us -> none  [the longest x1 0.88 us: per_device(): wa, wb = both_cores(exchange(jnp.broadcast_to(w[None], (32, 24, 384)), ZX))]
    all_gather x4, blocking collectives: 13.8 us -> 15.5 us  [both_cores(): lax.all_gather(part, 'c', axis=0)]
  transfers between devices with their start and end apart: 6 -> 6, of which waited for: 6 -> 5; matrix products, arithmetic and copies ran while one was open for 3% -> 3% of each run, Pallas kernels for 3% -> 6%
where the time goes in v7:
time: 157 us; the launch traced here: 156 us
  waiting for transfers between devices  58.7 us (37%)
  starting transfers between devices  42.2 us (27%)
  blocking collectives  24.1 us (15%)
  Pallas kernels  22.5 us (14%)
  local copies, waits for them, and re-layouts  5.88 us (4%)
    all_to_all x6, waiting for transfers between devices, exchange(): return lax.all_to_all(blocks, axes, 0, 0, tiled=True)  58.7 us
    all_to_all x6, starting transfers between devices, exchange(): return lax.all_to_all(blocks, axes, 0, 0, tiled=True)  42.2 us
    all_gather x4, blocking collectives, both_cores(): lax.all_gather(part, 'c', axis=0)  15.5 us
    pallas_call x7, Pallas kernels, kernel_call(): pl.pallas_call(body, out_shape=[jax.ShapeDtypeStruct(shape, kind) for sha...  12.7 us
    pallas_call x1, Pallas kernels, pool_call(): pl.pallas_call(pool_kernel, grid=(pairs,), out_shape=jax.ShapeDtypeStruct...  9.76 us
    all_gather x1, blocking collectives, per_device(): pooled = lax.all_gather(pooled, 'h', axis=0)  8.57 us
  transfers between devices with their start and end apart: 6, of which 5 were waited for; matrix products, arithmetic and copies ran while one was open for 3% of the time, Pallas kernels for 6%

profile of v7, /device:TPU:1, one launch (start us, length us, event | category | flops | bytes accessed | tf_op | source)
XLA Modules:
  0.0 155.9 jit_solution(566350449886212925)
XLA Ops:
  2.3 1.7 %shard_map.104 = bf16[768,320]{1,0:T(8,128)(2,1)} custom-call(s32[4]{0:T(128)S(1)} %pad_add_fusion.place_ref, bf16[13,1280]{1,0:T(8,128)(2,1)S(1)} %copy-done, bf16[10,1280]{1,0:T(8,128)(2,1)S(1)} %copy-done.1), custom_call_target="tpu_custom_call" | custom-call | tf_op jit(solution)/shard_map/pallas_call | solution.py:32
  4.0 13.7 %all-to-all-start = ((bf16[32,24,320]{2,1,0:T(8,128)(2,1)}), bf16[32,24,320]{2,1,0:T(8,128)(2,1)S(1)}, u32[]{:S(2)}, u32[]{:S(2)}) async-start(bf16[32,24,320]{2,1,0:T(8,128)(2,1)} %bitcast.4), calls=%async_computation | async-start | bytes 1179648 | tf_op jit(solution)/shard_map/all_to_all | solution.py:21
  19.1 9.8 %shard_map.103 = bf16[64,768]{1,0:T(8,128)(2,1)} custom-call(bf16[12,48,1664]{2,1,0:T(8,128)(2,1)} %img_ref.2, bf16[12,64,1280]{2,1,0:T(8,128)(2,1)} %txt_ref.2, f32[1664]{0:T(1024)} %ig_ref.3, f32[1280]{0:T(1024)} %tg_ref.3, f32[16,128]{1,0:T(8,128)} %pad.16.digits_ref), custom_call_target="tpu_custom_call" | custom-call | flops 19415040 | bytes 3883008 | tf_op jit(solution)/shard_map/pallas_call | solution.py:86
  28.9 8.6 %all-gather.pooled_ref = bf16[128,768]{1,0:T(8,128)(2,1)S(1)} all-gather(bf16[64,768]{1,0:T(8,128)(2,1)} %shard_map.103), channel_id=2, replica_groups=mesh['t'=4,'h'=2,'z'=8,'x'=4,'c'=2] {'h'}, dimensions={0}, use_global_device_ids=true | all-gather | bytes 294912 | tf_op jit(solution)/shard_map/all_gather | solution.py:390
  37.6 5.1 %all-gather.1 = bf16[32,24,320]{2,1,0:T(8,128)(2,1)S(1)} all-gather(bf16[16,24,320]{2,1,0:T(8,128)(2,1)S(1)} %get-tuple-element.24), channel_id=3, replica_groups=mesh['t'=4,'h'=2,'z'=8,'x'=4,'c'=2] {'c'}, dimensions={0}, use_global_device_ids=true | all-gather | bytes 737280 | tf_op jit(solution)/shard_map/all_gather | solution.py:26
  42.7 2.2 %all-gather.2 = bf16[32,24,320]{2,1,0:T(8,128)(2,1)S(1)} all-gather(bf16[16,24,320]{2,1,0:T(8,128)(2,1)S(1)} %get-tuple-element.23), channel_id=4, replica_groups=mesh['t'=4,'h'=2,'z'=8,'x'=4,'c'=2] {'c'}, dimensions={0}, use_global_device_ids=true | all-gather | bytes 737280 | tf_op jit(solution)/shard_map/all_gather | solution.py:26
  44.9 1.6 %shard_map.105 = bf16[192,640]{1,0:T(8,128)(2,1)} custom-call(s32[4]{0:T(128)S(1)} %pad_add_fusion.place_ref, bf16[128,768]{1,0:T(8,128)(2,1)S(1)} %all-gather.pooled_ref, bf16[768,320]{1,0:T(8,128)(2,1)S(1)} %bitcast.30, bf16[768,320]{1,0:T(8,128)(2,1)S(1)} %bitcast.32), custom_call_target="tpu_custom_call" | custom-call | tf_op jit(solution)/shard_map/pallas_call | solution.py:32
  46.5 7.4 %all-to-all-start.1 = ((bf16[8,24,640]{2,1,0:T(8,128)(2,1)}), bf16[8,24,640]{2,1,0:T(8,128)(2,1)S(1)}, u32[]{:S(2)}, u32[]{:S(2)}) async-start(bf16[8,24,640]{2,1,0:T(8,128)(2,1)} %bitcast.7), calls=%async_computation.1 | async-start | bytes 491520 | tf_op jit(solution)/shard_map/all_to_all | solution.py:21
  53.9 10.5 %all-to-all-done.1 = bf16[8,24,640]{2,1,0:T(8,128)(2,1)S(1)} async-done(((bf16[8,24,640]{2,1,0:T(8,128)(2,1)}), bf16[8,24,640]{2,1,0:T(8,128)(2,1)S(1)}, u32[]{:S(2)}, u32[]{:S(2)}) %all-to-all-start.1) | async-done | bytes 245792 | tf_op jit(solution)/shard_map/all_to_all | solution.py:21
  64.4 1.7 %shard_map.106 = (bf16[48,1280]{1,0:T(8,128)(2,1)S(1)}, bf16[256,1024]{1,0:T(8,128)(2,1)}, f32[8,128]{1,0:T(8,128)S(1)}) custom-call(s32[4]{0:T(128)S(1)} %pad_add_fusion.place_ref, bf16[192,640]{1,0:T(8,128)(2,1)S(1)} %bitcast.41, f32[1,128]{1,0:T(1,128)S(1)} %pad_bitcast_fusion.digits_ref), custom_call_target="tpu_custom_call" | custom-call | tf_op jit(solution)/shard_map/pallas_call | solution.py:32
  66.1 9.2 %all-to-all-start.2 = ((bf16[32,8,1024]{2,1,0:T(8,128)(2,1)}), bf16[32,8,1024]{2,1,0:T(8,128)(2,1)S(1)}, u32[]{:S(2)}, u32[]{:S(2)}) async-start(bf16[32,8,1024]{2,1,0:T(8,128)(2,1)} %bitcast.10), calls=%async_computation.2 | async-start | bytes 1048576 | tf_op jit(solution)/shard_map/all_to_all | solution.py:21
  76.4 13.5 %all-to-all-done.2 = bf16[32,8,1024]{2,1,0:T(8,128)(2,1)S(1)} async-done(((bf16[32,8,1024]{2,1,0:T(8,128)(2,1)}), bf16[32,8,1024]{2,1,0:T(8,128)(2,1)S(1)}, u32[]{:S(2)}, u32[]{:S(2)}) %all-to-all-start.2) | async-done | bytes 524320 | tf_op jit(solution)/shard_map/all_to_all | solution.py:21
  89.9 6.1 %all-gather.3 = bf16[32,8,1024]{2,1,0:T(8,128)(2,1)S(1)} all-gather(bf16[16,8,1024]{2,1,0:T(8,128)(2,1)S(1)} %get-tuple-element.26), channel_id=5, replica_groups=mesh['t'=4,'h'=2,'z'=8,'x'=4,'c'=2] {'c'}, dimensions={0}, use_global_device_ids=true | all-gather | bytes 786432 | tf_op jit(solution)/shard_map/all_gather | solution.py:26
  96.1 2.2 %all-gather.4 = bf16[32,8,1024]{2,1,0:T(8,128)(2,1)S(1)} all-gather(bf16[16,8,1024]{2,1,0:T(8,128)(2,1)S(1)} %get-tuple-element.25), channel_id=6, replica_groups=mesh['t'=4,'h'=2,'z'=8,'x'=4,'c'=2] {'c'}, dimensions={0}, use_global_device_ids=true | all-gather | bytes 786432 | tf_op jit(solution)/shard_map/all_gather | solution.py:26
  98.4 2.1 %shard_map.107 = (f32[48,512]{1,0:T(8,128)S(1)}, f32[256,128]{1,0:T(8,128)}) custom-call(s32[4]{0:T(128)S(1)} %pad_add_fusion.place_ref, f32[1]{0:T(128)S(6)} %copy.37.logit_ref, bf16[48,1280]{1,0:T(8,128)(2,1)S(1)} %get-tuple-element.12.rows_ref, bf16[256,1024]{1,0:T(8,128)(2,1)S(1)} %bitcast.34, bf16[256,1024]{1,0:T(8,128)(2,1)S(1)} %bitcast.36, ...), custom_call_target="tpu_custom_call" | custom-call | tf_op jit(solution)/shard_map/pallas_call | solution.py:32
  100.5 5.1 %all-to-all-start.3 = ((f32[64,4,128]{2,1,0:T(4,128)}), f32[64,4,128]{2,1,0:T(4,128)S(1)}, u32[]{:S(2)}, u32[]{:S(2)}) async-start(f32[64,4,128]{2,1,0:T(4,128)} %bitcast.14), calls=%async_computation.3 | async-start | bytes 262144 | tf_op jit(solution)/shard_map/all_to_all | solution.py:21
  105.8 10.8 %all-to-all-done.3 = f32[64,4,128]{2,1,0:T(4,128)S(1)} async-done(((f32[64,4,128]{2,1,0:T(4,128)}), f32[64,4,128]{2,1,0:T(4,128)S(1)}, u32[]{:S(2)}, u32[]{:S(2)}) %all-to-all-start.3) | async-done | bytes 131104 | tf_op jit(solution)/shard_map/all_to_all | solution.py:21
  116.7 2.2 %shard_map.108 = bf16[384,768]{1,0:T(8,128)(2,1)} custom-call(s32[4]{0:T(128)S(1)} %pad_add_fusion.place_ref, f32[1]{0:T(128)S(6)} %copy.37.logit_ref, f32[48,512]{1,0:T(8,128)S(1)} %get-tuple-element.14.scores_ref, f32[256,128]{1,0:T(8,128)S(1)} %bitcast.43, s32[48,1]{1,0:T(8,128)S(1)} %convert_element_type.42.row_pos_ref, ...), custom_call_target="tpu_custom_call" | custom-call | tf_op jit(solution)/shard_map/pallas_call | solution.py:32
  118.8 3.5 %all-to-all-start.4 = ((bf16[8,48,768]{2,1,0:T(8,128)(2,1)}), bf16[8,48,768]{2,1,0:T(8,128)(2,1)S(1)}, u32[]{:S(2)}, u32[]{:S(2)}) async-start(bf16[8,48,768]{2,1,0:T(8,128)(2,1)} %bitcast.18), calls=%async_computation.4 | async-start | bytes 1179648 | tf_op jit(solution)/shard_map/all_to_all | solution.py:21
  123.6 18.1 %all-to-all-done.4 = bf16[8,48,768]{2,1,0:T(8,128)(2,1)S(1)} async-done(((bf16[8,48,768]{2,1,0:T(8,128)(2,1)}), bf16[8,48,768]{2,1,0:T(8,128)(2,1)S(1)}, u32[]{:S(2)}, u32[]{:S(2)}) %all-to-all-start.4) | async-done | bytes 589856 | tf_op jit(solution)/shard_map/all_to_all | solution.py:21
  141.7 1.4 shard_map.109
  143.1 3.4 %all-to-all-start.5 = ((bf16[8,8,768]{2,1,0:T(8,128)(2,1)}), bf16[8,8,768]{2,1,0:T(8,128)(2,1)S(1)}, u32[]{:S(2)}, u32[]{:S(2)}) async-start(bf16[8,8,768]{2,1,0:T(8,128)(2,1)} %bitcast.21), calls=%async_computation.5 | async-start | bytes 196608 | tf_op jit(solution)/shard_map/all_to_all | solution.py:21
  148.1 5.8 %all-to-all-done.5 = bf16[8,8,768]{2,1,0:T(8,128)(2,1)S(1)} async-done(((bf16[8,8,768]{2,1,0:T(8,128)(2,1)}), bf16[8,8,768]{2,1,0:T(8,128)(2,1)S(1)}, u32[]{:S(2)}, u32[]{:S(2)}) %all-to-all-start.5) | async-done | bytes 98336 | tf_op jit(solution)/shard_map/all_to_all | solution.py:21
  153.8 2.0 %shard_map.110 = (bf16[144,1664]{1,0:T(8,128)(2,1)}, bf16[192,1280]{1,0:T(8,128)(2,1)}) custom-call(bf16[64,768]{1,0:T(8,128)(2,1)S(1)} %bitcast.44, f32[8,128]{1,0:T(8,128)S(1)} %get-tuple-element.18.inv_ref, bf16[144,1664]{1,0:T(8,128)(2,1)S(1)} %bitcast.40, bf16[192,1280]{1,0:T(8,128)(2,1)S(1)} %bitcast.39, f32[1664]{0:T(1024)S(1)} %copy-done.2, ...), custom_call_target="tpu_custom_call" | custom-call | tf_op jit(solution)/shard_map/pallas_call | solution.py:32
  (42 shorter events, 7.0 us)
Async XLA Ops:
  0.7 0.8 copy-start
  1.5 0.8 copy-start.1
  4.0 33.5 %all-to-all-start = ((bf16[32,24,320]{2,1,0:T(8,128)(2,1)}), bf16[32,24,320]{2,1,0:T(8,128)(2,1)S(1)}, u32[]{:S(2)}, u32[]{:S(2)}) async-start(bf16[32,24,320]{2,1,0:T(8,128)(2,1)} %bitcast.4), calls=%async_computation | async-start | bytes 1179648 | tf_op jit(solution)/shard_map/all_to_all | solution.py:21
  19.1 18.3 %copy-start.4 = (s32[12]{0:T(128)S(1)}, s32[12]{0:T(128)}, u32[]{:S(2)}) copy-start(s32[12]{0:T(128)} %param.15) | copy-start | bytes 148
  46.5 17.9 %all-to-all-start.1 = ((bf16[8,24,640]{2,1,0:T(8,128)(2,1)}), bf16[8,24,640]{2,1,0:T(8,128)(2,1)S(1)}, u32[]{:S(2)}, u32[]{:S(2)}) async-start(bf16[8,24,640]{2,1,0:T(8,128)(2,1)} %bitcast.7), calls=%async_computation.1 | async-start | bytes 491520 | tf_op jit(solution)/shard_map/all_to_all | solution.py:21
  66.1 23.8 %all-to-all-start.2 = ((bf16[32,8,1024]{2,1,0:T(8,128)(2,1)}), bf16[32,8,1024]{2,1,0:T(8,128)(2,1)S(1)}, u32[]{:S(2)}, u32[]{:S(2)}) async-start(bf16[32,8,1024]{2,1,0:T(8,128)(2,1)} %bitcast.10), calls=%async_computation.2 | async-start | bytes 1048576 | tf_op jit(solution)/shard_map/all_to_all | solution.py:21
  100.5 16.2 %all-to-all-start.3 = ((f32[64,4,128]{2,1,0:T(4,128)}), f32[64,4,128]{2,1,0:T(4,128)S(1)}, u32[]{:S(2)}, u32[]{:S(2)}) async-start(f32[64,4,128]{2,1,0:T(4,128)} %bitcast.14), calls=%async_computation.3 | async-start | bytes 262144 | tf_op jit(solution)/shard_map/all_to_all | solution.py:21
  118.8 22.9 %all-to-all-start.4 = ((bf16[8,48,768]{2,1,0:T(8,128)(2,1)}), bf16[8,48,768]{2,1,0:T(8,128)(2,1)S(1)}, u32[]{:S(2)}, u32[]{:S(2)}) async-start(bf16[8,48,768]{2,1,0:T(8,128)(2,1)} %bitcast.18), calls=%async_computation.4 | async-start | bytes 1179648 | tf_op jit(solution)/shard_map/all_to_all | solution.py:21
  122.4 31.4 %copy-start.2 = (f32[1664]{0:T(1024)S(1)}, f32[1664]{0:T(1024)}, u32[]{:S(2)}) copy-start(f32[1664]{0:T(1024)} %ig_ref.3) | copy-start | bytes 19972
  122.4 31.4 %copy-start.3 = (f32[1280]{0:T(1024)S(1)}, f32[1280]{0:T(1024)}, u32[]{:S(2)}) copy-start(f32[1280]{0:T(1024)} %tg_ref.3) | copy-start | bytes 15364
  143.1 10.7 %all-to-all-start.5 = ((bf16[8,8,768]{2,1,0:T(8,128)(2,1)}), bf16[8,8,768]{2,1,0:T(8,128)(2,1)S(1)}, u32[]{:S(2)}, u32[]{:S(2)}) async-start(bf16[8,8,768]{2,1,0:T(8,128)(2,1)} %bitcast.21), calls=%async_computation.5 | async-start | bytes 196608 | tf_op jit(solution)/shard_map/all_to_all | solution.py:21

commit v8 on v7

--- a/solution.py
+++ b/solution.py
@@ -45,82 +45,86 @@
     return ((dense // wide) % 2) * 384 + (dense // (2 * wide)) * 24 + skip + dense % wide
 
 
-def pool_kernel(img_ref, txt_ref, ig_ref, tg_ref, digits_ref, out_ref, img_rows, txt_rows):
-    step = pl.program_id(0)
-
-    @pl.when(step == 0)
-    def _():
-        img_rows[...] = jnp.zeros_like(img_rows)
-        txt_rows[...] = jnp.zeros_like(txt_rows)
-
-    for x_ref, gain_ref, rows in ((img_ref, ig_ref, img_rows), (txt_ref, tg_ref, txt_rows)):
-        values = x_ref[0].astype(F32)
-        center = values - jnp.mean(values, axis=1, keepdims=True)
-        spread = jnp.mean(center * center, axis=1, keepdims=True)
-        mean = jnp.mean(center * lax.rsqrt(spread + 1e-05), axis=0, keepdims=True)
-        rows[pl.ds(step, 1), :] = mean * gain_ref[...][None]
-
-    @pl.when(step == 11)
-    def _():
-        found = jnp.zeros((64, 768), F32)
-        for rows, wide, skip in ((img_rows, 13, 0), (txt_rows, 10, 13)):
-            width = 32 * wide
-            dense = lax.broadcasted_iota(jnp.int32, (width, 768), 0)
-            lane = lax.broadcasted_iota(jnp.int32, (width, 768), 1)
-            pick = jnp.where(lane == slab_place(dense, wide, skip), 1.0, 0.0).astype(BF)
-            held = rows[...]
-            quarters = [held[:, width * k : width * k + width] for k in range(4)]
-            quarters = jnp.concatenate(quarters, 0).astype(BF)
-            found += jnp.dot(quarters, pick, preferred_element_type=F32)
-        digits = digits_ref[...]
-        blank = jnp.zeros_like(digits)
-        digits = jnp.concatenate([digits, blank, digits, blank], 0)
-        found = jnp.concatenate([found[:, :128] + digits, found[:, 128:]], 1)
-        out_ref[...] = found.astype(BF)
-
-
-def pool_call(image_in, text_in, img_gain, txt_gain, digits):
+def pool_kernel(
+    pos_ref, img_ref, txt_ref, ig_ref, tg_ref, out_ref, img_held, txt_held, img_rows, txt_rows, digits, sems
+):
+    pairs = img_ref.shape[0]
+
+    def copies(k):
+        return (
+            pltpu.make_async_copy(img_ref.at[k], img_held.at[k], sems.at[0, k]),
+            pltpu.make_async_copy(txt_ref.at[k], txt_held.at[k], sems.at[1, k]),
+        )
+
+    for k in range(pairs):
+        for copy in copies(k):
+            copy.start()
+    for rows in (img_rows, txt_rows, digits):
+        rows[...] = jnp.zeros_like(rows)
+    spot = lax.broadcasted_iota(jnp.int32, (1, 128), 1)
+
+    def one_pair(k, carry):
+        for copy in copies(k):
+            copy.wait()
+        for held, gain_ref, rows in ((img_held, ig_ref, img_rows), (txt_held, tg_ref, txt_rows)):
+            values = held[k].astype(F32)
+            center = values - jnp.mean(values, axis=1, keepdims=True)
+            spread = jnp.mean(center * center, axis=1, keepdims=True)
+            mean = jnp.mean(center * lax.rsqrt(spread + 1e-05), axis=0, keepdims=True)
+            rows[pl.ds(k, 1), :] = mean * gain_ref[...][None]
+        place = pos_ref[k]
+        line = jnp.where(spot == 23, place // 32, jnp.where(spot == 47, place % 32, 0))
+        digits[pl.ds(k, 1), :] = line.astype(F32)
+        return carry
+
+    lax.fori_loop(0, pairs, one_pair, 0)
+    found = jnp.zeros((64, 768), F32)
+    for rows, wide, skip in ((img_rows, 13, 0), (txt_rows, 10, 13)):
+        width = 32 * wide
+        dense = lax.broadcasted_iota(jnp.int32, (width, 768), 0)
+        lane = lax.broadcasted_iota(jnp.int32, (width, 768), 1)
+        pick = jnp.where(lane == slab_place(dense, wide, skip), 1.0, 0.0).astype(BF)
+        held = rows[...]
+        quarters = [held[:, width * k : width * k + width] for k in range(4)]
+        quarters = jnp.concatenate(quarters, 0).astype(BF)
+        found += jnp.dot(quarters, pick, preferred_element_type=F32)
+    line = digits[...]
+    blank = jnp.zeros_like(line)
+    line = jnp.concatenate([line, blank, line, blank], 0)
+    found = jnp.concatenate([found[:, :128] + line, found[:, 128:]], 1)
+    out_ref[...] = found.astype(BF)
+
+
+def pool_call(image_in, text_in, img_gain, txt_gain, positive):
     pairs, count_i, width_i = image_in.shape
     _, count_t, width_t = text_in.shape
-    whole = lambda shape: pl.BlockSpec(shape, lambda k: (0,) * len(shape))
+    vmem = pl.BlockSpec(memory_space=pltpu.VMEM)
     return pl.pallas_call(
         pool_kernel,
-        grid=(pairs,),
         out_shape=jax.ShapeDtypeStruct((64, 768), BF),
         in_specs=[
-            pl.BlockSpec((1, count_i, width_i), lambda k: (k, 0, 0)),
-            pl.BlockSpec((1, count_t, width_t), lambda k: (k, 0, 0)),
-            whole((width_i,)),
-            whole((width_t,)),
-            whole((16, 128)),
+            pl.BlockSpec(memory_space=pltpu.SMEM),
+            pl.BlockSpec(memory_space=pl.ANY),
+            pl.BlockSpec(memory_space=pl.ANY),
+            vmem,
+            vmem,
         ],
-        out_specs=whole((64, 768)),
-        scratch_shapes=[pltpu.VMEM((16, width_i), F32), pltpu.VMEM((16, width_t), F32)],
+        out_specs=vmem,
+        scratch_shapes=[
+            pltpu.VMEM(image_in.shape, BF),
+            pltpu.VMEM(text_in.shape, BF),
+            pltpu.VMEM((16, width_i), F32),
+            pltpu.VMEM((16, width_t), F32),
+            pltpu.VMEM((16, 128), F32),
+            pltpu.SemaphoreType.DMA((2, pairs)),
+        ],
         cost_estimate=pl.CostEstimate(
             flops=10 * (image_in.size + text_in.size),
             bytes_accessed=2 * (image_in.size + text_in.size),
             transcendentals=0,
         ),
         compiler_params=pltpu.CompilerParams(vmem_limit_bytes=60 * 1024 * 1024),
-    )(image_in, text_in, img_gain, txt_gain, digits)
-
-
-def weight_kernel(place_ref, img_ref, txt_ref, out_ref):
-    width = out_ref.shape[1]
-    rows = jnp.concatenate(
-        [
-            img_ref[...].astype(F32),
-            txt_ref[...].astype(F32),
-            jnp.zeros((1, img_ref.shape[1]), F32),
-        ],
-        0,
-    )
-    mine = rows[:, :width]
-    for k in range(1, 4):
-        mine = jnp.where(place_ref[2] == k, rows[:, width * k : width * k + width], mine)
-    mine = jnp.concatenate([mine, mine], 0).astype(BF)
-    for k in range(16):
-        out_ref[48 * k : 48 * k + 48, :] = mine
+    )(positive, image_in, text_in, img_gain, txt_gain)
 
 
 def project_kernel(place_ref, pooled_ref, wa_ref, wb_ref, out_ref):
@@ -379,15 +383,13 @@
     emb = proj_img.shape[1]
 
     width = emb // 4
-    (w,) = kernel_call(weight_kernel, [((768, width), BF)], [place, proj_img, proj_txt], smem=(0,))
-    wa, wb = both_cores(exchange(w.reshape(32, 24, width), ZX))
-
-    spot = lax.iota(jnp.int32, 128)[None, :]
-    digits = jnp.where(spot == 23, positive[:, None] // 32, 0)
-    digits = jnp.where(spot == 47, positive[:, None] % 32, digits).astype(F32)
-    digits = jnp.pad(digits, ((0, 4), (0, 0)))
-    pooled = pool_call(image_in, text_in, img_gain, txt_gain, digits)
-    pooled = lax.all_gather(pooled, "h", axis=0)
+    w = jnp.concatenate([proj_img, proj_txt, jnp.zeros((1, emb), BF)], 0)
+    w = lax.dynamic_slice(w, (0, width * t_index), (24, width))
+    w = jnp.broadcast_to(w[None], (32, 24, width))
+    wa, wb = both_cores(exchange(w, ZX))
+
+    pooled = pool_call(image_in, text_in, img_gain, txt_gain, positive)
+    pooled = lax.all_gather(pooled, Y, axis=0, axis_index_groups=[[0, 6], [1, 7], [2, 4], [3, 5]])
     row_pos = pooled[:, :12, 23].astype(F32) * 32.0 + pooled[:, :12, 47].astype(F32)
     row_pos = jnp.pad(row_pos.reshape(8, 3), ((0, 0), (0, 3)), constant_values=-1.0)
     row_pos = row_pos.reshape(48, 1).astype(jnp.int32)

time: 157 us -> 148 us (0.943)
  Pallas kernels: 22.5 us -> 17.8 us
  starting transfers between devices: 42.2 us -> 38.3 us
    all_to_all x6, starting transfers between devices: 42.2 us -> 38.3 us  [exchange(): return lax.all_to_all(blocks, axes, 0, 0, tiled=True)]
    pallas_call x1, Pallas kernels: 9.76 us -> 6.87 us  [pool_call(): pl.pallas_call(pool_kernel, out_shape=jax.ShapeDtypeStruct((64, 768), BF)...]
    pallas_call x7 -> x6, Pallas kernels: 12.7 us -> 11 us  [kernel_call(): pl.pallas_call(body, out_shape=[jax.ShapeDtypeStruct(shape, kind) for sha...]
  transfers between devices with their start and end apart: 6 -> 6, of which waited for: 5 -> 6; matrix products, arithmetic and copies ran while one was open for 3% -> 3% of each run, Pallas kernels for 6% -> 5%
where the time goes in v8:
time: 148 us; the launch traced here: 147 us
  waiting for transfers between devices  60.1 us (41%)
  starting transfers between devices  38.3 us (26%)
  blocking collectives  23.8 us (16%)
  Pallas kernels  17.8 us (12%)
  local copies, waits for them, and re-layouts  4.67 us (3%)
    all_to_all x6, waiting for transfers between devices, exchange(): return lax.all_to_all(blocks, axes, 0, 0, tiled=True)  60.1 us
    all_to_all x6, starting transfers between devices, exchange(): return lax.all_to_all(blocks, axes, 0, 0, tiled=True)  38.3 us
    all_gather x4, blocking collectives, both_cores(): lax.all_gather(part, 'c', axis=0)  14.8 us
    pallas_call x6, Pallas kernels, kernel_call(): pl.pallas_call(body, out_shape=[jax.ShapeDtypeStruct(shape, kind) for sha...  11 us
    all_gather x1, blocking collectives, per_device(): lax.all_gather(pooled, Y, axis=0, axis_index_groups=[[0, 6], [1, 7], [2,...  9.02 us
    pallas_call x1, Pallas kernels, pool_call(): pl.pallas_call(pool_kernel, out_shape=jax.ShapeDtypeStruct((64, 768), BF)...  6.87 us
  transfers between devices with their start and end apart: 6, of which 6 were waited for; matrix products, arithmetic and copies ran while one was open for 3% of the time, Pallas kernels for 5%

profile of v8, /device:TPU:1, one launch (start us, length us, event | category | flops | bytes accessed | tf_op | source)
XLA Modules:
  0.0 147.3 jit_solution(7811433316634202669)
XLA Ops:
  2.4 13.7 %all-to-all-start = ((bf16[32,24,320]{2,1,0:T(8,128)(2,1)}), bf16[32,24,320]{2,1,0:T(8,128)(2,1)S(1)}, u32[]{:S(2)}, u32[]{:S(2)}) async-start(bf16[32,24,320]{2,1,0:T(8,128)(2,1)} %broadcast_in_dim.13), calls=%async_computation | async-start | bytes 1179648 | tf_op jit(solution)/shard_map/all_to_all | solution.py:21
  16.2 6.9 %shard_map.103 = bf16[64,768]{1,0:T(8,128)(2,1)} custom-call(s32[12]{0:T(128)} %pos_ref.1, bf16[12,48,1664]{2,1,0:T(8,128)(2,1)} %img_ref.1, bf16[12,64,1280]{2,1,0:T(8,128)(2,1)} %txt_ref.1, f32[1664]{0:T(1024)} %ig_ref.3, f32[1280]{0:T(1024)} %tg_ref.3), custom_call_target="tpu_custom_call" | custom-call | flops 19415040 | bytes 3883008 | tf_op jit(solution)/shard_map/pallas_call | solution.py:102
  23.0 9.0 %all-gather.pooled_ref = bf16[128,768]{1,0:T(8,128)(2,1)S(1)} all-gather(bf16[64,768]{1,0:T(8,128)(2,1)} %shard_map.103), channel_id=2, replica_groups={{0,320},{128,448},{256,64},{384,192},{1,321},{129,449},{257,65},{385,19..., dimensions={0}, use_global_device_ids=true | all-gather | bytes 294912 | tf_op jit(solution)/shard_map/all_gather | solution.py:392
  32.2 1.4 all-to-all-done
  33.7 4.3 %all-gather.1 = bf16[32,24,320]{2,1,0:T(8,128)(2,1)S(1)} all-gather(bf16[16,24,320]{2,1,0:T(8,128)(2,1)S(1)} %get-tuple-element.24), channel_id=3, replica_groups=mesh['t'=4,'h'=2,'z'=8,'x'=4,'c'=2] {'c'}, dimensions={0}, use_global_device_ids=true | all-gather | bytes 737280 | tf_op jit(solution)/shard_map/all_gather | solution.py:26
  38.0 2.2 %all-gather.2 = bf16[32,24,320]{2,1,0:T(8,128)(2,1)S(1)} all-gather(bf16[16,24,320]{2,1,0:T(8,128)(2,1)S(1)} %get-tuple-element.23), channel_id=4, replica_groups=mesh['t'=4,'h'=2,'z'=8,'x'=4,'c'=2] {'c'}, dimensions={0}, use_global_device_ids=true | all-gather | bytes 737280 | tf_op jit(solution)/shard_map/all_gather | solution.py:26
  40.2 1.6 %shard_map.104 = bf16[192,640]{1,0:T(8,128)(2,1)} custom-call(s32[4]{0:T(128)S(1)} %pad_add_fusion.place_ref, bf16[128,768]{1,0:T(8,128)(2,1)S(1)} %all-gather.pooled_ref, bf16[768,320]{1,0:T(8,128)(2,1)S(1)} %bitcast.30, bf16[768,320]{1,0:T(8,128)(2,1)S(1)} %bitcast.32), custom_call_target="tpu_custom_call" | custom-call | tf_op jit(solution)/shard_map/pallas_call | solution.py:32
  41.8 6.8 %all-to-all-start.1 = ((bf16[8,24,640]{2,1,0:T(8,128)(2,1)}), bf16[8,24,640]{2,1,0:T(8,128)(2,1)S(1)}, u32[]{:S(2)}, u32[]{:S(2)}) async-start(bf16[8,24,640]{2,1,0:T(8,128)(2,1)} %bitcast.6), calls=%async_computation.1 | async-start | bytes 491520 | tf_op jit(solution)/shard_map/all_to_all | solution.py:21
  48.8 10.4 %all-to-all-done.1 = bf16[8,24,640]{2,1,0:T(8,128)(2,1)S(1)} async-done(((bf16[8,24,640]{2,1,0:T(8,128)(2,1)}), bf16[8,24,640]{2,1,0:T(8,128)(2,1)S(1)}, u32[]{:S(2)}, u32[]{:S(2)}) %all-to-all-start.1) | async-done | bytes 245792 | tf_op jit(solution)/shard_map/all_to_all | solution.py:21
  59.2 1.7 %shard_map.105 = (bf16[48,1280]{1,0:T(8,128)(2,1)S(1)}, bf16[256,1024]{1,0:T(8,128)(2,1)}, f32[8,128]{1,0:T(8,128)S(1)}) custom-call(s32[4]{0:T(128)S(1)} %pad_add_fusion.place_ref, bf16[192,640]{1,0:T(8,128)(2,1)S(1)} %bitcast.41, f32[1,128]{1,0:T(1,128)S(1)} %pad_bitcast_fusion.digits_ref), custom_call_target="tpu_custom_call" | custom-call | tf_op jit(solution)/shard_map/pallas_call | solution.py:32
  60.9 5.9 %all-to-all-start.2 = ((bf16[32,8,1024]{2,1,0:T(8,128)(2,1)}), bf16[32,8,1024]{2,1,0:T(8,128)(2,1)S(1)}, u32[]{:S(2)}, u32[]{:S(2)}) async-start(bf16[32,8,1024]{2,1,0:T(8,128)(2,1)} %bitcast.9), calls=%async_computation.2 | async-start | bytes 1048576 | tf_op jit(solution)/shard_map/all_to_all | solution.py:21
  67.9 13.5 %all-to-all-done.2 = bf16[32,8,1024]{2,1,0:T(8,128)(2,1)S(1)} async-done(((bf16[32,8,1024]{2,1,0:T(8,128)(2,1)}), bf16[32,8,1024]{2,1,0:T(8,128)(2,1)S(1)}, u32[]{:S(2)}, u32[]{:S(2)}) %all-to-all-start.2) | async-done | bytes 524320 | tf_op jit(solution)/shard_map/all_to_all | solution.py:21
  81.4 6.1 %all-gather.3 = bf16[32,8,1024]{2,1,0:T(8,128)(2,1)S(1)} all-gather(bf16[16,8,1024]{2,1,0:T(8,128)(2,1)S(1)} %get-tuple-element.26), channel_id=5, replica_groups=mesh['t'=4,'h'=2,'z'=8,'x'=4,'c'=2] {'c'}, dimensions={0}, use_global_device_ids=true | all-gather | bytes 786432 | tf_op jit(solution)/shard_map/all_gather | solution.py:26
  87.5 2.2 %all-gather.4 = bf16[32,8,1024]{2,1,0:T(8,128)(2,1)S(1)} all-gather(bf16[16,8,1024]{2,1,0:T(8,128)(2,1)S(1)} %get-tuple-element.25), channel_id=6, replica_groups=mesh['t'=4,'h'=2,'z'=8,'x'=4,'c'=2] {'c'}, dimensions={0}, use_global_device_ids=true | all-gather | bytes 786432 | tf_op jit(solution)/shard_map/all_gather | solution.py:26
  89.8 2.1 %shard_map.106 = (f32[48,512]{1,0:T(8,128)S(1)}, f32[256,128]{1,0:T(8,128)}) custom-call(s32[4]{0:T(128)S(1)} %pad_add_fusion.place_ref, f32[1]{0:T(128)S(6)} %copy.37.logit_ref, bf16[48,1280]{1,0:T(8,128)(2,1)S(1)} %get-tuple-element.12.rows_ref, bf16[256,1024]{1,0:T(8,128)(2,1)S(1)} %bitcast.34, bf16[256,1024]{1,0:T(8,128)(2,1)S(1)} %bitcast.36, ...), custom_call_target="tpu_custom_call" | custom-call | tf_op jit(solution)/shard_map/pallas_call | solution.py:32
  92.0 5.1 %all-to-all-start.3 = ((f32[64,4,128]{2,1,0:T(4,128)}), f32[64,4,128]{2,1,0:T(4,128)S(1)}, u32[]{:S(2)}, u32[]{:S(2)}) async-start(f32[64,4,128]{2,1,0:T(4,128)} %bitcast.13), calls=%async_computation.3 | async-start | bytes 262144 | tf_op jit(solution)/shard_map/all_to_all | solution.py:21
  97.3 10.8 %all-to-all-done.3 = f32[64,4,128]{2,1,0:T(4,128)S(1)} async-done(((f32[64,4,128]{2,1,0:T(4,128)}), f32[64,4,128]{2,1,0:T(4,128)S(1)}, u32[]{:S(2)}, u32[]{:S(2)}) %all-to-all-start.3) | async-done | bytes 131104 | tf_op jit(solution)/shard_map/all_to_all | solution.py:21
  108.1 2.1 %shard_map.107 = bf16[384,768]{1,0:T(8,128)(2,1)} custom-call(s32[4]{0:T(128)S(1)} %pad_add_fusion.place_ref, f32[1]{0:T(128)S(6)} %copy.37.logit_ref, f32[48,512]{1,0:T(8,128)S(1)} %get-tuple-element.14.scores_ref, f32[256,128]{1,0:T(8,128)S(1)} %bitcast.43, s32[48,1]{1,0:T(8,128)S(1)} %convert_element_type.36.row_pos_ref, ...), custom_call_target="tpu_custom_call" | custom-call | tf_op jit(solution)/shard_map/pallas_call | solution.py:32
  110.3 3.5 %all-to-all-start.4 = ((bf16[8,48,768]{2,1,0:T(8,128)(2,1)}), bf16[8,48,768]{2,1,0:T(8,128)(2,1)S(1)}, u32[]{:S(2)}, u32[]{:S(2)}) async-start(bf16[8,48,768]{2,1,0:T(8,128)(2,1)} %bitcast.17), calls=%async_computation.4 | async-start | bytes 1179648 | tf_op jit(solution)/shard_map/all_to_all | solution.py:21
  115.0 18.1 %all-to-all-done.4 = bf16[8,48,768]{2,1,0:T(8,128)(2,1)S(1)} async-done(((bf16[8,48,768]{2,1,0:T(8,128)(2,1)}), bf16[8,48,768]{2,1,0:T(8,128)(2,1)S(1)}, u32[]{:S(2)}, u32[]{:S(2)}) %all-to-all-start.4) | async-done | bytes 589856 | tf_op jit(solution)/shard_map/all_to_all | solution.py:21
  133.1 1.4 shard_map.108
  134.5 3.4 %all-to-all-start.5 = ((bf16[8,8,768]{2,1,0:T(8,128)(2,1)}), bf16[8,8,768]{2,1,0:T(8,128)(2,1)S(1)}, u32[]{:S(2)}, u32[]{:S(2)}) async-start(bf16[8,8,768]{2,1,0:T(8,128)(2,1)} %bitcast.20), calls=%async_computation.5 | async-start | bytes 196608 | tf_op jit(solution)/shard_map/all_to_all | solution.py:21
  139.5 5.8 %all-to-all-done.5 = bf16[8,8,768]{2,1,0:T(8,128)(2,1)S(1)} async-done(((bf16[8,8,768]{2,1,0:T(8,128)(2,1)}), bf16[8,8,768]{2,1,0:T(8,128)(2,1)S(1)}, u32[]{:S(2)}, u32[]{:S(2)}) %all-to-all-start.5) | async-done | bytes 98336 | tf_op jit(solution)/shard_map/all_to_all | solution.py:21
  145.3 2.0 %shard_map.109 = (bf16[144,1664]{1,0:T(8,128)(2,1)}, bf16[192,1280]{1,0:T(8,128)(2,1)}) custom-call(bf16[64,768]{1,0:T(8,128)(2,1)S(1)} %bitcast.44, f32[8,128]{1,0:T(8,128)S(1)} %get-tuple-element.18.inv_ref, bf16[144,1664]{1,0:T(8,128)(2,1)S(1)} %bitcast.40, bf16[192,1280]{1,0:T(8,128)(2,1)S(1)} %bitcast.39, f32[1664]{0:T(1024)S(1)} %copy-done, ...), custom_call_target="tpu_custom_call" | custom-call | tf_op jit(solution)/shard_map/pallas_call | solution.py:32
  (36 shorter events, 5.8 us)
Async XLA Ops:
  2.4 31.2 %all-to-all-start = ((bf16[32,24,320]{2,1,0:T(8,128)(2,1)}), bf16[32,24,320]{2,1,0:T(8,128)(2,1)S(1)}, u32[]{:S(2)}, u32[]{:S(2)}) async-start(bf16[32,24,320]{2,1,0:T(8,128)(2,1)} %broadcast_in_dim.13), calls=%async_computation | async-start | bytes 1179648 | tf_op jit(solution)/shard_map/all_to_all | solution.py:21
  16.1 16.0 %copy-start.2 = (s32[12]{0:T(128)S(1)}, s32[12]{0:T(128)}, u32[]{:S(2)}) copy-start(s32[12]{0:T(128)} %pos_ref.1) | copy-start | bytes 148
  41.8 17.4 %all-to-all-start.1 = ((bf16[8,24,640]{2,1,0:T(8,128)(2,1)}), bf16[8,24,640]{2,1,0:T(8,128)(2,1)S(1)}, u32[]{:S(2)}, u32[]{:S(2)}) async-start(bf16[8,24,640]{2,1,0:T(8,128)(2,1)} %bitcast.6), calls=%async_computation.1 | async-start | bytes 491520 | tf_op jit(solution)/shard_map/all_to_all | solution.py:21
  60.9 20.5 %all-to-all-start.2 = ((bf16[32,8,1024]{2,1,0:T(8,128)(2,1)}), bf16[32,8,1024]{2,1,0:T(8,128)(2,1)S(1)}, u32[]{:S(2)}, u32[]{:S(2)}) async-start(bf16[32,8,1024]{2,1,0:T(8,128)(2,1)} %bitcast.9), calls=%async_computation.2 | async-start | bytes 1048576 | tf_op jit(solution)/shard_map/all_to_all | solution.py:21
  92.0 16.2 %all-to-all-start.3 = ((f32[64,4,128]{2,1,0:T(4,128)}), f32[64,4,128]{2,1,0:T(4,128)S(1)}, u32[]{:S(2)}, u32[]{:S(2)}) async-start(f32[64,4,128]{2,1,0:T(4,128)} %bitcast.13), calls=%async_computation.3 | async-start | bytes 262144 | tf_op jit(solution)/shard_map/all_to_all | solution.py:21
  110.3 22.9 %all-to-all-start.4 = ((bf16[8,48,768]{2,1,0:T(8,128)(2,1)}), bf16[8,48,768]{2,1,0:T(8,128)(2,1)S(1)}, u32[]{:S(2)}, u32[]{:S(2)}) async-start(bf16[8,48,768]{2,1,0:T(8,128)(2,1)} %bitcast.17), calls=%async_computation.4 | async-start | bytes 1179648 | tf_op jit(solution)/shard_map/all_to_all | solution.py:21
  113.8 31.4 %copy-start = (f32[1664]{0:T(1024)S(1)}, f32[1664]{0:T(1024)}, u32[]{:S(2)}) copy-start(f32[1664]{0:T(1024)} %ig_ref.3) | copy-start | bytes 19972
  113.8 31.4 %copy-start.1 = (f32[1280]{0:T(1024)S(1)}, f32[1280]{0:T(1024)}, u32[]{:S(2)}) copy-start(f32[1280]{0:T(1024)} %tg_ref.3) | copy-start | bytes 15364
  134.5 10.7 %all-to-all-start.5 = ((bf16[8,8,768]{2,1,0:T(8,128)(2,1)}), bf16[8,8,768]{2,1,0:T(8,128)(2,1)S(1)}, u32[]{:S(2)}, u32[]{:S(2)}) async-start(bf16[8,8,768]{2,1,0:T(8,128)(2,1)} %bitcast.20), calls=%async_computation.5 | async-start | bytes 196608 | tf_op jit(solution)/shard_map/all_to_all | solution.py:21

commit v9 on v8

--- a/solution.py
+++ b/solution.py
@@ -42,7 +42,13 @@
 
 
 def slab_place(dense, wide, skip):
-    return ((dense // wide) % 2) * 384 + (dense // (2 * wide)) * 24 + skip + dense % wide
+    row = skip + dense % wide
+    return (row // 8) * 256 + ((dense // wide) % 2) * 128 + (dense // (2 * wide)) * 8 + row % 8
+
+
+def slab_row(shape):
+    lane = lax.broadcasted_iota(jnp.int32, shape, 1)
+    return (lane // 256) * 8 + lane % 8
 
 
 def pool_kernel(
@@ -73,7 +79,7 @@
             mean = jnp.mean(center * lax.rsqrt(spread + 1e-05), axis=0, keepdims=True)
             rows[pl.ds(k, 1), :] = mean * gain_ref[...][None]
         place = pos_ref[k]
-        line = jnp.where(spot == 23, place // 32, jnp.where(spot == 47, place % 32, 0))
+        line = jnp.where(spot == 7, place // 32, jnp.where(spot == 15, place % 32, 0))
         digits[pl.ds(k, 1), :] = line.astype(F32)
         return carry
 
@@ -91,7 +97,7 @@
     line = digits[...]
     blank = jnp.zeros_like(line)
     line = jnp.concatenate([line, blank, line, blank], 0)
-    found = jnp.concatenate([found[:, :128] + line, found[:, 128:]], 1)
+    found = jnp.concatenate([found[:, :512], found[:, 512:640] + line, found[:, 640:]], 1)
     out_ref[...] = found.astype(BF)
 
 
@@ -128,8 +134,9 @@
 
 
 def project_kernel(place_ref, pooled_ref, wa_ref, wb_ref, out_ref):
-    part = jnp.zeros((48, wa_ref.shape[1]), F32)
-    inside = lax.broadcasted_iota(jnp.int32, (12, 768), 1) % 24
+    width = wa_ref.shape[1] // 3
+    part = jnp.zeros((48, width), F32)
+    inside = slab_row((12, 768))
     for a, w_ref in enumerate((wa_ref, wb_ref)):
         pieces = []
         for h in range(2):
@@ -140,7 +147,12 @@
             for t in range(4):
                 pieces += [img_rows[3 * t : 3 * t + 3], txt_rows[3 * t : 3 * t + 3]]
         left = jnp.concatenate(pieces, 0).astype(BF)
-        part += jnp.dot(left, w_ref[...], preferred_element_type=F32)
+        for j in range(3):
+            part += jnp.dot(
+                left[:, 256 * j : 256 * j + 256],
+                w_ref[:, width * j : width * j + width],
+                preferred_element_type=F32,
+            )
     packed = jnp.concatenate([part[:24], part[24:]], 1)
     out_ref[...] = jnp.concatenate([packed] * 8, 0).astype(BF)
 
@@ -242,8 +254,54 @@
     return parts
 
 
+def times_items(left, fa_ref, fb_ref):
+    def times(part, columns):
+        return jnp.dot(part[:, :256], fa_ref[:, columns], preferred_element_type=F32) + jnp.dot(
+            part[:, 256:], fb_ref[:, columns], preferred_element_type=F32
+        )
+
+    start = times(left, slice(0, 1024))
+    last = lax.broadcasted_iota(jnp.int32, left.shape, 1) % 4 == 3
+    wide = left.astype(F32)
+    ends = jnp.zeros((left.shape[0], 256), F32)
+    for q in range(3):
+        moved = jnp.where(last, pltpu.roll(wide, 3 - q, 1), 0.0).astype(BF)
+        ends += times(moved, slice(256 * q, 256 * q + 256))
+    return jnp.concatenate([start, ends], 1)
+
+
+def in_columns(parts, first):
+    column = lax.broadcasted_iota(jnp.int32, (48, 128), 1)
+    out = jnp.zeros((48, 128), F32)
+    for k, part in enumerate(parts):
+        out = jnp.where(column == first + k, part, out)
+    return out
+
+
+def row_kernel(place_ref, logit_ref, scores_ref, fa_ref, fb_ref, cot_ref, riders_ref):
+    logit = logit_ref[0]
+    scores = scores_ref[...]
+    valid = tile_masks(place_ref)[0]
+    masked = jnp.where(valid, scores, LOW)
+    row_part = log_total(masked, 1)
+    coef = jnp.where(valid, (0.5 * logit) * jnp.exp(masked - row_part), 0.0).astype(BF)
+    along = jnp.sum(coef.astype(F32) * scores, axis=1, keepdims=True) / logit
+    cot_ref[...] = times_items(coef, fa_ref, fb_ref)
+    riders_ref[...] = in_columns(in_parts(row_part, 3) + in_parts(along, 2), 0)
+
+
 def coef_kernel(
-    place_ref, logit_ref, scores_ref, far_ref, row_pos_ref, item_pos_ref, fa_ref, fb_ref, out_ref
+    place_ref,
+    logit_ref,
+    scores_ref,
+    far_ref,
+    row_pos_ref,
+    item_pos_ref,
+    fa_ref,
+    fb_ref,
+    by_row_ref,
+    riders_ref,
+    out_ref,
 ):
     logit = logit_ref[0]
     scores = scores_ref[...]
@@ -268,59 +326,36 @@
     matched = jnp.sum(jnp.where(lane == 3, summed, 0.0), axis=1, keepdims=True)
     value = lse_total - 2.0 * matched
     masked = jnp.where(valid, scores, LOW)
-    row_part = log_total(masked, 1)
-    by_row = (0.5 * logit) * jnp.exp(masked - row_part)
-    by_item = (0.5 * logit) * (jnp.exp(masked - item_lse) - jnp.where(hit, 2.0, 0.0))
-    coefs = [jnp.where(valid, part, 0.0).astype(BF) for part in (by_row, by_item)]
-    along = [
-        jnp.sum(part.astype(F32) * scores, axis=1, keepdims=True) / logit for part in coefs
-    ]
-    coef = jnp.concatenate(coefs, 0)
-
-    def times_items(left, columns):
-        return jnp.dot(left[:, :256], fa_ref[:, columns], preferred_element_type=F32) + jnp.dot(
-            left[:, 256:], fb_ref[:, columns], preferred_element_type=F32
-        )
-
-    cot = times_items(coef, slice(0, 1024))
-    last = lax.broadcasted_iota(jnp.int32, (96, 512), 1) % 4 == 3
-    wide = coef.astype(F32)
-    ends = jnp.zeros((96, 256), F32)
-    for q in range(3):
-        moved = jnp.where(last, pltpu.roll(wide, 3 - q, 1), 0.0).astype(BF)
-        ends += times_items(moved, slice(256 * q, 256 * q + 256))
-    cot = jnp.concatenate([cot, ends], 1)
-
-    riders = (
-        in_parts(row_part, 3)
-        + in_parts(along[0], 2)
-        + in_parts(along[1], 2)
-        + in_parts(jnp.broadcast_to(value, (48, 1)), 2)
-    )
-    column = lax.broadcasted_iota(jnp.int32, (48, 64), 1)
-    extra = jnp.zeros((48, 64), F32)
-    for k, rider in enumerate(riders):
-        extra = jnp.where(column == k, rider, extra)
+    coef = (0.5 * logit) * (jnp.exp(masked - item_lse) - jnp.where(hit, 2.0, 0.0))
+    coef = jnp.where(valid, coef, 0.0).astype(BF)
+    along = jnp.sum(coef.astype(F32) * scores, axis=1, keepdims=True) / logit
+    by_item = times_items(coef, fa_ref, fb_ref)
+    by_row = by_row_ref[...]
+    value = jnp.broadcast_to(value, (48, 1))
+    extra = riders_ref[...] + in_columns(in_parts(along, 2) + in_parts(value, 2), 5)
+    extra = extra[:, :64]
     blank = jnp.zeros((48, 64), F32)
-    width = cot.shape[1] // 4
+    width = by_row.shape[1] // 4
+    ways = []
     for k in range(4):
-        part = cot[:, width * k : width * k + width]
-        way = jnp.concatenate([part[:48], extra, part[48:], blank], 1).astype(BF)
-        out_ref[48 * k : 48 * k + 48, :] = way
-        out_ref[192 + 48 * k : 240 + 48 * k, :] = way
-
-
-def back_kernel(got_ref, unit_ref, wa_ref, wb_ref, out_ref, loss_ref):
+        span = slice(width * k, width * k + width)
+        ways.append(jnp.concatenate([by_row[:, span], extra, by_item[:, span], blank], 1))
+    ways = [way[:24] for way in ways] + [way[24:] for way in ways]
+    out_ref[...] = jnp.concatenate(ways, 0).astype(BF)
+
+
+def back_kernel(got_ref, unit_ref, w_ref, out_ref, loss_ref):
     width = unit_ref.shape[1]
-    got = [got_ref[48 * k : 48 * k + 48, :].astype(F32) for k in range(8)]
+    every = got_ref[...].astype(F32)
+    got = [every[24 * k : 24 * k + 24] for k in range(8)]
     riders = [[part[:, width + k : width + k + 1] for k in range(9)] for part in got]
     parts = [r[0] + r[1] + r[2] for r in riders]
     largest = functools.reduce(jnp.maximum, parts)
     total = sum(jnp.exp(part - largest) for part in parts)
     lse = largest + jnp.log(total)
-    along = jnp.zeros((48, 1), F32)
-    value = jnp.zeros((48, 1), F32)
-    summed = jnp.zeros((48, width), F32)
+    along = jnp.zeros((24, 1), F32)
+    value = jnp.zeros((24, 1), F32)
+    summed = jnp.zeros((24, width), F32)
     for part, r, own in zip(got, riders, parts):
         weight = jnp.exp(own - lse)
         along += weight * (r[3] + r[4]) + (r[5] + r[6])
@@ -328,16 +363,25 @@
         summed += weight * part[:, :width] + part[:, width + 64 : 2 * width + 64]
     loss_ref[...] = jnp.broadcast_to(value[:8] / (2.0 * 1536), (8, 128))
     proj_cot = (summed - unit_ref[...].astype(F32) * along).astype(BF)
+    is_img = slab_row((24, 768)) < 13
     mixed = []
-    for ref in (wa_ref, wb_ref):
-        pool = lax.dot_general(proj_cot, ref[...], ROWS_DOT, preferred_element_type=F32)
-        is_img = lax.broadcasted_iota(jnp.int32, pool.shape, 1) % 24 < 13
-        mixed.append(jnp.where(is_img, pool, pltpu.roll(pool, 45, 0)))
-    blank = jnp.zeros((1, pool.shape[1]), F32)
+    for k in range(4):
+        pool = [
+            lax.dot_general(
+                proj_cot,
+                w_ref[256 * k : 256 * k + 256, width * j : width * j + width],
+                ROWS_DOT,
+                preferred_element_type=F32,
+            )
+            for j in range(3)
+        ]
+        pool = jnp.concatenate(pool, 1)
+        mixed.append(jnp.where(is_img, pool, pltpu.roll(pool, 21, 0)))
+    blank = jnp.zeros((1, 768), F32)
     pieces = []
-    for k in range(8):
+    for t in range(4):
         for pool in mixed:
-            pieces += [pool[6 * k : 6 * k + 3], blank]
+            pieces += [pool[6 * t : 6 * t + 3], blank]
     out_ref[...] = jnp.concatenate(pieces, 0).astype(BF)
 
 
@@ -352,14 +396,8 @@
         lane = lax.broadcasted_iota(jnp.int32, (768, 32 * wide), 0)
         pick = jnp.where(lane == slab_place(dense, wide, skip), 1.0, 0.0).astype(BF)
         found = jnp.dot(pool, pick, preferred_element_type=F32)
-        halves = [
-            found[32 * k : 32 * k + 8]
-            + found[32 * k + 8 : 32 * k + 16]
-            + found[32 * k + 16 : 32 * k + 24]
-            + found[32 * k + 24 : 32 * k + 32]
-            for k in range(2)
-        ]
-        cot = jnp.concatenate([halves[0][:4], halves[0][4:], halves[1][:4], halves[1][4:]], 1)
+        found = found[:16] + found[16:32] + found[32:48] + found[48:]
+        cot = jnp.concatenate([found[4 * k : 4 * k + 4] for k in range(4)], 1)
         cot = cot * inv[at : at + 4] * gain_ref[...][None]
         mean_cot = jnp.mean(cot, axis=1, keepdims=True)
         count = x_ref.shape[0] // 3
@@ -385,12 +423,13 @@
     width = emb // 4
     w = jnp.concatenate([proj_img, proj_txt, jnp.zeros((1, emb), BF)], 0)
     w = lax.dynamic_slice(w, (0, width * t_index), (24, width))
-    w = jnp.broadcast_to(w[None], (32, 24, width))
+    w = jnp.concatenate([w[:8], w[8:16], w[16:]], 1)
+    w = jnp.broadcast_to(w[None], (32, 8, 3 * width))
     wa, wb = both_cores(exchange(w, ZX))
 
     pooled = pool_call(image_in, text_in, img_gain, txt_gain, positive)
     pooled = lax.all_gather(pooled, Y, axis=0, axis_index_groups=[[0, 6], [1, 7], [2, 4], [3, 5]])
-    row_pos = pooled[:, :12, 23].astype(F32) * 32.0 + pooled[:, :12, 47].astype(F32)
+    row_pos = pooled[:, :12, 519].astype(F32) * 32.0 + pooled[:, :12, 527].astype(F32)
     row_pos = jnp.pad(row_pos.reshape(8, 3), ((0, 0), (0, 3)), constant_values=-1.0)
     row_pos = row_pos.reshape(48, 1).astype(jnp.int32)
 
@@ -412,6 +451,8 @@
         scratch=[pltpu.VMEM((64, emb), F32), pltpu.VMEM((64, 128), F32)],
         smem=(0,),
     )
+    w_mine, far = lax.optimization_barrier((jnp.concatenate([wa, wb], 0), far))
+    w_all = lax.all_gather(w_mine, "h", axis=0, tiled=True)
     fa, fb = both_cores(exchange(far.reshape(32, 8, 1024), ZX))
 
     scores, far = kernel_call(
@@ -427,19 +468,25 @@
     item_pos = item_pos[:, :3] * 32.0 + item_pos[:, 3:]
     item_pos = jnp.pad(item_pos, ((0, 0), (0, 5)), constant_values=-1.0).reshape(1, 512)
     item_pos = item_pos.astype(jnp.int32)
+    by_row, riders = kernel_call(
+        row_kernel,
+        [((48, emb), F32), ((48, 128), F32)],
+        [place, logit_scale, scores, fa, fb],
+        smem=(0, 1),
+    )
     (ways,) = kernel_call(
         coef_kernel,
-        [((384, 768), BF)],
-        [place, logit_scale, scores, far, row_pos, item_pos, fa, fb],
+        [((192, 768), BF)],
+        [place, logit_scale, scores, far, row_pos, item_pos, fa, fb, by_row, riders],
         smem=(0, 1),
     )
-    got = exchange(ways.reshape(8, 48, 768), Y).reshape(384, 768)
-    unit_part = lax.dynamic_slice(rows, (0, width * t_index), (48, width))
+    got = exchange(ways.reshape(8, 24, 768), Y).reshape(192, 768)
+    unit_part = lax.dynamic_slice(rows, (24 * h_index, width * t_index), (24, width))
     pool, loss = kernel_call(
-        back_kernel, [((64, 768), BF), ((8, 128), F32)], [got, unit_part, wa, wb]
+        back_kernel, [((64, 768), BF), ((8, 128), F32)], [got, unit_part, w_all]
     )
     mean_loss = loss[0, :1]
-    pool = exchange(pool.reshape(8, 8, 768), Y).reshape(64, 768)
+    pool = exchange(pool.reshape(4, 16, 768), "t").reshape(64, 768)
     count_i, width_i = image_in.shape[1:]
     count_t, width_t = text_in.shape[1:]
     img_own = lax.dynamic_slice_in_dim(image_in, 3 * t_index, 3, 0).reshape(-1, width_i)

time: 148 us -> 169 us (1.14)
  between operations: 1.43 us -> 14.8 us
  waiting for transfers between devices: 60.1 us -> 62 us
    all_gather x0 -> x1, waiting for transfers between devices: none -> 9.23 us  [per_device(): w_all = lax.all_gather(w_mine, 'h', axis=0, tiled=True)]
    all_to_all x6, waiting for transfers between devices: 60.1 us -> 52.7 us  [exchange(): return lax.all_to_all(blocks, axes, 0, 0, tiled=True)]
    pallas_call x6 -> x7, Pallas kernels: 11 us -> 12.3 us  [kernel_call(): pl.pallas_call(body, out_shape=[jax.ShapeDtypeStruct(shape, kind) for sha...]
  transfers between devices with their start and end apart: 6 -> 7, of which waited for: 6 -> 6; matrix products, arithmetic and copies ran while one was open for 3% -> 3% of each run, Pallas kernels for 5% -> 7%
where the time goes in v9:
time: 169 us; the launch traced here: 168 us
  waiting for transfers between devices  62 us (37%)
  starting transfers between devices  39.8 us (24%)
  blocking collectives  23.5 us (14%)
  Pallas kernels  19.4 us (11%)
  between operations  14.8 us (9%)
  local copies, waits for them, and re-layouts  6.25 us (4%)
  other arithmetic  2.34 us (1%)
    all_to_all x6, waiting for transfers between devices, exchange(): return lax.all_to_all(blocks, axes, 0, 0, tiled=True)  52.7 us
    all_to_all x6, starting transfers between devices, exchange(): return lax.all_to_all(blocks, axes, 0, 0, tiled=True)  39.7 us
    all_gather x4, blocking collectives, both_cores(): lax.all_gather(part, 'c', axis=0)  14.5 us
    pallas_call x7, Pallas kernels, kernel_call(): pl.pallas_call(body, out_shape=[jax.ShapeDtypeStruct(shape, kind) for sha...  12.3 us
    all_gather x1, waiting for transfers between devices, per_device(): w_all = lax.all_gather(w_mine, 'h', axis=0, tiled=True)  9.23 us
    all_gather x1, blocking collectives, per_device(): lax.all_gather(pooled, Y, axis=0, axis_index_groups=[[0, 6], [1, 7], [2,...  9.03 us
    pallas_call x1, Pallas kernels, pool_call(): pl.pallas_call(pool_kernel, out_shape=jax.ShapeDtypeStruct((64, 768), BF)...  7.15 us
  transfers between devices with their start and end apart: 7, of which 6 were waited for; matrix products, arithmetic and copies ran while one was open for 3% of the time, Pallas kernels for 7%

profile of v9, /device:TPU:1, one launch (start us, length us, event | category | flops | bytes accessed | tf_op | source)
XLA Modules:
  0.0 168.2 jit_solution(10062148269983346942)
XLA Ops:
  9.0 13.7 %all-to-all-start = ((bf16[32,8,960]{2,1,0:T(8,128)(2,1)}), bf16[32,8,960]{2,1,0:T(8,128)(2,1)S(1)}, u32[]{:S(2)}, u32[]{:S(2)}) async-start(bf16[32,8,960]{2,1,0:T(8,128)(2,1)} %broadcast_in_dim.13), calls=%async_computation | async-start | bytes 1048576 | tf_op jit(solution)/shard_map/all_to_all | solution.py:21
  22.8 7.2 %shard_map.103 = bf16[64,768]{1,0:T(8,128)(2,1)} custom-call(s32[12]{0:T(128)} %pos_ref.1, bf16[12,48,1664]{2,1,0:T(8,128)(2,1)} %img_ref.1, bf16[12,64,1280]{2,1,0:T(8,128)(2,1)} %txt_ref.1, f32[1664]{0:T(1024)} %ig_ref.3, f32[1280]{0:T(1024)} %tg_ref.3), custom_call_target="tpu_custom_call" | custom-call | flops 19415040 | bytes 3883008 | tf_op jit(solution)/shard_map/pallas_call | solution.py:108
  29.9 9.0 %all-gather.pooled_ref = bf16[128,768]{1,0:T(8,128)(2,1)S(1)} all-gather(bf16[64,768]{1,0:T(8,128)(2,1)} %shard_map.103), channel_id=2, replica_groups={{0,320},{128,448},{256,64},{384,192},{1,321},{129,449},{257,65},{385,19..., dimensions={0}, use_global_device_ids=true | all-gather | bytes 294912 | tf_op jit(solution)/shard_map/all_gather | solution.py:431
  39.2 4.1 %all-gather.1 = bf16[32,8,960]{2,1,0:T(8,128)(2,1)S(1)} all-gather(bf16[16,8,960]{2,1,0:T(8,128)(2,1)S(1)} %get-tuple-element.34), channel_id=3, replica_groups=mesh['t'=4,'h'=2,'z'=8,'x'=4,'c'=2] {'c'}, dimensions={0}, use_global_device_ids=true | all-gather | bytes 737280 | tf_op jit(solution)/shard_map/all_gather | solution.py:26
  43.3 2.2 %all-gather.2 = bf16[32,8,960]{2,1,0:T(8,128)(2,1)S(1)} all-gather(bf16[16,8,960]{2,1,0:T(8,128)(2,1)S(1)} %get-tuple-element.33), channel_id=4, replica_groups=mesh['t'=4,'h'=2,'z'=8,'x'=4,'c'=2] {'c'}, dimensions={0}, use_global_device_ids=true | all-gather | bytes 737280 | tf_op jit(solution)/shard_map/all_gather | solution.py:26
  45.4 1.7 shard_map.104
  47.1 6.8 %all-to-all-start.1 = ((bf16[8,24,640]{2,1,0:T(8,128)(2,1)}), bf16[8,24,640]{2,1,0:T(8,128)(2,1)S(1)}, u32[]{:S(2)}, u32[]{:S(2)}) async-start(bf16[8,24,640]{2,1,0:T(8,128)(2,1)} %bitcast.6), calls=%async_computation.1 | async-start | bytes 491520 | tf_op jit(solution)/shard_map/all_to_all | solution.py:21
  55.1 9.3 %all-to-all-done.1 = bf16[8,24,640]{2,1,0:T(8,128)(2,1)S(1)} async-done(((bf16[8,24,640]{2,1,0:T(8,128)(2,1)}), bf16[8,24,640]{2,1,0:T(8,128)(2,1)S(1)}, u32[]{:S(2)}, u32[]{:S(2)}) %all-to-all-start.1) | async-done | bytes 245792 | tf_op jit(solution)/shard_map/all_to_all | solution.py:21
  64.5 1.7 shard_map.105
  66.1 7.4 %all-to-all-start.2 = ((bf16[32,8,1024]{2,1,0:T(8,128)(2,1)}), bf16[32,8,1024]{2,1,0:T(8,128)(2,1)S(1)}, u32[]{:S(2)}, u32[]{:S(2)}) async-start(bf16[32,8,1024]{2,1,0:T(8,128)(2,1)} %bitcast.9), calls=%async_computation.2 | async-start | bytes 1048576 | tf_op jit(solution)/shard_map/all_to_all | solution.py:21
  74.8 13.4 %all-to-all-done.2 = bf16[32,8,1024]{2,1,0:T(8,128)(2,1)S(1)} async-done(((bf16[32,8,1024]{2,1,0:T(8,128)(2,1)}), bf16[32,8,1024]{2,1,0:T(8,128)(2,1)S(1)}, u32[]{:S(2)}, u32[]{:S(2)}) %all-to-all-start.2) | async-done | bytes 524320 | tf_op jit(solution)/shard_map/all_to_all | solution.py:21
  88.2 6.1 %all-gather.4 = bf16[32,8,1024]{2,1,0:T(8,128)(2,1)S(1)} all-gather(bf16[16,8,1024]{2,1,0:T(8,128)(2,1)S(1)} %get-tuple-element.31), channel_id=6, replica_groups=mesh['t'=4,'h'=2,'z'=8,'x'=4,'c'=2] {'c'}, dimensions={0}, use_global_device_ids=true | all-gather | bytes 786432 | tf_op jit(solution)/shard_map/all_gather | solution.py:26
  94.3 2.2 %all-gather.3 = bf16[32,8,1024]{2,1,0:T(8,128)(2,1)S(1)} all-gather(bf16[16,8,1024]{2,1,0:T(8,128)(2,1)S(1)} %get-tuple-element.32), channel_id=5, replica_groups=mesh['t'=4,'h'=2,'z'=8,'x'=4,'c'=2] {'c'}, dimensions={0}, use_global_device_ids=true | all-gather | bytes 786432 | tf_op jit(solution)/shard_map/all_gather | solution.py:26
  96.5 2.1 %shard_map.106 = (f32[48,512]{1,0:T(8,128)S(1)}, f32[256,128]{1,0:T(8,128)}) custom-call(s32[4]{0:T(128)S(1)} %pad_add_fusion.place_ref, f32[1]{0:T(128)S(6)} %copy.37.logit_ref, bf16[48,1280]{1,0:T(8,128)(2,1)S(1)} %get-tuple-element.16.rows_ref, bf16[256,1024]{1,0:T(8,128)(2,1)S(1)} %bitcast.33, bf16[256,1024]{1,0:T(8,128)(2,1)S(1)} %bitcast.30, ...), custom_call_target="tpu_custom_call" | custom-call | tf_op jit(solution)/shard_map/pallas_call | solution.py:32
  98.6 5.1 %all-to-all-start.3 = ((f32[64,4,128]{2,1,0:T(4,128)}), f32[64,4,128]{2,1,0:T(4,128)S(1)}, u32[]{:S(2)}, u32[]{:S(2)}) async-start(f32[64,4,128]{2,1,0:T(4,128)} %bitcast.13), calls=%async_computation.3 | async-start | bytes 262144 | tf_op jit(solution)/shard_map/all_to_all | solution.py:21
  105.3 9.5 %all-to-all-done.3 = f32[64,4,128]{2,1,0:T(4,128)S(1)} async-done(((f32[64,4,128]{2,1,0:T(4,128)}), f32[64,4,128]{2,1,0:T(4,128)S(1)}, u32[]{:S(2)}, u32[]{:S(2)}) %all-to-all-start.3) | async-done | bytes 131104 | tf_op jit(solution)/shard_map/all_to_all | solution.py:21
  114.8 1.9 %shard_map.108 = bf16[192,768]{1,0:T(8,128)(2,1)} custom-call(s32[4]{0:T(128)S(1)} %pad_add_fusion.place_ref, f32[1]{0:T(128)S(6)} %copy.37.logit_ref, f32[48,512]{1,0:T(8,128)S(1)} %get-tuple-element.19.scores_ref, f32[256,128]{1,0:T(8,128)S(1)} %bitcast.45, s32[48,1]{1,0:T(8,128)S(1)} %convert_element_type.36.row_pos_ref, ...), custom_call_target="tpu_custom_call" | custom-call | tf_op jit(solution)/shard_map/pallas_call | solution.py:32
  116.7 3.4 %all-to-all-start.4 = ((bf16[8,24,768]{2,1,0:T(8,128)(2,1)}), bf16[8,24,768]{2,1,0:T(8,128)(2,1)S(1)}, u32[]{:S(2)}, u32[]{:S(2)}) async-start(bf16[8,24,768]{2,1,0:T(8,128)(2,1)} %bitcast.17), calls=%async_computation.4 | async-start | bytes 589824 | tf_op jit(solution)/shard_map/all_to_all | solution.py:21
  121.3 17.5 %all-to-all-done.4 = bf16[8,24,768]{2,1,0:T(8,128)(2,1)S(1)} async-done(((bf16[8,24,768]{2,1,0:T(8,128)(2,1)}), bf16[8,24,768]{2,1,0:T(8,128)(2,1)S(1)}, u32[]{:S(2)}, u32[]{:S(2)}) %all-to-all-start.4) | async-done | bytes 294944 | tf_op jit(solution)/shard_map/all_to_all | solution.py:21
  138.8 9.2 %all-gather.7.cloned.1.call-done.w_ref = bf16[1024,960]{1,0:T(8,128)(2,1)} async-done(((bf16[512,960]{1,0:T(8,128)(2,1)}), bf16[1024,960]{1,0:T(8,128)(2,1)}) %all-gather.7.cloned.1.call-update) | async-done | bytes 1966096 | tf_op jit(solution)/shard_map/all_gather | solution.py:455
  149.6 1.7 %shard_map.109 = (bf16[64,768]{1,0:T(8,128)(2,1)}, f32[8,128]{1,0:T(8,128)S(1)}) custom-call(bf16[192,768]{1,0:T(8,128)(2,1)S(1)} %bitcast.42, bf16[24,320]{1,0:T(8,128)(2,1)S(1)} %dynamic_slice.17.unit_ref, bf16[1024,960]{1,0:T(8,128)(2,1)S(1)} %copy-done), custom_call_target="tpu_custom_call" | custom-call | tf_op jit(solution)/shard_map/pallas_call | solution.py:32
  151.3 3.3 %all-to-all-start.5 = ((bf16[4,16,768]{2,1,0:T(8,128)(2,1)}), bf16[4,16,768]{2,1,0:T(8,128)(2,1)S(1)}, u32[]{:S(2)}, u32[]{:S(2)}) async-start(bf16[4,16,768]{2,1,0:T(8,128)(2,1)} %bitcast.20), calls=%async_computation.5 | async-start | bytes 196608 | tf_op jit(solution)/shard_map/all_to_all | solution.py:21
  156.2 3.1 %all-to-all-done.5 = bf16[4,16,768]{2,1,0:T(8,128)(2,1)S(1)} async-done(((bf16[4,16,768]{2,1,0:T(8,128)(2,1)}), bf16[4,16,768]{2,1,0:T(8,128)(2,1)S(1)}, u32[]{:S(2)}, u32[]{:S(2)}) %all-to-all-start.5) | async-done | bytes 98336 | tf_op jit(solution)/shard_map/all_to_all | solution.py:21
  159.3 2.0 %shard_map.110 = (bf16[144,1664]{1,0:T(8,128)(2,1)}, bf16[192,1280]{1,0:T(8,128)(2,1)}) custom-call(bf16[64,768]{1,0:T(8,128)(2,1)S(1)} %bitcast.46, f32[8,128]{1,0:T(8,128)S(1)} %get-tuple-element.26.inv_ref, bf16[144,1664]{1,0:T(8,128)(2,1)S(1)} %bitcast.41, bf16[192,1280]{1,0:T(8,128)(2,1)S(1)} %bitcast.40, f32[1664]{0:T(1024)S(1)} %copy-done.1, ...), custom_call_target="tpu_custom_call" | custom-call | tf_op jit(solution)/shard_map/pallas_call | solution.py:32
  (45 shorter events, 9.8 us)
Async XLA Ops:
  9.0 30.1 %all-to-all-start = ((bf16[32,8,960]{2,1,0:T(8,128)(2,1)}), bf16[32,8,960]{2,1,0:T(8,128)(2,1)S(1)}, u32[]{:S(2)}, u32[]{:S(2)}) async-start(bf16[32,8,960]{2,1,0:T(8,128)(2,1)} %broadcast_in_dim.13), calls=%async_computation | async-start | bytes 1048576 | tf_op jit(solution)/shard_map/all_to_all | solution.py:21
  22.8 16.3 %copy-start.3 = (s32[12]{0:T(128)S(1)}, s32[12]{0:T(128)}, u32[]{:S(2)}) copy-start(s32[12]{0:T(128)} %pos_ref.1) | copy-start | bytes 148
  47.1 17.3 %all-to-all-start.1 = ((bf16[8,24,640]{2,1,0:T(8,128)(2,1)}), bf16[8,24,640]{2,1,0:T(8,128)(2,1)S(1)}, u32[]{:S(2)}, u32[]{:S(2)}) async-start(bf16[8,24,640]{2,1,0:T(8,128)(2,1)} %bitcast.6), calls=%async_computation.1 | async-start | bytes 491520 | tf_op jit(solution)/shard_map/all_to_all | solution.py:21
  66.1 22.0 %all-to-all-start.2 = ((bf16[32,8,1024]{2,1,0:T(8,128)(2,1)}), bf16[32,8,1024]{2,1,0:T(8,128)(2,1)S(1)}, u32[]{:S(2)}, u32[]{:S(2)}) async-start(bf16[32,8,1024]{2,1,0:T(8,128)(2,1)} %bitcast.9), calls=%async_computation.2 | async-start | bytes 1048576 | tf_op jit(solution)/shard_map/all_to_all | solution.py:21
  73.6 74.5 %all-gather.7.cloned.1.call-start = ((), (), s32[]{:S(2)}) async-start(), calls=%async_computation.6 | async-start | bytes 3145728 | tf_op jit(solution)/shard_map/all_gather | solution.py:455
  98.6 16.2 %all-to-all-start.3 = ((f32[64,4,128]{2,1,0:T(4,128)}), f32[64,4,128]{2,1,0:T(4,128)S(1)}, u32[]{:S(2)}, u32[]{:S(2)}) async-start(f32[64,4,128]{2,1,0:T(4,128)} %bitcast.13), calls=%async_computation.3 | async-start | bytes 262144 | tf_op jit(solution)/shard_map/all_to_all | solution.py:21
  116.7 22.1 %all-to-all-start.4 = ((bf16[8,24,768]{2,1,0:T(8,128)(2,1)}), bf16[8,24,768]{2,1,0:T(8,128)(2,1)S(1)}, u32[]{:S(2)}, u32[]{:S(2)}) async-start(bf16[8,24,768]{2,1,0:T(8,128)(2,1)} %bitcast.17), calls=%async_computation.4 | async-start | bytes 589824 | tf_op jit(solution)/shard_map/all_to_all | solution.py:21
  120.1 39.2 %copy-start.1 = (f32[1664]{0:T(1024)S(1)}, f32[1664]{0:T(1024)}, u32[]{:S(2)}) copy-start(f32[1664]{0:T(1024)} %ig_ref.3) | copy-start | bytes 19972
  120.1 39.1 %copy-start.2 = (f32[1280]{0:T(1024)S(1)}, f32[1280]{0:T(1024)}, u32[]{:S(2)}) copy-start(f32[1280]{0:T(1024)} %tg_ref.3) | copy-start | bytes 15364
  148.0 1.6 copy-start
  151.3 8.0 %all-to-all-start.5 = ((bf16[4,16,768]{2,1,0:T(8,128)(2,1)}), bf16[4,16,768]{2,1,0:T(8,128)(2,1)S(1)}, u32[]{:S(2)}, u32[]{:S(2)}) async-start(bf16[4,16,768]{2,1,0:T(8,128)(2,1)} %bitcast.20), calls=%async_computation.5 | async-start | bytes 196608 | tf_op jit(solution)/shard_map/all_to_all | solution.py:21
Sparse Core Ops, SparseCore 0:
  76.5 71.4 all-gather.6

commit v10 on v9

--- a/solution.py
+++ b/solution.py
@@ -52,7 +52,19 @@
 
 
 def pool_kernel(
-    pos_ref, img_ref, txt_ref, ig_ref, tg_ref, out_ref, img_held, txt_held, img_rows, txt_rows, digits, sems
+    pos_ref,
+    img_ref,
+    txt_ref,
+    ig_ref,
+    tg_ref,
+    w_ref,
+    out_ref,
+    img_held,
+    txt_held,
+    img_rows,
+    txt_rows,
+    digits,
+    sems,
 ):
     pairs = img_ref.shape[0]
 
@@ -98,20 +110,22 @@
     blank = jnp.zeros_like(line)
     line = jnp.concatenate([line, blank, line, blank], 0)
     found = jnp.concatenate([found[:, :512], found[:, 512:640] + line, found[:, 640:]], 1)
-    out_ref[...] = found.astype(BF)
-
-
-def pool_call(image_in, text_in, img_gain, txt_gain, positive):
+    out_ref[:64, :] = found.astype(BF)
+    out_ref[64:, :] = w_ref[...]
+
+
+def pool_call(image_in, text_in, img_gain, txt_gain, positive, w_theirs):
     pairs, count_i, width_i = image_in.shape
     _, count_t, width_t = text_in.shape
     vmem = pl.BlockSpec(memory_space=pltpu.VMEM)
     return pl.pallas_call(
         pool_kernel,
-        out_shape=jax.ShapeDtypeStruct((64, 768), BF),
+        out_shape=jax.ShapeDtypeStruct((80, 768), BF),
         in_specs=[
             pl.BlockSpec(memory_space=pltpu.SMEM),
             pl.BlockSpec(memory_space=pl.ANY),
             pl.BlockSpec(memory_space=pl.ANY),
+            vmem,
             vmem,
             vmem,
         ],
@@ -130,7 +144,7 @@
             transcendentals=0,
         ),
         compiler_params=pltpu.CompilerParams(vmem_limit_bytes=60 * 1024 * 1024),
-    )(positive, image_in, text_in, img_gain, txt_gain)
+    )(positive, image_in, text_in, img_gain, txt_gain, w_theirs)
 
 
 def project_kernel(place_ref, pooled_ref, wa_ref, wb_ref, out_ref):
@@ -140,7 +154,7 @@
     for a, w_ref in enumerate((wa_ref, wb_ref)):
         pieces = []
         for h in range(2):
-            start = pl.multiple_of(64 * h + 32 * place_ref[1] + 16 * a, 16)
+            start = pl.multiple_of(80 * h + 32 * place_ref[1] + 16 * a, 16)
             rows = pooled_ref[pl.ds(start, 16), :].astype(F32)[:12]
             img_rows = jnp.where(inside < 13, rows, 0.0)
             txt_rows = jnp.where((inside >= 13) & (inside < 23), rows, 0.0)
@@ -344,7 +358,7 @@
     out_ref[...] = jnp.concatenate(ways, 0).astype(BF)
 
 
-def back_kernel(got_ref, unit_ref, w_ref, out_ref, loss_ref):
+def back_kernel(place_ref, got_ref, unit_ref, wa_ref, wb_ref, wo_ref, out_ref, loss_ref):
     width = unit_ref.shape[1]
     every = got_ref[...].astype(F32)
     got = [every[24 * k : 24 * k + 24] for k in range(8)]
@@ -364,19 +378,27 @@
     loss_ref[...] = jnp.broadcast_to(value[:8] / (2.0 * 1536), (8, 128))
     proj_cot = (summed - unit_ref[...].astype(F32) * along).astype(BF)
     is_img = slab_row((24, 768)) < 13
-    mixed = []
-    for k in range(4):
+
+    def features(w):
         pool = [
             lax.dot_general(
                 proj_cot,
-                w_ref[256 * k : 256 * k + 256, width * j : width * j + width],
+                w[:, width * j : width * j + width],
                 ROWS_DOT,
                 preferred_element_type=F32,
             )
             for j in range(3)
         ]
         pool = jnp.concatenate(pool, 1)
-        mixed.append(jnp.where(is_img, pool, pltpu.roll(pool, 21, 0)))
+        return jnp.where(is_img, pool, pltpu.roll(pool, 21, 0))
+
+    own = [features(wa_ref[...]), features(wb_ref[...])]
+    other = []
+    for a in range(2):
+        parts = [wo_ref[k + 128 * a : k + 128 * a + 128, :] for k in (0, 256)]
+        other.append(features(jnp.concatenate(parts, 0)))
+    first = place_ref[1] == 0
+    mixed = [jnp.where(first, x, y) for x, y in zip(own + other, other + own)]
     blank = jnp.zeros((1, 768), F32)
     pieces = []
     for t in range(4):
@@ -422,12 +444,19 @@
 
     width = emb // 4
     w = jnp.concatenate([proj_img, proj_txt, jnp.zeros((1, emb), BF)], 0)
-    w = lax.dynamic_slice(w, (0, width * t_index), (24, width))
-    w = jnp.concatenate([w[:8], w[8:16], w[16:]], 1)
-    w = jnp.broadcast_to(w[None], (32, 8, 3 * width))
-    wa, wb = both_cores(exchange(w, ZX))
-
-    pooled = pool_call(image_in, text_in, img_gain, txt_gain, positive)
+
+    def columns_of(tower):
+        part = lax.dynamic_slice(w, (0, width * tower), (24, width))
+        return jnp.concatenate([part[:8], part[8:16], part[16:]], 1)
+
+    w_sent = jnp.broadcast_to(columns_of(t_index)[None], (32, 8, 3 * width))
+    wa, wb = both_cores(exchange(w_sent, ZX))
+
+    w_theirs = columns_of((t_index + 2) % 4)
+    w_theirs = jnp.concatenate(
+        [w_theirs[:, :768], jnp.pad(w_theirs[:, 768:], ((0, 0), (0, 1536 - 3 * width)))], 0
+    )
+    pooled = pool_call(image_in, text_in, img_gain, txt_gain, positive, w_theirs)
     pooled = lax.all_gather(pooled, Y, axis=0, axis_index_groups=[[0, 6], [1, 7], [2, 4], [3, 5]])
     row_pos = pooled[:, :12, 519].astype(F32) * 32.0 + pooled[:, :12, 527].astype(F32)
     row_pos = jnp.pad(row_pos.reshape(8, 3), ((0, 0), (0, 3)), constant_values=-1.0)
@@ -436,7 +465,7 @@
     (part,) = kernel_call(
         project_kernel,
         [((192, 2 * width), BF)],
-        [place, pooled.reshape(128, 768), wa, wb],
+        [place, pooled.reshape(160, 768), wa, wb],
         smem=(0,),
     )
     parts = exchange(part.reshape(8, 24, 2 * width), Y).reshape(192, 2 * width)
@@ -451,8 +480,9 @@
         scratch=[pltpu.VMEM((64, emb), F32), pltpu.VMEM((64, 128), F32)],
         smem=(0,),
     )
-    w_mine, far = lax.optimization_barrier((jnp.concatenate([wa, wb], 0), far))
-    w_all = lax.all_gather(w_mine, "h", axis=0, tiled=True)
+    w_other = lax.dynamic_slice(pooled, (1 - h_index, 64, 0), (1, 16, 768))[0]
+    w_other = jnp.concatenate([w_other[:8], w_other[8:, : 3 * width - 768]], 1)
+    w_other = lax.all_gather(w_other, ("c", "z", "x"), axis=0, tiled=True)
     fa, fb = both_cores(exchange(far.reshape(32, 8, 1024), ZX))
 
     scores, far = kernel_call(
@@ -483,7 +513,7 @@
     got = exchange(ways.reshape(8, 24, 768), Y).reshape(192, 768)
     unit_part = lax.dynamic_slice(rows, (24 * h_index, width * t_index), (24, width))
     pool, loss = kernel_call(
-        back_kernel, [((64, 768), BF), ((8, 128), F32)], [got, unit_part, w_all]
+        back_kernel, [((64, 768), BF), ((8, 128), F32)], [place, got, unit_part, wa, wb, w_other], smem=(0,)
     )
     mean_loss = loss[0, :1]
     pool = exchange(pool.reshape(4, 16, 768), "t").reshape(64, 768)

time: 169 us -> 269 us (1.59)
  the two profiles are of different devices: /device:TPU:1 before, /device:TPU:256 now
where the time goes in v10:
time: 269 us; the launch traced here: 268 us
  blocking collectives  163 us (61%)
  starting transfers between devices  43.7 us (16%)
  waiting for transfers between devices  32.8 us (12%)
  Pallas kernels  20 us (7%)
  local copies, waits for them, and re-layouts  4.54 us (2%)
    all_gather x1, blocking collectives, per_device(): w_other = lax.all_gather(w_other, ('c', 'z', 'x'), axis=0, tiled=True)  144 us
    all_to_all x6, starting transfers between devices, exchange(): return lax.all_to_all(blocks, axes, 0, 0, tiled=True)  43.7 us
    all_to_all x6, waiting for transfers between devices, exchange(): return lax.all_to_all(blocks, axes, 0, 0, tiled=True)  32.8 us
    pallas_call x7, Pallas kernels, kernel_call(): pl.pallas_call(body, out_shape=[jax.ShapeDtypeStruct(shape, kind) for sha...  12.9 us
    all_gather x1, blocking collectives, per_device(): lax.all_gather(pooled, Y, axis=0, axis_index_groups=[[0, 6], [1, 7], [2,...  9.79 us
    all_gather x4, blocking collectives, both_cores(): lax.all_gather(part, 'c', axis=0)  8.7 us
    pallas_call x1, Pallas kernels, pool_call(): pl.pallas_call(pool_kernel, out_shape=jax.ShapeDtypeStruct((80, 768), BF)...  7.16 us
  transfers between devices with their start and end apart: 6, of which 4 were waited for; matrix products, arithmetic and copies ran while one was open for 2% of the time, Pallas kernels for 3%

profile of v10, /device:TPU:256, one launch (start us, length us, event | category | flops | bytes accessed | tf_op | source)
XLA Modules:
  0.0 267.6 jit_solution(11259714298321977768)
XLA Ops:
  2.7 9.9 %all-to-all-start = ((bf16[32,8,960]{2,1,0:T(8,128)(2,1)}), bf16[32,8,960]{2,1,0:T(8,128)(2,1)S(1)}, u32[]{:S(2)}, u32[]{:S(2)}) async-start(bf16[32,8,960]{2,1,0:T(8,128)(2,1)} %broadcast_in_dim.13), calls=%async_computation | async-start | bytes 1048576 | tf_op jit(solution)/shard_map/all_to_all | solution.py:21
  13.3 7.2 %shard_map.103 = bf16[80,768]{1,0:T(8,128)(2,1)} custom-call(s32[12]{0:T(128)} %pos_ref.1, bf16[12,48,1664]{2,1,0:T(8,128)(2,1)} %img_ref.1, bf16[12,64,1280]{2,1,0:T(8,128)(2,1)} %txt_ref.1, f32[1664]{0:T(1024)} %ig_ref.3, f32[1280]{0:T(1024)} %tg_ref.3, bf16[16,768]{1,0:T(8,128)(2,1)} %fusion.1.w_ref), custom_call_target="tpu_custom_call" | custom-call | flops 19415040 | bytes 3883008 | tf_op jit(solution)/shard_map/pallas_call | solution.py:121
  20.5 9.8 %all-gather.pooled_ref = bf16[160,768]{1,0:T(8,128)(2,1)S(1)} all-gather(bf16[80,768]{1,0:T(8,128)(2,1)} %shard_map.103), channel_id=2, replica_groups={{0,320},{128,448},{256,64},{384,192},{1,321},{129,449},{257,65},{385,19..., dimensions={0}, use_global_device_ids=true | all-gather | bytes 368640 | tf_op jit(solution)/shard_map/all_gather | solution.py:460
  30.5 2.2 all-gather.1
  32.7 2.2 all-gather.2
  34.8 1.7 shard_map.104
  36.5 6.7 %all-to-all-start.1 = ((bf16[8,24,640]{2,1,0:T(8,128)(2,1)}), bf16[8,24,640]{2,1,0:T(8,128)(2,1)S(1)}, u32[]{:S(2)}, u32[]{:S(2)}) async-start(bf16[8,24,640]{2,1,0:T(8,128)(2,1)} %bitcast.6), calls=%async_computation.1 | async-start | bytes 491520 | tf_op jit(solution)/shard_map/all_to_all | solution.py:21
  43.3 11.7 %all-to-all-done.1 = bf16[8,24,640]{2,1,0:T(8,128)(2,1)S(1)} async-done(((bf16[8,24,640]{2,1,0:T(8,128)(2,1)}), bf16[8,24,640]{2,1,0:T(8,128)(2,1)S(1)}, u32[]{:S(2)}, u32[]{:S(2)}) %all-to-all-start.1) | async-done | bytes 245792 | tf_op jit(solution)/shard_map/all_to_all | solution.py:21
  55.0 1.7 shard_map.105
  56.7 9.8 %all-to-all-start.2 = ((bf16[32,8,1024]{2,1,0:T(8,128)(2,1)}), bf16[32,8,1024]{2,1,0:T(8,128)(2,1)S(1)}, u32[]{:S(2)}, u32[]{:S(2)}) async-start(bf16[32,8,1024]{2,1,0:T(8,128)(2,1)} %bitcast.9), calls=%async_computation.2 | async-start | bytes 1048576 | tf_op jit(solution)/shard_map/all_to_all | solution.py:21
  68.6 10.4 %all-to-all-done.2 = bf16[32,8,1024]{2,1,0:T(8,128)(2,1)S(1)} async-done(((bf16[32,8,1024]{2,1,0:T(8,128)(2,1)}), bf16[32,8,1024]{2,1,0:T(8,128)(2,1)S(1)}, u32[]{:S(2)}, u32[]{:S(2)}) %all-to-all-start.2) | async-done | bytes 524320 | tf_op jit(solution)/shard_map/all_to_all | solution.py:21
  79.0 2.2 all-gather.3
  81.2 2.2 all-gather.4
  83.4 2.1 shard_map.106
  85.6 1.2 shard_map.107
  87.0 9.1 %all-to-all-start.3 = ((f32[64,4,128]{2,1,0:T(4,128)}), f32[64,4,128]{2,1,0:T(4,128)S(1)}, u32[]{:S(2)}, u32[]{:S(2)}) async-start(f32[64,4,128]{2,1,0:T(4,128)} %bitcast.13), calls=%async_computation.3 | async-start | bytes 262144 | tf_op jit(solution)/shard_map/all_to_all | solution.py:21
  96.3 6.3 %all-to-all-done.3 = f32[64,4,128]{2,1,0:T(4,128)S(1)} async-done(((f32[64,4,128]{2,1,0:T(4,128)}), f32[64,4,128]{2,1,0:T(4,128)S(1)}, u32[]{:S(2)}, u32[]{:S(2)}) %all-to-all-start.3) | async-done | bytes 131104 | tf_op jit(solution)/shard_map/all_to_all | solution.py:21
  102.6 1.9 shard_map.108
  104.5 3.4 %all-to-all-start.4 = ((bf16[8,24,768]{2,1,0:T(8,128)(2,1)}), bf16[8,24,768]{2,1,0:T(8,128)(2,1)S(1)}, u32[]{:S(2)}, u32[]{:S(2)}) async-start(bf16[8,24,768]{2,1,0:T(8,128)(2,1)} %bitcast.17), calls=%async_computation.4 | async-start | bytes 589824 | tf_op jit(solution)/shard_map/all_to_all | solution.py:21
  108.0 144.4 %all_gather.43.wo_ref = bf16[512,960]{1,0:T(8,128)(2,1)S(1)} all-gather(bf16[8,960]{1,0:T(8,128)(2,1)S(1)} %pad_maximum_fusion.3), channel_id=1, replica_groups=mesh['t'=4,'h'=2,'z'=8,'x'=4,'c'=2] {'c','z','x'}, dimensions={0}, use_global_device_ids=true | all-gather | bytes 998400 | tf_op jit(solution)/shard_map/all_gather | solution.py:485
  252.5 2.3 shard_map.109
  254.8 5.0 %all-to-all-start.5 = ((bf16[4,16,768]{2,1,0:T(8,128)(2,1)}), bf16[4,16,768]{2,1,0:T(8,128)(2,1)S(1)}, u32[]{:S(2)}, u32[]{:S(2)}) async-start(bf16[4,16,768]{2,1,0:T(8,128)(2,1)} %bitcast.22), calls=%async_computation.5 | async-start | bytes 196608 | tf_op jit(solution)/shard_map/all_to_all | solution.py:21
  261.3 4.3 %all-to-all-done.5 = bf16[4,16,768]{2,1,0:T(8,128)(2,1)S(1)} async-done(((bf16[4,16,768]{2,1,0:T(8,128)(2,1)}), bf16[4,16,768]{2,1,0:T(8,128)(2,1)S(1)}, u32[]{:S(2)}, u32[]{:S(2)}) %all-to-all-start.5) | async-done | bytes 98336 | tf_op jit(solution)/shard_map/all_to_all | solution.py:21
  265.6 2.1 shard_map.110
  (43 shorter events, 6.7 us)
Async XLA Ops:
  2.7 27.8 %all-to-all-start = ((bf16[32,8,960]{2,1,0:T(8,128)(2,1)}), bf16[32,8,960]{2,1,0:T(8,128)(2,1)S(1)}, u32[]{:S(2)}, u32[]{:S(2)}) async-start(bf16[32,8,960]{2,1,0:T(8,128)(2,1)} %broadcast_in_dim.13), calls=%async_computation | async-start | bytes 1048576 | tf_op jit(solution)/shard_map/all_to_all | solution.py:21
  13.3 17.0 %copy-start.2 = (s32[12]{0:T(128)S(1)}, s32[12]{0:T(128)}, u32[]{:S(2)}) copy-start(s32[12]{0:T(128)} %pos_ref.1) | copy-start | bytes 148
  36.5 18.5 %all-to-all-start.1 = ((bf16[8,24,640]{2,1,0:T(8,128)(2,1)}), bf16[8,24,640]{2,1,0:T(8,128)(2,1)S(1)}, u32[]{:S(2)}, u32[]{:S(2)}) async-start(bf16[8,24,640]{2,1,0:T(8,128)(2,1)} %bitcast.6), calls=%async_computation.1 | async-start | bytes 491520 | tf_op jit(solution)/shard_map/all_to_all | solution.py:21
  56.7 22.3 %all-to-all-start.2 = ((bf16[32,8,1024]{2,1,0:T(8,128)(2,1)}), bf16[32,8,1024]{2,1,0:T(8,128)(2,1)S(1)}, u32[]{:S(2)}, u32[]{:S(2)}) async-start(bf16[32,8,1024]{2,1,0:T(8,128)(2,1)} %bitcast.9), calls=%async_computation.2 | async-start | bytes 1048576 | tf_op jit(solution)/shard_map/all_to_all | solution.py:21
  87.0 15.7 %all-to-all-start.3 = ((f32[64,4,128]{2,1,0:T(4,128)}), f32[64,4,128]{2,1,0:T(4,128)S(1)}, u32[]{:S(2)}, u32[]{:S(2)}) async-start(f32[64,4,128]{2,1,0:T(4,128)} %bitcast.13), calls=%async_computation.3 | async-start | bytes 262144 | tf_op jit(solution)/shard_map/all_to_all | solution.py:21
  104.5 148.0 %all-to-all-start.4 = ((bf16[8,24,768]{2,1,0:T(8,128)(2,1)}), bf16[8,24,768]{2,1,0:T(8,128)(2,1)S(1)}, u32[]{:S(2)}, u32[]{:S(2)}) async-start(bf16[8,24,768]{2,1,0:T(8,128)(2,1)} %bitcast.17), calls=%async_computation.4 | async-start | bytes 589824 | tf_op jit(solution)/shard_map/all_to_all | solution.py:21
  252.4 13.1 %copy-start = (f32[1664]{0:T(1024)S(1)}, f32[1664]{0:T(1024)}, u32[]{:S(2)}) copy-start(f32[1664]{0:T(1024)} %ig_ref.3) | copy-start | bytes 19972
  252.4 13.1 %copy-start.1 = (f32[1280]{0:T(1024)S(1)}, f32[1280]{0:T(1024)}, u32[]{:S(2)}) copy-start(f32[1280]{0:T(1024)} %tg_ref.3) | copy-start | bytes 15364
  254.8 10.8 %all-to-all-start.5 = ((bf16[4,16,768]{2,1,0:T(8,128)(2,1)}), bf16[4,16,768]{2,1,0:T(8,128)(2,1)S(1)}, u32[]{:S(2)}, u32[]{:S(2)}) async-start(bf16[4,16,768]{2,1,0:T(8,128)(2,1)} %bitcast.22), calls=%async_computation.5 | async-start | bytes 196608 | tf_op jit(solution)/shard_map/all_to_all | solution.py:21

commit v11 on v10

--- a/solution.py
+++ b/solution.py
@@ -395,8 +395,7 @@
     own = [features(wa_ref[...]), features(wb_ref[...])]
     other = []
     for a in range(2):
-        parts = [wo_ref[k + 128 * a : k + 128 * a + 128, :] for k in (0, 256)]
-        other.append(features(jnp.concatenate(parts, 0)))
+        other.append(features(wo_ref[256 * a : 256 * a + 256, :]))
     first = place_ref[1] == 0
     mixed = [jnp.where(first, x, y) for x, y in zip(own + other, other + own)]
     blank = jnp.zeros((1, 768), F32)
@@ -481,8 +480,9 @@
         smem=(0,),
     )
     w_other = lax.dynamic_slice(pooled, (1 - h_index, 64, 0), (1, 16, 768))[0]
-    w_other = jnp.concatenate([w_other[:8], w_other[8:, : 3 * width - 768]], 1)
-    w_other = lax.all_gather(w_other, ("c", "z", "x"), axis=0, tiled=True)
+    w_other = jnp.concatenate([w_other[:8], w_other[8:, :384]], 1)
+    w_other = lax.all_gather(w_other, ZXC, axis=0, tiled=True)
+    w_other = w_other.reshape(2, 16, 2, 8, 1152).transpose(0, 2, 1, 3, 4).reshape(512, 1152)
     fa, fb = both_cores(exchange(far.reshape(32, 8, 1024), ZX))
 
     scores, far = kernel_call(

time: 269 us -> 183 us (0.68)
  the two profiles are of different devices: /device:TPU:256 before, /device:TPU:1 now
where the time goes in v11:
time: 183 us; the launch traced here: 182 us
  waiting for transfers between devices  73.6 us (40%)
  starting transfers between devices  42.1 us (23%)
  blocking collectives  23.2 us (13%)
  Pallas kernels  20 us (11%)
  between operations  14.9 us (8%)
  local copies, waits for them, and re-layouts  5.91 us (3%)
  other arithmetic  2.75 us (2%)
    all_to_all x6, starting transfers between devices, exchange(): return lax.all_to_all(blocks, axes, 0, 0, tiled=True)  42.1 us
    all_to_all x6, waiting for transfers between devices, exchange(): return lax.all_to_all(blocks, axes, 0, 0, tiled=True)  37.4 us
    all_gather x1, waiting for transfers between devices, per_device(): w_other = lax.all_gather(w_other, ZXC, axis=0, tiled=True)  36.1 us
    pallas_call x7, Pallas kernels, kernel_call(): pl.pallas_call(body, out_shape=[jax.ShapeDtypeStruct(shape, kind) for sha...  12.9 us
    all_gather x4, blocking collectives, both_cores(): lax.all_gather(part, 'c', axis=0)  12.8 us
    all_gather x1, blocking collectives, per_device(): lax.all_gather(pooled, Y, axis=0, axis_index_groups=[[0, 6], [1, 7], [2,...  10.4 us
    pallas_call x1, Pallas kernels, pool_call(): pl.pallas_call(pool_kernel, out_shape=jax.ShapeDtypeStruct((80, 768), BF)...  7.16 us
  transfers between devices with their start and end apart: 7, of which 5 were waited for; matrix products, arithmetic and copies ran while one was open for 4% of the time, Pallas kernels for 7%

profile of v11, /device:TPU:1, one launch (start us, length us, event | category | flops | bytes accessed | tf_op | source)
XLA Modules:
  0.0 182.5 jit_solution(9529510504128943111)
XLA Ops:
  9.2 13.7 %all-to-all-start = ((bf16[32,8,960]{2,1,0:T(8,128)(2,1)}), bf16[32,8,960]{2,1,0:T(8,128)(2,1)S(1)}, u32[]{:S(2)}, u32[]{:S(2)}) async-start(bf16[32,8,960]{2,1,0:T(8,128)(2,1)} %broadcast_in_dim.13), calls=%async_computation | async-start | bytes 1048576 | tf_op jit(solution)/shard_map/all_to_all | solution.py:21
  23.7 7.2 %shard_map.103 = bf16[80,768]{1,0:T(8,128)(2,1)} custom-call(s32[12]{0:T(128)} %pos_ref.1, bf16[12,48,1664]{2,1,0:T(8,128)(2,1)} %img_ref.1, bf16[12,64,1280]{2,1,0:T(8,128)(2,1)} %txt_ref.1, f32[1664]{0:T(1024)} %ig_ref.3, f32[1280]{0:T(1024)} %tg_ref.3, bf16[16,768]{1,0:T(8,128)(2,1)} %fusion.1.w_ref), custom_call_target="tpu_custom_call" | custom-call | flops 19415040 | bytes 3883008 | tf_op jit(solution)/shard_map/pallas_call | solution.py:121
  30.9 10.4 %all-gather.pooled_ref = bf16[160,768]{1,0:T(8,128)(2,1)S(1)} all-gather(bf16[80,768]{1,0:T(8,128)(2,1)} %shard_map.103), channel_id=2, replica_groups={{0,320},{128,448},{256,64},{384,192},{1,321},{129,449},{257,65},{385,19..., dimensions={0}, use_global_device_ids=true | all-gather | bytes 368640 | tf_op jit(solution)/shard_map/all_gather | solution.py:459
  41.5 2.4 %all-gather.1 = bf16[32,8,960]{2,1,0:T(8,128)(2,1)S(1)} all-gather(bf16[16,8,960]{2,1,0:T(8,128)(2,1)S(1)} %get-tuple-element.30), channel_id=3, replica_groups=mesh['t'=4,'h'=2,'z'=8,'x'=4,'c'=2] {'c'}, dimensions={0}, use_global_device_ids=true | all-gather | bytes 737280 | tf_op jit(solution)/shard_map/all_gather | solution.py:26
  43.9 2.2 %all-gather.2 = bf16[32,8,960]{2,1,0:T(8,128)(2,1)S(1)} all-gather(bf16[16,8,960]{2,1,0:T(8,128)(2,1)S(1)} %get-tuple-element.29), channel_id=4, replica_groups=mesh['t'=4,'h'=2,'z'=8,'x'=4,'c'=2] {'c'}, dimensions={0}, use_global_device_ids=true | all-gather | bytes 737280 | tf_op jit(solution)/shard_map/all_gather | solution.py:26
  46.1 1.7 shard_map.104
  47.8 6.4 %all-to-all-start.1 = ((bf16[8,24,640]{2,1,0:T(8,128)(2,1)}), bf16[8,24,640]{2,1,0:T(8,128)(2,1)S(1)}, u32[]{:S(2)}, u32[]{:S(2)}) async-start(bf16[8,24,640]{2,1,0:T(8,128)(2,1)} %bitcast.6), calls=%async_computation.1 | async-start | bytes 491520 | tf_op jit(solution)/shard_map/all_to_all | solution.py:21
  54.3 10.4 %all-to-all-done.1 = bf16[8,24,640]{2,1,0:T(8,128)(2,1)S(1)} async-done(((bf16[8,24,640]{2,1,0:T(8,128)(2,1)}), bf16[8,24,640]{2,1,0:T(8,128)(2,1)S(1)}, u32[]{:S(2)}, u32[]{:S(2)}) %all-to-all-start.1) | async-done | bytes 245792 | tf_op jit(solution)/shard_map/all_to_all | solution.py:21
  64.7 1.7 shard_map.105
  66.4 9.2 %all-to-all-start.2 = ((bf16[32,8,1024]{2,1,0:T(8,128)(2,1)}), bf16[32,8,1024]{2,1,0:T(8,128)(2,1)S(1)}, u32[]{:S(2)}, u32[]{:S(2)}) async-start(bf16[32,8,1024]{2,1,0:T(8,128)(2,1)} %bitcast.9), calls=%async_computation.2 | async-start | bytes 1048576 | tf_op jit(solution)/shard_map/all_to_all | solution.py:21
  77.3 12.9 %all-to-all-done.2 = bf16[32,8,1024]{2,1,0:T(8,128)(2,1)S(1)} async-done(((bf16[32,8,1024]{2,1,0:T(8,128)(2,1)}), bf16[32,8,1024]{2,1,0:T(8,128)(2,1)S(1)}, u32[]{:S(2)}, u32[]{:S(2)}) %all-to-all-start.2) | async-done | bytes 524320 | tf_op jit(solution)/shard_map/all_to_all | solution.py:21
  90.2 6.1 %all-gather.3 = bf16[32,8,1024]{2,1,0:T(8,128)(2,1)S(1)} all-gather(bf16[16,8,1024]{2,1,0:T(8,128)(2,1)S(1)} %get-tuple-element.28), channel_id=5, replica_groups=mesh['t'=4,'h'=2,'z'=8,'x'=4,'c'=2] {'c'}, dimensions={0}, use_global_device_ids=true | all-gather | bytes 786432 | tf_op jit(solution)/shard_map/all_gather | solution.py:26
  96.3 2.2 %all-gather.4 = bf16[32,8,1024]{2,1,0:T(8,128)(2,1)S(1)} all-gather(bf16[16,8,1024]{2,1,0:T(8,128)(2,1)S(1)} %get-tuple-element.27), channel_id=6, replica_groups=mesh['t'=4,'h'=2,'z'=8,'x'=4,'c'=2] {'c'}, dimensions={0}, use_global_device_ids=true | all-gather | bytes 786432 | tf_op jit(solution)/shard_map/all_gather | solution.py:26
  98.5 2.1 %shard_map.106 = (f32[48,512]{1,0:T(8,128)S(1)}, f32[256,128]{1,0:T(8,128)}) custom-call(s32[4]{0:T(128)S(1)} %pad_add_fusion.place_ref, f32[1]{0:T(128)S(6)} %copy.33.logit_ref, bf16[48,1280]{1,0:T(8,128)(2,1)S(1)} %get-tuple-element.14.rows_ref, bf16[256,1024]{1,0:T(8,128)(2,1)S(1)} %bitcast.36, bf16[256,1024]{1,0:T(8,128)(2,1)S(1)} %bitcast.39, ...), custom_call_target="tpu_custom_call" | custom-call | tf_op jit(solution)/shard_map/pallas_call | solution.py:32
  102.0 5.1 %all-to-all-start.3 = ((f32[64,4,128]{2,1,0:T(4,128)}), f32[64,4,128]{2,1,0:T(4,128)S(1)}, u32[]{:S(2)}, u32[]{:S(2)}) async-start(f32[64,4,128]{2,1,0:T(4,128)} %bitcast.13), calls=%async_computation.3 | async-start | bytes 262144 | tf_op jit(solution)/shard_map/all_to_all | solution.py:21
  107.4 11.0 %all-to-all-done.3 = f32[64,4,128]{2,1,0:T(4,128)S(1)} async-done(((f32[64,4,128]{2,1,0:T(4,128)}), f32[64,4,128]{2,1,0:T(4,128)S(1)}, u32[]{:S(2)}, u32[]{:S(2)}) %all-to-all-start.3) | async-done | bytes 131104 | tf_op jit(solution)/shard_map/all_to_all | solution.py:21
  118.3 1.9 %shard_map.108 = bf16[192,768]{1,0:T(8,128)(2,1)} custom-call(s32[4]{0:T(128)S(1)} %pad_add_fusion.place_ref, f32[1]{0:T(128)S(6)} %copy.33.logit_ref, f32[48,512]{1,0:T(8,128)S(1)} %get-tuple-element.16.scores_ref, f32[256,128]{1,0:T(8,128)S(1)} %bitcast.54, s32[48,1]{1,0:T(8,128)S(1)} %convert_element_type.38.row_pos_ref, ...), custom_call_target="tpu_custom_call" | custom-call | tf_op jit(solution)/shard_map/pallas_call | solution.py:32
  120.2 3.4 %all-to-all-start.4 = ((bf16[8,24,768]{2,1,0:T(8,128)(2,1)}), bf16[8,24,768]{2,1,0:T(8,128)(2,1)S(1)}, u32[]{:S(2)}, u32[]{:S(2)}) async-start(bf16[8,24,768]{2,1,0:T(8,128)(2,1)} %bitcast.17), calls=%async_computation.4 | async-start | bytes 589824 | tf_op jit(solution)/shard_map/all_to_all | solution.py:21
  124.8 36.1 %all-gather.7.cloned.1.call-done = bf16[512,1152]{1,0:T(8,128)(2,1)} async-done(((bf16[8,1152]{1,0:T(8,128)(2,1)}), bf16[512,1152]{1,0:T(8,128)(2,1)}) %all-gather.7.cloned.1.call-update) | async-done | bytes 1179664 | tf_op jit(solution)/shard_map/all_gather | solution.py:484
  160.9 1.4 copy.30
  162.3 2.3 %shard_map.109 = (bf16[64,768]{1,0:T(8,128)(2,1)}, f32[8,128]{1,0:T(8,128)S(1)}) custom-call(s32[4]{0:T(128)S(1)} %pad_add_fusion.place_ref, bf16[192,768]{1,0:T(8,128)(2,1)S(1)} %bitcast.52, bf16[24,320]{1,0:T(8,128)(2,1)S(1)} %dynamic_slice.24.unit_ref, bf16[256,960]{1,0:T(8,128)(2,1)S(1)} %bitcast.43, bf16[256,960]{1,0:T(8,128)(2,1)S(1)} %bitcast.45, ...), custom_call_target="tpu_custom_call" | custom-call | tf_op jit(solution)/shard_map/pallas_call | solution.py:32
  164.6 4.3 %all-to-all-start.5 = ((bf16[4,16,768]{2,1,0:T(8,128)(2,1)}), bf16[4,16,768]{2,1,0:T(8,128)(2,1)S(1)}, u32[]{:S(2)}, u32[]{:S(2)}) async-start(bf16[4,16,768]{2,1,0:T(8,128)(2,1)} %bitcast.25), calls=%async_computation.5 | async-start | bytes 196608 | tf_op jit(solution)/shard_map/all_to_all | solution.py:21
  170.5 3.1 %all-to-all-done.5 = bf16[4,16,768]{2,1,0:T(8,128)(2,1)S(1)} async-done(((bf16[4,16,768]{2,1,0:T(8,128)(2,1)}), bf16[4,16,768]{2,1,0:T(8,128)(2,1)S(1)}, u32[]{:S(2)}, u32[]{:S(2)}) %all-to-all-start.5) | async-done | bytes 98336 | tf_op jit(solution)/shard_map/all_to_all | solution.py:21
  173.6 2.0 %shard_map.110 = (bf16[144,1664]{1,0:T(8,128)(2,1)}, bf16[192,1280]{1,0:T(8,128)(2,1)}) custom-call(bf16[64,768]{1,0:T(8,128)(2,1)S(1)} %bitcast.55, f32[8,128]{1,0:T(8,128)S(1)} %get-tuple-element.22.inv_ref, bf16[144,1664]{1,0:T(8,128)(2,1)S(1)} %bitcast.48, bf16[192,1280]{1,0:T(8,128)(2,1)S(1)} %bitcast.47, f32[1664]{0:T(1024)S(1)} %copy-done, ...), custom_call_target="tpu_custom_call" | custom-call | tf_op jit(solution)/shard_map/pallas_call | solution.py:32
  (46 shorter events, 8.6 us)
Async XLA Ops:
  9.2 32.3 %all-to-all-start = ((bf16[32,8,960]{2,1,0:T(8,128)(2,1)}), bf16[32,8,960]{2,1,0:T(8,128)(2,1)S(1)}, u32[]{:S(2)}, u32[]{:S(2)}) async-start(bf16[32,8,960]{2,1,0:T(8,128)(2,1)} %broadcast_in_dim.13), calls=%async_computation | async-start | bytes 1048576 | tf_op jit(solution)/shard_map/all_to_all | solution.py:21
  23.7 17.7 %copy-start.2 = (s32[12]{0:T(128)S(1)}, s32[12]{0:T(128)}, u32[]{:S(2)}) copy-start(s32[12]{0:T(128)} %pos_ref.1) | copy-start | bytes 148
  47.8 16.9 %all-to-all-start.1 = ((bf16[8,24,640]{2,1,0:T(8,128)(2,1)}), bf16[8,24,640]{2,1,0:T(8,128)(2,1)S(1)}, u32[]{:S(2)}, u32[]{:S(2)}) async-start(bf16[8,24,640]{2,1,0:T(8,128)(2,1)} %bitcast.6), calls=%async_computation.1 | async-start | bytes 491520 | tf_op jit(solution)/shard_map/all_to_all | solution.py:21
  66.4 23.8 %all-to-all-start.2 = ((bf16[32,8,1024]{2,1,0:T(8,128)(2,1)}), bf16[32,8,1024]{2,1,0:T(8,128)(2,1)S(1)}, u32[]{:S(2)}, u32[]{:S(2)}) async-start(bf16[32,8,1024]{2,1,0:T(8,128)(2,1)} %bitcast.9), calls=%async_computation.2 | async-start | bytes 1048576 | tf_op jit(solution)/shard_map/all_to_all | solution.py:21
  75.6 85.3 %all-gather.7.cloned.1.call-start = ((), (), s32[]{:S(2)}) async-start(), calls=%async_computation.6 | async-start | bytes 1198080 | tf_op jit(solution)/shard_map/all_gather | solution.py:484
  102.0 16.3 %all-to-all-start.3 = ((f32[64,4,128]{2,1,0:T(4,128)}), f32[64,4,128]{2,1,0:T(4,128)S(1)}, u32[]{:S(2)}, u32[]{:S(2)}) async-start(f32[64,4,128]{2,1,0:T(4,128)} %bitcast.13), calls=%async_computation.3 | async-start | bytes 262144 | tf_op jit(solution)/shard_map/all_to_all | solution.py:21
  120.2 42.1 %all-to-all-start.4 = ((bf16[8,24,768]{2,1,0:T(8,128)(2,1)}), bf16[8,24,768]{2,1,0:T(8,128)(2,1)S(1)}, u32[]{:S(2)}, u32[]{:S(2)}) async-start(bf16[8,24,768]{2,1,0:T(8,128)(2,1)} %bitcast.17), calls=%async_computation.4 | async-start | bytes 589824 | tf_op jit(solution)/shard_map/all_to_all | solution.py:21
  162.3 11.3 %copy-start = (f32[1664]{0:T(1024)S(1)}, f32[1664]{0:T(1024)}, u32[]{:S(2)}) copy-start(f32[1664]{0:T(1024)} %ig_ref.3) | copy-start | bytes 19972
  162.3 11.3 %copy-start.1 = (f32[1280]{0:T(1024)S(1)}, f32[1280]{0:T(1024)}, u32[]{:S(2)}) copy-start(f32[1280]{0:T(1024)} %tg_ref.3) | copy-start | bytes 15364
  164.6 9.0 %all-to-all-start.5 = ((bf16[4,16,768]{2,1,0:T(8,128)(2,1)}), bf16[4,16,768]{2,1,0:T(8,128)(2,1)S(1)}, u32[]{:S(2)}, u32[]{:S(2)}) async-start(bf16[4,16,768]{2,1,0:T(8,128)(2,1)} %bitcast.25), calls=%async_computation.5 | async-start | bytes 196608 | tf_op jit(solution)/shard_map/all_to_all | solution.py:21
Sparse Core Ops, SparseCore 0:
  80.3 80.6 all-gather.6

commit v12 on v8

--- a/solution.py
+++ b/solution.py
@@ -42,48 +42,73 @@
 
 
 def slab_place(dense, wide, skip):
-    return ((dense // wide) % 2) * 384 + (dense // (2 * wide)) * 24 + skip + dense % wide
+    row = skip + dense % wide
+    return (row // 8) * 256 + ((dense // wide) % 2) * 128 + (dense // (2 * wide)) * 8 + row % 8
+
+
+def slab_row(shape):
+    lane = lax.broadcasted_iota(jnp.int32, shape, 1)
+    return (lane // 256) * 8 + lane % 8
 
 
 def pool_kernel(
-    pos_ref, img_ref, txt_ref, ig_ref, tg_ref, out_ref, img_held, txt_held, img_rows, txt_rows, digits, sems
+    place_ref,
+    pos_ref,
+    img_ref,
+    txt_ref,
+    ig_ref,
+    tg_ref,
+    mine_ref,
+    theirs_ref,
+    img_held,
+    txt_held,
+    img_rows,
+    txt_rows,
+    digits,
+    sems,
 ):
-    pairs = img_ref.shape[0]
+    steps = img_ref.shape[0] // 2
 
     def copies(k):
+        span = pl.ds(2 * k, 2)
         return (
-            pltpu.make_async_copy(img_ref.at[k], img_held.at[k], sems.at[0, k]),
-            pltpu.make_async_copy(txt_ref.at[k], txt_held.at[k], sems.at[1, k]),
+            pltpu.make_async_copy(img_ref.at[span], img_held.at[span], sems.at[0, k]),
+            pltpu.make_async_copy(txt_ref.at[span], txt_held.at[span], sems.at[1, k]),
         )
 
-    for k in range(pairs):
+    for k in range(steps):
         for copy in copies(k):
             copy.start()
     for rows in (img_rows, txt_rows, digits):
         rows[...] = jnp.zeros_like(rows)
     spot = lax.broadcasted_iota(jnp.int32, (1, 128), 1)
 
-    def one_pair(k, carry):
+    def two_pairs(k, carry):
         for copy in copies(k):
             copy.wait()
         for held, gain_ref, rows in ((img_held, ig_ref, img_rows), (txt_held, tg_ref, txt_rows)):
-            values = held[k].astype(F32)
-            center = values - jnp.mean(values, axis=1, keepdims=True)
-            spread = jnp.mean(center * center, axis=1, keepdims=True)
-            mean = jnp.mean(center * lax.rsqrt(spread + 1e-05), axis=0, keepdims=True)
-            rows[pl.ds(k, 1), :] = mean * gain_ref[...][None]
-        place = pos_ref[k]
-        line = jnp.where(spot == 23, place // 32, jnp.where(spot == 47, place % 32, 0))
-        digits[pl.ds(k, 1), :] = line.astype(F32)
+            values = held[pl.ds(2 * k, 2)].astype(F32)
+            center = values - jnp.mean(values, axis=2, keepdims=True)
+            spread = jnp.mean(center * center, axis=2, keepdims=True)
+            mean = jnp.mean(center * lax.rsqrt(spread + 1e-05), axis=1)
+            for b in range(2):
+                rows[pl.ds(2 * k + b, 1), :] = mean[b : b + 1] * gain_ref[...][None]
+        for b in range(2):
+            place = pos_ref[2 * k + b]
+            line = jnp.where(spot == 7, place // 32, jnp.where(spot == 15, place % 32, 0))
+            digits[pl.ds(2 * k + b, 1), :] = line.astype(F32)
         return carry
 
-    lax.fori_loop(0, pairs, one_pair, 0)
+    lax.fori_loop(0, steps, two_pairs, 0)
     found = jnp.zeros((64, 768), F32)
+    lane = lax.broadcasted_iota(jnp.int32, (1, 768), 1)
+    slab = (lane % 128) // 8 * 2 + (lane // 128) % 2
     for rows, wide, skip in ((img_rows, 13, 0), (txt_rows, 10, 13)):
         width = 32 * wide
+        row = slab_row((1, 768)) - skip
+        wanted = jnp.where((row >= 0) & (row < wide), slab * wide + row, -1)
         dense = lax.broadcasted_iota(jnp.int32, (width, 768), 0)
-        lane = lax.broadcasted_iota(jnp.int32, (width, 768), 1)
-        pick = jnp.where(lane == slab_place(dense, wide, skip), 1.0, 0.0).astype(BF)
+        pick = jnp.where(dense == wanted, 1.0, 0.0).astype(BF)
         held = rows[...]
         quarters = [held[:, width * k : width * k + width] for k in range(4)]
         quarters = jnp.concatenate(quarters, 0).astype(BF)
@@ -91,32 +116,30 @@
     line = digits[...]
     blank = jnp.zeros_like(line)
     line = jnp.concatenate([line, blank, line, blank], 0)
-    found = jnp.concatenate([found[:, :128] + line, found[:, 128:]], 1)
-    out_ref[...] = found.astype(BF)
-
-
-def pool_call(image_in, text_in, img_gain, txt_gain, positive):
-    pairs, count_i, width_i = image_in.shape
-    _, count_t, width_t = text_in.shape
+    found = jnp.concatenate([found[:, :512], found[:, 512:640] + line, found[:, 640:]], 1)
+    first = place_ref[1] == 0
+    mine_ref[...] = jnp.where(first, found[:32], found[32:]).astype(BF)
+    theirs_ref[...] = jnp.where(first, found[32:], found[:32]).astype(BF)
+
+
+def pool_call(place, image_in, text_in, img_gain, txt_gain, positive):
+    pairs, _, width_i = image_in.shape
+    width_t = text_in.shape[2]
     vmem = pl.BlockSpec(memory_space=pltpu.VMEM)
+    smem = pl.BlockSpec(memory_space=pltpu.SMEM)
+    whole = pl.BlockSpec(memory_space=pl.ANY)
     return pl.pallas_call(
         pool_kernel,
-        out_shape=jax.ShapeDtypeStruct((64, 768), BF),
-        in_specs=[
-            pl.BlockSpec(memory_space=pltpu.SMEM),
-            pl.BlockSpec(memory_space=pl.ANY),
-            pl.BlockSpec(memory_space=pl.ANY),
-            vmem,
-            vmem,
-        ],
-        out_specs=vmem,
+        out_shape=[jax.ShapeDtypeStruct((32, 768), BF)] * 2,
+        in_specs=[smem, smem, whole, whole, vmem, vmem],
+        out_specs=[vmem, vmem],
         scratch_shapes=[
             pltpu.VMEM(image_in.shape, BF),
             pltpu.VMEM(text_in.shape, BF),
             pltpu.VMEM((16, width_i), F32),
             pltpu.VMEM((16, width_t), F32),
             pltpu.VMEM((16, 128), F32),
-            pltpu.SemaphoreType.DMA((2, pairs)),
+            pltpu.SemaphoreType.DMA((2, pairs // 2)),
         ],
         cost_estimate=pl.CostEstimate(
             flops=10 * (image_in.size + text_in.size),
@@ -124,23 +147,37 @@
             transcendentals=0,
         ),
         compiler_params=pltpu.CompilerParams(vmem_limit_bytes=60 * 1024 * 1024),
-    )(positive, image_in, text_in, img_gain, txt_gain)
-
-
-def project_kernel(place_ref, pooled_ref, wa_ref, wb_ref, out_ref):
-    part = jnp.zeros((48, wa_ref.shape[1]), F32)
-    inside = lax.broadcasted_iota(jnp.int32, (12, 768), 1) % 24
-    for a, w_ref in enumerate((wa_ref, wb_ref)):
+    )(place, positive, image_in, text_in, img_gain, txt_gain)
+
+
+def weight_quarter(w_ref, a):
+    return jnp.concatenate([w_ref[k + 128 * a : k + 128 * a + 128, :] for k in (0, 256)], 0)
+
+
+def project_kernel(place_ref, mine_ref, theirs_ref, w_ref, out_ref):
+    width = w_ref.shape[1] // 3
+    part = jnp.zeros((48, width), F32)
+    inside = slab_row((12, 768))
+    for a in range(2):
         pieces = []
         for h in range(2):
-            start = pl.multiple_of(64 * h + 32 * place_ref[1] + 16 * a, 16)
-            rows = pooled_ref[pl.ds(start, 16), :].astype(F32)[:12]
+            rows = jnp.where(
+                place_ref[1] == h,
+                mine_ref[16 * a : 16 * a + 16, :].astype(F32),
+                theirs_ref[32 * h + 16 * a : 32 * h + 16 * a + 16, :].astype(F32),
+            )[:12]
             img_rows = jnp.where(inside < 13, rows, 0.0)
             txt_rows = jnp.where((inside >= 13) & (inside < 23), rows, 0.0)
             for t in range(4):
                 pieces += [img_rows[3 * t : 3 * t + 3], txt_rows[3 * t : 3 * t + 3]]
         left = jnp.concatenate(pieces, 0).astype(BF)
-        part += jnp.dot(left, w_ref[...], preferred_element_type=F32)
+        quarter = weight_quarter(w_ref, a)
+        for j in range(3):
+            part += jnp.dot(
+                left[:, 256 * j : 256 * j + 256],
+                quarter[:, width * j : width * j + width],
+                preferred_element_type=F32,
+            )
     packed = jnp.concatenate([part[:24], part[24:]], 1)
     out_ref[...] = jnp.concatenate([packed] * 8, 0).astype(BF)
 
@@ -242,6 +279,22 @@
     return parts
 
 
+def times_items(left, fa_ref, fb_ref):
+    def times(part, columns):
+        return jnp.dot(part[:, :256], fa_ref[:, columns], preferred_element_type=F32) + jnp.dot(
+            part[:, 256:], fb_ref[:, columns], preferred_element_type=F32
+        )
+
+    start = times(left, slice(0, 1024))
+    last = lax.broadcasted_iota(jnp.int32, left.shape, 1) % 4 == 3
+    wide = left.astype(F32)
+    ends = jnp.zeros((left.shape[0], 256), F32)
+    for q in range(3):
+        moved = jnp.where(last, pltpu.roll(wide, 3 - q, 1), 0.0).astype(BF)
+        ends += times(moved, slice(256 * q, 256 * q + 256))
+    return jnp.concatenate([start, ends], 1)
+
+
 def coef_kernel(
     place_ref, logit_ref, scores_ref, far_ref, row_pos_ref, item_pos_ref, fa_ref, fb_ref, out_ref
 ):
@@ -275,22 +328,7 @@
     along = [
         jnp.sum(part.astype(F32) * scores, axis=1, keepdims=True) / logit for part in coefs
     ]
-    coef = jnp.concatenate(coefs, 0)
-
-    def times_items(left, columns):
-        return jnp.dot(left[:, :256], fa_ref[:, columns], preferred_element_type=F32) + jnp.dot(
-            left[:, 256:], fb_ref[:, columns], preferred_element_type=F32
-        )
-
-    cot = times_items(coef, slice(0, 1024))
-    last = lax.broadcasted_iota(jnp.int32, (96, 512), 1) % 4 == 3
-    wide = coef.astype(F32)
-    ends = jnp.zeros((96, 256), F32)
-    for q in range(3):
-        moved = jnp.where(last, pltpu.roll(wide, 3 - q, 1), 0.0).astype(BF)
-        ends += times_items(moved, slice(256 * q, 256 * q + 256))
-    cot = jnp.concatenate([cot, ends], 1)
-
+    cot = times_items(jnp.concatenate(coefs, 0), fa_ref, fb_ref)
     riders = (
         in_parts(row_part, 3)
         + in_parts(along[0], 2)
@@ -310,7 +348,7 @@
         out_ref[192 + 48 * k : 240 + 48 * k, :] = way
 
 
-def back_kernel(got_ref, unit_ref, wa_ref, wb_ref, out_ref, loss_ref):
+def back_kernel(got_ref, unit_ref, w_ref, out_ref, loss_ref):
     width = unit_ref.shape[1]
     got = [got_ref[48 * k : 48 * k + 48, :].astype(F32) for k in range(8)]
     riders = [[part[:, width + k : width + k + 1] for k in range(9)] for part in got]
@@ -328,10 +366,20 @@
         summed += weight * part[:, :width] + part[:, width + 64 : 2 * width + 64]
     loss_ref[...] = jnp.broadcast_to(value[:8] / (2.0 * 1536), (8, 128))
     proj_cot = (summed - unit_ref[...].astype(F32) * along).astype(BF)
+    is_img = slab_row((48, 768)) < 13
     mixed = []
-    for ref in (wa_ref, wb_ref):
-        pool = lax.dot_general(proj_cot, ref[...], ROWS_DOT, preferred_element_type=F32)
-        is_img = lax.broadcasted_iota(jnp.int32, pool.shape, 1) % 24 < 13
+    for a in range(2):
+        quarter = weight_quarter(w_ref, a)
+        pool = [
+            lax.dot_general(
+                proj_cot,
+                quarter[:, width * j : width * j + width],
+                ROWS_DOT,
+                preferred_element_type=F32,
+            )
+            for j in range(3)
+        ]
+        pool = jnp.concatenate(pool, 1)
         mixed.append(jnp.where(is_img, pool, pltpu.roll(pool, 45, 0)))
     blank = jnp.zeros((1, pool.shape[1]), F32)
     pieces = []
@@ -385,19 +433,22 @@
     width = emb // 4
     w = jnp.concatenate([proj_img, proj_txt, jnp.zeros((1, emb), BF)], 0)
     w = lax.dynamic_slice(w, (0, width * t_index), (24, width))
-    w = jnp.broadcast_to(w[None], (32, 24, width))
-    wa, wb = both_cores(exchange(w, ZX))
-
-    pooled = pool_call(image_in, text_in, img_gain, txt_gain, positive)
-    pooled = lax.all_gather(pooled, Y, axis=0, axis_index_groups=[[0, 6], [1, 7], [2, 4], [3, 5]])
-    row_pos = pooled[:, :12, 23].astype(F32) * 32.0 + pooled[:, :12, 47].astype(F32)
+    w = jnp.concatenate([w[:8], w[8:16], w[16:]], 1)
+    w = jnp.broadcast_to(w[None], (32, 8, 3 * width))
+    w = lax.all_gather(exchange(w, ZX), "c", axis=0).reshape(512, 3 * width)
+
+    mine, theirs = pool_call(place, image_in, text_in, img_gain, txt_gain, positive)
+    theirs = lax.all_gather(theirs, Y, axis=0, axis_index_groups=[[0, 6], [1, 7], [2, 4], [3, 5]])
+    row_pos = theirs[:, :12, 519].astype(F32) * 32.0 + theirs[:, :12, 527].astype(F32)
+    is_mine = lax.iota(jnp.int32, 2)[:, None] == h_index
+    row_pos = jnp.where(is_mine, positive.astype(F32)[None], row_pos)
     row_pos = jnp.pad(row_pos.reshape(8, 3), ((0, 0), (0, 3)), constant_values=-1.0)
     row_pos = row_pos.reshape(48, 1).astype(jnp.int32)
 
     (part,) = kernel_call(
         project_kernel,
         [((192, 2 * width), BF)],
-        [place, pooled.reshape(128, 768), wa, wb],
+        [place, mine, theirs.reshape(64, 768), w],
         smem=(0,),
     )
     parts = exchange(part.reshape(8, 24, 2 * width), Y).reshape(192, 2 * width)
@@ -436,7 +487,7 @@
     got = exchange(ways.reshape(8, 48, 768), Y).reshape(384, 768)
     unit_part = lax.dynamic_slice(rows, (0, width * t_index), (48, width))
     pool, loss = kernel_call(
-        back_kernel, [((64, 768), BF), ((8, 128), F32)], [got, unit_part, wa, wb]
+        back_kernel, [((64, 768), BF), ((8, 128), F32)], [got, unit_part, w]
     )
     mean_loss = loss[0, :1]
     pool = exchange(pool.reshape(8, 8, 768), Y).reshape(64, 768)

time: 148 us -> 145 us (0.980)
  blocking collectives: 23.8 us -> 19.5 us
    all_gather x4 -> x2, blocking collectives: 14.8 us -> 8.23 us  [both_cores(): lax.all_gather(part, 'c', axis=0)]
    all_gather x1 -> x2, blocking collectives: 9.02 us -> 11.2 us  [the longest x1 6.68 us: per_device(): lax.all_gather(theirs, Y, axis=0, axis_index_groups=[[0, 6], [1, 7], [2,...]
  transfers between devices with their start and end apart: 6 -> 6, of which waited for: 6 -> 6; matrix products, arithmetic and copies ran while one was open for 3% -> 3% of each run, Pallas kernels for 5% -> 4%
where the time goes in v12:
time: 145 us; the launch traced here: 144 us
  waiting for transfers between devices  61.3 us (42%)
  starting transfers between devices  37.7 us (26%)
  blocking collectives  19.5 us (13%)
  Pallas kernels  16.7 us (12%)
  local copies, waits for them, and re-layouts  6.01 us (4%)
  other arithmetic  1.8 us (1%)
    all_to_all x6, waiting for transfers between devices, exchange(): return lax.all_to_all(blocks, axes, 0, 0, tiled=True)  61.3 us
    all_to_all x6, starting transfers between devices, exchange(): return lax.all_to_all(blocks, axes, 0, 0, tiled=True)  37.7 us
    pallas_call x6, Pallas kernels, kernel_call(): pl.pallas_call(body, out_shape=[jax.ShapeDtypeStruct(shape, kind) for sha...  11.1 us
    all_gather x2, blocking collectives, both_cores(): lax.all_gather(part, 'c', axis=0)  8.23 us
    all_gather x1, blocking collectives, per_device(): lax.all_gather(theirs, Y, axis=0, axis_index_groups=[[0, 6], [1, 7], [2,...  6.68 us
    pallas_call x1, Pallas kernels, pool_call(): pl.pallas_call(pool_kernel, out_shape=[jax.ShapeDtypeStruct((32, 768), BF...  5.56 us
    all_gather x1, blocking collectives, per_device(): w = lax.all_gather(exchange(w, ZX), 'c', axis=0).reshape(512, 3 * width)  4.56 us
  transfers between devices with their start and end apart: 6, of which 6 were waited for; matrix products, arithmetic and copies ran while one was open for 3% of the time, Pallas kernels for 4%

profile of v12, /device:TPU:1, one launch (start us, length us, event | category | flops | bytes accessed | tf_op | source)
XLA Modules:
  0.0 144.4 jit_solution(2388062135252515592)
XLA Ops:
  2.5 13.7 %all-to-all-start = ((bf16[32,8,960]{2,1,0:T(8,128)(2,1)}), bf16[32,8,960]{2,1,0:T(8,128)(2,1)S(1)}, u32[]{:S(2)}, u32[]{:S(2)}) async-start(bf16[32,8,960]{2,1,0:T(8,128)(2,1)} %broadcast_in_dim.39), calls=%async_computation | async-start | bytes 1048576 | tf_op jit(solution)/shard_map/all_to_all | solution.py:21
  16.8 5.6 %shard_map.103 = (bf16[32,768]{1,0:T(8,128)(2,1)}, bf16[32,768]{1,0:T(8,128)(2,1)}) custom-call(s32[4]{0:T(128)} %pad_add_fusion.place_ref, s32[12]{0:T(128)} %pos_ref.1, bf16[12,48,1664]{2,1,0:T(8,128)(2,1)} %img_ref.1, bf16[12,64,1280]{2,1,0:T(8,128)(2,1)} %txt_ref.1, f32[1664]{0:T(1024)} %ig_ref.3, f32[1280]{0:T(1024)} %tg_ref.3), custom_call_target="tpu_custom_call" | custom-call | flops 19415040 | bytes 3883008 | tf_op jit(solution)/shard_map/pallas_call | solution.py:131
  22.4 6.7 %all-gather.theirs_ref = bf16[64,768]{1,0:T(8,128)(2,1)S(1)} all-gather(bf16[32,768]{1,0:T(8,128)(2,1)} %get-tuple-element.15), channel_id=2, replica_groups={{0,320},{128,448},{256,64},{384,192},{1,321},{129,449},{257,65},{385,19..., dimensions={0}, use_global_device_ids=true | all-gather | bytes 147456 | tf_op jit(solution)/shard_map/all_gather | solution.py:441
  29.2 3.3 %all-to-all-done = bf16[32,8,960]{2,1,0:T(8,128)(2,1)S(1)} async-done(((bf16[32,8,960]{2,1,0:T(8,128)(2,1)}), bf16[32,8,960]{2,1,0:T(8,128)(2,1)S(1)}, u32[]{:S(2)}, u32[]{:S(2)}) %all-to-all-start) | async-done | bytes 491552 | tf_op jit(solution)/shard_map/all_to_all | solution.py:21
  32.5 4.6 %all-gather.1 = bf16[64,8,960]{2,1,0:T(8,128)(2,1)S(1)} all-gather(bf16[32,8,960]{2,1,0:T(8,128)(2,1)S(1)} %all-to-all-done), channel_id=3, replica_groups=mesh['t'=4,'h'=2,'z'=8,'x'=4,'c'=2] {'c'}, dimensions={0}, use_global_device_ids=true | all-gather | bytes 1474560 | tf_op jit(solution)/shard_map/all_gather | solution.py:438
  37.8 1.7 %shard_map.104 = bf16[192,640]{1,0:T(8,128)(2,1)} custom-call(s32[4]{0:T(128)S(1)} %copy-done.3, bf16[32,768]{1,0:T(8,128)(2,1)S(1)} %copy-done, bf16[64,768]{1,0:T(8,128)(2,1)S(1)} %all-gather.theirs_ref, bf16[512,960]{1,0:T(8,128)(2,1)S(1)} %bitcast.31), custom_call_target="tpu_custom_call" | custom-call | tf_op jit(solution)/shard_map/pallas_call | solution.py:32
  39.5 6.8 %all-to-all-start.1 = ((bf16[8,24,640]{2,1,0:T(8,128)(2,1)}), bf16[8,24,640]{2,1,0:T(8,128)(2,1)S(1)}, u32[]{:S(2)}, u32[]{:S(2)}) async-start(bf16[8,24,640]{2,1,0:T(8,128)(2,1)} %bitcast.5), calls=%async_computation.1 | async-start | bytes 491520 | tf_op jit(solution)/shard_map/all_to_all | solution.py:21
  46.4 10.4 %all-to-all-done.1 = bf16[8,24,640]{2,1,0:T(8,128)(2,1)S(1)} async-done(((bf16[8,24,640]{2,1,0:T(8,128)(2,1)}), bf16[8,24,640]{2,1,0:T(8,128)(2,1)S(1)}, u32[]{:S(2)}, u32[]{:S(2)}) %all-to-all-start.1) | async-done | bytes 245792 | tf_op jit(solution)/shard_map/all_to_all | solution.py:21
  56.9 1.7 %shard_map.105 = (bf16[48,1280]{1,0:T(8,128)(2,1)S(1)}, bf16[256,1024]{1,0:T(8,128)(2,1)}, f32[8,128]{1,0:T(8,128)S(1)}) custom-call(s32[4]{0:T(128)S(1)} %copy-done.3, bf16[192,640]{1,0:T(8,128)(2,1)S(1)} %bitcast.40, f32[1,128]{1,0:T(1,128)S(1)} %pad_bitcast_fusion.digits_ref), custom_call_target="tpu_custom_call" | custom-call | tf_op jit(solution)/shard_map/pallas_call | solution.py:32
  58.6 5.2 %all-to-all-start.2 = ((bf16[32,8,1024]{2,1,0:T(8,128)(2,1)}), bf16[32,8,1024]{2,1,0:T(8,128)(2,1)S(1)}, u32[]{:S(2)}, u32[]{:S(2)}) async-start(bf16[32,8,1024]{2,1,0:T(8,128)(2,1)} %bitcast.8), calls=%async_computation.2 | async-start | bytes 1048576 | tf_op jit(solution)/shard_map/all_to_all | solution.py:21
  65.5 12.8 %all-to-all-done.2 = bf16[32,8,1024]{2,1,0:T(8,128)(2,1)S(1)} async-done(((bf16[32,8,1024]{2,1,0:T(8,128)(2,1)}), bf16[32,8,1024]{2,1,0:T(8,128)(2,1)S(1)}, u32[]{:S(2)}, u32[]{:S(2)}) %all-to-all-start.2) | async-done | bytes 524320 | tf_op jit(solution)/shard_map/all_to_all | solution.py:21
  78.4 6.1 %all-gather.2 = bf16[32,8,1024]{2,1,0:T(8,128)(2,1)S(1)} all-gather(bf16[16,8,1024]{2,1,0:T(8,128)(2,1)S(1)} %get-tuple-element.28), channel_id=4, replica_groups=mesh['t'=4,'h'=2,'z'=8,'x'=4,'c'=2] {'c'}, dimensions={0}, use_global_device_ids=true | all-gather | bytes 786432 | tf_op jit(solution)/shard_map/all_gather | solution.py:26
  84.5 2.2 %all-gather.3 = bf16[32,8,1024]{2,1,0:T(8,128)(2,1)S(1)} all-gather(bf16[16,8,1024]{2,1,0:T(8,128)(2,1)S(1)} %get-tuple-element.27), channel_id=5, replica_groups=mesh['t'=4,'h'=2,'z'=8,'x'=4,'c'=2] {'c'}, dimensions={0}, use_global_device_ids=true | all-gather | bytes 786432 | tf_op jit(solution)/shard_map/all_gather | solution.py:26
  86.8 2.1 %shard_map.106 = (f32[48,512]{1,0:T(8,128)S(1)}, f32[256,128]{1,0:T(8,128)}) custom-call(s32[4]{0:T(128)S(1)} %copy-done.3, f32[1]{0:T(128)S(6)} %copy.46.logit_ref, bf16[48,1280]{1,0:T(8,128)(2,1)S(1)} %get-tuple-element.16.rows_ref, bf16[256,1024]{1,0:T(8,128)(2,1)S(1)} %bitcast.33, bf16[256,1024]{1,0:T(8,128)(2,1)S(1)} %bitcast.35, ...), custom_call_target="tpu_custom_call" | custom-call | tf_op jit(solution)/shard_map/pallas_call | solution.py:32
  89.0 5.1 %all-to-all-start.3 = ((f32[64,4,128]{2,1,0:T(4,128)}), f32[64,4,128]{2,1,0:T(4,128)S(1)}, u32[]{:S(2)}, u32[]{:S(2)}) async-start(f32[64,4,128]{2,1,0:T(4,128)} %bitcast.12), calls=%async_computation.3 | async-start | bytes 262144 | tf_op jit(solution)/shard_map/all_to_all | solution.py:21
  94.3 10.8 %all-to-all-done.3 = f32[64,4,128]{2,1,0:T(4,128)S(1)} async-done(((f32[64,4,128]{2,1,0:T(4,128)}), f32[64,4,128]{2,1,0:T(4,128)S(1)}, u32[]{:S(2)}, u32[]{:S(2)}) %all-to-all-start.3) | async-done | bytes 131104 | tf_op jit(solution)/shard_map/all_to_all | solution.py:21
  105.2 2.1 %shard_map.107 = bf16[384,768]{1,0:T(8,128)(2,1)} custom-call(s32[4]{0:T(128)S(1)} %copy-done.3, f32[1]{0:T(128)S(6)} %copy.46.logit_ref, f32[48,512]{1,0:T(8,128)S(1)} %get-tuple-element.18.scores_ref, f32[256,128]{1,0:T(8,128)S(1)} %bitcast.41, s32[48,1]{1,0:T(8,128)S(1)} %convert_element_type.40.row_pos_ref, ...), custom_call_target="tpu_custom_call" | custom-call | tf_op jit(solution)/shard_map/pallas_call | solution.py:32
  107.3 3.5 %all-to-all-start.4 = ((bf16[8,48,768]{2,1,0:T(8,128)(2,1)}), bf16[8,48,768]{2,1,0:T(8,128)(2,1)S(1)}, u32[]{:S(2)}, u32[]{:S(2)}) async-start(bf16[8,48,768]{2,1,0:T(8,128)(2,1)} %bitcast.16), calls=%async_computation.4 | async-start | bytes 1179648 | tf_op jit(solution)/shard_map/all_to_all | solution.py:21
  110.9 1.1 constant_dynamic-slice_fusion
  112.0 18.1 %all-to-all-done.4 = bf16[8,48,768]{2,1,0:T(8,128)(2,1)S(1)} async-done(((bf16[8,48,768]{2,1,0:T(8,128)(2,1)}), bf16[8,48,768]{2,1,0:T(8,128)(2,1)S(1)}, u32[]{:S(2)}, u32[]{:S(2)}) %all-to-all-start.4) | async-done | bytes 589856 | tf_op jit(solution)/shard_map/all_to_all | solution.py:21
  130.2 1.4 shard_map.108
  131.6 3.4 %all-to-all-start.5 = ((bf16[8,8,768]{2,1,0:T(8,128)(2,1)}), bf16[8,8,768]{2,1,0:T(8,128)(2,1)S(1)}, u32[]{:S(2)}, u32[]{:S(2)}) async-start(bf16[8,8,768]{2,1,0:T(8,128)(2,1)} %bitcast.19), calls=%async_computation.5 | async-start | bytes 196608 | tf_op jit(solution)/shard_map/all_to_all | solution.py:21
  136.5 5.8 %all-to-all-done.5 = bf16[8,8,768]{2,1,0:T(8,128)(2,1)S(1)} async-done(((bf16[8,8,768]{2,1,0:T(8,128)(2,1)}), bf16[8,8,768]{2,1,0:T(8,128)(2,1)S(1)}, u32[]{:S(2)}, u32[]{:S(2)}) %all-to-all-start.5) | async-done | bytes 98336 | tf_op jit(solution)/shard_map/all_to_all | solution.py:21
  142.3 2.0 %shard_map.109 = (bf16[144,1664]{1,0:T(8,128)(2,1)}, bf16[192,1280]{1,0:T(8,128)(2,1)}) custom-call(bf16[64,768]{1,0:T(8,128)(2,1)S(1)} %bitcast.43, f32[8,128]{1,0:T(8,128)S(1)} %get-tuple-element.22.inv_ref, bf16[144,1664]{1,0:T(8,128)(2,1)S(1)} %bitcast.39, bf16[192,1280]{1,0:T(8,128)(2,1)S(1)} %bitcast.38, f32[1664]{0:T(1024)S(1)} %copy-done.1, ...), custom_call_target="tpu_custom_call" | custom-call | tf_op jit(solution)/shard_map/pallas_call | solution.py:32
  (51 shorter events, 6.7 us)
Async XLA Ops:
  2.5 30.0 %all-to-all-start = ((bf16[32,8,960]{2,1,0:T(8,128)(2,1)}), bf16[32,8,960]{2,1,0:T(8,128)(2,1)S(1)}, u32[]{:S(2)}, u32[]{:S(2)}) async-start(bf16[32,8,960]{2,1,0:T(8,128)(2,1)} %broadcast_in_dim.39), calls=%async_computation | async-start | bytes 1048576 | tf_op jit(solution)/shard_map/all_to_all | solution.py:21
  16.8 12.3 %copy-start.4 = (s32[12]{0:T(128)S(1)}, s32[12]{0:T(128)}, u32[]{:S(2)}) copy-start(s32[12]{0:T(128)} %pos_ref.1) | copy-start | bytes 148
  16.8 20.2 %copy-start.3 = (s32[4]{0:T(128)S(1)}, s32[4]{0:T(128)}, u32[]{:S(2)}) copy-start(s32[4]{0:T(128)} %pad_add_fusion.place_ref) | copy-start | bytes 52
  37.0 0.8 copy-start
  39.5 17.4 %all-to-all-start.1 = ((bf16[8,24,640]{2,1,0:T(8,128)(2,1)}), bf16[8,24,640]{2,1,0:T(8,128)(2,1)S(1)}, u32[]{:S(2)}, u32[]{:S(2)}) async-start(bf16[8,24,640]{2,1,0:T(8,128)(2,1)} %bitcast.5), calls=%async_computation.1 | async-start | bytes 491520 | tf_op jit(solution)/shard_map/all_to_all | solution.py:21
  58.6 19.8 %all-to-all-start.2 = ((bf16[32,8,1024]{2,1,0:T(8,128)(2,1)}), bf16[32,8,1024]{2,1,0:T(8,128)(2,1)S(1)}, u32[]{:S(2)}, u32[]{:S(2)}) async-start(bf16[32,8,1024]{2,1,0:T(8,128)(2,1)} %bitcast.8), calls=%async_computation.2 | async-start | bytes 1048576 | tf_op jit(solution)/shard_map/all_to_all | solution.py:21
  89.0 16.2 %all-to-all-start.3 = ((f32[64,4,128]{2,1,0:T(4,128)}), f32[64,4,128]{2,1,0:T(4,128)S(1)}, u32[]{:S(2)}, u32[]{:S(2)}) async-start(f32[64,4,128]{2,1,0:T(4,128)} %bitcast.12), calls=%async_computation.3 | async-start | bytes 262144 | tf_op jit(solution)/shard_map/all_to_all | solution.py:21
  107.3 22.9 %all-to-all-start.4 = ((bf16[8,48,768]{2,1,0:T(8,128)(2,1)}), bf16[8,48,768]{2,1,0:T(8,128)(2,1)S(1)}, u32[]{:S(2)}, u32[]{:S(2)}) async-start(bf16[8,48,768]{2,1,0:T(8,128)(2,1)} %bitcast.16), calls=%async_computation.4 | async-start | bytes 1179648 | tf_op jit(solution)/shard_map/all_to_all | solution.py:21
  110.8 31.5 %copy-start.1 = (f32[1664]{0:T(1024)S(1)}, f32[1664]{0:T(1024)}, u32[]{:S(2)}) copy-start(f32[1664]{0:T(1024)} %ig_ref.3) | copy-start | bytes 19972
  110.9 31.5 %copy-start.2 = (f32[1280]{0:T(1024)S(1)}, f32[1280]{0:T(1024)}, u32[]{:S(2)}) copy-start(f32[1280]{0:T(1024)} %tg_ref.3) | copy-start | bytes 15364
  131.6 10.7 %all-to-all-start.5 = ((bf16[8,8,768]{2,1,0:T(8,128)(2,1)}), bf16[8,8,768]{2,1,0:T(8,128)(2,1)S(1)}, u32[]{:S(2)}, u32[]{:S(2)}) async-start(bf16[8,8,768]{2,1,0:T(8,128)(2,1)} %bitcast.19), calls=%async_computation.5 | async-start | bytes 196608 | tf_op jit(solution)/shard_map/all_to_all | solution.py:21

commit v13 on v12

--- a/solution.py
+++ b/solution.py
@@ -217,14 +217,15 @@
 
 def tile_masks(place_ref):
     h, t, g = place_ref[1], place_ref[2], place_ref[3]
-    row = lax.broadcasted_iota(jnp.int32, (48, 512), 0)
-    item = lax.broadcasted_iota(jnp.int32, (48, 512), 1)
+    row = lax.broadcasted_iota(jnp.int32, (48, 1), 0)
+    item = lax.broadcasted_iota(jnp.int32, (1, 512), 1)
     item_g = ((item // 256) * 16 + (item % 128) // 8) * 2 + (item // 128) % 2
     item_pair = (h * 64 + item_g) * 12 + 3 * t + item % 4
     row_pair = ((row // 24) * 64 + g) * 12 + ((row // 6) % 4) * 3 + row % 3
-    row_txt, item_txt = (row % 6) // 3, (item % 8) // 4
-    valid = (row_txt != item_txt) & (item % 4 < 3)
-    return valid, row_pair, item_pair, row_txt, item
+    row_txt = (row % 6) // 3
+    item_txt = jnp.where(item % 4 < 3, (item % 8) // 4, -1)
+    valid = item_txt == 1 - row_txt
+    return valid, row_pair, item_pair, row_txt, item_txt
 
 
 def log_total(values, axis):
@@ -256,10 +257,10 @@
         scores += jnp.where(lane == q, moved, 0.0)
     scores = logit_ref[0] * scores
     scores_ref[...] = scores
-    valid, _, item_pair, row_txt, _ = tile_masks(place_ref)
+    valid, _, item_pair, row_txt, item_txt = tile_masks(place_ref)
     masked = jnp.where(valid, scores, LOW)
     item_part = log_total(masked, 0)
-    hit = valid & (row_txt == 0) & (row_pos_ref[...] == item_pair)
+    hit = jnp.where(item_txt == 1, item_pair, -1) == jnp.where(row_txt == 0, row_pos_ref[...], -2)
     matched = jnp.sum(
         jnp.sum(jnp.where(hit, scores, 0.0), axis=1, keepdims=True), axis=0, keepdims=True
     )
@@ -309,21 +310,22 @@
     item_lse = jnp.concatenate([lines[k : k + 1] for k in range(4)], 1)
     summed = jnp.sum(seen, axis=0)
     summed = summed[:1] + summed[4:5]
-    valid, row_pair, item_pair, row_txt, item = tile_masks(place_ref)
-    from_img = row_txt == 0
-    hit = valid & (
-        jnp.where(from_img, row_pos_ref[...], row_pair)
-        == jnp.where(from_img, item_pair, item_pos_ref[...])
-    )
-    real = item[:1] % 4 < 3
-    lse_total = jnp.sum(jnp.where(real, item_lse, 0.0), axis=1, keepdims=True)
+    valid, row_pair, item_pair, row_txt, item_txt = tile_masks(place_ref)
+    img_hit = jnp.where(item_txt == 1, item_pair, -1) == jnp.where(
+        row_txt == 0, row_pos_ref[...], -2
+    )
+    txt_hit = jnp.where(item_txt == 0, item_pos_ref[...], -1) == jnp.where(
+        row_txt == 1, row_pair, -2
+    )
+    twice = jnp.where(img_hit, 2.0, jnp.where(txt_hit, 2.0, 0.0))
+    lse_total = jnp.sum(jnp.where(item_txt >= 0, item_lse, 0.0), axis=1, keepdims=True)
     lane = lax.broadcasted_iota(jnp.int32, (1, 128), 1)
     matched = jnp.sum(jnp.where(lane == 3, summed, 0.0), axis=1, keepdims=True)
     value = lse_total - 2.0 * matched
     masked = jnp.where(valid, scores, LOW)
     row_part = log_total(masked, 1)
     by_row = (0.5 * logit) * jnp.exp(masked - row_part)
-    by_item = (0.5 * logit) * (jnp.exp(masked - item_lse) - jnp.where(hit, 2.0, 0.0))
+    by_item = (0.5 * logit) * (jnp.exp(masked - item_lse) - twice)
     coefs = [jnp.where(valid, part, 0.0).astype(BF) for part in (by_row, by_item)]
     along = [
         jnp.sum(part.astype(F32) * scores, axis=1, keepdims=True) / logit for part in coefs
@@ -339,19 +341,18 @@
     extra = jnp.zeros((48, 64), F32)
     for k, rider in enumerate(riders):
         extra = jnp.where(column == k, rider, extra)
-    blank = jnp.zeros((48, 64), F32)
-    width = cot.shape[1] // 4
-    for k in range(4):
-        part = cot[:, width * k : width * k + width]
-        way = jnp.concatenate([part[:48], extra, part[48:], blank], 1).astype(BF)
+    width = cot.shape[1] // 8
+    for k in range(8):
+        first = width * (2 * (k % 4) + k // 4)
+        part = cot[:, first : first + width]
+        way = jnp.concatenate([part[:48], part[48:], extra], 1).astype(BF)
         out_ref[48 * k : 48 * k + 48, :] = way
-        out_ref[192 + 48 * k : 240 + 48 * k, :] = way
-
-
-def back_kernel(got_ref, unit_ref, w_ref, out_ref, loss_ref):
+
+
+def back_kernel(place_ref, got_ref, unit_ref, w_ref, other_ref, out_ref, loss_ref):
     width = unit_ref.shape[1]
     got = [got_ref[48 * k : 48 * k + 48, :].astype(F32) for k in range(8)]
-    riders = [[part[:, width + k : width + k + 1] for k in range(9)] for part in got]
+    riders = [[part[:, 2 * width + k : 2 * width + k + 1] for k in range(9)] for part in got]
     parts = [r[0] + r[1] + r[2] for r in riders]
     largest = functools.reduce(jnp.maximum, parts)
     total = sum(jnp.exp(part - largest) for part in parts)
@@ -363,25 +364,32 @@
         weight = jnp.exp(own - lse)
         along += weight * (r[3] + r[4]) + (r[5] + r[6])
         value += r[7] + r[8]
-        summed += weight * part[:, :width] + part[:, width + 64 : 2 * width + 64]
+        summed += weight * part[:, :width] + part[:, width : 2 * width]
     loss_ref[...] = jnp.broadcast_to(value[:8] / (2.0 * 1536), (8, 128))
     proj_cot = (summed - unit_ref[...].astype(F32) * along).astype(BF)
     is_img = slab_row((48, 768)) < 13
-    mixed = []
+    first = place_ref[1] == 0
+
+    def features(columns):
+        pool = [
+            lax.dot_general(proj_cot, part, ROWS_DOT, preferred_element_type=F32)
+            for part in columns
+        ]
+        pool = jnp.concatenate(pool, 1)
+        return jnp.where(is_img, pool, pltpu.roll(pool, 45, 0))
+
+    own, other = [], []
     for a in range(2):
         quarter = weight_quarter(w_ref, a)
-        pool = [
-            lax.dot_general(
-                proj_cot,
-                quarter[:, width * j : width * j + width],
-                ROWS_DOT,
-                preferred_element_type=F32,
-            )
-            for j in range(3)
-        ]
-        pool = jnp.concatenate(pool, 1)
-        mixed.append(jnp.where(is_img, pool, pltpu.roll(pool, 45, 0)))
-    blank = jnp.zeros((1, pool.shape[1]), F32)
+        columns = []
+        for j in range(3):
+            pair = quarter[:, 2 * width * j : 2 * width * j + 2 * width]
+            columns.append(jnp.where(first, pair[:, :width], pair[:, width:]))
+        own.append(features(columns))
+        quarter = weight_quarter(other_ref, a)
+        other.append(features([quarter[:, width * j : width * j + width] for j in range(3)]))
+    mixed = [jnp.where(first, x, y) for x, y in zip(own + other, other + own)]
+    blank = jnp.zeros((1, 768), F32)
     pieces = []
     for k in range(8):
         for pool in mixed:
@@ -400,14 +408,8 @@
         lane = lax.broadcasted_iota(jnp.int32, (768, 32 * wide), 0)
         pick = jnp.where(lane == slab_place(dense, wide, skip), 1.0, 0.0).astype(BF)
         found = jnp.dot(pool, pick, preferred_element_type=F32)
-        halves = [
-            found[32 * k : 32 * k + 8]
-            + found[32 * k + 8 : 32 * k + 16]
-            + found[32 * k + 16 : 32 * k + 24]
-            + found[32 * k + 24 : 32 * k + 32]
-            for k in range(2)
-        ]
-        cot = jnp.concatenate([halves[0][:4], halves[0][4:], halves[1][:4], halves[1][4:]], 1)
+        found = sum(found[16 * k : 16 * k + 16] for k in range(8))
+        cot = jnp.concatenate([found[4 * k : 4 * k + 4] for k in range(4)], 1)
         cot = cot * inv[at : at + 4] * gain_ref[...][None]
         mean_cot = jnp.mean(cot, axis=1, keepdims=True)
         count = x_ref.shape[0] // 3
@@ -463,7 +465,13 @@
         scratch=[pltpu.VMEM((64, emb), F32), pltpu.VMEM((64, 128), F32)],
         smem=(0,),
     )
+    half = width // 2
+    w_held, far = lax.optimization_barrier((w, far))
+    parts = w_held.reshape(512, 3, 2, half)
+    w_other = jnp.where(h_index == 0, parts[:, :, 1], parts[:, :, 0]).reshape(512, 3 * half)
+    w_other = lax.ppermute(w_other, "h", [(0, 1), (1, 0)])
     fa, fb = both_cores(exchange(far.reshape(32, 8, 1024), ZX))
+    fa, w_other = lax.optimization_barrier((fa, w_other))
 
     scores, far = kernel_call(
         score_kernel,
@@ -480,17 +488,20 @@
     item_pos = item_pos.astype(jnp.int32)
     (ways,) = kernel_call(
         coef_kernel,
-        [((384, 768), BF)],
+        [((384, 384), BF)],
         [place, logit_scale, scores, far, row_pos, item_pos, fa, fb],
         smem=(0, 1),
     )
-    got = exchange(ways.reshape(8, 48, 768), Y).reshape(384, 768)
-    unit_part = lax.dynamic_slice(rows, (0, width * t_index), (48, width))
+    got = exchange(ways.reshape(8, 48, 384), Y).reshape(384, 384)
+    unit_part = lax.dynamic_slice(rows, (0, half * (2 * t_index + h_index)), (48, half))
     pool, loss = kernel_call(
-        back_kernel, [((64, 768), BF), ((8, 128), F32)], [got, unit_part, w]
+        back_kernel,
+        [((128, 768), BF), ((8, 128), F32)],
+        [place, got, unit_part, w, w_other],
+        smem=(0,),
     )
     mean_loss = loss[0, :1]
-    pool = exchange(pool.reshape(8, 8, 768), Y).reshape(64, 768)
+    pool = exchange(pool.reshape(8, 16, 768), Y).reshape(128, 768)
     count_i, width_i = image_in.shape[1:]
     count_t, width_t = text_in.shape[1:]
     img_own = lax.dynamic_slice_in_dim(image_in, 3 * t_index, 3, 0).reshape(-1, width_i)

time: 145 us -> 160 us (1.10)
  starting transfers between devices: 37.7 us -> 45.3 us
  waiting for transfers between devices: 61.3 us -> 63.8 us
  blocking collectives: 19.5 us -> 21.7 us
    ppermute x0 -> x1, waiting for transfers between devices: none -> 10.9 us  [per_device(): w_other = lax.ppermute(w_other, 'h', [(0, 1), (1, 0)])]
    all_to_all x6, waiting for transfers between devices: 61.3 us -> 52.9 us  [exchange(): return lax.all_to_all(blocks, axes, 0, 0, tiled=True)]
    all_to_all x6, starting transfers between devices: 37.7 us -> 42.6 us  [exchange(): return lax.all_to_all(blocks, axes, 0, 0, tiled=True)]
    ppermute x0 -> x1, starting transfers between devices: none -> 2.78 us  [per_device(): w_other = lax.ppermute(w_other, 'h', [(0, 1), (1, 0)])]
    all_gather x2, blocking collectives: 8.23 us -> 10.4 us  [both_cores(): lax.all_gather(part, 'c', axis=0)]
  transfers between devices with their start and end apart: 6 -> 7, of which waited for: 6 -> 7; matrix products, arithmetic and copies ran while one was open for 3% -> 4% of each run, Pallas kernels for 4% -> 3%
where the time goes in v13:
time: 160 us; the launch traced here: 159 us
  waiting for transfers between devices  63.8 us (40%)
  starting transfers between devices  45.3 us (28%)
  blocking collectives  21.7 us (14%)
  Pallas kernels  17.5 us (11%)
  local copies, waits for them, and re-layouts  7.52 us (5%)
  other arithmetic  1.84 us (1%)
    all_to_all x6, waiting for transfers between devices, exchange(): return lax.all_to_all(blocks, axes, 0, 0, tiled=True)  52.9 us
    all_to_all x6, starting transfers between devices, exchange(): return lax.all_to_all(blocks, axes, 0, 0, tiled=True)  42.6 us
    pallas_call x6, Pallas kernels, kernel_call(): pl.pallas_call(body, out_shape=[jax.ShapeDtypeStruct(shape, kind) for sha...  11.9 us
    ppermute x1, waiting for transfers between devices, per_device(): w_other = lax.ppermute(w_other, 'h', [(0, 1), (1, 0)])  10.9 us
    all_gather x2, blocking collectives, both_cores(): lax.all_gather(part, 'c', axis=0)  10.4 us
    all_gather x1, blocking collectives, per_device(): lax.all_gather(theirs, Y, axis=0, axis_index_groups=[[0, 6], [1, 7], [2,...  6.68 us
    pallas_call x1, Pallas kernels, pool_call(): pl.pallas_call(pool_kernel, out_shape=[jax.ShapeDtypeStruct((32, 768), BF...  5.56 us
    all_gather x1, blocking collectives, per_device(): w = lax.all_gather(exchange(w, ZX), 'c', axis=0).reshape(512, 3 * width)  4.56 us
  transfers between devices with their start and end apart: 7, of which 7 were waited for; matrix products, arithmetic and copies ran while one was open for 4% of the time, Pallas kernels for 3%

profile of v13, /device:TPU:1, one launch (start us, length us, event | category | flops | bytes accessed | tf_op | source)
XLA Modules:
  0.0 159.2 jit_solution(3035433396344481237)
XLA Ops:
  2.5 13.7 %all-to-all-start = ((bf16[32,8,960]{2,1,0:T(8,128)(2,1)}), bf16[32,8,960]{2,1,0:T(8,128)(2,1)S(1)}, u32[]{:S(2)}, u32[]{:S(2)}) async-start(bf16[32,8,960]{2,1,0:T(8,128)(2,1)} %broadcast_in_dim.39), calls=%async_computation | async-start | bytes 1048576 | tf_op jit(solution)/shard_map/all_to_all | solution.py:21
  16.8 5.6 %shard_map.103 = (bf16[32,768]{1,0:T(8,128)(2,1)}, bf16[32,768]{1,0:T(8,128)(2,1)}) custom-call(s32[4]{0:T(128)} %pad_add_fusion.place_ref, s32[12]{0:T(128)} %pos_ref.1, bf16[12,48,1664]{2,1,0:T(8,128)(2,1)} %img_ref.1, bf16[12,64,1280]{2,1,0:T(8,128)(2,1)} %txt_ref.1, f32[1664]{0:T(1024)} %ig_ref.3, f32[1280]{0:T(1024)} %tg_ref.3), custom_call_target="tpu_custom_call" | custom-call | flops 19415040 | bytes 3883008 | tf_op jit(solution)/shard_map/pallas_call | solution.py:131
  22.4 6.7 %all-gather.theirs_ref = bf16[64,768]{1,0:T(8,128)(2,1)S(1)} all-gather(bf16[32,768]{1,0:T(8,128)(2,1)} %get-tuple-element.19), channel_id=2, replica_groups={{0,320},{128,448},{256,64},{384,192},{1,321},{129,449},{257,65},{385,19..., dimensions={0}, use_global_device_ids=true | all-gather | bytes 147456 | tf_op jit(solution)/shard_map/all_gather | solution.py:443
  29.2 3.3 %all-to-all-done = bf16[32,8,960]{2,1,0:T(8,128)(2,1)S(1)} async-done(((bf16[32,8,960]{2,1,0:T(8,128)(2,1)}), bf16[32,8,960]{2,1,0:T(8,128)(2,1)S(1)}, u32[]{:S(2)}, u32[]{:S(2)}) %all-to-all-start) | async-done | bytes 491552 | tf_op jit(solution)/shard_map/all_to_all | solution.py:21
  32.5 4.6 %all-gather.1 = bf16[64,8,960]{2,1,0:T(8,128)(2,1)S(1)} all-gather(bf16[32,8,960]{2,1,0:T(8,128)(2,1)S(1)} %all-to-all-done), channel_id=3, replica_groups=mesh['t'=4,'h'=2,'z'=8,'x'=4,'c'=2] {'c'}, dimensions={0}, use_global_device_ids=true | all-gather | bytes 1474560 | tf_op jit(solution)/shard_map/all_gather | solution.py:440
  37.8 1.7 %shard_map.104 = bf16[192,640]{1,0:T(8,128)(2,1)} custom-call(s32[4]{0:T(128)S(1)} %copy-done.3, bf16[32,768]{1,0:T(8,128)(2,1)S(1)} %copy-done, bf16[64,768]{1,0:T(8,128)(2,1)S(1)} %all-gather.theirs_ref, bf16[512,960]{1,0:T(8,128)(2,1)S(1)} %bitcast.34), custom_call_target="tpu_custom_call" | custom-call | tf_op jit(solution)/shard_map/pallas_call | solution.py:32
  39.5 6.8 %all-to-all-start.1 = ((bf16[8,24,640]{2,1,0:T(8,128)(2,1)}), bf16[8,24,640]{2,1,0:T(8,128)(2,1)S(1)}, u32[]{:S(2)}, u32[]{:S(2)}) async-start(bf16[8,24,640]{2,1,0:T(8,128)(2,1)} %bitcast.5), calls=%async_computation.1 | async-start | bytes 491520 | tf_op jit(solution)/shard_map/all_to_all | solution.py:21
  46.5 10.4 %all-to-all-done.1 = bf16[8,24,640]{2,1,0:T(8,128)(2,1)S(1)} async-done(((bf16[8,24,640]{2,1,0:T(8,128)(2,1)}), bf16[8,24,640]{2,1,0:T(8,128)(2,1)S(1)}, u32[]{:S(2)}, u32[]{:S(2)}) %all-to-all-start.1) | async-done | bytes 245792 | tf_op jit(solution)/shard_map/all_to_all | solution.py:21
  58.6 5.2 %all-to-all-start.2 = ((bf16[32,8,1024]{2,1,0:T(8,128)(2,1)}), bf16[32,8,1024]{2,1,0:T(8,128)(2,1)S(1)}, u32[]{:S(2)}, u32[]{:S(2)}) async-start(bf16[32,8,1024]{2,1,0:T(8,128)(2,1)} %bitcast.8), calls=%async_computation.2 | async-start | bytes 1048576 | tf_op jit(solution)/shard_map/all_to_all | solution.py:21
  66.3 2.8 %collective-permute-start = (bf16[512,480]{1,0:T(8,128)(2,1)}, bf16[512,480]{1,0:T(8,128)(2,1)S(1)}, u32[]{:S(2)}, u32[]{:S(2)}) collective-permute-start(bf16[512,480]{1,0:T(8,128)(2,1)} %copy.36), channel_id=1, source_target_pairs={{0,64},{64,0},{1,65},{65,1},{2,66},{66,2},{3,67},{67,3},{4,68},{68... | collective-permute-start | bytes 1474568 | tf_op jit(solution)/shard_map/ppermute | solution.py:472
  69.9 8.4 %all-to-all-done.2 = bf16[32,8,1024]{2,1,0:T(8,128)(2,1)S(1)} async-done(((bf16[32,8,1024]{2,1,0:T(8,128)(2,1)}), bf16[32,8,1024]{2,1,0:T(8,128)(2,1)S(1)}, u32[]{:S(2)}, u32[]{:S(2)}) %all-to-all-start.2) | async-done | bytes 524320 | tf_op jit(solution)/shard_map/all_to_all | solution.py:21
  78.4 6.1 %all-gather.2 = bf16[32,8,1024]{2,1,0:T(8,128)(2,1)S(1)} all-gather(bf16[16,8,1024]{2,1,0:T(8,128)(2,1)S(1)} %get-tuple-element.36), channel_id=4, replica_groups=mesh['t'=4,'h'=2,'z'=8,'x'=4,'c'=2] {'c'}, dimensions={0}, use_global_device_ids=true | all-gather | bytes 786432 | tf_op jit(solution)/shard_map/all_gather | solution.py:26
  84.4 10.9 %collective-permute-done.other_ref = bf16[512,480]{1,0:T(8,128)(2,1)S(1)} collective-permute-done((bf16[512,480]{1,0:T(8,128)(2,1)}, bf16[512,480]{1,0:T(8,128)(2,1)S(1)}, u32[]{:S(2)}, u32[]{:S(2)}) %collective-permute-start) | collective-permute-done | bytes 491552 | tf_op jit(solution)/shard_map/ppermute | solution.py:472
  95.5 4.4 %all-gather.3 = bf16[32,8,1024]{2,1,0:T(8,128)(2,1)S(1)} all-gather(bf16[16,8,1024]{2,1,0:T(8,128)(2,1)S(1)} %get-tuple-element.35), channel_id=5, replica_groups=mesh['t'=4,'h'=2,'z'=8,'x'=4,'c'=2] {'c'}, dimensions={0}, use_global_device_ids=true | all-gather | bytes 786432 | tf_op jit(solution)/shard_map/all_gather | solution.py:26
  100.0 2.1 %shard_map.106 = (f32[48,512]{1,0:T(8,128)S(1)}, f32[256,128]{1,0:T(8,128)}) custom-call(s32[4]{0:T(128)S(1)} %copy-done.3, f32[1]{0:T(128)S(6)} %copy.51.logit_ref, bf16[48,1280]{1,0:T(8,128)(2,1)S(1)} %get-tuple-element.20.rows_ref, bf16[256,1024]{1,0:T(8,128)(2,1)S(1)} %bitcast.39, bf16[256,1024]{1,0:T(8,128)(2,1)S(1)} %bitcast.37, ...), custom_call_target="tpu_custom_call" | custom-call | tf_op jit(solution)/shard_map/pallas_call | solution.py:32
  102.1 10.0 %all-to-all-start.3 = ((f32[64,4,128]{2,1,0:T(4,128)}), f32[64,4,128]{2,1,0:T(4,128)S(1)}, u32[]{:S(2)}, u32[]{:S(2)}) async-start(f32[64,4,128]{2,1,0:T(4,128)} %bitcast.14), calls=%async_computation.3 | async-start | bytes 262144 | tf_op jit(solution)/shard_map/all_to_all | solution.py:21
  112.5 10.8 %all-to-all-done.3 = f32[64,4,128]{2,1,0:T(4,128)S(1)} async-done(((f32[64,4,128]{2,1,0:T(4,128)}), f32[64,4,128]{2,1,0:T(4,128)S(1)}, u32[]{:S(2)}, u32[]{:S(2)}) %all-to-all-start.3) | async-done | bytes 131104 | tf_op jit(solution)/shard_map/all_to_all | solution.py:21
  123.3 2.0 %shard_map.107 = bf16[384,384]{1,0:T(8,128)(2,1)} custom-call(s32[4]{0:T(128)S(1)} %copy-done.3, f32[1]{0:T(128)S(6)} %copy.51.logit_ref, f32[48,512]{1,0:T(8,128)S(1)} %get-tuple-element.25.scores_ref, f32[256,128]{1,0:T(8,128)S(1)} %bitcast.46, s32[48,1]{1,0:T(8,128)S(1)} %convert_element_type.40.row_pos_ref, ...), custom_call_target="tpu_custom_call" | custom-call | tf_op jit(solution)/shard_map/pallas_call | solution.py:32
  125.3 3.4 %all-to-all-start.4 = ((bf16[8,48,384]{2,1,0:T(8,128)(2,1)}), bf16[8,48,384]{2,1,0:T(8,128)(2,1)S(1)}, u32[]{:S(2)}, u32[]{:S(2)}) async-start(bf16[8,48,384]{2,1,0:T(8,128)(2,1)} %bitcast.19), calls=%async_computation.4 | async-start | bytes 589824 | tf_op jit(solution)/shard_map/all_to_all | solution.py:21
  128.8 12.9 %all-to-all-done.4 = bf16[8,48,384]{2,1,0:T(8,128)(2,1)S(1)} async-done(((bf16[8,48,384]{2,1,0:T(8,128)(2,1)}), bf16[8,48,384]{2,1,0:T(8,128)(2,1)S(1)}, u32[]{:S(2)}, u32[]{:S(2)}) %all-to-all-start.4) | async-done | bytes 294944 | tf_op jit(solution)/shard_map/all_to_all | solution.py:21
  141.7 2.4 %shard_map.108 = (bf16[128,768]{1,0:T(8,128)(2,1)}, f32[8,128]{1,0:T(8,128)S(1)}) custom-call(s32[4]{0:T(128)S(1)} %copy-done.3, bf16[384,384]{1,0:T(8,128)(2,1)S(1)} %bitcast.43, bf16[48,160]{1,0:T(8,128)(2,1)S(1)} %constant_dynamic-slice_fusion.2.unit_ref, bf16[512,960]{1,0:T(8,128)(2,1)S(1)} %bitcast.36, bf16[512,480]{1,0:T(8,128)(2,1)S(1)} %collective-permute-done.other_ref), custom_call_target="tpu_custom_call" | custom-call | tf_op jit(solution)/shard_map/pallas_call | solution.py:32
  144.1 3.4 %all-to-all-start.5 = ((bf16[8,16,768]{2,1,0:T(8,128)(2,1)}), bf16[8,16,768]{2,1,0:T(8,128)(2,1)S(1)}, u32[]{:S(2)}, u32[]{:S(2)}) async-start(bf16[8,16,768]{2,1,0:T(8,128)(2,1)} %bitcast.22), calls=%async_computation.5 | async-start | bytes 393216 | tf_op jit(solution)/shard_map/all_to_all | solution.py:21
  150.2 7.0 %all-to-all-done.5 = bf16[8,16,768]{2,1,0:T(8,128)(2,1)S(1)} async-done(((bf16[8,16,768]{2,1,0:T(8,128)(2,1)}), bf16[8,16,768]{2,1,0:T(8,128)(2,1)S(1)}, u32[]{:S(2)}, u32[]{:S(2)}) %all-to-all-start.5) | async-done | bytes 196640 | tf_op jit(solution)/shard_map/all_to_all | solution.py:21
  157.2 2.0 %shard_map.109 = (bf16[144,1664]{1,0:T(8,128)(2,1)}, bf16[192,1280]{1,0:T(8,128)(2,1)}) custom-call(bf16[128,768]{1,0:T(8,128)(2,1)S(1)} %bitcast.45, f32[8,128]{1,0:T(8,128)S(1)} %get-tuple-element.30.inv_ref, bf16[144,1664]{1,0:T(8,128)(2,1)S(1)} %bitcast.42, bf16[192,1280]{1,0:T(8,128)(2,1)S(1)} %bitcast.41, f32[1664]{0:T(1024)S(1)} %copy-done.1, ...), custom_call_target="tpu_custom_call" | custom-call | tf_op jit(solution)/shard_map/pallas_call | solution.py:32
  (56 shorter events, 11.0 us)
Async XLA Ops:
  2.5 30.0 %all-to-all-start = ((bf16[32,8,960]{2,1,0:T(8,128)(2,1)}), bf16[32,8,960]{2,1,0:T(8,128)(2,1)S(1)}, u32[]{:S(2)}, u32[]{:S(2)}) async-start(bf16[32,8,960]{2,1,0:T(8,128)(2,1)} %broadcast_in_dim.39), calls=%async_computation | async-start | bytes 1048576 | tf_op jit(solution)/shard_map/all_to_all | solution.py:21
  16.8 12.3 %copy-start.4 = (s32[12]{0:T(128)S(1)}, s32[12]{0:T(128)}, u32[]{:S(2)}) copy-start(s32[12]{0:T(128)} %pos_ref.1) | copy-start | bytes 148
  16.8 20.2 %copy-start.3 = (s32[4]{0:T(128)S(1)}, s32[4]{0:T(128)}, u32[]{:S(2)}) copy-start(s32[4]{0:T(128)} %pad_add_fusion.place_ref) | copy-start | bytes 52
  37.0 0.8 copy-start
  39.5 17.4 %all-to-all-start.1 = ((bf16[8,24,640]{2,1,0:T(8,128)(2,1)}), bf16[8,24,640]{2,1,0:T(8,128)(2,1)S(1)}, u32[]{:S(2)}, u32[]{:S(2)}) async-start(bf16[8,24,640]{2,1,0:T(8,128)(2,1)} %bitcast.5), calls=%async_computation.1 | async-start | bytes 491520 | tf_op jit(solution)/shard_map/all_to_all | solution.py:21
  58.6 19.8 %all-to-all-start.2 = ((bf16[32,8,1024]{2,1,0:T(8,128)(2,1)}), bf16[32,8,1024]{2,1,0:T(8,128)(2,1)S(1)}, u32[]{:S(2)}, u32[]{:S(2)}) async-start(bf16[32,8,1024]{2,1,0:T(8,128)(2,1)} %bitcast.8), calls=%async_computation.2 | async-start | bytes 1048576 | tf_op jit(solution)/shard_map/all_to_all | solution.py:21
  66.3 29.1 %collective-permute-start = (bf16[512,480]{1,0:T(8,128)(2,1)}, bf16[512,480]{1,0:T(8,128)(2,1)S(1)}, u32[]{:S(2)}, u32[]{:S(2)}) collective-permute-start(bf16[512,480]{1,0:T(8,128)(2,1)} %copy.36), channel_id=1, source_target_pairs={{0,64},{64,0},{1,65},{65,1},{2,66},{66,2},{3,67},{67,3},{4,68},{68... | collective-permute-start | bytes 1474568 | tf_op jit(solution)/shard_map/ppermute | solution.py:472
  102.1 21.1 %all-to-all-start.3 = ((f32[64,4,128]{2,1,0:T(4,128)}), f32[64,4,128]{2,1,0:T(4,128)S(1)}, u32[]{:S(2)}, u32[]{:S(2)}) async-start(f32[64,4,128]{2,1,0:T(4,128)} %bitcast.14), calls=%async_computation.3 | async-start | bytes 262144 | tf_op jit(solution)/shard_map/all_to_all | solution.py:21
  125.3 16.4 %all-to-all-start.4 = ((bf16[8,48,384]{2,1,0:T(8,128)(2,1)}), bf16[8,48,384]{2,1,0:T(8,128)(2,1)S(1)}, u32[]{:S(2)}, u32[]{:S(2)}) async-start(bf16[8,48,384]{2,1,0:T(8,128)(2,1)} %bitcast.19), calls=%async_computation.4 | async-start | bytes 589824 | tf_op jit(solution)/shard_map/all_to_all | solution.py:21
  141.7 15.4 %copy-start.1 = (f32[1664]{0:T(1024)S(1)}, f32[1664]{0:T(1024)}, u32[]{:S(2)}) copy-start(f32[1664]{0:T(1024)} %ig_ref.3) | copy-start | bytes 19972
  141.7 15.4 %copy-start.2 = (f32[1280]{0:T(1024)S(1)}, f32[1280]{0:T(1024)}, u32[]{:S(2)}) copy-start(f32[1280]{0:T(1024)} %tg_ref.3) | copy-start | bytes 15364
  144.1 13.0 %all-to-all-start.5 = ((bf16[8,16,768]{2,1,0:T(8,128)(2,1)}), bf16[8,16,768]{2,1,0:T(8,128)(2,1)S(1)}, u32[]{:S(2)}, u32[]{:S(2)}) async-start(bf16[8,16,768]{2,1,0:T(8,128)(2,1)} %bitcast.22), calls=%async_computation.5 | async-start | bytes 393216 | tf_op jit(solution)/shard_map/all_to_all | solution.py:21

commit v14 on v13

--- a/solution.py
+++ b/solution.py
@@ -150,8 +150,8 @@
     )(place, positive, image_in, text_in, img_gain, txt_gain)
 
 
-def weight_quarter(w_ref, a):
-    return jnp.concatenate([w_ref[k + 128 * a : k + 128 * a + 128, :] for k in (0, 256)], 0)
+def weight_quarter(core_refs, a):
+    return jnp.concatenate([ref[128 * a : 128 * a + 128, :] for ref in core_refs], 0)
 
 
 def project_kernel(place_ref, mine_ref, theirs_ref, w_ref, out_ref):
@@ -171,7 +171,7 @@
             for t in range(4):
                 pieces += [img_rows[3 * t : 3 * t + 3], txt_rows[3 * t : 3 * t + 3]]
         left = jnp.concatenate(pieces, 0).astype(BF)
-        quarter = weight_quarter(w_ref, a)
+        quarter = weight_quarter((w_ref.at[:256], w_ref.at[256:]), a)
         for j in range(3):
             part += jnp.dot(
                 left[:, 256 * j : 256 * j + 256],
@@ -349,7 +349,9 @@
         out_ref[48 * k : 48 * k + 48, :] = way
 
 
-def back_kernel(place_ref, got_ref, unit_ref, w_ref, other_ref, out_ref, loss_ref):
+def back_kernel(
+    place_ref, got_ref, unit_ref, w_ref, first_ref, second_ref, out_ref, loss_ref
+):
     width = unit_ref.shape[1]
     got = [got_ref[48 * k : 48 * k + 48, :].astype(F32) for k in range(8)]
     riders = [[part[:, 2 * width + k : 2 * width + k + 1] for k in range(9)] for part in got]
@@ -380,13 +382,13 @@
 
     own, other = [], []
     for a in range(2):
-        quarter = weight_quarter(w_ref, a)
+        quarter = weight_quarter((w_ref.at[:256], w_ref.at[256:]), a)
         columns = []
         for j in range(3):
             pair = quarter[:, 2 * width * j : 2 * width * j + 2 * width]
             columns.append(jnp.where(first, pair[:, :width], pair[:, width:]))
         own.append(features(columns))
-        quarter = weight_quarter(other_ref, a)
+        quarter = weight_quarter((first_ref, second_ref), a)
         other.append(features([quarter[:, width * j : width * j + width] for j in range(3)]))
     mixed = [jnp.where(first, x, y) for x, y in zip(own + other, other + own)]
     blank = jnp.zeros((1, 768), F32)
@@ -466,12 +468,16 @@
         smem=(0,),
     )
     half = width // 2
+    swap = [(0, 1), (1, 0)]
+
+    def columns_for_other(rows):
+        parts = rows.reshape(256, 3, 2, half)
+        return jnp.where(h_index == 0, parts[:, :, 1], parts[:, :, 0]).reshape(256, 3 * half)
+
     w_held, far = lax.optimization_barrier((w, far))
-    parts = w_held.reshape(512, 3, 2, half)
-    w_other = jnp.where(h_index == 0, parts[:, :, 1], parts[:, :, 0]).reshape(512, 3 * half)
-    w_other = lax.ppermute(w_other, "h", [(0, 1), (1, 0)])
+    w_first = lax.ppermute(columns_for_other(w_held[:256]), "h", swap)
     fa, fb = both_cores(exchange(far.reshape(32, 8, 1024), ZX))
-    fa, w_other = lax.optimization_barrier((fa, w_other))
+    fa, w_first = lax.optimization_barrier((fa, w_first))
 
     scores, far = kernel_call(
         score_kernel,
@@ -479,7 +485,10 @@
         [place, logit_scale, rows, fa, fb, row_pos],
         smem=(0, 1),
     )
+    w_held, far = lax.optimization_barrier((w, far))
+    w_second = lax.ppermute(columns_for_other(w_held[256:]), "h", swap)
     far = exchange(far.reshape(64, 4, 128), ZXC).reshape(256, 128)
+    far, w_second = lax.optimization_barrier((far, w_second))
 
     item_pos = jnp.concatenate([fa.reshape(32, 8, 1024)[:, 3, 768:774], fb.reshape(32, 8, 1024)[:, 3, 768:774]])
     item_pos = item_pos.astype(F32)
@@ -497,7 +506,7 @@
     pool, loss = kernel_call(
         back_kernel,
         [((128, 768), BF), ((8, 128), F32)],
-        [place, got, unit_part, w, w_other],
+        [place, got, unit_part, w, w_first, w_second],
         smem=(0,),
     )
     mean_loss = loss[0, :1]

time: 160 us -> 158 us (0.988)
  waiting for transfers between devices: 63.8 us -> 58 us
  starting transfers between devices: 45.3 us -> 48.2 us
    all_to_all x6, waiting for transfers between devices: 52.9 us -> 43.2 us  [exchange(): return lax.all_to_all(blocks, axes, 0, 0, tiled=True)]
    ppermute x1 -> x2, waiting for transfers between devices: 10.9 us -> 14.8 us  [the longest x1 14.8 us: per_device(): w_second = lax.ppermute(columns_for_other(w_held[256:]), 'h', swap)]
    ppermute x1 -> x2, starting transfers between devices: 2.78 us -> 5.63 us  [the longest x1 2.84 us: per_device(): w_second = lax.ppermute(columns_for_other(w_held[256:]), 'h', swap)]
  transfers between devices with their start and end apart: 7 -> 8, of which waited for: 7 -> 6; matrix products, arithmetic and copies ran while one was open for 4% -> 5% of each run, Pallas kernels for 3% -> 4%
where the time goes in v14:
time: 158 us; the launch traced here: 156 us
  waiting for transfers between devices  58 us (37%)
  starting transfers between devices  48.2 us (31%)
  blocking collectives  20.7 us (13%)
  Pallas kernels  17.5 us (11%)
  local copies, waits for them, and re-layouts  7.55 us (5%)
  other arithmetic  2.89 us (2%)
    all_to_all x6, waiting for transfers between devices, exchange(): return lax.all_to_all(blocks, axes, 0, 0, tiled=True)  43.2 us
    all_to_all x6, starting transfers between devices, exchange(): return lax.all_to_all(blocks, axes, 0, 0, tiled=True)  42.5 us
    ppermute x1, waiting for transfers between devices, per_device(): w_second = lax.ppermute(columns_for_other(w_held[256:]), 'h', swap)  14.8 us
    pallas_call x6, Pallas kernels, kernel_call(): pl.pallas_call(body, out_shape=[jax.ShapeDtypeStruct(shape, kind) for sha...  12 us
    all_gather x2, blocking collectives, both_cores(): lax.all_gather(part, 'c', axis=0)  9.48 us
    all_gather x1, blocking collectives, per_device(): lax.all_gather(theirs, Y, axis=0, axis_index_groups=[[0, 6], [1, 7], [2,...  6.68 us
    pallas_call x1, Pallas kernels, pool_call(): pl.pallas_call(pool_kernel, out_shape=[jax.ShapeDtypeStruct((32, 768), BF...  5.56 us
    all_gather x1, blocking collectives, per_device(): w = lax.all_gather(exchange(w, ZX), 'c', axis=0).reshape(512, 3 * width)  4.56 us
  transfers between devices with their start and end apart: 8, of which 6 were waited for; matrix products, arithmetic and copies ran while one was open for 5% of the time, Pallas kernels for 4%

profile of v14, /device:TPU:1, one launch (start us, length us, event | category | flops | bytes accessed | tf_op | source)
XLA Modules:
  0.0 156.3 jit_solution(4990824237434101606)
XLA Ops:
  2.5 13.7 %all-to-all-start = ((bf16[32,8,960]{2,1,0:T(8,128)(2,1)}), bf16[32,8,960]{2,1,0:T(8,128)(2,1)S(1)}, u32[]{:S(2)}, u32[]{:S(2)}) async-start(bf16[32,8,960]{2,1,0:T(8,128)(2,1)} %broadcast_in_dim.39), calls=%async_computation | async-start | bytes 1048576 | tf_op jit(solution)/shard_map/all_to_all | solution.py:21
  16.8 5.6 %shard_map.103 = (bf16[32,768]{1,0:T(8,128)(2,1)}, bf16[32,768]{1,0:T(8,128)(2,1)}) custom-call(s32[4]{0:T(128)} %pad_add_fusion.place_ref, s32[12]{0:T(128)} %pos_ref.1, bf16[12,48,1664]{2,1,0:T(8,128)(2,1)} %img_ref.1, bf16[12,64,1280]{2,1,0:T(8,128)(2,1)} %txt_ref.1, f32[1664]{0:T(1024)} %ig_ref.3, f32[1280]{0:T(1024)} %tg_ref.3), custom_call_target="tpu_custom_call" | custom-call | flops 19415040 | bytes 3883008 | tf_op jit(solution)/shard_map/pallas_call | solution.py:131
  22.4 6.7 %all-gather.theirs_ref = bf16[64,768]{1,0:T(8,128)(2,1)S(1)} all-gather(bf16[32,768]{1,0:T(8,128)(2,1)} %get-tuple-element.23), channel_id=2, replica_groups={{0,320},{128,448},{256,64},{384,192},{1,321},{129,449},{257,65},{385,19..., dimensions={0}, use_global_device_ids=true | all-gather | bytes 147456 | tf_op jit(solution)/shard_map/all_gather | solution.py:445
  29.2 3.3 %all-to-all-done = bf16[32,8,960]{2,1,0:T(8,128)(2,1)S(1)} async-done(((bf16[32,8,960]{2,1,0:T(8,128)(2,1)}), bf16[32,8,960]{2,1,0:T(8,128)(2,1)S(1)}, u32[]{:S(2)}, u32[]{:S(2)}) %all-to-all-start) | async-done | bytes 491552 | tf_op jit(solution)/shard_map/all_to_all | solution.py:21
  32.5 4.6 %all-gather.1 = bf16[64,8,960]{2,1,0:T(8,128)(2,1)S(1)} all-gather(bf16[32,8,960]{2,1,0:T(8,128)(2,1)S(1)} %all-to-all-done), channel_id=3, replica_groups=mesh['t'=4,'h'=2,'z'=8,'x'=4,'c'=2] {'c'}, dimensions={0}, use_global_device_ids=true | all-gather | bytes 1474560 | tf_op jit(solution)/shard_map/all_gather | solution.py:442
  37.9 1.7 %shard_map.104 = bf16[192,640]{1,0:T(8,128)(2,1)} custom-call(s32[4]{0:T(128)S(1)} %copy-done.3, bf16[32,768]{1,0:T(8,128)(2,1)S(1)} %copy-done, bf16[64,768]{1,0:T(8,128)(2,1)S(1)} %all-gather.theirs_ref, bf16[512,960]{1,0:T(8,128)(2,1)S(1)} %bitcast.36), custom_call_target="tpu_custom_call" | custom-call | tf_op jit(solution)/shard_map/pallas_call | solution.py:32
  39.6 6.8 %all-to-all-start.1 = ((bf16[8,24,640]{2,1,0:T(8,128)(2,1)}), bf16[8,24,640]{2,1,0:T(8,128)(2,1)S(1)}, u32[]{:S(2)}, u32[]{:S(2)}) async-start(bf16[8,24,640]{2,1,0:T(8,128)(2,1)} %bitcast.5), calls=%async_computation.1 | async-start | bytes 491520 | tf_op jit(solution)/shard_map/all_to_all | solution.py:21
  46.5 10.4 %all-to-all-done.1 = bf16[8,24,640]{2,1,0:T(8,128)(2,1)S(1)} async-done(((bf16[8,24,640]{2,1,0:T(8,128)(2,1)}), bf16[8,24,640]{2,1,0:T(8,128)(2,1)S(1)}, u32[]{:S(2)}, u32[]{:S(2)}) %all-to-all-start.1) | async-done | bytes 245792 | tf_op jit(solution)/shard_map/all_to_all | solution.py:21
  58.6 5.1 %all-to-all-start.2 = ((bf16[32,8,1024]{2,1,0:T(8,128)(2,1)}), bf16[32,8,1024]{2,1,0:T(8,128)(2,1)S(1)}, u32[]{:S(2)}, u32[]{:S(2)}) async-start(bf16[32,8,1024]{2,1,0:T(8,128)(2,1)} %bitcast.8), calls=%async_computation.2 | async-start | bytes 1048576 | tf_op jit(solution)/shard_map/all_to_all | solution.py:21
  65.9 2.8 %collective-permute-start = (bf16[256,480]{1,0:T(8,128)(2,1)S(1)}, bf16[256,480]{1,0:T(8,128)(2,1)S(1)}, u32[]{:S(2)}, u32[]{:S(2)}) collective-permute-start(bf16[256,480]{1,0:T(8,128)(2,1)S(1)} %copy.40), channel_id=1, source_target_pairs={{0,64},{64,0},{1,65},{65,1},{2,66},{66,2},{3,67},{67,3},{4,68},{68... | collective-permute-start | bytes 737288 | tf_op jit(solution)/shard_map/ppermute | solution.py:478
  68.7 9.6 %all-to-all-done.2 = bf16[32,8,1024]{2,1,0:T(8,128)(2,1)S(1)} async-done(((bf16[32,8,1024]{2,1,0:T(8,128)(2,1)}), bf16[32,8,1024]{2,1,0:T(8,128)(2,1)S(1)}, u32[]{:S(2)}, u32[]{:S(2)}) %all-to-all-start.2) | async-done | bytes 524320 | tf_op jit(solution)/shard_map/all_to_all | solution.py:21
  78.4 6.1 %all-gather.2 = bf16[32,8,1024]{2,1,0:T(8,128)(2,1)S(1)} all-gather(bf16[16,8,1024]{2,1,0:T(8,128)(2,1)S(1)} %get-tuple-element.44), channel_id=4, replica_groups=mesh['t'=4,'h'=2,'z'=8,'x'=4,'c'=2] {'c'}, dimensions={0}, use_global_device_ids=true | all-gather | bytes 786432 | tf_op jit(solution)/shard_map/all_gather | solution.py:26
  84.4 3.4 %all-gather.3 = bf16[32,8,1024]{2,1,0:T(8,128)(2,1)S(1)} all-gather(bf16[16,8,1024]{2,1,0:T(8,128)(2,1)S(1)} %get-tuple-element.43), channel_id=5, replica_groups=mesh['t'=4,'h'=2,'z'=8,'x'=4,'c'=2] {'c'}, dimensions={0}, use_global_device_ids=true | all-gather | bytes 786432 | tf_op jit(solution)/shard_map/all_gather | solution.py:26
  87.9 2.1 %shard_map.106 = (f32[48,512]{1,0:T(8,128)S(1)}, f32[256,128]{1,0:T(8,128)}) custom-call(s32[4]{0:T(128)S(1)} %copy-done.3, f32[1]{0:T(128)S(6)} %copy.57.logit_ref, bf16[48,1280]{1,0:T(8,128)(2,1)S(1)} %get-tuple-element.24.rows_ref, bf16[256,1024]{1,0:T(8,128)(2,1)S(1)} %bitcast.42, bf16[256,1024]{1,0:T(8,128)(2,1)S(1)} %bitcast.40, ...), custom_call_target="tpu_custom_call" | custom-call | tf_op jit(solution)/shard_map/pallas_call | solution.py:32
  90.0 10.0 %all-to-all-start.3 = ((f32[64,4,128]{2,1,0:T(4,128)}), f32[64,4,128]{2,1,0:T(4,128)S(1)}, u32[]{:S(2)}, u32[]{:S(2)}) async-start(f32[64,4,128]{2,1,0:T(4,128)} %bitcast.14), calls=%async_computation.3 | async-start | bytes 262144 | tf_op jit(solution)/shard_map/all_to_all | solution.py:21
  102.3 2.8 %collective-permute-start.1 = (bf16[256,480]{1,0:T(8,128)(2,1)S(1)}, bf16[256,480]{1,0:T(8,128)(2,1)S(1)}, u32[]{:S(2)}, u32[]{:S(2)}) collective-permute-start(bf16[256,480]{1,0:T(8,128)(2,1)S(1)} %copy.48), channel_id=1, source_target_pairs={{0,64},{64,0},{1,65},{65,1},{2,66},{66,2},{3,67},{67,3},{4,68},{68... | collective-permute-start | bytes 737288 | tf_op jit(solution)/shard_map/ppermute | solution.py:489
  105.7 14.8 %collective-permute-done.1.second_ref = bf16[256,480]{1,0:T(8,128)(2,1)S(1)} collective-permute-done((bf16[256,480]{1,0:T(8,128)(2,1)S(1)}, bf16[256,480]{1,0:T(8,128)(2,1)S(1)}, u32[]{:S(2)}, u32[]{:S(2)}) %collective-permute-start.1) | collective-permute-done | bytes 245792 | tf_op jit(solution)/shard_map/ppermute | solution.py:489
  120.5 2.0 %shard_map.107 = bf16[384,384]{1,0:T(8,128)(2,1)} custom-call(s32[4]{0:T(128)S(1)} %copy-done.3, f32[1]{0:T(128)S(6)} %copy.57.logit_ref, f32[48,512]{1,0:T(8,128)S(1)} %get-tuple-element.29.scores_ref, f32[256,128]{1,0:T(8,128)S(1)} %bitcast.49, s32[48,1]{1,0:T(8,128)S(1)} %convert_element_type.40.row_pos_ref, ...), custom_call_target="tpu_custom_call" | custom-call | tf_op jit(solution)/shard_map/pallas_call | solution.py:32
  122.5 3.4 %all-to-all-start.4 = ((bf16[8,48,384]{2,1,0:T(8,128)(2,1)}), bf16[8,48,384]{2,1,0:T(8,128)(2,1)S(1)}, u32[]{:S(2)}, u32[]{:S(2)}) async-start(bf16[8,48,384]{2,1,0:T(8,128)(2,1)} %bitcast.21), calls=%async_computation.4 | async-start | bytes 589824 | tf_op jit(solution)/shard_map/all_to_all | solution.py:21
  126.0 12.9 %all-to-all-done.4 = bf16[8,48,384]{2,1,0:T(8,128)(2,1)S(1)} async-done(((bf16[8,48,384]{2,1,0:T(8,128)(2,1)}), bf16[8,48,384]{2,1,0:T(8,128)(2,1)S(1)}, u32[]{:S(2)}, u32[]{:S(2)}) %all-to-all-start.4) | async-done | bytes 294944 | tf_op jit(solution)/shard_map/all_to_all | solution.py:21
  138.9 2.4 %shard_map.108 = (bf16[128,768]{1,0:T(8,128)(2,1)}, f32[8,128]{1,0:T(8,128)S(1)}) custom-call(s32[4]{0:T(128)S(1)} %copy-done.3, bf16[384,384]{1,0:T(8,128)(2,1)S(1)} %bitcast.46, bf16[48,160]{1,0:T(8,128)(2,1)S(1)} %constant_dynamic-slice_fusion.2.unit_ref, bf16[512,960]{1,0:T(8,128)(2,1)S(1)} %bitcast.39, ...), custom_call_target="tpu_custom_call" | custom-call | tf_op jit(solution)/shard_map/pallas_call | solution.py:32
  141.3 3.4 %all-to-all-start.5 = ((bf16[8,16,768]{2,1,0:T(8,128)(2,1)}), bf16[8,16,768]{2,1,0:T(8,128)(2,1)S(1)}, u32[]{:S(2)}, u32[]{:S(2)}) async-start(bf16[8,16,768]{2,1,0:T(8,128)(2,1)} %bitcast.24), calls=%async_computation.5 | async-start | bytes 393216 | tf_op jit(solution)/shard_map/all_to_all | solution.py:21
  147.4 6.9 %all-to-all-done.5 = bf16[8,16,768]{2,1,0:T(8,128)(2,1)S(1)} async-done(((bf16[8,16,768]{2,1,0:T(8,128)(2,1)}), bf16[8,16,768]{2,1,0:T(8,128)(2,1)S(1)}, u32[]{:S(2)}, u32[]{:S(2)}) %all-to-all-start.5) | async-done | bytes 196640 | tf_op jit(solution)/shard_map/all_to_all | solution.py:21
  154.3 2.0 %shard_map.109 = (bf16[144,1664]{1,0:T(8,128)(2,1)}, bf16[192,1280]{1,0:T(8,128)(2,1)}) custom-call(bf16[128,768]{1,0:T(8,128)(2,1)S(1)} %bitcast.48, f32[8,128]{1,0:T(8,128)S(1)} %get-tuple-element.38.inv_ref, bf16[144,1664]{1,0:T(8,128)(2,1)S(1)} %bitcast.45, bf16[192,1280]{1,0:T(8,128)(2,1)S(1)} %bitcast.44, f32[1664]{0:T(1024)S(1)} %copy-done.1, ...), custom_call_target="tpu_custom_call" | custom-call | tf_op jit(solution)/shard_map/pallas_call | solution.py:32
  (63 shorter events, 12.1 us)
Async XLA Ops:
  2.5 30.0 %all-to-all-start = ((bf16[32,8,960]{2,1,0:T(8,128)(2,1)}), bf16[32,8,960]{2,1,0:T(8,128)(2,1)S(1)}, u32[]{:S(2)}, u32[]{:S(2)}) async-start(bf16[32,8,960]{2,1,0:T(8,128)(2,1)} %broadcast_in_dim.39), calls=%async_computation | async-start | bytes 1048576 | tf_op jit(solution)/shard_map/all_to_all | solution.py:21
  16.8 12.3 %copy-start.4 = (s32[12]{0:T(128)S(1)}, s32[12]{0:T(128)}, u32[]{:S(2)}) copy-start(s32[12]{0:T(128)} %pos_ref.1) | copy-start | bytes 148
  16.8 20.2 %copy-start.3 = (s32[4]{0:T(128)S(1)}, s32[4]{0:T(128)}, u32[]{:S(2)}) copy-start(s32[4]{0:T(128)} %pad_add_fusion.place_ref) | copy-start | bytes 52
  37.1 0.8 copy-start
  39.6 17.4 %all-to-all-start.1 = ((bf16[8,24,640]{2,1,0:T(8,128)(2,1)}), bf16[8,24,640]{2,1,0:T(8,128)(2,1)S(1)}, u32[]{:S(2)}, u32[]{:S(2)}) async-start(bf16[8,24,640]{2,1,0:T(8,128)(2,1)} %bitcast.5), calls=%async_computation.1 | async-start | bytes 491520 | tf_op jit(solution)/shard_map/all_to_all | solution.py:21
  58.6 19.8 %all-to-all-start.2 = ((bf16[32,8,1024]{2,1,0:T(8,128)(2,1)}), bf16[32,8,1024]{2,1,0:T(8,128)(2,1)S(1)}, u32[]{:S(2)}, u32[]{:S(2)}) async-start(bf16[32,8,1024]{2,1,0:T(8,128)(2,1)} %bitcast.8), calls=%async_computation.2 | async-start | bytes 1048576 | tf_op jit(solution)/shard_map/all_to_all | solution.py:21
  65.9 18.5 %collective-permute-start = (bf16[256,480]{1,0:T(8,128)(2,1)S(1)}, bf16[256,480]{1,0:T(8,128)(2,1)S(1)}, u32[]{:S(2)}, u32[]{:S(2)}) collective-permute-start(bf16[256,480]{1,0:T(8,128)(2,1)S(1)} %copy.40), channel_id=1, source_target_pairs={{0,64},{64,0},{1,65},{65,1},{2,66},{66,2},{3,67},{67,3},{4,68},{68... | collective-permute-start | bytes 737288 | tf_op jit(solution)/shard_map/ppermute | solution.py:478
  90.0 30.5 %all-to-all-start.3 = ((f32[64,4,128]{2,1,0:T(4,128)}), f32[64,4,128]{2,1,0:T(4,128)S(1)}, u32[]{:S(2)}, u32[]{:S(2)}) async-start(f32[64,4,128]{2,1,0:T(4,128)} %bitcast.14), calls=%async_computation.3 | async-start | bytes 262144 | tf_op jit(solution)/shard_map/all_to_all | solution.py:21
  102.3 18.2 %collective-permute-start.1 = (bf16[256,480]{1,0:T(8,128)(2,1)S(1)}, bf16[256,480]{1,0:T(8,128)(2,1)S(1)}, u32[]{:S(2)}, u32[]{:S(2)}) collective-permute-start(bf16[256,480]{1,0:T(8,128)(2,1)S(1)} %copy.48), channel_id=1, source_target_pairs={{0,64},{64,0},{1,65},{65,1},{2,66},{66,2},{3,67},{67,3},{4,68},{68... | collective-permute-start | bytes 737288 | tf_op jit(solution)/shard_map/ppermute | solution.py:489
  122.5 16.4 %all-to-all-start.4 = ((bf16[8,48,384]{2,1,0:T(8,128)(2,1)}), bf16[8,48,384]{2,1,0:T(8,128)(2,1)S(1)}, u32[]{:S(2)}, u32[]{:S(2)}) async-start(bf16[8,48,384]{2,1,0:T(8,128)(2,1)} %bitcast.21), calls=%async_computation.4 | async-start | bytes 589824 | tf_op jit(solution)/shard_map/all_to_all | solution.py:21
  138.9 15.4 %copy-start.1 = (f32[1664]{0:T(1024)S(1)}, f32[1664]{0:T(1024)}, u32[]{:S(2)}) copy-start(f32[1664]{0:T(1024)} %ig_ref.3) | copy-start | bytes 19972
  138.9 15.4 %copy-start.2 = (f32[1280]{0:T(1024)S(1)}, f32[1280]{0:T(1024)}, u32[]{:S(2)}) copy-start(f32[1280]{0:T(1024)} %tg_ref.3) | copy-start | bytes 15364
  141.3 13.0 %all-to-all-start.5 = ((bf16[8,16,768]{2,1,0:T(8,128)(2,1)}), bf16[8,16,768]{2,1,0:T(8,128)(2,1)S(1)}, u32[]{:S(2)}, u32[]{:S(2)}) async-start(bf16[8,16,768]{2,1,0:T(8,128)(2,1)} %bitcast.24), calls=%async_computation.5 | async-start | bytes 393216 | tf_op jit(solution)/shard_map/all_to_all | solution.py:21

commit v15 on v13

--- a/solution.py
+++ b/solution.py
@@ -471,7 +471,6 @@
     w_other = jnp.where(h_index == 0, parts[:, :, 1], parts[:, :, 0]).reshape(512, 3 * half)
     w_other = lax.ppermute(w_other, "h", [(0, 1), (1, 0)])
     fa, fb = both_cores(exchange(far.reshape(32, 8, 1024), ZX))
-    fa, w_other = lax.optimization_barrier((fa, w_other))
 
     scores, far = kernel_call(
         score_kernel,
@@ -480,6 +479,7 @@
         smem=(0, 1),
     )
     far = exchange(far.reshape(64, 4, 128), ZXC).reshape(256, 128)
+    far, w_other = lax.optimization_barrier((far, w_other))
 
     item_pos = jnp.concatenate([fa.reshape(32, 8, 1024)[:, 3, 768:774], fb.reshape(32, 8, 1024)[:, 3, 768:774]])
     item_pos = item_pos.astype(F32)

time: 160 us -> 142 us (0.89)
  waiting for transfers between devices: 63.8 us -> 52.9 us
  starting transfers between devices: 45.3 us -> 40.4 us
  blocking collectives: 21.7 us -> 19.5 us
    ppermute x1, waiting for transfers between devices: 10.9 us -> 1.92 us  [per_device(): w_other = lax.ppermute(w_other, 'h', [(0, 1), (1, 0)])]
    all_to_all x6, starting transfers between devices: 42.6 us -> 37.6 us  [exchange(): return lax.all_to_all(blocks, axes, 0, 0, tiled=True)]
    all_gather x2, blocking collectives: 10.4 us -> 8.22 us  [both_cores(): lax.all_gather(part, 'c', axis=0)]
    all_to_all x6, waiting for transfers between devices: 52.9 us -> 51 us  [exchange(): return lax.all_to_all(blocks, axes, 0, 0, tiled=True)]
  transfers between devices with their start and end apart: 7 -> 7, of which waited for: 7 -> 7; matrix products, arithmetic and copies ran while one was open for 4% -> 5% of each run, Pallas kernels for 3% -> 5%
where the time goes in v15:
time: 142 us; the launch traced here: 141 us
  waiting for transfers between devices  52.9 us (37%)
  starting transfers between devices  40.4 us (28%)
  blocking collectives  19.5 us (14%)
  Pallas kernels  17.5 us (12%)
  local copies, waits for them, and re-layouts  7.53 us (5%)
  other arithmetic  1.85 us (1%)
  between operations  1.46 us (1%)
    all_to_all x6, waiting for transfers between devices, exchange(): return lax.all_to_all(blocks, axes, 0, 0, tiled=True)  51 us
    all_to_all x6, starting transfers between devices, exchange(): return lax.all_to_all(blocks, axes, 0, 0, tiled=True)  37.6 us
    pallas_call x6, Pallas kernels, kernel_call(): pl.pallas_call(body, out_shape=[jax.ShapeDtypeStruct(shape, kind) for sha...  11.9 us
    all_gather x2, blocking collectives, both_cores(): lax.all_gather(part, 'c', axis=0)  8.22 us
    all_gather x1, blocking collectives, per_device(): lax.all_gather(theirs, Y, axis=0, axis_index_groups=[[0, 6], [1, 7], [2,...  6.68 us
    pallas_call x1, Pallas kernels, pool_call(): pl.pallas_call(pool_kernel, out_shape=[jax.ShapeDtypeStruct((32, 768), BF...  5.56 us
    all_gather x1, blocking collectives, per_device(): w = lax.all_gather(exchange(w, ZX), 'c', axis=0).reshape(512, 3 * width)  4.56 us
  transfers between devices with their start and end apart: 7, of which 7 were waited for; matrix products, arithmetic and copies ran while one was open for 5% of the time, Pallas kernels for 5%

profile of v15, /device:TPU:1, one launch (start us, length us, event | category | flops | bytes accessed | tf_op | source)
XLA Modules:
  0.0 141.0 jit_solution(12866249436926587035)
XLA Ops:
  2.5 13.7 %all-to-all-start = ((bf16[32,8,960]{2,1,0:T(8,128)(2,1)}), bf16[32,8,960]{2,1,0:T(8,128)(2,1)S(1)}, u32[]{:S(2)}, u32[]{:S(2)}) async-start(bf16[32,8,960]{2,1,0:T(8,128)(2,1)} %broadcast_in_dim.39), calls=%async_computation | async-start | bytes 1048576 | tf_op jit(solution)/shard_map/all_to_all | solution.py:21
  16.8 5.6 %shard_map.103 = (bf16[32,768]{1,0:T(8,128)(2,1)}, bf16[32,768]{1,0:T(8,128)(2,1)}) custom-call(s32[4]{0:T(128)} %pad_add_fusion.place_ref, s32[12]{0:T(128)} %pos_ref.1, bf16[12,48,1664]{2,1,0:T(8,128)(2,1)} %img_ref.1, bf16[12,64,1280]{2,1,0:T(8,128)(2,1)} %txt_ref.1, f32[1664]{0:T(1024)} %ig_ref.3, f32[1280]{0:T(1024)} %tg_ref.3), custom_call_target="tpu_custom_call" | custom-call | flops 19415040 | bytes 3883008 | tf_op jit(solution)/shard_map/pallas_call | solution.py:131
  22.4 6.7 %all-gather.theirs_ref = bf16[64,768]{1,0:T(8,128)(2,1)S(1)} all-gather(bf16[32,768]{1,0:T(8,128)(2,1)} %get-tuple-element.19), channel_id=2, replica_groups={{0,320},{128,448},{256,64},{384,192},{1,321},{129,449},{257,65},{385,19..., dimensions={0}, use_global_device_ids=true | all-gather | bytes 147456 | tf_op jit(solution)/shard_map/all_gather | solution.py:443
  29.2 3.3 %all-to-all-done = bf16[32,8,960]{2,1,0:T(8,128)(2,1)S(1)} async-done(((bf16[32,8,960]{2,1,0:T(8,128)(2,1)}), bf16[32,8,960]{2,1,0:T(8,128)(2,1)S(1)}, u32[]{:S(2)}, u32[]{:S(2)}) %all-to-all-start) | async-done | bytes 491552 | tf_op jit(solution)/shard_map/all_to_all | solution.py:21
  32.5 4.6 %all-gather.1 = bf16[64,8,960]{2,1,0:T(8,128)(2,1)S(1)} all-gather(bf16[32,8,960]{2,1,0:T(8,128)(2,1)S(1)} %all-to-all-done), channel_id=3, replica_groups=mesh['t'=4,'h'=2,'z'=8,'x'=4,'c'=2] {'c'}, dimensions={0}, use_global_device_ids=true | all-gather | bytes 1474560 | tf_op jit(solution)/shard_map/all_gather | solution.py:440
  37.8 1.7 %shard_map.104 = bf16[192,640]{1,0:T(8,128)(2,1)} custom-call(s32[4]{0:T(128)S(1)} %copy-done.3, bf16[32,768]{1,0:T(8,128)(2,1)S(1)} %copy-done, bf16[64,768]{1,0:T(8,128)(2,1)S(1)} %all-gather.theirs_ref, bf16[512,960]{1,0:T(8,128)(2,1)S(1)} %bitcast.33), custom_call_target="tpu_custom_call" | custom-call | tf_op jit(solution)/shard_map/pallas_call | solution.py:32
  39.5 6.8 %all-to-all-start.1 = ((bf16[8,24,640]{2,1,0:T(8,128)(2,1)}), bf16[8,24,640]{2,1,0:T(8,128)(2,1)S(1)}, u32[]{:S(2)}, u32[]{:S(2)}) async-start(bf16[8,24,640]{2,1,0:T(8,128)(2,1)} %bitcast.5), calls=%async_computation.1 | async-start | bytes 491520 | tf_op jit(solution)/shard_map/all_to_all | solution.py:21
  46.5 10.4 %all-to-all-done.1 = bf16[8,24,640]{2,1,0:T(8,128)(2,1)S(1)} async-done(((bf16[8,24,640]{2,1,0:T(8,128)(2,1)}), bf16[8,24,640]{2,1,0:T(8,128)(2,1)S(1)}, u32[]{:S(2)}, u32[]{:S(2)}) %all-to-all-start.1) | async-done | bytes 245792 | tf_op jit(solution)/shard_map/all_to_all | solution.py:21
  58.6 5.2 %all-to-all-start.2 = ((bf16[32,8,1024]{2,1,0:T(8,128)(2,1)}), bf16[32,8,1024]{2,1,0:T(8,128)(2,1)S(1)}, u32[]{:S(2)}, u32[]{:S(2)}) async-start(bf16[32,8,1024]{2,1,0:T(8,128)(2,1)} %bitcast.8), calls=%async_computation.2 | async-start | bytes 1048576 | tf_op jit(solution)/shard_map/all_to_all | solution.py:21
  67.1 2.8 %collective-permute-start = (bf16[512,480]{1,0:T(8,128)(2,1)}, bf16[512,480]{1,0:T(8,128)(2,1)S(1)}, u32[]{:S(2)}, u32[]{:S(2)}) collective-permute-start(bf16[512,480]{1,0:T(8,128)(2,1)} %copy.43), channel_id=1, source_target_pairs={{0,64},{64,0},{1,65},{65,1},{2,66},{66,2},{3,67},{67,3},{4,68},{68... | collective-permute-start | bytes 1474568 | tf_op jit(solution)/shard_map/ppermute | solution.py:472
  69.9 8.4 %all-to-all-done.2 = bf16[32,8,1024]{2,1,0:T(8,128)(2,1)S(1)} async-done(((bf16[32,8,1024]{2,1,0:T(8,128)(2,1)}), bf16[32,8,1024]{2,1,0:T(8,128)(2,1)S(1)}, u32[]{:S(2)}, u32[]{:S(2)}) %all-to-all-start.2) | async-done | bytes 524320 | tf_op jit(solution)/shard_map/all_to_all | solution.py:21
  78.4 6.1 %all-gather.2 = bf16[32,8,1024]{2,1,0:T(8,128)(2,1)S(1)} all-gather(bf16[16,8,1024]{2,1,0:T(8,128)(2,1)S(1)} %get-tuple-element.36), channel_id=4, replica_groups=mesh['t'=4,'h'=2,'z'=8,'x'=4,'c'=2] {'c'}, dimensions={0}, use_global_device_ids=true | all-gather | bytes 786432 | tf_op jit(solution)/shard_map/all_gather | solution.py:26
  84.4 2.2 %all-gather.3 = bf16[32,8,1024]{2,1,0:T(8,128)(2,1)S(1)} all-gather(bf16[16,8,1024]{2,1,0:T(8,128)(2,1)S(1)} %get-tuple-element.35), channel_id=5, replica_groups=mesh['t'=4,'h'=2,'z'=8,'x'=4,'c'=2] {'c'}, dimensions={0}, use_global_device_ids=true | all-gather | bytes 786432 | tf_op jit(solution)/shard_map/all_gather | solution.py:26
  86.8 2.1 %shard_map.106 = (f32[48,512]{1,0:T(8,128)S(1)}, f32[256,128]{1,0:T(8,128)}) custom-call(s32[4]{0:T(128)S(1)} %copy-done.3, f32[1]{0:T(128)S(6)} %copy.52.logit_ref, bf16[48,1280]{1,0:T(8,128)(2,1)S(1)} %get-tuple-element.20.rows_ref, bf16[256,1024]{1,0:T(8,128)(2,1)S(1)} %bitcast.36, bf16[256,1024]{1,0:T(8,128)(2,1)S(1)} %bitcast.38, ...), custom_call_target="tpu_custom_call" | custom-call | tf_op jit(solution)/shard_map/pallas_call | solution.py:32
  89.0 5.0 %all-to-all-start.3 = ((f32[64,4,128]{2,1,0:T(4,128)}), f32[64,4,128]{2,1,0:T(4,128)S(1)}, u32[]{:S(2)}, u32[]{:S(2)}) async-start(f32[64,4,128]{2,1,0:T(4,128)} %bitcast.12), calls=%async_computation.3 | async-start | bytes 262144 | tf_op jit(solution)/shard_map/all_to_all | solution.py:21
  94.3 1.9 %collective-permute-done.other_ref = bf16[512,480]{1,0:T(8,128)(2,1)S(1)} collective-permute-done((bf16[512,480]{1,0:T(8,128)(2,1)}, bf16[512,480]{1,0:T(8,128)(2,1)S(1)}, u32[]{:S(2)}, u32[]{:S(2)}) %collective-permute-start) | collective-permute-done | bytes 491552 | tf_op jit(solution)/shard_map/ppermute | solution.py:472
  96.2 8.9 %all-to-all-done.3 = f32[64,4,128]{2,1,0:T(4,128)S(1)} async-done(((f32[64,4,128]{2,1,0:T(4,128)}), f32[64,4,128]{2,1,0:T(4,128)S(1)}, u32[]{:S(2)}, u32[]{:S(2)}) %all-to-all-start.3) | async-done | bytes 131104 | tf_op jit(solution)/shard_map/all_to_all | solution.py:21
  105.1 2.0 %shard_map.107 = bf16[384,384]{1,0:T(8,128)(2,1)} custom-call(s32[4]{0:T(128)S(1)} %copy-done.3, f32[1]{0:T(128)S(6)} %copy.52.logit_ref, f32[48,512]{1,0:T(8,128)S(1)} %get-tuple-element.23.scores_ref, f32[256,128]{1,0:T(8,128)S(1)} %bitcast.45, s32[48,1]{1,0:T(8,128)S(1)} %convert_element_type.40.row_pos_ref, ...), custom_call_target="tpu_custom_call" | custom-call | tf_op jit(solution)/shard_map/pallas_call | solution.py:32
  107.2 3.4 %all-to-all-start.4 = ((bf16[8,48,384]{2,1,0:T(8,128)(2,1)}), bf16[8,48,384]{2,1,0:T(8,128)(2,1)S(1)}, u32[]{:S(2)}, u32[]{:S(2)}) async-start(bf16[8,48,384]{2,1,0:T(8,128)(2,1)} %bitcast.18), calls=%async_computation.4 | async-start | bytes 589824 | tf_op jit(solution)/shard_map/all_to_all | solution.py:21
  110.7 12.9 %all-to-all-done.4 = bf16[8,48,384]{2,1,0:T(8,128)(2,1)S(1)} async-done(((bf16[8,48,384]{2,1,0:T(8,128)(2,1)}), bf16[8,48,384]{2,1,0:T(8,128)(2,1)S(1)}, u32[]{:S(2)}, u32[]{:S(2)}) %all-to-all-start.4) | async-done | bytes 294944 | tf_op jit(solution)/shard_map/all_to_all | solution.py:21
  123.6 2.4 %shard_map.108 = (bf16[128,768]{1,0:T(8,128)(2,1)}, f32[8,128]{1,0:T(8,128)S(1)}) custom-call(s32[4]{0:T(128)S(1)} %copy-done.3, bf16[384,384]{1,0:T(8,128)(2,1)S(1)} %bitcast.42, bf16[48,160]{1,0:T(8,128)(2,1)S(1)} %constant_dynamic-slice_fusion.2.unit_ref, bf16[512,960]{1,0:T(8,128)(2,1)S(1)} %bitcast.35, bf16[512,480]{1,0:T(8,128)(2,1)S(1)} %collective-permute-done.other_ref), custom_call_target="tpu_custom_call" | custom-call | tf_op jit(solution)/shard_map/pallas_call | solution.py:32
  126.0 3.4 %all-to-all-start.5 = ((bf16[8,16,768]{2,1,0:T(8,128)(2,1)}), bf16[8,16,768]{2,1,0:T(8,128)(2,1)S(1)}, u32[]{:S(2)}, u32[]{:S(2)}) async-start(bf16[8,16,768]{2,1,0:T(8,128)(2,1)} %bitcast.21), calls=%async_computation.5 | async-start | bytes 393216 | tf_op jit(solution)/shard_map/all_to_all | solution.py:21
  132.0 7.0 %all-to-all-done.5 = bf16[8,16,768]{2,1,0:T(8,128)(2,1)S(1)} async-done(((bf16[8,16,768]{2,1,0:T(8,128)(2,1)}), bf16[8,16,768]{2,1,0:T(8,128)(2,1)S(1)}, u32[]{:S(2)}, u32[]{:S(2)}) %all-to-all-start.5) | async-done | bytes 196640 | tf_op jit(solution)/shard_map/all_to_all | solution.py:21
  139.0 2.0 %shard_map.109 = (bf16[144,1664]{1,0:T(8,128)(2,1)}, bf16[192,1280]{1,0:T(8,128)(2,1)}) custom-call(bf16[128,768]{1,0:T(8,128)(2,1)S(1)} %bitcast.44, f32[8,128]{1,0:T(8,128)S(1)} %get-tuple-element.30.inv_ref, bf16[144,1664]{1,0:T(8,128)(2,1)S(1)} %bitcast.41, bf16[192,1280]{1,0:T(8,128)(2,1)S(1)} %bitcast.40, f32[1664]{0:T(1024)S(1)} %copy-done.1, ...), custom_call_target="tpu_custom_call" | custom-call | tf_op jit(solution)/shard_map/pallas_call | solution.py:32
  (56 shorter events, 11.0 us)
Async XLA Ops:
  2.5 30.0 %all-to-all-start = ((bf16[32,8,960]{2,1,0:T(8,128)(2,1)}), bf16[32,8,960]{2,1,0:T(8,128)(2,1)S(1)}, u32[]{:S(2)}, u32[]{:S(2)}) async-start(bf16[32,8,960]{2,1,0:T(8,128)(2,1)} %broadcast_in_dim.39), calls=%async_computation | async-start | bytes 1048576 | tf_op jit(solution)/shard_map/all_to_all | solution.py:21
  16.8 12.3 %copy-start.4 = (s32[12]{0:T(128)S(1)}, s32[12]{0:T(128)}, u32[]{:S(2)}) copy-start(s32[12]{0:T(128)} %pos_ref.1) | copy-start | bytes 148
  16.8 20.2 %copy-start.3 = (s32[4]{0:T(128)S(1)}, s32[4]{0:T(128)}, u32[]{:S(2)}) copy-start(s32[4]{0:T(128)} %pad_add_fusion.place_ref) | copy-start | bytes 52
  37.0 0.8 copy-start
  39.5 17.4 %all-to-all-start.1 = ((bf16[8,24,640]{2,1,0:T(8,128)(2,1)}), bf16[8,24,640]{2,1,0:T(8,128)(2,1)S(1)}, u32[]{:S(2)}, u32[]{:S(2)}) async-start(bf16[8,24,640]{2,1,0:T(8,128)(2,1)} %bitcast.5), calls=%async_computation.1 | async-start | bytes 491520 | tf_op jit(solution)/shard_map/all_to_all | solution.py:21
  58.6 19.8 %all-to-all-start.2 = ((bf16[32,8,1024]{2,1,0:T(8,128)(2,1)}), bf16[32,8,1024]{2,1,0:T(8,128)(2,1)S(1)}, u32[]{:S(2)}, u32[]{:S(2)}) async-start(bf16[32,8,1024]{2,1,0:T(8,128)(2,1)} %bitcast.8), calls=%async_computation.2 | async-start | bytes 1048576 | tf_op jit(solution)/shard_map/all_to_all | solution.py:21
  67.1 29.1 %collective-permute-start = (bf16[512,480]{1,0:T(8,128)(2,1)}, bf16[512,480]{1,0:T(8,128)(2,1)S(1)}, u32[]{:S(2)}, u32[]{:S(2)}) collective-permute-start(bf16[512,480]{1,0:T(8,128)(2,1)} %copy.43), channel_id=1, source_target_pairs={{0,64},{64,0},{1,65},{65,1},{2,66},{66,2},{3,67},{67,3},{4,68},{68... | collective-permute-start | bytes 1474568 | tf_op jit(solution)/shard_map/ppermute | solution.py:472
  89.0 16.2 %all-to-all-start.3 = ((f32[64,4,128]{2,1,0:T(4,128)}), f32[64,4,128]{2,1,0:T(4,128)S(1)}, u32[]{:S(2)}, u32[]{:S(2)}) async-start(f32[64,4,128]{2,1,0:T(4,128)} %bitcast.12), calls=%async_computation.3 | async-start | bytes 262144 | tf_op jit(solution)/shard_map/all_to_all | solution.py:21
  107.2 16.4 %all-to-all-start.4 = ((bf16[8,48,384]{2,1,0:T(8,128)(2,1)}), bf16[8,48,384]{2,1,0:T(8,128)(2,1)S(1)}, u32[]{:S(2)}, u32[]{:S(2)}) async-start(bf16[8,48,384]{2,1,0:T(8,128)(2,1)} %bitcast.18), calls=%async_computation.4 | async-start | bytes 589824 | tf_op jit(solution)/shard_map/all_to_all | solution.py:21
  123.6 15.4 %copy-start.1 = (f32[1664]{0:T(1024)S(1)}, f32[1664]{0:T(1024)}, u32[]{:S(2)}) copy-start(f32[1664]{0:T(1024)} %ig_ref.3) | copy-start | bytes 19972
  123.6 15.4 %copy-start.2 = (f32[1280]{0:T(1024)S(1)}, f32[1280]{0:T(1024)}, u32[]{:S(2)}) copy-start(f32[1280]{0:T(1024)} %tg_ref.3) | copy-start | bytes 15364
  126.0 13.0 %all-to-all-start.5 = ((bf16[8,16,768]{2,1,0:T(8,128)(2,1)}), bf16[8,16,768]{2,1,0:T(8,128)(2,1)S(1)}, u32[]{:S(2)}, u32[]{:S(2)}) async-start(bf16[8,16,768]{2,1,0:T(8,128)(2,1)} %bitcast.21), calls=%async_computation.5 | async-start | bytes 393216 | tf_op jit(solution)/shard_map/all_to_all | solution.py:21

commit v16 on v15

--- a/solution.py
+++ b/solution.py
@@ -52,7 +52,7 @@
 
 
 def pool_kernel(
-    place_ref,
+    h_ref,
     pos_ref,
     img_ref,
     txt_ref,
@@ -117,12 +117,12 @@
     blank = jnp.zeros_like(line)
     line = jnp.concatenate([line, blank, line, blank], 0)
     found = jnp.concatenate([found[:, :512], found[:, 512:640] + line, found[:, 640:]], 1)
-    first = place_ref[1] == 0
+    first = h_ref[0] == 0
     mine_ref[...] = jnp.where(first, found[:32], found[32:]).astype(BF)
     theirs_ref[...] = jnp.where(first, found[32:], found[:32]).astype(BF)
 
 
-def pool_call(place, image_in, text_in, img_gain, txt_gain, positive):
+def pool_call(h_index, image_in, text_in, img_gain, txt_gain, positive):
     pairs, _, width_i = image_in.shape
     width_t = text_in.shape[2]
     vmem = pl.BlockSpec(memory_space=pltpu.VMEM)
@@ -147,7 +147,7 @@
             transcendentals=0,
         ),
         compiler_params=pltpu.CompilerParams(vmem_limit_bytes=60 * 1024 * 1024),
-    )(place, positive, image_in, text_in, img_gain, txt_gain)
+    )(h_index.astype(jnp.int32).reshape(1), positive, image_in, text_in, img_gain, txt_gain)
 
 
 def weight_quarter(w_ref, a):
@@ -379,15 +379,10 @@
         return jnp.where(is_img, pool, pltpu.roll(pool, 45, 0))
 
     own, other = [], []
-    for a in range(2):
-        quarter = weight_quarter(w_ref, a)
-        columns = []
-        for j in range(3):
-            pair = quarter[:, 2 * width * j : 2 * width * j + 2 * width]
-            columns.append(jnp.where(first, pair[:, :width], pair[:, width:]))
-        own.append(features(columns))
-        quarter = weight_quarter(other_ref, a)
-        other.append(features([quarter[:, width * j : width * j + width] for j in range(3)]))
+    for out, ref in ((own, w_ref), (other, other_ref)):
+        for a in range(2):
+            quarter = weight_quarter(ref, a)
+            out.append(features([quarter[:, width * j : width * j + width] for j in range(3)]))
     mixed = [jnp.where(first, x, y) for x, y in zip(own + other, other + own)]
     blank = jnp.zeros((1, 768), F32)
     pieces = []
@@ -439,7 +434,7 @@
     w = jnp.broadcast_to(w[None], (32, 8, 3 * width))
     w = lax.all_gather(exchange(w, ZX), "c", axis=0).reshape(512, 3 * width)
 
-    mine, theirs = pool_call(place, image_in, text_in, img_gain, txt_gain, positive)
+    mine, theirs = pool_call(h_index, image_in, text_in, img_gain, txt_gain, positive)
     theirs = lax.all_gather(theirs, Y, axis=0, axis_index_groups=[[0, 6], [1, 7], [2, 4], [3, 5]])
     row_pos = theirs[:, :12, 519].astype(F32) * 32.0 + theirs[:, :12, 527].astype(F32)
     is_mine = lax.iota(jnp.int32, 2)[:, None] == h_index
@@ -469,6 +464,7 @@
     w_held, far = lax.optimization_barrier((w, far))
     parts = w_held.reshape(512, 3, 2, half)
     w_other = jnp.where(h_index == 0, parts[:, :, 1], parts[:, :, 0]).reshape(512, 3 * half)
+    w_own = jnp.where(h_index == 0, parts[:, :, 0], parts[:, :, 1]).reshape(512, 3 * half)
     w_other = lax.ppermute(w_other, "h", [(0, 1), (1, 0)])
     fa, fb = both_cores(exchange(far.reshape(32, 8, 1024), ZX))
 
@@ -497,7 +493,7 @@
     pool, loss = kernel_call(
         back_kernel,
         [((128, 768), BF), ((8, 128), F32)],
-        [place, got, unit_part, w, w_other],
+        [place, got, unit_part, w_own, w_other],
         smem=(0,),
     )
     mean_loss = loss[0, :1]

time: 142 us -> 141 us (level)
  no operation moved by 1% of the time
where the time goes in v16:
time: 141 us; the launch traced here: 140 us
  waiting for transfers between devices  53.2 us (38%)
  starting transfers between devices  39.7 us (28%)
  blocking collectives  19.5 us (14%)
  Pallas kernels  17.2 us (12%)
  local copies, waits for them, and re-layouts  7.75 us (5%)
  between operations  1.48 us (1%)
    all_to_all x6, waiting for transfers between devices, exchange(): return lax.all_to_all(blocks, axes, 0, 0, tiled=True)  51.3 us
    all_to_all x6, starting transfers between devices, exchange(): return lax.all_to_all(blocks, axes, 0, 0, tiled=True)  37 us
    pallas_call x6, Pallas kernels, kernel_call(): pl.pallas_call(body, out_shape=[jax.ShapeDtypeStruct(shape, kind) for sha...  11.7 us
    all_gather x2, blocking collectives, both_cores(): lax.all_gather(part, 'c', axis=0)  8.22 us
    all_gather x1, blocking collectives, per_device(): lax.all_gather(theirs, Y, axis=0, axis_index_groups=[[0, 6], [1, 7], [2,...  6.68 us
    pallas_call x1, Pallas kernels, pool_call(): pl.pallas_call(pool_kernel, out_shape=[jax.ShapeDtypeStruct((32, 768), BF...  5.48 us
    all_gather x1, blocking collectives, per_device(): w = lax.all_gather(exchange(w, ZX), 'c', axis=0).reshape(512, 3 * width)  4.56 us
  transfers between devices with their start and end apart: 7, of which 7 were waited for; matrix products, arithmetic and copies ran while one was open for 5% of the time, Pallas kernels for 5%

profile of v16, /device:TPU:1, one launch (start us, length us, event | category | flops | bytes accessed | tf_op | source)
XLA Modules:
  0.0 140.2 jit_solution(7162243415130286385)
XLA Ops:
  2.5 13.7 %all-to-all-start = ((bf16[32,8,960]{2,1,0:T(8,128)(2,1)}), bf16[32,8,960]{2,1,0:T(8,128)(2,1)S(1)}, u32[]{:S(2)}, u32[]{:S(2)}) async-start(bf16[32,8,960]{2,1,0:T(8,128)(2,1)} %broadcast_in_dim.39), calls=%async_computation | async-start | bytes 1048576 | tf_op jit(solution)/shard_map/all_to_all | solution.py:21
  16.2 5.5 %shard_map.103 = (bf16[32,768]{1,0:T(8,128)(2,1)}, bf16[32,768]{1,0:T(8,128)(2,1)}) custom-call(s32[1]{0:T(128)} %bitcast.1.h_ref, s32[12]{0:T(128)} %pos_ref.1, bf16[12,48,1664]{2,1,0:T(8,128)(2,1)} %img_ref.1, bf16[12,64,1280]{2,1,0:T(8,128)(2,1)} %txt_ref.1, f32[1664]{0:T(1024)} %ig_ref.3, f32[1280]{0:T(1024)} %tg_ref.3), custom_call_target="tpu_custom_call" | custom-call | flops 19415040 | bytes 3883008 | tf_op jit(solution)/shard_map/pallas_call | solution.py:131
  21.7 6.7 %all-gather.theirs_ref = bf16[64,768]{1,0:T(8,128)(2,1)S(1)} all-gather(bf16[32,768]{1,0:T(8,128)(2,1)} %get-tuple-element.19), channel_id=2, replica_groups={{0,320},{128,448},{256,64},{384,192},{1,321},{129,449},{257,65},{385,19..., dimensions={0}, use_global_device_ids=true | all-gather | bytes 147456 | tf_op jit(solution)/shard_map/all_gather | solution.py:438
  28.6 3.9 %all-to-all-done = bf16[32,8,960]{2,1,0:T(8,128)(2,1)S(1)} async-done(((bf16[32,8,960]{2,1,0:T(8,128)(2,1)}), bf16[32,8,960]{2,1,0:T(8,128)(2,1)S(1)}, u32[]{:S(2)}, u32[]{:S(2)}) %all-to-all-start) | async-done | bytes 491552 | tf_op jit(solution)/shard_map/all_to_all | solution.py:21
  32.5 4.6 %all-gather.1 = bf16[64,8,960]{2,1,0:T(8,128)(2,1)S(1)} all-gather(bf16[32,8,960]{2,1,0:T(8,128)(2,1)S(1)} %all-to-all-done), channel_id=3, replica_groups=mesh['t'=4,'h'=2,'z'=8,'x'=4,'c'=2] {'c'}, dimensions={0}, use_global_device_ids=true | all-gather | bytes 1474560 | tf_op jit(solution)/shard_map/all_gather | solution.py:435
  37.8 1.7 %shard_map.104 = bf16[192,640]{1,0:T(8,128)(2,1)} custom-call(s32[4]{0:T(128)S(1)} %pad_add_fusion.place_ref, bf16[32,768]{1,0:T(8,128)(2,1)S(1)} %copy-done, bf16[64,768]{1,0:T(8,128)(2,1)S(1)} %all-gather.theirs_ref, bf16[512,960]{1,0:T(8,128)(2,1)S(1)} %bitcast.34), custom_call_target="tpu_custom_call" | custom-call | tf_op jit(solution)/shard_map/pallas_call | solution.py:32
  39.5 6.8 %all-to-all-start.1 = ((bf16[8,24,640]{2,1,0:T(8,128)(2,1)}), bf16[8,24,640]{2,1,0:T(8,128)(2,1)S(1)}, u32[]{:S(2)}, u32[]{:S(2)}) async-start(bf16[8,24,640]{2,1,0:T(8,128)(2,1)} %bitcast.5), calls=%async_computation.1 | async-start | bytes 491520 | tf_op jit(solution)/shard_map/all_to_all | solution.py:21
  46.4 10.4 %all-to-all-done.1 = bf16[8,24,640]{2,1,0:T(8,128)(2,1)S(1)} async-done(((bf16[8,24,640]{2,1,0:T(8,128)(2,1)}), bf16[8,24,640]{2,1,0:T(8,128)(2,1)S(1)}, u32[]{:S(2)}, u32[]{:S(2)}) %all-to-all-start.1) | async-done | bytes 245792 | tf_op jit(solution)/shard_map/all_to_all | solution.py:21
  58.5 4.6 %all-to-all-start.2 = ((bf16[32,8,1024]{2,1,0:T(8,128)(2,1)}), bf16[32,8,1024]{2,1,0:T(8,128)(2,1)S(1)}, u32[]{:S(2)}, u32[]{:S(2)}) async-start(bf16[32,8,1024]{2,1,0:T(8,128)(2,1)} %bitcast.8), calls=%async_computation.2 | async-start | bytes 1048576 | tf_op jit(solution)/shard_map/all_to_all | solution.py:21
  66.5 2.8 %collective-permute-start = (bf16[512,480]{1,0:T(8,128)(2,1)}, bf16[512,480]{1,0:T(8,128)(2,1)S(1)}, u32[]{:S(2)}, u32[]{:S(2)}) collective-permute-start(bf16[512,480]{1,0:T(8,128)(2,1)} %copy.44), channel_id=1, source_target_pairs={{0,64},{64,0},{1,65},{65,1},{2,66},{66,2},{3,67},{67,3},{4,68},{68... | collective-permute-start | bytes 1474568 | tf_op jit(solution)/shard_map/ppermute | solution.py:468
  69.3 8.4 %all-to-all-done.2 = bf16[32,8,1024]{2,1,0:T(8,128)(2,1)S(1)} async-done(((bf16[32,8,1024]{2,1,0:T(8,128)(2,1)}), bf16[32,8,1024]{2,1,0:T(8,128)(2,1)S(1)}, u32[]{:S(2)}, u32[]{:S(2)}) %all-to-all-start.2) | async-done | bytes 524320 | tf_op jit(solution)/shard_map/all_to_all | solution.py:21
  77.8 6.1 %all-gather.2 = bf16[32,8,1024]{2,1,0:T(8,128)(2,1)S(1)} all-gather(bf16[16,8,1024]{2,1,0:T(8,128)(2,1)S(1)} %get-tuple-element.38), channel_id=4, replica_groups=mesh['t'=4,'h'=2,'z'=8,'x'=4,'c'=2] {'c'}, dimensions={0}, use_global_device_ids=true | all-gather | bytes 786432 | tf_op jit(solution)/shard_map/all_gather | solution.py:26
  83.8 2.2 %all-gather.3 = bf16[32,8,1024]{2,1,0:T(8,128)(2,1)S(1)} all-gather(bf16[16,8,1024]{2,1,0:T(8,128)(2,1)S(1)} %get-tuple-element.37), channel_id=5, replica_groups=mesh['t'=4,'h'=2,'z'=8,'x'=4,'c'=2] {'c'}, dimensions={0}, use_global_device_ids=true | all-gather | bytes 786432 | tf_op jit(solution)/shard_map/all_gather | solution.py:26
  86.2 2.1 %shard_map.106 = (f32[48,512]{1,0:T(8,128)S(1)}, f32[256,128]{1,0:T(8,128)}) custom-call(s32[4]{0:T(128)S(1)} %pad_add_fusion.place_ref, f32[1]{0:T(128)S(6)} %copy.54.logit_ref, bf16[48,1280]{1,0:T(8,128)(2,1)S(1)} %get-tuple-element.20.rows_ref, bf16[256,1024]{1,0:T(8,128)(2,1)S(1)} %bitcast.36, bf16[256,1024]{1,0:T(8,128)(2,1)S(1)} %bitcast.38, ...), custom_call_target="tpu_custom_call" | custom-call | tf_op jit(solution)/shard_map/pallas_call | solution.py:32
  88.4 5.0 %all-to-all-start.3 = ((f32[64,4,128]{2,1,0:T(4,128)}), f32[64,4,128]{2,1,0:T(4,128)S(1)}, u32[]{:S(2)}, u32[]{:S(2)}) async-start(f32[64,4,128]{2,1,0:T(4,128)} %bitcast.12), calls=%async_computation.3 | async-start | bytes 262144 | tf_op jit(solution)/shard_map/all_to_all | solution.py:21
  93.7 1.9 %collective-permute-done.other_ref = bf16[512,480]{1,0:T(8,128)(2,1)S(1)} collective-permute-done((bf16[512,480]{1,0:T(8,128)(2,1)}, bf16[512,480]{1,0:T(8,128)(2,1)S(1)}, u32[]{:S(2)}, u32[]{:S(2)}) %collective-permute-start) | collective-permute-done | bytes 491552 | tf_op jit(solution)/shard_map/ppermute | solution.py:468
  95.6 8.9 %all-to-all-done.3 = f32[64,4,128]{2,1,0:T(4,128)S(1)} async-done(((f32[64,4,128]{2,1,0:T(4,128)}), f32[64,4,128]{2,1,0:T(4,128)S(1)}, u32[]{:S(2)}, u32[]{:S(2)}) %all-to-all-start.3) | async-done | bytes 131104 | tf_op jit(solution)/shard_map/all_to_all | solution.py:21
  104.5 2.0 %shard_map.107 = bf16[384,384]{1,0:T(8,128)(2,1)} custom-call(s32[4]{0:T(128)S(1)} %pad_add_fusion.place_ref, f32[1]{0:T(128)S(6)} %copy.54.logit_ref, f32[48,512]{1,0:T(8,128)S(1)} %get-tuple-element.23.scores_ref, f32[256,128]{1,0:T(8,128)S(1)} %bitcast.45, s32[48,1]{1,0:T(8,128)S(1)} %convert_element_type.40.row_pos_ref, ...), custom_call_target="tpu_custom_call" | custom-call | tf_op jit(solution)/shard_map/pallas_call | solution.py:32
  106.5 3.4 %all-to-all-start.4 = ((bf16[8,48,384]{2,1,0:T(8,128)(2,1)}), bf16[8,48,384]{2,1,0:T(8,128)(2,1)S(1)}, u32[]{:S(2)}, u32[]{:S(2)}) async-start(bf16[8,48,384]{2,1,0:T(8,128)(2,1)} %bitcast.18), calls=%async_computation.4 | async-start | bytes 589824 | tf_op jit(solution)/shard_map/all_to_all | solution.py:21
  110.3 12.6 %all-to-all-done.4 = bf16[8,48,384]{2,1,0:T(8,128)(2,1)S(1)} async-done(((bf16[8,48,384]{2,1,0:T(8,128)(2,1)}), bf16[8,48,384]{2,1,0:T(8,128)(2,1)S(1)}, u32[]{:S(2)}, u32[]{:S(2)}) %all-to-all-start.4) | async-done | bytes 294944 | tf_op jit(solution)/shard_map/all_to_all | solution.py:21
  122.9 2.2 %shard_map.108 = (bf16[128,768]{1,0:T(8,128)(2,1)}, f32[8,128]{1,0:T(8,128)S(1)}) custom-call(s32[4]{0:T(128)S(1)} %pad_add_fusion.place_ref, bf16[384,384]{1,0:T(8,128)(2,1)S(1)} %bitcast.42, bf16[48,160]{1,0:T(8,128)(2,1)S(1)} %constant_dynamic-slice_fusion.2.unit_ref, bf16[512,480]{1,0:T(8,128)(2,1)S(1)} %copy.49.w_ref, ...), custom_call_target="tpu_custom_call" | custom-call | tf_op jit(solution)/shard_map/pallas_call | solution.py:32
  125.1 3.4 %all-to-all-start.5 = ((bf16[8,16,768]{2,1,0:T(8,128)(2,1)}), bf16[8,16,768]{2,1,0:T(8,128)(2,1)S(1)}, u32[]{:S(2)}, u32[]{:S(2)}) async-start(bf16[8,16,768]{2,1,0:T(8,128)(2,1)} %bitcast.22), calls=%async_computation.5 | async-start | bytes 393216 | tf_op jit(solution)/shard_map/all_to_all | solution.py:21
  131.2 7.0 %all-to-all-done.5 = bf16[8,16,768]{2,1,0:T(8,128)(2,1)S(1)} async-done(((bf16[8,16,768]{2,1,0:T(8,128)(2,1)}), bf16[8,16,768]{2,1,0:T(8,128)(2,1)S(1)}, u32[]{:S(2)}, u32[]{:S(2)}) %all-to-all-start.5) | async-done | bytes 196640 | tf_op jit(solution)/shard_map/all_to_all | solution.py:21
  138.2 2.0 %shard_map.109 = (bf16[144,1664]{1,0:T(8,128)(2,1)}, bf16[192,1280]{1,0:T(8,128)(2,1)}) custom-call(bf16[128,768]{1,0:T(8,128)(2,1)S(1)} %bitcast.44, f32[8,128]{1,0:T(8,128)S(1)} %get-tuple-element.30.inv_ref, bf16[144,1664]{1,0:T(8,128)(2,1)S(1)} %bitcast.41, bf16[192,1280]{1,0:T(8,128)(2,1)S(1)} %bitcast.40, f32[1664]{0:T(1024)S(1)} %copy-done.1, ...), custom_call_target="tpu_custom_call" | custom-call | tf_op jit(solution)/shard_map/pallas_call | solution.py:32
  (55 shorter events, 10.7 us)
Async XLA Ops:
  2.5 30.0 %all-to-all-start = ((bf16[32,8,960]{2,1,0:T(8,128)(2,1)}), bf16[32,8,960]{2,1,0:T(8,128)(2,1)S(1)}, u32[]{:S(2)}, u32[]{:S(2)}) async-start(bf16[32,8,960]{2,1,0:T(8,128)(2,1)} %broadcast_in_dim.39), calls=%async_computation | async-start | bytes 1048576 | tf_op jit(solution)/shard_map/all_to_all | solution.py:21
  16.2 12.3 %copy-start.3 = (s32[12]{0:T(128)S(1)}, s32[12]{0:T(128)}, u32[]{:S(2)}) copy-start(s32[12]{0:T(128)} %pos_ref.1) | copy-start | bytes 148
  37.0 0.8 copy-start
  39.5 17.4 %all-to-all-start.1 = ((bf16[8,24,640]{2,1,0:T(8,128)(2,1)}), bf16[8,24,640]{2,1,0:T(8,128)(2,1)S(1)}, u32[]{:S(2)}, u32[]{:S(2)}) async-start(bf16[8,24,640]{2,1,0:T(8,128)(2,1)} %bitcast.5), calls=%async_computation.1 | async-start | bytes 491520 | tf_op jit(solution)/shard_map/all_to_all | solution.py:21
  58.5 19.2 %all-to-all-start.2 = ((bf16[32,8,1024]{2,1,0:T(8,128)(2,1)}), bf16[32,8,1024]{2,1,0:T(8,128)(2,1)S(1)}, u32[]{:S(2)}, u32[]{:S(2)}) async-start(bf16[32,8,1024]{2,1,0:T(8,128)(2,1)} %bitcast.8), calls=%async_computation.2 | async-start | bytes 1048576 | tf_op jit(solution)/shard_map/all_to_all | solution.py:21
  66.5 29.1 %collective-permute-start = (bf16[512,480]{1,0:T(8,128)(2,1)}, bf16[512,480]{1,0:T(8,128)(2,1)S(1)}, u32[]{:S(2)}, u32[]{:S(2)}) collective-permute-start(bf16[512,480]{1,0:T(8,128)(2,1)} %copy.44), channel_id=1, source_target_pairs={{0,64},{64,0},{1,65},{65,1},{2,66},{66,2},{3,67},{67,3},{4,68},{68... | collective-permute-start | bytes 1474568 | tf_op jit(solution)/shard_map/ppermute | solution.py:468
  88.4 16.2 %all-to-all-start.3 = ((f32[64,4,128]{2,1,0:T(4,128)}), f32[64,4,128]{2,1,0:T(4,128)S(1)}, u32[]{:S(2)}, u32[]{:S(2)}) async-start(f32[64,4,128]{2,1,0:T(4,128)} %bitcast.12), calls=%async_computation.3 | async-start | bytes 262144 | tf_op jit(solution)/shard_map/all_to_all | solution.py:21
  106.5 16.4 %all-to-all-start.4 = ((bf16[8,48,384]{2,1,0:T(8,128)(2,1)}), bf16[8,48,384]{2,1,0:T(8,128)(2,1)S(1)}, u32[]{:S(2)}, u32[]{:S(2)}) async-start(bf16[8,48,384]{2,1,0:T(8,128)(2,1)} %bitcast.18), calls=%async_computation.4 | async-start | bytes 589824 | tf_op jit(solution)/shard_map/all_to_all | solution.py:21
  110.2 28.0 %copy-start.1 = (f32[1664]{0:T(1024)S(1)}, f32[1664]{0:T(1024)}, u32[]{:S(2)}) copy-start(f32[1664]{0:T(1024)} %ig_ref.3) | copy-start | bytes 19972
  110.2 28.0 %copy-start.2 = (f32[1280]{0:T(1024)S(1)}, f32[1280]{0:T(1024)}, u32[]{:S(2)}) copy-start(f32[1280]{0:T(1024)} %tg_ref.3) | copy-start | bytes 15364
  125.1 13.0 %all-to-all-start.5 = ((bf16[8,16,768]{2,1,0:T(8,128)(2,1)}), bf16[8,16,768]{2,1,0:T(8,128)(2,1)S(1)}, u32[]{:S(2)}, u32[]{:S(2)}) async-start(bf16[8,16,768]{2,1,0:T(8,128)(2,1)} %bitcast.22), calls=%async_computation.5 | async-start | bytes 393216 | tf_op jit(solution)/shard_map/all_to_all | solution.py:21
